TPU v7x, 256 devices: a whole 4x4x8 slice. The times are simulated.
256 devices in a mesh: sec: 32 (over z, x), tile: 8 (over y, core).
Axes of the slice: x: 4, y: 4, z: 8, core: 2. Of those that a mesh axis runs over, the one named last changes fastest.
Arguments:
- ov_first: int32 [32768], P(('sec', 'tile')), may hold values from 0 to 8191, as said below
- ov_second: int32 [32768], P(('sec', 'tile')), may hold values from 0 to 8191, as said below
- match_count: int32 [32768], P(('sec', 'tile')), may hold values from 1 to 32, as said below
- cell_first: int32 [32, 32768], P(None, ('sec', 'tile')), may hold values from 0 to 48
- cell_second: int32 [32, 32768], P(None, ('sec', 'tile')), may hold values from 0 to 48
- frac_first: float32 [2, 32, 32768], P(None, None, ('sec', 'tile')), may hold values from 0 to 1
- frac_second: float32 [2, 32, 32768], P(None, None, ('sec', 'tile')), may hold values from 0 to 1
- target: float32 [2, 32, 32768], P(None, None, ('sec', 'tile')), may hold values from -6 to 6
- stiffness: float32 [256, 32], P('tile', 'sec'), may hold values from 0.3 to 3
Outputs:
- solution_field: float32 [256, 32, 128], P('tile', 'sec')
- residual: float32 [256, 32, 128], P('tile', 'sec')
Inputs may be any that keep to these rules, and one draw needn't show every extreme that they name: `ov_first`: the first tile of each correlation among one device's 128 rows is a tile of that device (tile numbers are tile * 32 + section). `ov_second`: the second tile differs from the first and lies in the same section or in the section numbered one less. `match_count`: the first correlation among each device's rows has all 32 matches live. `cell_first`: cell row * 7 + column of the 7 x 7 cells of a tile's node grid. `cell_second`: cell row * 7 + column of the 7 x 7 cells of a tile's node grid.
All inputs are finite; a program needn't handle non-finite values.
Results may differ from a plain program's by a relative error of at most 0.00017.
Values sent between devices are 32-bit elements; how exact they have to be, the bound alone decides.
No kernel may reach another device: no remote copies, remote signals or barrier semaphores. Data moves between devices by JAX's collectives and lax.ppermute only.
A program may use at most 64 MiB of HBM per device.

v0:
```python
import jax
import jax.numpy as jnp
from jax import lax
from jax.sharding import PartitionSpec as P

ITERS = 4


DAMPING = 0.5
HIGH = lax.Precision.HIGHEST


def shifted(block, axis, distance):
    devices = range(lax.axis_size(axis))
    route = [(i - distance, i) for i in devices if i - distance in devices]
    return lax.ppermute(block, axis, route)


def dense_weights(cell_ids, fraction):
    corner_base = cell_ids // 7 * 8 + cell_ids % 7
    across = fraction[0]
    along = fraction[1]
    node_rows = lax.broadcasted_iota(jnp.int32, (64,) + cell_ids.shape, 0)
    offsets = (0, 1, 8, 9)
    factors = (
        (1.0 - across) * (1.0 - along),
        across * (1.0 - along),
        (1.0 - across) * along,
        across * along,
    )
    table = jnp.zeros((64,) + cell_ids.shape, jnp.float32)
    for corner in range(4):
        table = table + jnp.where(
            node_rows == (corner_base + offsets[corner])[None], factors[corner][None], 0.0
        )
    return table


def sample(picked_rows, table):
    return jnp.stack(
        [
            jnp.einsum(
                "nmo,on->mo",
                table,
                picked_rows[:, component * 64 : (component + 1) * 64],
                precision=HIGH,
            )
            for component in range(2)
        ]
    )


def spread(mismatch, table):
    return jnp.concatenate(
        [
            jnp.einsum("nmo,mo->on", table, mismatch[component], precision=HIGH)
            for component in range(2)
        ],
        1,
    )


def laplace(field_now):
    lane_ids = jnp.arange(128, dtype=jnp.int32)
    has_right = jnp.where(lane_ids % 8 < 7, 1.0, 0.0).astype(jnp.float32)
    has_down = jnp.where(lane_ids // 8 % 8 < 7, 1.0, 0.0).astype(jnp.float32)
    step_right = (jnp.roll(field_now, -1, -1) - field_now) * has_right
    step_down = (jnp.roll(field_now, -8, -1) - field_now) * has_down
    return jnp.roll(step_right, 1, -1) - step_right + jnp.roll(step_down, 8, -1) - step_down


def on_device(
    ov_first,
    ov_second,
    match_count,
    cell_first,
    cell_second,
    frac_first,
    frac_second,
    target,
    stiffness,
):
    tps_dev = stiffness.shape[0]
    sec_dev = stiffness.shape[1]
    sections = sec_dev * lax.axis_size("sec")
    tps_all = tps_dev * lax.axis_size("tile")
    base_tile = lax.axis_index("tile") * tps_dev
    base_sec = lax.axis_index("sec") * sec_dev
    local_first = (ov_first // sections - base_tile) * sec_dev + ov_first % sections - base_sec
    wide_second = ov_second // sections * (sec_dev + 1) + ov_second % sections - base_sec + 1
    num_over = ov_first.shape[0]
    live_mask = (
        lax.broadcasted_iota(jnp.int32, cell_first.shape, 0) < match_count[None, :]
    ).astype(jnp.float32)
    table_first = dense_weights(cell_first, frac_first)
    table_second = dense_weights(cell_second, frac_second)
    owner_first = (
        lax.broadcasted_iota(jnp.int32, (tps_dev * sec_dev, num_over), 0) == local_first[None, :]
    ).astype(jnp.float32)
    owner_second = (
        lax.broadcasted_iota(jnp.int32, (tps_all * (sec_dev + 1), num_over), 0)
        == wide_second[None, :]
    ).astype(jnp.float32)

    def return_forces(mismatch):
        local_forces = jnp.dot(owner_first, spread(mismatch, table_first), precision=HIGH).reshape(
            tps_dev, sec_dev, 128
        )
        spread_table = -jnp.dot(
            owner_second, spread(mismatch, table_second), precision=HIGH
        ).reshape(tps_all, sec_dev + 1, 128)
        from_above = shifted(spread_table[:, 0, :], "sec", -1)
        upper_part = spread_table[:, 1:, :].at[:, -1, :].add(from_above)
        gathered_forces = lax.psum_scatter(upper_part, "tile", scatter_dimension=0, tiled=True)
        return local_forces + gathered_forces

    def squares(vector):
        return lax.psum(jnp.sum(vector * vector), ("sec", "tile"))

    right_side = return_forces(live_mask[None] * target)
    solution_field = jnp.zeros_like(right_side)
    residual = right_side
    direction = right_side
    norm_now = squares(residual)
    for iteration in range(ITERS):
        rows_first = direction.reshape(-1, 128)[local_first]
        gathered = lax.all_gather(direction, "tile", axis=0, tiled=True)
        from_below = shifted(gathered[:, -1, :], "sec", 1)
        lookup = jnp.concatenate([from_below[:, None, :], gathered], 1).reshape(-1, 128)
        rows_second = lookup[wide_second]
        operate_mismatch = live_mask[None] * (
            sample(rows_first, table_first) - sample(rows_second, table_second)
        )
        applied = (
            return_forces(operate_mismatch)
            + stiffness[..., None] * laplace(direction)
            + DAMPING * direction
        )
        step_size = norm_now / lax.psum(jnp.sum(direction * applied), ("sec", "tile"))
        solution_field = solution_field + step_size * direction
        residual = residual - step_size * applied
        norm_next = squares(residual)
        direction = residual + norm_next / norm_now * direction
        norm_now = norm_next
    return (solution_field, residual)


def solution(mesh):
    in_specs = (
        P(("sec", "tile")),
        P(("sec", "tile")),
        P(("sec", "tile")),
        P(None, ("sec", "tile")),
        P(None, ("sec", "tile")),
        P(None, None, ("sec", "tile")),
        P(None, None, ("sec", "tile")),
        P(None, None, ("sec", "tile")),
        P("tile", "sec"),
    )
    out_specs = (P("tile", "sec", None), P("tile", "sec", None))
    return jax.shard_map(
        on_device, mesh=mesh, in_specs=in_specs, out_specs=out_specs, check_vma=False
    )
```

profile of v0, /device:TPU:1, one launch (start us, length us, event | category | flops | bytes accessed | tf_op | source)
XLA Modules:
  0.0 869.7 jit_solution(17227783929484490449)
XLA Ops:
  14.5 5.0 collective-permute-done
  20.7 36.7 %reduce-scatter.6.cloned.1.call-done = f32[32,1,128]{2,0,1:T(8,128)} async-done(((f32[256,1,128]{2,0,1:T(8,128)}), f32[32,1,128]{2,0,1:T(8,128)}) %reduce-scatter.6.cloned.1.call-update) | async-done | bytes 16400 | tf_op jit(solution)/shard_map/reduce_scatter | solution.py:114
  58.0 15.6 %all_gather.12 = f32[256,1,128]{2,0,1:T(8,128)S(1)} all-gather(f32[32,1,128]{2,0,1:T(8,128)S(1)} %add.289), channel_id=1, replica_groups=mesh['sec'=32,'tile'=8] {'tile'}, dimensions={0}, use_global_device_ids=true | all-gather | bytes 147456 | tf_op jit(solution)/shard_map/all_gather | solution.py:127
  73.6 3.2 collective-permute-start.1
  84.8 5.5 collective-permute-done.2
  91.7 32.7 %reduce-scatter.8.cloned.1.call-done = f32[32,1,128]{2,0,1:T(8,128)} async-done(((f32[256,1,128]{2,0,1:T(8,128)}), f32[32,1,128]{2,0,1:T(8,128)}) %reduce-scatter.8.cloned.1.call-update) | async-done | bytes 16400 | tf_op jit(solution)/shard_map/reduce_scatter | solution.py:114
  126.5 78.3 %all-reduce = (f32[]{:T(128)}, f32[]{:T(128)}) all-reduce(f32[]{:T(128)} %get-tuple-element.113, f32[]{:T(128)} %get-tuple-element.112), channel_id=1, replica_groups=mesh['sec'=32,'tile'=8] {'sec','tile'}, use_global_device_ids=true, to_apply=%region_2.3 | all-reduce | flops 2 | bytes 16 | tf_op jit(solution)/shard_map/psum | solution.py:118
  206.8 73.4 %psum.58 = f32[]{:T(128)} all-reduce(f32[]{:T(128)} %multiply_reduce_fusion.41), channel_id=1, replica_groups=mesh['sec'=32,'tile'=8] {'sec','tile'}, use_global_device_ids=true, to_apply=%region_7.8 | all-reduce | flops 1 | bytes 8 | tf_op jit(solution)/shard_map/psum | solution.py:118
  281.6 13.2 %all_gather.13 = f32[256,1,128]{2,0,1:T(8,128)S(1)} all-gather(f32[32,1,128]{2,0,1:T(8,128)S(1)} %multiply_add_fusion.3), channel_id=1, replica_groups=mesh['sec'=32,'tile'=8] {'tile'}, dimensions={0}, use_global_device_ids=true | all-gather | bytes 147456 | tf_op jit(solution)/shard_map/all_gather | solution.py:127
  294.8 2.5 collective-permute-start.3
  305.1 5.5 collective-permute-done.4
  312.0 31.8 %reduce-scatter.10.cloned.1.call-done = f32[32,1,128]{2,0,1:T(8,128)} async-done(((f32[256,1,128]{2,0,1:T(8,128)}), f32[32,1,128]{2,0,1:T(8,128)}) %reduce-scatter.10.cloned.1.call-update) | async-done | bytes 16400 | tf_op jit(solution)/shard_map/reduce_scatter | solution.py:114
  345.3 78.2 %psum.59 = f32[]{:T(128)} all-reduce(f32[]{:T(128)} %get-tuple-element.124), channel_id=1, replica_groups=mesh['sec'=32,'tile'=8] {'sec','tile'}, use_global_device_ids=true, to_apply=%region_10.11 | all-reduce | flops 1 | bytes 8 | tf_op jit(solution)/shard_map/psum | solution.py:139
  425.5 73.4 %psum.60 = f32[]{:T(128)} all-reduce(f32[]{:T(128)} %get-tuple-element.122), channel_id=1, replica_groups=mesh['sec'=32,'tile'=8] {'sec','tile'}, use_global_device_ids=true, to_apply=%region_12.13 | all-reduce | flops 1 | bytes 8 | tf_op jit(solution)/shard_map/psum | solution.py:118
  500.2 13.2 %all_gather.14 = f32[256,1,128]{2,0,1:T(8,128)S(1)} all-gather(f32[32,1,128]{2,0,1:T(8,128)S(1)} %multiply_add_fusion.2), channel_id=1, replica_groups=mesh['sec'=32,'tile'=8] {'tile'}, dimensions={0}, use_global_device_ids=true | all-gather | bytes 147456 | tf_op jit(solution)/shard_map/all_gather | solution.py:127
  513.4 2.2 collective-permute-start.5
  523.6 5.5 collective-permute-done.6
  530.5 31.8 %reduce-scatter.12.cloned.1.call-done = f32[32,1,128]{2,0,1:T(8,128)} async-done(((f32[256,1,128]{2,0,1:T(8,128)}), f32[32,1,128]{2,0,1:T(8,128)}) %reduce-scatter.12.cloned.1.call-update) | async-done | bytes 16400 | tf_op jit(solution)/shard_map/reduce_scatter | solution.py:114
  563.7 78.1 %psum.61 = f32[]{:T(128)} all-reduce(f32[]{:T(128)} %get-tuple-element.120), channel_id=1, replica_groups=mesh['sec'=32,'tile'=8] {'sec','tile'}, use_global_device_ids=true, to_apply=%region_15.16 | all-reduce | flops 1 | bytes 8 | tf_op jit(solution)/shard_map/psum | solution.py:139
  643.8 73.9 %psum.62 = f32[]{:T(128)} all-reduce(f32[]{:T(128)} %get-tuple-element.118), channel_id=1, replica_groups=mesh['sec'=32,'tile'=8] {'sec','tile'}, use_global_device_ids=true, to_apply=%region_17.18 | all-reduce | flops 1 | bytes 8 | tf_op jit(solution)/shard_map/psum | solution.py:118
  719.0 13.2 %all_gather.15 = f32[256,1,128]{2,0,1:T(8,128)S(1)} all-gather(f32[32,1,128]{2,0,1:T(8,128)S(1)} %multiply_add_fusion.1), channel_id=1, replica_groups=mesh['sec'=32,'tile'=8] {'tile'}, dimensions={0}, use_global_device_ids=true | all-gather | bytes 147456 | tf_op jit(solution)/shard_map/all_gather | solution.py:127
  742.3 5.5 collective-permute-done.8
  749.1 31.9 %reduce-scatter.14.cloned.1.call-done = f32[32,1,128]{2,0,1:T(8,128)} async-done(((f32[256,1,128]{2,0,1:T(8,128)}), f32[32,1,128]{2,0,1:T(8,128)}) %reduce-scatter.14.cloned.1.call-update) | async-done | bytes 16400 | tf_op jit(solution)/shard_map/reduce_scatter | solution.py:114
  782.4 78.2 %psum.63 = f32[]{:T(128)} all-reduce(f32[]{:T(128)} %get-tuple-element.116), channel_id=1, replica_groups=mesh['sec'=32,'tile'=8] {'sec','tile'}, use_global_device_ids=true, to_apply=%region_20.21 | all-reduce | flops 1 | bytes 8 | tf_op jit(solution)/shard_map/psum | solution.py:139
  (182 shorter events, 57.3 us)
Async XLA Ops:
  7.2 50.1 %reduce-scatter.6.cloned.1.call-start = ((), (), s32[]{:S(2)}) async-start(), calls=%async_computation.5 | async-start | bytes 147456 | tf_op jit(solution)/shard_map/reduce_scatter | solution.py:114
  7.2 0.8 copy-start.3
  8.0 0.7 copy-start.5
  8.0 0.8 copy-start
  8.8 0.8 copy-start.2
  9.5 0.8 copy-start.1
  12.0 0.7 copy-start.6
  12.0 0.7 copy-start.7
  13.2 6.3 collective-permute-start
  20.2 104.2 %reduce-scatter.8.cloned.1.call-start = ((), (), s32[]{:S(2)}) async-start(), calls=%async_computation.6 | async-start | bytes 147456 | tf_op jit(solution)/shard_map/reduce_scatter | solution.py:114
  73.6 5.9 collective-permute-start.1
  83.4 7.0 collective-permute-start.2
  91.0 252.9 %reduce-scatter.10.cloned.1.call-start = ((), (), s32[]{:S(2)}) async-start(), calls=%async_computation.7 | async-start | bytes 147456 | tf_op jit(solution)/shard_map/reduce_scatter | solution.py:114
  124.4 0.7 copy-start.4
  294.8 5.0 collective-permute-start.3
  303.7 7.0 collective-permute-start.4
  311.3 251.0 %reduce-scatter.12.cloned.1.call-start = ((), (), s32[]{:S(2)}) async-start(), calls=%async_computation.8 | async-start | bytes 147456 | tf_op jit(solution)/shard_map/reduce_scatter | solution.py:114
  513.4 4.9 collective-permute-start.5
  522.2 7.0 collective-permute-start.6
  529.8 251.2 %reduce-scatter.14.cloned.1.call-start = ((), (), s32[]{:S(2)}) async-start(), calls=%async_computation.9 | async-start | bytes 147456 | tf_op jit(solution)/shard_map/reduce_scatter | solution.py:114
  732.3 4.7 collective-permute-start.7
  740.8 7.0 collective-permute-start.8
Sparse Core Ops, SparseCore 0:
  20.3 36.9 reduce-scatter.5
  91.1 33.2 reduce-scatter.7
  311.5 32.3 reduce-scatter.9
  529.9 32.3 reduce-scatter.11
  748.6 32.3 reduce-scatter.13
where the time goes:
time: 872 us; the launch traced here: 870 us
  blocking collectives  589 us (68%)
  waiting for transfers between devices  197 us (23%)
  other arithmetic  25.5 us (3%)
  between operations  23.8 us (3%)
  starting transfers between devices  16.4 us (2%)
  local copies, waits for them, and re-layouts  15.4 us (2%)
    psum x4, blocking collectives, squares(): return lax.psum(jnp.sum(vector * vector), ('sec', 'tile'))  299 us
    psum x3, blocking collectives, on_device(): lax.psum(jnp.sum(direction * applied), ('sec', 'tile'))  235 us
    reduce_scatter x5, waiting for transfers between devices, return_forces(): lax.psum_scatter(upper_part, 'tile', scatter_dimension=0, tiled=True)  165 us
    all_gather x4, blocking collectives, on_device(): gathered = lax.all_gather(direction, 'tile', axis=0, tiled=True)  55.3 us
    ppermute x9, waiting for transfers between devices, shifted(): return lax.ppermute(block, axis, route)  32.1 us
  transfers between devices with their start and end apart: 14, of which 14 were waited for; matrix products, arithmetic and copies ran while one was open for 1% of the time, Pallas kernels for 0%

commit v1 on v0

v1 whole, which is shorter than its diff:
```python
import functools

import jax
import jax.numpy as jnp
from jax import lax
from jax.experimental import pallas as pl
from jax.experimental.pallas import tpu as pltpu
from jax.sharding import PartitionSpec as P

ITERS = 4
DAMPING = 0.5
SHIFT = 10.0
SCALE = 1.0 / 128.0
BACK = 25.0 / 16384.0
PAIRS = [(i, j) for i in range(5) for j in range(i, 5) if (i, j) != (4, 4)]
VMEM = pl.BlockSpec(memory_space=pltpu.VMEM)
F32 = jnp.float32
NT = (((1,), (1,)), ((), ()))


def split3(x):
    a = x.astype(jnp.bfloat16)
    rest = x - a.astype(F32)
    b = rest.astype(jnp.bfloat16)
    c = (rest - b.astype(F32)).astype(jnp.bfloat16)
    return jnp.concatenate([a, b, c], 0)


def merge3(x):
    n = x.shape[0] // 3
    return x[:n] + (x[n : 2 * n] + x[2 * n :])


def sublane_ids():
    return lax.broadcasted_iota(jnp.int32, (8, 128), 0)


def fold_rows(parts):
    sub = sublane_ids()
    low = sub < 4
    half = [
        jnp.where(low, parts[p], parts[p + 4])
        + pltpu.roll(jnp.where(low, parts[p + 4], parts[p]), 4, 0)
        for p in range(4)
    ]
    two = (sub & 2) != 0
    quarter = [
        jnp.where(two, half[p + 2] + pltpu.roll(half[p + 2], 2, 0), half[p] + pltpu.roll(half[p], 6, 0))
        for p in range(2)
    ]
    one = (sub & 1) != 0
    return jnp.where(
        one, quarter[1] + pltpu.roll(quarter[1], 1, 0), quarter[0] + pltpu.roll(quarter[0], 7, 0)
    )


def spread_block(tops, sides, out_ref, lanes, lead=()):
    for q in range(8):
        parts = []
        for p in range(8):
            acc = tops[q][0] * sides[p][0]
            for group in range(1, 4):
                acc = acc + tops[q][group] * sides[p][group]
            parts.append(acc)
        out_ref[lead + (slice(8 * q, 8 * q + 8), lanes)] = fold_rows(parts)


def sample_block(rows_ref, lanes, wy_ref, fx_ref, col_ref, blk, side):
    out = []
    for group in range(4):
        ms = slice(8 * group, 8 * group + 8)
        col = col_ref[blk, side, ms, :]
        nxt = col + 1
        fx = fx_ref[blk, side, ms, :]
        acc = None
        for q in range(8):
            row = rows_ref[8 * q : 8 * q + 8, lanes]
            left = jnp.take_along_axis(row, col, axis=0, mode="promise_in_bounds")
            right = jnp.take_along_axis(row, nxt, axis=0, mode="promise_in_bounds")
            term = wy_ref[blk, side, q, ms, :] * (left + fx * (right - left))
            acc = term if acc is None else acc + term
        out.append(acc)
    return out


def load_table(ref, blk, side):
    return [[ref[blk, side, p, 8 * g : 8 * g + 8, :] for g in range(4)] for p in range(8)]


def lanes_of(blk):
    return pl.ds(pl.multiple_of(blk * 128, 128), 128)


def tables_kernel(
    comp_ref, data_ref, wx_ref, wy_ref, fx_ref, col_ref, live_ref, ohf_ref, ohs_ref, own_ref, down_ref, f_ref
):
    comp = comp_ref[0]

    def body(blk, carry):
        lanes = lanes_of(blk)
        count = data_ref[blk, 258, :][None, :]
        for group in range(4):
            ms = slice(8 * group, 8 * group + 8)
            slot = (sublane_ids() + 8 * group).astype(F32)
            live_ref[blk, ms, :] = jnp.where(slot < count, SCALE, 0.0)
        for side in range(2):
            for group in range(4):
                ms = slice(8 * group, 8 * group + 8)
                cell = data_ref[blk, 32 * side + 8 * group : 32 * side + 8 * group + 8, :].astype(jnp.int32)
                base = 64 + 64 * side + 8 * group
                fx = data_ref[blk, base : base + 8, :]
                fy = data_ref[blk, base + 32 : base + 40, :]
                row = (cell * 37) >> 8
                col = cell - 7 * row
                fx_ref[blk, side, ms, :] = fx
                col_ref[blk, side, ms, :] = col
                for k in range(8):
                    wx_ref[blk, side, k, ms, :] = jnp.where(
                        col == k, 1.0 - fx, jnp.where(col == k - 1, fx, 0.0)
                    )
                    wy_ref[blk, side, k, ms, :] = jnp.where(
                        row == k, 1.0 - fy, jnp.where(row == k - 1, fy, 0.0)
                    )
        first = data_ref[blk, 256, :][None, :].astype(jnp.int32)
        second = data_ref[blk, 257, :][None, :].astype(jnp.int32)
        ids = lax.broadcasted_iota(jnp.int32, (256, 128), 0)
        ohf_ref[:, lanes] = jnp.where(ids == first, 1.0, 0.0).astype(jnp.bfloat16)
        ohs_ref[0:256, lanes] = jnp.where(ids == second, 1.0, 0.0).astype(jnp.bfloat16)
        ohs_ref[256:512, lanes] = jnp.where(ids + 256 == second, 1.0, 0.0).astype(jnp.bfloat16)
        goal = []
        for group in range(4):
            at = pl.multiple_of(192 + 32 * comp + 8 * group, 8)
            goal.append(
                data_ref[blk, pl.ds(at, 8), :] * (live_ref[blk, 8 * group : 8 * group + 8, :] * (1.0 / SCALE))
            )
        for side in range(2):
            tops = load_table(wy_ref, blk, side)
            tops = [[tops[q][g] * goal[g] for g in range(4)] for q in range(8)]
            spread_block(tops, load_table(wx_ref, blk, side), f_ref, lanes, (side,))
        return carry

    lax.fori_loop(0, 8, body, 0)
    at_first = merge3(lax.dot_general(split3(f_ref[0]), ohf_ref[...], NT, preferred_element_type=F32))
    at_second = merge3(lax.dot_general(split3(f_ref[1]), ohs_ref[...], NT, preferred_element_type=F32))
    own_ref[...] = at_first - at_second[:, :256]
    down_ref[...] = at_second[:, 256:]


def stencil_kernel(wx_ref, wy_ref, live_ref, ohf_ref, ohs_ref, stiff_ref, own_ref, down_ref, f_ref):
    def body(blk, carry):
        lanes = lanes_of(blk)
        live = [live_ref[blk, 8 * g : 8 * g + 8, :] for g in range(4)]
        for side in range(2):
            zero = [jnp.zeros((8, 128), F32)] * 4
            for kind_x in range(2):
                wx = load_table(wx_ref, blk, side) + [zero]
                sides = [[wx[p][g] * wx[p + kind_x][g] for g in range(4)] for p in range(8)]
                for kind_y in range(2):
                    wy = load_table(wy_ref, blk, side) + [zero]
                    tops = [[wy[q][g] * wy[q + kind_y][g] * live[g] for g in range(4)] for q in range(8)]
                    spread_block(tops, sides, f_ref, lanes, (side, 2 * kind_y + kind_x))
        return carry

    lax.fori_loop(0, 8, body, 0)
    node = lax.broadcasted_iota(jnp.int32, (64, 256), 0)
    p = node & 7
    q = node >> 3
    one = lambda cond: jnp.where(cond, 1.0, 0.0)
    stiff = stiff_ref[...] * SCALE
    degree = one(p < 7) + one(p > 0) + one(q < 7) + one(q > 0)
    extra = [
        stiff * degree + (DAMPING - SHIFT) * SCALE,
        -stiff * one(p < 7),
        -stiff * one(q < 7),
        None,
    ]
    for kind in range(4):
        at_first = merge3(lax.dot_general(split3(f_ref[0, kind]), ohf_ref[...], NT, preferred_element_type=F32))
        at_second = merge3(lax.dot_general(split3(f_ref[1, kind]), ohs_ref[...], NT, preferred_element_type=F32))
        total = at_first + at_second[:, :256]
        own_ref[kind] = total if extra[kind] is None else total + extra[kind]
        down_ref[kind] = at_second[:, 256:]


def up_kernel(v_ref, ohf_ref, ohs_ref, wx_ref, wy_ref, fx_ref, col_ref, live_ref, own_ref, down_ref, g_ref, f_ref):
    g_ref[...] = merge3(jnp.dot(split3(v_ref[...]), ohf_ref[...], preferred_element_type=F32))

    def body(blk, carry):
        lanes = lanes_of(blk)
        got = sample_block(g_ref, lanes, wy_ref, fx_ref, col_ref, blk, 0)
        got = [got[g] * live_ref[blk, 8 * g : 8 * g + 8, :] for g in range(4)]
        tops = load_table(wy_ref, blk, 1)
        tops = [[tops[q][g] * got[g] for g in range(4)] for q in range(8)]
        spread_block(tops, load_table(wx_ref, blk, 1), f_ref, lanes)
        return carry

    lax.fori_loop(0, 8, body, 0)
    forces = merge3(lax.dot_general(split3(f_ref[...]), ohs_ref[...], NT, preferred_element_type=F32))
    own_ref[...] = forces[:, :256]
    down_ref[...] = forces[:, 256:]


def down_kernel(
    v_ref, below_ref, prev_ref, part_ref, band_ref, band2_ref,
    ohf_ref, ohs_ref, wx_ref, wy_ref, fx_ref, col_ref, live_ref, out_ref, g_ref, f_ref, *, back
):
    rows = jnp.concatenate([split3(v_ref[...]), split3(below_ref[...])], 1)
    g_ref[...] = merge3(jnp.dot(rows, ohs_ref[...], preferred_element_type=F32))

    def body(blk, carry):
        lanes = lanes_of(blk)
        got = sample_block(g_ref, lanes, wy_ref, fx_ref, col_ref, blk, 1)
        got = [got[g] * live_ref[blk, 8 * g : 8 * g + 8, :] for g in range(4)]
        tops = load_table(wy_ref, blk, 0)
        tops = [[tops[q][g] * got[g] for g in range(4)] for q in range(8)]
        spread_block(tops, load_table(wx_ref, blk, 0), f_ref, lanes)
        return carry

    lax.fori_loop(0, 8, body, 0)
    forces = merge3(lax.dot_general(split3(f_ref[...]), ohf_ref[...], NT, preferred_element_type=F32))
    v = v_ref[...]
    band = [band_ref[k] + band2_ref[k] for k in range(4)]
    up = lambda x, d: pltpu.roll(x, 64 - d, 0)
    dn = lambda x, d: pltpu.roll(x, d, 0)
    total = band[0] * v
    total = total + band[1] * up(v, 1) + dn(band[1] * v, 1)
    total = total + band[2] * up(v, 8) + dn(band[2] * v, 8)
    total = total + band[3] * up(v, 9) + dn(band[3] * v, 9)
    total = total + dn(band[3] * up(v, 8), 1) + dn(band[3] * up(v, 1), 8)
    total = total - forces - part_ref[...]
    if back:
        total = total - BACK * prev_ref[...]
    out_ref[...] = total


def two_sum(a, b):
    s = a + b
    t = s - a
    return s, (a - (s - t)) + (b - t)


def halves(a):
    c = 4097.0 * a
    high = c - (c - a)
    return high, a - high


def two_prod(a, b):
    p = a * b
    ah, al = halves(a)
    bh, bl = halves(b)
    return p, ((ah * bh - p) + ah * bl + al * bh) + al * bl


def quick(a, b):
    s = a + b
    return s, b - (s - a)


def dd_add(x, y):
    s, e = two_sum(x[0], y[0])
    return quick(s, e + (x[1] + y[1]))


def dd_mul(x, y):
    p, e = two_prod(x[0], y[0])
    return quick(p, e + (x[0] * y[1] + x[1] * y[0]))


def dd_neg(x):
    return (-x[0], -x[1])


def dd_div(x, y):
    q = x[0] / y[0]
    rest = dd_add(x, dd_neg(dd_mul(y, (q, jnp.zeros_like(q)))))
    return quick(q, rest[0] / y[0])


def dots_kernel(*refs):
    out_ref = refs[5]
    fields = [r[...] for r in refs[:5]]
    sub = lax.broadcasted_iota(jnp.int32, (16, 128), 0)
    lane = lax.broadcasted_iota(jnp.int32, (16, 128), 1)
    high = jnp.zeros((16, 128), F32)
    low = jnp.zeros((16, 128), F32)
    for k, (i, j) in enumerate(PAIRS):
        acc = two_prod(fields[i], fields[j])
        acc = dd_add((acc[0][:, :128], acc[1][:, :128]), (acc[0][:, 128:], acc[1][:, 128:]))
        n = 64
        while n > 8:
            n //= 2
            acc = dd_add((acc[0][:n], acc[1][:n]), (acc[0][n:], acc[1][n:]))
        for d in (4, 2, 1):
            acc = dd_add(acc, (pltpu.roll(acc[0], d, 0), pltpu.roll(acc[1], d, 0)))
        wide = [jnp.concatenate([a, a], 0) for a in acc]
        high = jnp.where(sub == k, wide[0], high)
        low = jnp.where(sub == k, wide[1], low)
    acc = (high, low)
    for d in (64, 32, 16, 8, 4, 2, 1):
        acc = dd_add(acc, (pltpu.roll(acc[0], d, 1), pltpu.roll(acc[1], d, 1)))
    row = jnp.where(lane == sub, acc[0], 0.0) + jnp.where(lane == sub + 16, acc[1], 0.0)
    out_ref[...] = jnp.sum(row, 0, keepdims=True)


def finish_kernel(tile_ref, gram_ref, gram2_ref, v0, v1, v2, v3, v4, mine_ref, other_ref):
    rows = jnp.concatenate([gram_ref[...], gram2_ref[...]], 0)
    acc = (rows, pltpu.roll(rows, 112, 1))
    n = 64
    while n > 8:
        n //= 2
        acc = dd_add((acc[0][:n], acc[1][:n]), (acc[0][n:], acc[1][n:]))
    for d in (4, 2, 1):
        acc = dd_add(acc, (pltpu.roll(acc[0], d, 0), pltpu.roll(acc[1], d, 0)))
    gram = {}
    for k, (i, j) in enumerate(PAIRS):
        pair = tuple(jnp.broadcast_to(a[:, k : k + 1], (8, 128)) for a in acc)
        gram[(i, j)] = pair
        gram[(j, i)] = pair
    zero = jnp.zeros((8, 128), F32)
    const = lambda c: (jnp.full((8, 128), c, F32), zero)

    def form(a, b):
        total = None
        for j, bj in enumerate(b):
            inner = None
            for i, ai in enumerate(a):
                term = dd_mul(ai, gram[(i, j)])
                inner = term if inner is None else dd_add(inner, term)
            inner = dd_mul(inner, bj)
            total = inner if total is None else dd_add(total, inner)
        return total

    def apply(p):
        out = [const(0.0) for _ in range(len(p) + 1)]
        for k, c in enumerate(p):
            out[k + 1] = dd_add(out[k + 1], (c[0] * 128.0, c[1] * 128.0))
            out[k] = dd_add(out[k], dd_mul(c, const(SHIFT)))
            if k >= 1:
                out[k - 1] = dd_add(out[k - 1], dd_mul(c, const(BACK * 128.0)))
        return out

    def axpy(a, x, y):
        out = []
        for k in range(max(len(x), len(y))):
            if k >= len(x):
                out.append(y[k])
            elif k >= len(y):
                out.append(dd_mul(a, x[k]))
            else:
                out.append(dd_add(y[k], dd_mul(a, x[k])))
        return out

    res = [const(1.0)]
    direc = [const(1.0)]
    sol = []
    norm = gram[(0, 0)]
    for it in range(ITERS):
        image = apply(direc)
        step = dd_div(norm, form(direc, image))
        sol = axpy(step, direc, sol)
        res = axpy(dd_neg(step), image, res)
        if it < ITERS - 1:
            new = form(res, res)
            direc = axpy(dd_div(new, norm), direc, res)
            norm = new
    fields = [r[...] for r in (v0, v1, v2, v3, v4)]

    def combine(coefs):
        total = None
        for c, f in zip(coefs, fields):
            term = c[0][0:1, 0:1] * f
            total = term if total is None else total + term
        return total

    tile = tile_ref[0]
    ids = lax.broadcasted_iota(jnp.int32, (64, 256), 1)
    want = lax.broadcasted_iota(jnp.int32, (64, 256), 0)
    swap = tile + 1 - 2 * (tile & 1)
    want = jnp.where(want < 32, tile * 32 + want, swap * 32 + want - 32)
    pick = jnp.where(ids == want, 1.0, 0.0).astype(jnp.bfloat16)
    for k, coefs in enumerate((sol, res)):
        parts = lax.dot_general(pick, split3(combine(coefs)), NT, preferred_element_type=F32)
        both = parts[:, :64] + (parts[:, 64:128] + parts[:, 128:192])
        mine_ref[k] = both[:32]
        other_ref[k] = both[32:]


def call(kernel, outs, n_in, scratch=(), smem=0, flops=10**7):
    return pl.pallas_call(
        kernel,
        out_shape=[jax.ShapeDtypeStruct(s, d) for s, d in outs],
        in_specs=[pl.BlockSpec(memory_space=pltpu.SMEM)] * smem + [VMEM] * (n_in - smem),
        out_specs=[VMEM] * len(outs),
        scratch_shapes=[pltpu.VMEM(s, d) for s, d in scratch],
        compiler_params=pltpu.CompilerParams(vmem_limit_bytes=48 * 1024 * 1024),
        cost_estimate=pl.CostEstimate(flops=flops, bytes_accessed=1 << 20, transcendentals=0),
    )


def shifted(block, distance):
    devices = range(lax.axis_size("sec"))
    route = [(i - distance, i) for i in devices if i - distance in devices]
    return lax.ppermute(block, "sec", route)


def swapped(block):
    return lax.ppermute(block, "tile", [(i, i ^ 1) for i in range(8)])


def on_device(
    ov_first, ov_second, match_count, cell_first, cell_second, frac_first, frac_second, target, stiffness
):
    sec = lax.axis_index("sec")
    tile = lax.axis_index("tile")
    core = tile % 2
    sections = lax.axis_size("sec")
    second = ov_second // sections + jnp.where(ov_second % sections == sec, 0, 256)
    rows = [
        cell_first.astype(F32),
        cell_second.astype(F32),
        frac_first.reshape(64, 128),
        frac_second.reshape(64, 128),
        target.reshape(64, 128),
        (ov_first // sections).astype(F32)[None],
        second.astype(F32)[None],
        match_count.astype(F32)[None],
        jnp.pad(stiffness.reshape(1, 32), ((0, 0), (0, 96))),
        jnp.zeros((4, 128), F32),
    ]
    packed = jnp.concatenate(rows, 0)
    groups = [[0, 2, 4, 6], [1, 3, 5, 7]]
    same = lax.all_to_all(
        jnp.broadcast_to(packed[None], (4, 264, 128)), "tile", 0, 0, tiled=True, axis_index_groups=groups
    )
    data = jnp.concatenate([same, swapped(same)], 0)
    pair = data[:, 259, :32].reshape(2, 4, 32)
    pair = jnp.where(core == 0, pair, pair[::-1])
    stiff = jnp.transpose(pair, (1, 0, 2)).reshape(1, 256)

    field = ((64, 256), F32)
    bf16 = jnp.bfloat16
    wx, wy, fx, col, live, ohf, ohs, own, down = call(
        tables_kernel,
        [
            ((8, 2, 8, 32, 128), F32),
            ((8, 2, 8, 32, 128), F32),
            ((8, 2, 32, 128), F32),
            ((8, 2, 32, 128), jnp.int32),
            ((8, 32, 128), F32),
            ((256, 1024), bf16),
            ((512, 1024), bf16),
            field,
            field,
        ],
        2,
        [((2, 64, 1024), F32)],
        smem=1,
    )(core.reshape(1), data)
    start_down = shifted(down, -1)
    band, band_down = call(
        stencil_kernel,
        [((4, 64, 256), F32), ((4, 64, 256), F32)],
        6,
        [((2, 4, 64, 1024), F32)],
    )(wx, wy, live, ohf, ohs, stiff)
    band2 = shifted(band_down, -1)
    tables = (ohf, ohs, wx, wy, fx, col, live)
    scratch = [((64, 1024), F32), ((64, 1024), F32)]
    fields = [own - start_down]
    for k in range(ITERS):
        v = fields[-1]
        below = shifted(v, 1)
        part, down = call(up_kernel, [field, field], 8, scratch)(v, *tables)
        above = shifted(down, -1)
        partial = call(functools.partial(down_kernel, back=k > 0), [field], 13, scratch)(
            v, below, fields[max(k - 1, 0)], part, band, band2, *tables
        )[0]
        fields.append(partial - above)
    gram = call(dots_kernel, [((1, 128), F32)], 5)(*fields)[0]
    gram = lax.all_to_all(jnp.broadcast_to(gram, (32, 128)), "sec", 0, 0, tiled=True)
    mine, other = call(
        finish_kernel, [((2, 32, 64), F32), ((2, 32, 64), F32)], 8, smem=1
    )(tile.reshape(1), gram, swapped(gram), *fields)
    other = swapped(other)
    first = jnp.where(core == 0, mine, other)
    last = jnp.where(core == 0, other, mine)
    out = jnp.concatenate([first, last], 2)[:, :, None, :]
    return (out[0], out[1])


def solution(mesh):
    in_specs = (
        P(("sec", "tile")),
        P(("sec", "tile")),
        P(("sec", "tile")),
        P(None, ("sec", "tile")),
        P(None, ("sec", "tile")),
        P(None, None, ("sec", "tile")),
        P(None, None, ("sec", "tile")),
        P(None, None, ("sec", "tile")),
        P("tile", "sec"),
    )
    out_specs = (P("tile", "sec", None), P("tile", "sec", None))
    return jax.shard_map(
        on_device, mesh=mesh, in_specs=in_specs, out_specs=out_specs, check_vma=False
    )
```

time: 872 us -> 142 us (0.16)
  blocking collectives: 589 us -> 41.8 us
  waiting for transfers between devices: 197 us -> 13.5 us
  Pallas kernels: 0 us -> 45.6 us
  between operations: 23.8 us -> 0.89 us
  other arithmetic: 25.5 us -> 3.54 us
  starting transfers between devices: 16.4 us -> 32.7 us
  local copies, waits for them, and re-layouts: 15.4 us -> 3.22 us
    psum x7 -> x0, blocking collectives: 534 us -> none  [the longest x4 299 us: squares(): return lax.psum(jnp.sum(vector * vector), ('sec', 'tile'))]
    reduce_scatter x5 -> x0, waiting for transfers between devices: 165 us -> none  [return_forces(): lax.psum_scatter(upper_part, 'tile', scatter_dimension=0, tiled=True)]
    all_gather x4 -> x0, blocking collectives: 55.3 us -> none  [on_device(): gathered = lax.all_gather(direction, 'tile', axis=0, tiled=True)]
    pallas_call x0 -> x12, Pallas kernels: none -> 45.6 us  [the longest x4 14 us: on_device(): part, down = call(up_kernel, [field, field], 8, scratch)(v, *tables)]
    all_to_all x0 -> x2, blocking collectives: none -> 41.8 us  [the longest x1 28.2 us: on_device(): lax.all_to_all(jnp.broadcast_to(gram, (32, 128)), 'sec', 0, 0, tiled=True)]
    ppermute x9 -> x13, waiting for transfers between devices: 32.1 us -> 13.5 us  [the longest x10 10.2 us: shifted(): return lax.ppermute(block, 'sec', route)]
    ppermute x9 -> x13, starting transfers between devices: 16.2 us -> 32.7 us  [the longest x10 24.8 us: shifted(): return lax.ppermute(block, 'sec', route)]
  transfers between devices with their start and end apart: 14 -> 13, of which waited for: 14 -> 8; matrix products, arithmetic and copies ran while one was open for 1% -> 0% of each run, Pallas kernels for 0% -> 20%
where the time goes in v1:
time: 142 us; the launch traced here: 141 us
  Pallas kernels  45.6 us (32%)
  blocking collectives  41.8 us (29%)
  starting transfers between devices  32.7 us (23%)
  waiting for transfers between devices  13.5 us (10%)
  other arithmetic  3.54 us (2%)
  local copies, waits for them, and re-layouts  3.22 us (2%)
    all_to_all x1, blocking collectives, on_device(): lax.all_to_all(jnp.broadcast_to(gram, (32, 128)), 'sec', 0, 0, tiled=True)  28.2 us
    ppermute x10, starting transfers between devices, shifted(): return lax.ppermute(block, 'sec', route)  24.8 us
    pallas_call x4, Pallas kernels, on_device(): part, down = call(up_kernel, [field, field], 8, scratch)(v, *tables)  14 us
    pallas_call x4, Pallas kernels, on_device(): call(functools.partial(down_kernel, back=k > 0), [field], 13, scratch)  13.8 us
    all_to_all x1, blocking collectives, on_device(): lax.all_to_all(jnp.broadcast_to(packed[None], (4, 264, 128)), 'tile', 0,...  13.5 us
    pallas_call x1, Pallas kernels, on_device(): call(stencil_kernel, [((4, 64, 256), F32), ((4, 64, 256), F32)], 6, [((2,...  10.6 us
    ppermute x10, waiting for transfers between devices, shifted(): return lax.ppermute(block, 'sec', route)  10.2 us
    ppermute x3, starting transfers between devices, swapped(): return lax.ppermute(block, 'tile', [(i, i ^ 1) for i in range(8)])  7.83 us
  transfers between devices with their start and end apart: 13, of which 8 were waited for; matrix products, arithmetic and copies ran while one was open for 0% of the time, Pallas kernels for 20%

profile of v1, /device:TPU:1, one launch (start us, length us, event | category | flops | bytes accessed | tf_op | source)
XLA Modules:
  0.0 141.2 jit_solution(4734872780196372574)
XLA Ops:
  4.1 2.3 %concatenate.9 = f32[264,128]{1,0:T(8,128)S(1)} concatenate(f32[32,128]{1,0:T(8,128)S(1)} %convert_element_type.17, f32[32,128]{1,0:T(8,128)S(1)} %convert_element_type.18, f32[64,128]{1,0:T(8,128)} %bitcast.28, f32[64,128]{1,0:T(8,128)} %bitcast.29, f32[64,128]{1,0:T(8,128)} %bitcast.30, f32[1,128]{1,0:T(1,128)S(1)} %convert_bitcast_fusion.2, f32[1,128]{1,0:T(1,128)S(1)} %get-tuple-element.53, ...), dimensions={0} | concatenate | bytes 270336 | tf_op jit(solution)/shard_map/concatenate | solution.py:431
  6.4 13.5 %all_to_all.13 = f32[4,264,128]{2,1,0:T(8,128)S(1)} all-to-all(f32[4,264,128]{2,1,0:T(8,128)S(1)} %broadcast_in_dim.35), channel_id=1, replica_groups={{0,2,4,6},{1,3,5,7},{8,10,12,14},{9,11,13,15},{16,18,20,22},{17,19,21,2..., dimensions={0} | all-to-all | bytes 1081344 | tf_op jit(solution)/shard_map/all_to_all | solution.py:433
  20.0 1.9 %collective-permute-start = (f32[4,264,128]{2,1,0:T(8,128)S(1)}, f32[4,264,128]{2,1,0:T(8,128)S(1)}, u32[]{:S(2)}, u32[]{:S(2)}) collective-permute-start(f32[4,264,128]{2,1,0:T(8,128)S(1)} %all_to_all.13), channel_id=1, source_target_pairs={{0,1},{1,0},{2,3},{3,2},{4,5},{5,4},{6,7},{7,6},{8,9},{9,8},{10,11... | collective-permute-start | bytes 1622024 | tf_op jit(solution)/shard_map/ppermute | solution.py:408
  21.9 1.5 %collective-permute-done = f32[4,264,128]{2,1,0:T(8,128)S(1)} collective-permute-done((f32[4,264,128]{2,1,0:T(8,128)S(1)}, f32[4,264,128]{2,1,0:T(8,128)S(1)}, u32[]{:S(2)}, u32[]{:S(2)}) %collective-permute-start) | collective-permute-done | bytes 540704 | tf_op jit(solution)/shard_map/ppermute | solution.py:408
  23.6 4.7 %shard_map.104 = (f32[8,2,8,32,128]{4,3,2,1,0:T(8,128)S(1)}, f32[8,2,8,32,128]{4,3,2,1,0:T(8,128)}, f32[8,2,32,128]{3,2,1,0:T(8,128)S(1)}, s32[8,2,32,128]{3,2,1...) custom-call(s32[1]{0:T(128)} %bitcast.1.comp_ref, ...), custom_call_target="tpu_custom_call" | custom-call | flops 10000000 | bytes 1048576 | tf_op jit(solution)/shard_map/pallas_call | solution.py:443
  28.3 10.6 %shard_map.106 = (f32[4,64,256]{2,1,0:T(8,128)S(1)}, f32[4,64,256]{2,1,0:T(8,128)S(1)}) custom-call(f32[8,2,8,32,128]{4,3,2,1,0:T(8,128)S(1)} %get-tuple-element.27.wx_ref, f32[8,2,8,32,128]{4,3,2,1,0:T(8,128)} %get-tuple-element.28.wy_ref, f32[8,32,128]{2,1,0:T(8,128)S(1)} %get-tuple-element.31.live_ref, bf16[256,1024]{1,0:T(8,128)(2,1)S(1)} %get-tuple-element.25.ohf_ref, ...), custom_call_target="tpu_custom_call" | custom-call | flops 10000000 | bytes 1048576 | tf_op jit(solution)/shard_map/pallas_call | solution.py:461
  41.5 8.2 %collective-permute-done.1 = f32[64,256]{1,0:T(8,128)S(1)} collective-permute-done((f32[64,256]{1,0:T(8,128)S(1)}, f32[64,256]{1,0:T(8,128)S(1)}, u32[]{:S(2)}, u32[]{:S(2)}) %collective-permute-start.1) | collective-permute-done | bytes 65568 | tf_op jit(solution)/shard_map/ppermute | solution.py:404
  49.7 3.1 %collective-permute-start.2 = (f32[64,256]{1,0:T(8,128)S(1)}, f32[64,256]{1,0:T(8,128)S(1)}, u32[]{:S(2)}, u32[]{:S(2)}) collective-permute-start(f32[64,256]{1,0:T(8,128)S(1)} %sub.27.v_ref.prev_ref.refs_0_.v0), channel_id=1, source_target_pairs={{0,8},{8,16},{16,24},{24,32},{32,40},{40,48},{48,56},{56,64},{64,7... | collective-permute-start | bytes 196616 | tf_op jit(solution)/shard_map/ppermute | solution.py:404
  52.9 3.5 %shard_map.105 = (f32[64,256]{1,0:T(8,128)S(1)}, f32[64,256]{1,0:T(8,128)S(1)}) custom-call(f32[64,256]{1,0:T(8,128)S(1)} %sub.27.v_ref.prev_ref.refs_0_.v0, bf16[256,1024]{1,0:T(8,128)(2,1)S(1)} %get-tuple-element.25.ohf_ref, bf16[512,1024]{1,0:T(8,128)(2,1)S(1)} %get-tuple-element.26.ohs_ref, f32[8,2,8,32,128]{4,3,2,1,0:T(8,128)S(1)} %get-tuple-element.27.wx_ref, ...), custom_call_target="tpu_custom_call" | custom-call | flops 10000000 | bytes 1048576 | tf_op jit(solution)/shard_map/pallas_call | solution.py:474
  57.7 3.4 %shard_map.107 = f32[64,256]{1,0:T(8,128)S(1)} custom-call(f32[64,256]{1,0:T(8,128)S(1)} %sub.27.v_ref.prev_ref.refs_0_.v0, f32[64,256]{1,0:T(8,128)S(1)} %collective-permute-done.2.below_ref, f32[64,256]{1,0:T(8,128)S(1)} %sub.27.v_ref.prev_ref.refs_0_.v0, f32[64,256]{1,0:T(8,128)S(1)} %get-tuple-element.32.part_ref, ...), custom_call_target="tpu_custom_call" | custom-call | flops 10000000 | bytes 1048576 | tf_op jit(solution)/shard_map/pallas_call | solution.py:476
  61.4 4.7 %collective-permute-start.5 = (f32[64,256]{1,0:T(8,128)S(1)}, f32[64,256]{1,0:T(8,128)S(1)}, u32[]{:S(2)}, u32[]{:S(2)}) collective-permute-start(f32[64,256]{1,0:T(8,128)S(1)} %sub.28.v_ref.prev_ref.refs_1_.v1), channel_id=1, source_target_pairs={{0,8},{8,16},{16,24},{24,32},{32,40},{40,48},{48,56},{56,64},{64,7... | collective-permute-start | bytes 196616 | tf_op jit(solution)/shard_map/ppermute | solution.py:404
  66.1 3.5 %shard_map.108 = (f32[64,256]{1,0:T(8,128)S(1)}, f32[64,256]{1,0:T(8,128)S(1)}) custom-call(f32[64,256]{1,0:T(8,128)S(1)} %sub.28.v_ref.prev_ref.refs_1_.v1, bf16[256,1024]{1,0:T(8,128)(2,1)S(1)} %get-tuple-element.25.ohf_ref, bf16[512,1024]{1,0:T(8,128)(2,1)S(1)} %get-tuple-element.26.ohs_ref, f32[8,2,8,32,128]{4,3,2,1,0:T(8,128)S(1)} %get-tuple-element.27.wx_ref, ...), custom_call_target="tpu_custom_call" | custom-call | flops 10000000 | bytes 1048576 | tf_op jit(solution)/shard_map/pallas_call | solution.py:474
  70.9 3.4 %shard_map.109 = f32[64,256]{1,0:T(8,128)S(1)} custom-call(f32[64,256]{1,0:T(8,128)S(1)} %sub.28.v_ref.prev_ref.refs_1_.v1, f32[64,256]{1,0:T(8,128)S(1)} %collective-permute-done.5.below_ref, f32[64,256]{1,0:T(8,128)S(1)} %sub.27.v_ref.prev_ref.refs_0_.v0, f32[64,256]{1,0:T(8,128)S(1)} %get-tuple-element.36.part_ref, ...), custom_call_target="tpu_custom_call" | custom-call | flops 10000000 | bytes 1048576 | tf_op jit(solution)/shard_map/pallas_call | solution.py:476
  75.0 3.8 %collective-permute-start.7 = (f32[64,256]{1,0:T(8,128)S(1)}, f32[64,256]{1,0:T(8,128)S(1)}, u32[]{:S(2)}, u32[]{:S(2)}) collective-permute-start(f32[64,256]{1,0:T(8,128)S(1)} %sub.29.v_ref.prev_ref.refs_2_.v2), channel_id=1, source_target_pairs={{0,8},{8,16},{16,24},{24,32},{32,40},{40,48},{48,56},{56,64},{64,7... | collective-permute-start | bytes 196616 | tf_op jit(solution)/shard_map/ppermute | solution.py:404
  78.8 3.5 %shard_map.110 = (f32[64,256]{1,0:T(8,128)S(1)}, f32[64,256]{1,0:T(8,128)S(1)}) custom-call(f32[64,256]{1,0:T(8,128)S(1)} %sub.29.v_ref.prev_ref.refs_2_.v2, bf16[256,1024]{1,0:T(8,128)(2,1)S(1)} %get-tuple-element.25.ohf_ref, bf16[512,1024]{1,0:T(8,128)(2,1)S(1)} %get-tuple-element.26.ohs_ref, f32[8,2,8,32,128]{4,3,2,1,0:T(8,128)S(1)} %get-tuple-element.27.wx_ref, ...), custom_call_target="tpu_custom_call" | custom-call | flops 10000000 | bytes 1048576 | tf_op jit(solution)/shard_map/pallas_call | solution.py:474
  82.3 1.3 collective-permute-start.8
  83.6 3.5 %shard_map.111 = f32[64,256]{1,0:T(8,128)S(1)} custom-call(f32[64,256]{1,0:T(8,128)S(1)} %sub.29.v_ref.prev_ref.refs_2_.v2, f32[64,256]{1,0:T(8,128)S(1)} %collective-permute-done.7.below_ref, f32[64,256]{1,0:T(8,128)S(1)} %sub.28.v_ref.prev_ref.refs_1_.v1, f32[64,256]{1,0:T(8,128)S(1)} %get-tuple-element.38.part_ref, ...), custom_call_target="tpu_custom_call" | custom-call | flops 10000000 | bytes 1048576 | tf_op jit(solution)/shard_map/pallas_call | solution.py:476
  87.6 5.5 %collective-permute-start.9 = (f32[64,256]{1,0:T(8,128)S(1)}, f32[64,256]{1,0:T(8,128)S(1)}, u32[]{:S(2)}, u32[]{:S(2)}) collective-permute-start(f32[64,256]{1,0:T(8,128)S(1)} %sub.30.v_ref.refs_3_.v3), channel_id=1, source_target_pairs={{0,8},{8,16},{16,24},{24,32},{32,40},{40,48},{48,56},{56,64},{64,7... | collective-permute-start | bytes 196616 | tf_op jit(solution)/shard_map/ppermute | solution.py:404
  93.1 3.5 %shard_map.112 = (f32[64,256]{1,0:T(8,128)S(1)}, f32[64,256]{1,0:T(8,128)S(1)}) custom-call(f32[64,256]{1,0:T(8,128)S(1)} %sub.30.v_ref.refs_3_.v3, bf16[256,1024]{1,0:T(8,128)(2,1)S(1)} %get-tuple-element.25.ohf_ref, bf16[512,1024]{1,0:T(8,128)(2,1)S(1)} %get-tuple-element.26.ohs_ref, f32[8,2,8,32,128]{4,3,2,1,0:T(8,128)S(1)} %get-tuple-element.27.wx_ref, ...), custom_call_target="tpu_custom_call" | custom-call | flops 10000000 | bytes 1048576 | tf_op jit(solution)/shard_map/pallas_call | solution.py:474
  96.6 1.3 collective-permute-start.10
  97.9 3.5 %shard_map.113 = f32[64,256]{1,0:T(8,128)S(1)} custom-call(f32[64,256]{1,0:T(8,128)S(1)} %sub.30.v_ref.refs_3_.v3, f32[64,256]{1,0:T(8,128)S(1)} %collective-permute-done.9.below_ref, f32[64,256]{1,0:T(8,128)S(1)} %sub.29.v_ref.prev_ref.refs_2_.v2, f32[64,256]{1,0:T(8,128)S(1)} %get-tuple-element.40.part_ref, f32[4,64,256]{2,1,0:T(8,128)S(1)} %get-tuple-element.33.band_ref, ...), custom_call_target="tpu_custom_call" | custom-call | flops 10000000 | bytes 1048576 | tf_op jit(solution)/shard_map/pallas_call | solution.py:476
  103.3 28.2 %all_to_all.14 = f32[32,1,128]{2,1,0:T(1,128)S(1)} all-to-all(f32[32,1,128]{2,1,0:T(1,128)S(1)} %broadcast_in_dim.36), channel_id=1, replica_groups=mesh['sec'=32,'tile'=8] {'sec'}, dimensions={0} | all-to-all | bytes 32768 | tf_op jit(solution)/shard_map/all_to_all | solution.py:481
  131.5 5.5 %collective-permute-start.11 = (f32[32,128]{1,0:T(8,128)S(1)}, f32[32,128]{1,0:T(8,128)S(1)}, u32[]{:S(2)}, u32[]{:S(2)}) collective-permute-start(f32[32,128]{1,0:T(8,128)S(1)} %bitcast.23), channel_id=1, source_target_pairs={{0,1},{1,0},{2,3},{3,2},{4,5},{5,4},{6,7},{7,6},{8,9},{9,8},{10,11... | collective-permute-start | bytes 49160 | tf_op jit(solution)/shard_map/ppermute | solution.py:408
  137.9 1.3 shard_map.115
  (39 shorter events, 15.1 us)
Async XLA Ops:
  20.0 3.5 %collective-permute-start = (f32[4,264,128]{2,1,0:T(8,128)S(1)}, f32[4,264,128]{2,1,0:T(8,128)S(1)}, u32[]{:S(2)}, u32[]{:S(2)}) collective-permute-start(f32[4,264,128]{2,1,0:T(8,128)S(1)} %all_to_all.13), channel_id=1, source_target_pairs={{0,1},{1,0},{2,3},{3,2},{4,5},{5,4},{6,7},{7,6},{8,9},{9,8},{10,11... | collective-permute-start | bytes 1622024 | tf_op jit(solution)/shard_map/ppermute | solution.py:408
  38.9 18.8 %collective-permute-start.3 = (f32[4,64,256]{2,1,0:T(8,128)S(1)}, f32[4,64,256]{2,1,0:T(8,128)S(1)}, u32[]{:S(2)}, u32[]{:S(2)}) collective-permute-start(f32[4,64,256]{2,1,0:T(8,128)S(1)} %get-tuple-element.34), channel_id=1, source_target_pairs={{8,0},{16,8},{24,16},{32,24},{40,32},{48,40},{56,48},{64,56},{72,6... | collective-permute-start | bytes 786440 | tf_op jit(solution)/shard_map/ppermute | solution.py:404
  40.2 9.5 %collective-permute-start.1 = (f32[64,256]{1,0:T(8,128)S(1)}, f32[64,256]{1,0:T(8,128)S(1)}, u32[]{:S(2)}, u32[]{:S(2)}) collective-permute-start(f32[64,256]{1,0:T(8,128)S(1)} %get-tuple-element.24), channel_id=1, source_target_pairs={{8,0},{16,8},{24,16},{32,24},{40,32},{48,40},{56,48},{64,56},{72,6... | collective-permute-start | bytes 196616 | tf_op jit(solution)/shard_map/ppermute | solution.py:404
  49.7 7.9 %collective-permute-start.2 = (f32[64,256]{1,0:T(8,128)S(1)}, f32[64,256]{1,0:T(8,128)S(1)}, u32[]{:S(2)}, u32[]{:S(2)}) collective-permute-start(f32[64,256]{1,0:T(8,128)S(1)} %sub.27.v_ref.prev_ref.refs_0_.v0), channel_id=1, source_target_pairs={{0,8},{8,16},{16,24},{24,32},{32,40},{40,48},{48,56},{56,64},{64,7... | collective-permute-start | bytes 196616 | tf_op jit(solution)/shard_map/ppermute | solution.py:404
  56.4 5.0 %collective-permute-start.4 = (f32[64,256]{1,0:T(8,128)S(1)}, f32[64,256]{1,0:T(8,128)S(1)}, u32[]{:S(2)}, u32[]{:S(2)}) collective-permute-start(f32[64,256]{1,0:T(8,128)S(1)} %get-tuple-element.35), channel_id=1, source_target_pairs={{8,0},{16,8},{24,16},{32,24},{40,32},{48,40},{56,48},{64,56},{72,6... | collective-permute-start | bytes 196616 | tf_op jit(solution)/shard_map/ppermute | solution.py:404
  61.4 9.5 %collective-permute-start.5 = (f32[64,256]{1,0:T(8,128)S(1)}, f32[64,256]{1,0:T(8,128)S(1)}, u32[]{:S(2)}, u32[]{:S(2)}) collective-permute-start(f32[64,256]{1,0:T(8,128)S(1)} %sub.28.v_ref.prev_ref.refs_1_.v1), channel_id=1, source_target_pairs={{0,8},{8,16},{16,24},{24,32},{32,40},{40,48},{48,56},{56,64},{64,7... | collective-permute-start | bytes 196616 | tf_op jit(solution)/shard_map/ppermute | solution.py:404
  69.6 5.4 %collective-permute-start.6 = (f32[64,256]{1,0:T(8,128)S(1)}, f32[64,256]{1,0:T(8,128)S(1)}, u32[]{:S(2)}, u32[]{:S(2)}) collective-permute-start(f32[64,256]{1,0:T(8,128)S(1)} %get-tuple-element.37), channel_id=1, source_target_pairs={{8,0},{16,8},{24,16},{32,24},{40,32},{48,40},{56,48},{64,56},{72,6... | collective-permute-start | bytes 196616 | tf_op jit(solution)/shard_map/ppermute | solution.py:404
  75.0 8.6 %collective-permute-start.7 = (f32[64,256]{1,0:T(8,128)S(1)}, f32[64,256]{1,0:T(8,128)S(1)}, u32[]{:S(2)}, u32[]{:S(2)}) collective-permute-start(f32[64,256]{1,0:T(8,128)S(1)} %sub.29.v_ref.prev_ref.refs_2_.v2), channel_id=1, source_target_pairs={{0,8},{8,16},{16,24},{24,32},{32,40},{40,48},{48,56},{56,64},{64,7... | collective-permute-start | bytes 196616 | tf_op jit(solution)/shard_map/ppermute | solution.py:404
  82.3 5.3 %collective-permute-start.8 = (f32[64,256]{1,0:T(8,128)S(1)}, f32[64,256]{1,0:T(8,128)S(1)}, u32[]{:S(2)}, u32[]{:S(2)}) collective-permute-start(f32[64,256]{1,0:T(8,128)S(1)} %get-tuple-element.39), channel_id=1, source_target_pairs={{8,0},{16,8},{24,16},{32,24},{40,32},{48,40},{56,48},{64,56},{72,6... | collective-permute-start | bytes 196616 | tf_op jit(solution)/shard_map/ppermute | solution.py:404
  87.6 10.3 %collective-permute-start.9 = (f32[64,256]{1,0:T(8,128)S(1)}, f32[64,256]{1,0:T(8,128)S(1)}, u32[]{:S(2)}, u32[]{:S(2)}) collective-permute-start(f32[64,256]{1,0:T(8,128)S(1)} %sub.30.v_ref.refs_3_.v3), channel_id=1, source_target_pairs={{0,8},{8,16},{16,24},{24,32},{32,40},{40,48},{48,56},{56,64},{64,7... | collective-permute-start | bytes 196616 | tf_op jit(solution)/shard_map/ppermute | solution.py:404
  96.6 5.4 %collective-permute-start.10 = (f32[64,256]{1,0:T(8,128)S(1)}, f32[64,256]{1,0:T(8,128)S(1)}, u32[]{:S(2)}, u32[]{:S(2)}) collective-permute-start(f32[64,256]{1,0:T(8,128)S(1)} %get-tuple-element.41), channel_id=1, source_target_pairs={{8,0},{16,8},{24,16},{32,24},{40,32},{48,40},{56,48},{64,56},{72,6... | collective-permute-start | bytes 196616 | tf_op jit(solution)/shard_map/ppermute | solution.py:404
  131.5 6.3 %collective-permute-start.11 = (f32[32,128]{1,0:T(8,128)S(1)}, f32[32,128]{1,0:T(8,128)S(1)}, u32[]{:S(2)}, u32[]{:S(2)}) collective-permute-start(f32[32,128]{1,0:T(8,128)S(1)} %bitcast.23), channel_id=1, source_target_pairs={{0,1},{1,0},{2,3},{3,2},{4,5},{5,4},{6,7},{7,6},{8,9},{9,8},{10,11... | collective-permute-start | bytes 49160 | tf_op jit(solution)/shard_map/ppermute | solution.py:408
  139.2 1.3 collective-permute-start.12

commit v2 on v1

--- a/solution.py
+++ b/solution.py
@@ -91,25 +91,47 @@
     return pl.ds(pl.multiple_of(blk * 128, 128), 128)
 
 
+def pack_kernel(
+    first_ref, second_ref, count_ref, cell1_ref, cell2_ref, frac1_ref, frac2_ref, target_ref, stiff_ref, out_ref
+):
+    for k in range(4):
+        out_ref[k, 0:32, :] = cell1_ref[...].astype(F32)
+        out_ref[k, 32:64, :] = cell2_ref[...].astype(F32)
+        for c in range(2):
+            at = slice(32 * c, 32 * c + 32)
+            out_ref[k, 64 + at.start : 64 + at.stop, :] = frac1_ref[c]
+            out_ref[k, 128 + at.start : 128 + at.stop, :] = frac2_ref[c]
+            out_ref[k, 192 + at.start : 192 + at.stop, :] = target_ref[c]
+        rows = [first_ref[...], second_ref[...], count_ref[...]]
+        tail = jnp.concatenate([r.astype(F32) for r in rows] + [stiff_ref[...], jnp.zeros((4, 128), F32)], 0)
+        out_ref[k, 256:264, :] = tail
+
+
 def tables_kernel(
-    comp_ref, data_ref, wx_ref, wy_ref, fx_ref, col_ref, live_ref, ohf_ref, ohs_ref, own_ref, down_ref, f_ref
+    comp_ref, same_ref, other_ref,
+    wx_ref, wy_ref, fx_ref, col_ref, live_ref, ohf_ref, ohs_ref, own_ref, down_ref, f_ref
 ):
     comp = comp_ref[0]
 
-    def body(blk, carry):
+    def fill(data_ref, at_blk, blk):
         lanes = lanes_of(blk)
-        count = data_ref[blk, 258, :][None, :]
+        count = data_ref[at_blk, 258, :][None, :]
+        goal = []
         for group in range(4):
             ms = slice(8 * group, 8 * group + 8)
             slot = (sublane_ids() + 8 * group).astype(F32)
-            live_ref[blk, ms, :] = jnp.where(slot < count, SCALE, 0.0)
+            live = slot < count
+            live_ref[blk, ms, :] = jnp.where(live, SCALE, 0.0)
+            at = pl.multiple_of(192 + 32 * comp + 8 * group, 8)
+            goal.append(jnp.where(live, data_ref[at_blk, pl.ds(at, 8), :], 0.0))
         for side in range(2):
             for group in range(4):
                 ms = slice(8 * group, 8 * group + 8)
-                cell = data_ref[blk, 32 * side + 8 * group : 32 * side + 8 * group + 8, :].astype(jnp.int32)
+                at = 32 * side + 8 * group
+                cell = data_ref[at_blk, at : at + 8, :].astype(jnp.int32)
                 base = 64 + 64 * side + 8 * group
-                fx = data_ref[blk, base : base + 8, :]
-                fy = data_ref[blk, base + 32 : base + 40, :]
+                fx = data_ref[at_blk, base : base + 8, :]
+                fy = data_ref[at_blk, base + 32 : base + 40, :]
                 row = (cell * 37) >> 8
                 col = cell - 7 * row
                 fx_ref[blk, side, ms, :] = fx
@@ -121,76 +143,71 @@
                     wy_ref[blk, side, k, ms, :] = jnp.where(
                         row == k, 1.0 - fy, jnp.where(row == k - 1, fy, 0.0)
                     )
-        first = data_ref[blk, 256, :][None, :].astype(jnp.int32)
-        second = data_ref[blk, 257, :][None, :].astype(jnp.int32)
+        first = data_ref[at_blk, 256, :][None, :].astype(jnp.int32)
+        second = data_ref[at_blk, 257, :][None, :].astype(jnp.int32)
         ids = lax.broadcasted_iota(jnp.int32, (256, 128), 0)
         ohf_ref[:, lanes] = jnp.where(ids == first, 1.0, 0.0).astype(jnp.bfloat16)
         ohs_ref[0:256, lanes] = jnp.where(ids == second, 1.0, 0.0).astype(jnp.bfloat16)
         ohs_ref[256:512, lanes] = jnp.where(ids + 256 == second, 1.0, 0.0).astype(jnp.bfloat16)
-        goal = []
-        for group in range(4):
-            at = pl.multiple_of(192 + 32 * comp + 8 * group, 8)
-            goal.append(
-                data_ref[blk, pl.ds(at, 8), :] * (live_ref[blk, 8 * group : 8 * group + 8, :] * (1.0 / SCALE))
-            )
         for side in range(2):
             tops = load_table(wy_ref, blk, side)
             tops = [[tops[q][g] * goal[g] for g in range(4)] for q in range(8)]
             spread_block(tops, load_table(wx_ref, blk, side), f_ref, lanes, (side,))
+
+    def body(blk, carry):
+        fill(same_ref, blk, blk)
+        fill(other_ref, blk, blk + 4)
         return carry
 
-    lax.fori_loop(0, 8, body, 0)
+    lax.fori_loop(0, 4, body, 0)
     at_first = merge3(lax.dot_general(split3(f_ref[0]), ohf_ref[...], NT, preferred_element_type=F32))
     at_second = merge3(lax.dot_general(split3(f_ref[1]), ohs_ref[...], NT, preferred_element_type=F32))
     own_ref[...] = at_first - at_second[:, :256]
     down_ref[...] = at_second[:, 256:]
 
 
-def stencil_kernel(wx_ref, wy_ref, live_ref, ohf_ref, ohs_ref, stiff_ref, own_ref, down_ref, f_ref):
+def stencil_kernel(comp_ref, wx_ref, wy_ref, live_ref, ohs_ref, half_ref, f_ref):
+    step = comp_ref[0]
+
     def body(blk, carry):
         lanes = lanes_of(blk)
         live = [live_ref[blk, 8 * g : 8 * g + 8, :] for g in range(4)]
-        for side in range(2):
-            zero = [jnp.zeros((8, 128), F32)] * 4
-            for kind_x in range(2):
-                wx = load_table(wx_ref, blk, side) + [zero]
-                sides = [[wx[p][g] * wx[p + kind_x][g] for g in range(4)] for p in range(8)]
-                for kind_y in range(2):
-                    wy = load_table(wy_ref, blk, side) + [zero]
-                    tops = [[wy[q][g] * wy[q + kind_y][g] * live[g] for g in range(4)] for q in range(8)]
-                    spread_block(tops, sides, f_ref, lanes, (side, 2 * kind_y + kind_x))
+        zero = [jnp.zeros((8, 128), F32)] * 4
+        wy = load_table(wy_ref, blk, 1) + [zero]
+        tops = [
+            [wy[q][g] * jnp.where(step == 0, wy[q][g], wy[q + 1][g]) * live[g] for g in range(4)]
+            for q in range(8)
+        ]
+        for kind in range(2):
+            wx = load_table(wx_ref, blk, 1) + [zero]
+            sides = [[wx[p][g] * wx[p + kind][g] for g in range(4)] for p in range(8)]
+            spread_block(tops, sides, f_ref, lanes, (kind,))
         return carry
 
     lax.fori_loop(0, 8, body, 0)
-    node = lax.broadcasted_iota(jnp.int32, (64, 256), 0)
-    p = node & 7
-    q = node >> 3
-    one = lambda cond: jnp.where(cond, 1.0, 0.0)
-    stiff = stiff_ref[...] * SCALE
-    degree = one(p < 7) + one(p > 0) + one(q < 7) + one(q > 0)
-    extra = [
-        stiff * degree + (DAMPING - SHIFT) * SCALE,
-        -stiff * one(p < 7),
-        -stiff * one(q < 7),
-        None,
-    ]
-    for kind in range(4):
-        at_first = merge3(lax.dot_general(split3(f_ref[0, kind]), ohf_ref[...], NT, preferred_element_type=F32))
-        at_second = merge3(lax.dot_general(split3(f_ref[1, kind]), ohs_ref[...], NT, preferred_element_type=F32))
-        total = at_first + at_second[:, :256]
-        own_ref[kind] = total if extra[kind] is None else total + extra[kind]
-        down_ref[kind] = at_second[:, 256:]
-
-
-def up_kernel(v_ref, ohf_ref, ohs_ref, wx_ref, wy_ref, fx_ref, col_ref, live_ref, own_ref, down_ref, g_ref, f_ref):
-    g_ref[...] = merge3(jnp.dot(split3(v_ref[...]), ohf_ref[...], preferred_element_type=F32))
+    for kind in range(2):
+        half_ref[kind] = merge3(
+            lax.dot_general(split3(f_ref[kind]), ohs_ref[256:512, :], NT, preferred_element_type=F32)
+        )
+
+
+def up_kernel(
+    v_ref, ohf_ref, ohs_ref, wx_ref, wy_ref, fx_ref, col_ref, live_ref,
+    own_ref, down_ref, gap_ref, g_ref, h_ref, f_ref
+):
+    parts = split3(v_ref[...])
+    g_ref[...] = merge3(jnp.dot(parts, ohf_ref[...], preferred_element_type=F32))
+    h_ref[...] = merge3(jnp.dot(parts, ohs_ref[0:256, :], preferred_element_type=F32))
 
     def body(blk, carry):
         lanes = lanes_of(blk)
         got = sample_block(g_ref, lanes, wy_ref, fx_ref, col_ref, blk, 0)
-        got = [got[g] * live_ref[blk, 8 * g : 8 * g + 8, :] for g in range(4)]
+        less = sample_block(h_ref, lanes, wy_ref, fx_ref, col_ref, blk, 1)
+        gap = [(got[g] - less[g]) * live_ref[blk, 8 * g : 8 * g + 8, :] for g in range(4)]
+        for g in range(4):
+            gap_ref[blk, 8 * g : 8 * g + 8, :] = gap[g]
         tops = load_table(wy_ref, blk, 1)
-        tops = [[tops[q][g] * got[g] for g in range(4)] for q in range(8)]
+        tops = [[tops[q][g] * gap[g] for g in range(4)] for q in range(8)]
         spread_block(tops, load_table(wx_ref, blk, 1), f_ref, lanes)
         return carry
 
@@ -201,33 +218,41 @@
 
 
 def down_kernel(
-    v_ref, below_ref, prev_ref, part_ref, band_ref, band2_ref,
+    comp_ref, v_ref, below_ref, prev_ref, part_ref, gap_ref, mine_ref, other_ref, stiff_ref,
     ohf_ref, ohs_ref, wx_ref, wy_ref, fx_ref, col_ref, live_ref, out_ref, g_ref, f_ref, *, back
 ):
-    rows = jnp.concatenate([split3(v_ref[...]), split3(below_ref[...])], 1)
-    g_ref[...] = merge3(jnp.dot(rows, ohs_ref[...], preferred_element_type=F32))
+    g_ref[...] = merge3(jnp.dot(split3(below_ref[...]), ohs_ref[256:512, :], preferred_element_type=F32))
 
     def body(blk, carry):
         lanes = lanes_of(blk)
         got = sample_block(g_ref, lanes, wy_ref, fx_ref, col_ref, blk, 1)
-        got = [got[g] * live_ref[blk, 8 * g : 8 * g + 8, :] for g in range(4)]
+        gap = [
+            gap_ref[blk, 8 * g : 8 * g + 8, :] - got[g] * live_ref[blk, 8 * g : 8 * g + 8, :]
+            for g in range(4)
+        ]
         tops = load_table(wy_ref, blk, 0)
-        tops = [[tops[q][g] * got[g] for g in range(4)] for q in range(8)]
+        tops = [[tops[q][g] * gap[g] for g in range(4)] for q in range(8)]
         spread_block(tops, load_table(wx_ref, blk, 0), f_ref, lanes)
         return carry
 
     lax.fori_loop(0, 8, body, 0)
     forces = merge3(lax.dot_general(split3(f_ref[...]), ohf_ref[...], NT, preferred_element_type=F32))
     v = v_ref[...]
-    band = [band_ref[k] + band2_ref[k] for k in range(4)]
     up = lambda x, d: pltpu.roll(x, 64 - d, 0)
     dn = lambda x, d: pltpu.roll(x, d, 0)
-    total = band[0] * v
+    node = lax.broadcasted_iota(jnp.int32, (64, 256), 0)
+    right = jnp.where((node & 7) < 7, up(v, 1) - v, 0.0)
+    below = jnp.where(node < 56, up(v, 8) - v, 0.0)
+    bend = (dn(right, 1) - right) + (dn(below, 8) - below)
+    total = forces - part_ref[...] + (stiff_ref[...] * SCALE) * bend + ((DAMPING - SHIFT) * SCALE) * v
+    first = comp_ref[0] == 0
+    band = [jnp.where(first, mine_ref[k], other_ref[k]) for k in range(2)]
+    band += [jnp.where(first, other_ref[k], mine_ref[k]) for k in range(2)]
+    total = total + band[0] * v
     total = total + band[1] * up(v, 1) + dn(band[1] * v, 1)
     total = total + band[2] * up(v, 8) + dn(band[2] * v, 8)
     total = total + band[3] * up(v, 9) + dn(band[3] * v, 9)
     total = total + dn(band[3] * up(v, 8), 1) + dn(band[3] * up(v, 1), 8)
-    total = total - forces - part_ref[...]
     if back:
         total = total - BACK * prev_ref[...]
     out_ref[...] = total
@@ -386,15 +411,15 @@
         other_ref[k] = both[32:]
 
 
-def call(kernel, outs, n_in, scratch=(), smem=0, flops=10**7):
+def call(kernel, outs, n_in, scratch=(), smem=0, us=2.0):
     return pl.pallas_call(
         kernel,
         out_shape=[jax.ShapeDtypeStruct(s, d) for s, d in outs],
         in_specs=[pl.BlockSpec(memory_space=pltpu.SMEM)] * smem + [VMEM] * (n_in - smem),
         out_specs=[VMEM] * len(outs),
         scratch_shapes=[pltpu.VMEM(s, d) for s, d in scratch],
-        compiler_params=pltpu.CompilerParams(vmem_limit_bytes=48 * 1024 * 1024),
-        cost_estimate=pl.CostEstimate(flops=flops, bytes_accessed=1 << 20, transcendentals=0),
+        compiler_params=pltpu.CompilerParams(vmem_limit_bytes=20 * 1024 * 1024),
+        cost_estimate=pl.CostEstimate(flops=int(us * 1e9), bytes_accessed=1 << 18, transcendentals=0),
     )
 
 
@@ -416,30 +441,27 @@
     core = tile % 2
     sections = lax.axis_size("sec")
     second = ov_second // sections + jnp.where(ov_second % sections == sec, 0, 256)
-    rows = [
-        cell_first.astype(F32),
-        cell_second.astype(F32),
-        frac_first.reshape(64, 128),
-        frac_second.reshape(64, 128),
-        target.reshape(64, 128),
-        (ov_first // sections).astype(F32)[None],
-        second.astype(F32)[None],
-        match_count.astype(F32)[None],
+    packed = call(pack_kernel, [((4, 264, 128), F32)], 9)(
+        (ov_first // sections).reshape(1, 128),
+        second.reshape(1, 128),
+        match_count.reshape(1, 128),
+        cell_first,
+        cell_second,
+        frac_first,
+        frac_second,
+        target,
         jnp.pad(stiffness.reshape(1, 32), ((0, 0), (0, 96))),
-        jnp.zeros((4, 128), F32),
-    ]
-    packed = jnp.concatenate(rows, 0)
+    )[0]
     groups = [[0, 2, 4, 6], [1, 3, 5, 7]]
-    same = lax.all_to_all(
-        jnp.broadcast_to(packed[None], (4, 264, 128)), "tile", 0, 0, tiled=True, axis_index_groups=groups
-    )
-    data = jnp.concatenate([same, swapped(same)], 0)
-    pair = data[:, 259, :32].reshape(2, 4, 32)
+    same = lax.all_to_all(packed, "tile", 0, 0, tiled=True, axis_index_groups=groups)
+    other = swapped(same)
+    pair = jnp.stack([same[:, 259, :32], other[:, 259, :32]])
     pair = jnp.where(core == 0, pair, pair[::-1])
     stiff = jnp.transpose(pair, (1, 0, 2)).reshape(1, 256)
 
     field = ((64, 256), F32)
     bf16 = jnp.bfloat16
+    comp = core.reshape(1)
     wx, wy, fx, col, live, ohf, ohs, own, down = call(
         tables_kernel,
         [
@@ -453,28 +475,26 @@
             field,
             field,
         ],
-        2,
+        3,
         [((2, 64, 1024), F32)],
         smem=1,
-    )(core.reshape(1), data)
+    )(comp, same, other)
     start_down = shifted(down, -1)
-    band, band_down = call(
-        stencil_kernel,
-        [((4, 64, 256), F32), ((4, 64, 256), F32)],
-        6,
-        [((2, 4, 64, 1024), F32)],
-    )(wx, wy, live, ohf, ohs, stiff)
-    band2 = shifted(band_down, -1)
+    half = call(stencil_kernel, [((2, 64, 256), F32)], 5, [((2, 64, 1024), F32)], smem=1, us=4.0)(
+        comp, wx, wy, live, ohs
+    )[0]
+    mine = shifted(half, -1)
+    other = swapped(mine)
     tables = (ohf, ohs, wx, wy, fx, col, live)
-    scratch = [((64, 1024), F32), ((64, 1024), F32)]
+    wide = ((64, 1024), F32)
     fields = [own - start_down]
     for k in range(ITERS):
         v = fields[-1]
         below = shifted(v, 1)
-        part, down = call(up_kernel, [field, field], 8, scratch)(v, *tables)
+        part, down, gap = call(up_kernel, [field, field, ((8, 32, 128), F32)], 8, [wide, wide, wide])(v, *tables)
         above = shifted(down, -1)
-        partial = call(functools.partial(down_kernel, back=k > 0), [field], 13, scratch)(
-            v, below, fields[max(k - 1, 0)], part, band, band2, *tables
+        partial = call(functools.partial(down_kernel, back=k > 0), [field], 16, [wide, wide], smem=1)(
+            comp, v, below, fields[max(k - 1, 0)], part, gap, mine, other, stiff, *tables
         )[0]
         fields.append(partial - above)
     gram = call(dots_kernel, [((1, 128), F32)], 5)(*fields)[0]

time: 142 us -> 126 us (0.89)
  Pallas kernels: 45.6 us -> 24.8 us
  local copies, waits for them, and re-layouts: 3.22 us -> 10.9 us
  blocking collectives: 41.8 us -> 38.9 us
  other arithmetic: 3.54 us -> 1.44 us
    pallas_call x9 -> x10, Pallas kernels: 38.4 us -> 18.7 us  [the longest x4 9.18 us: on_device(): call(up_kernel, [field, field, ((8, 32, 128), F32)], 8, [wide, wide, wide])]
    unnamed x1 -> x38, local copies, waits for them, and re-layouts: 0.04 us -> 10.1 us
    all_to_all x1, blocking collectives: 28.2 us -> 25.4 us  [on_device(): lax.all_to_all(jnp.broadcast_to(gram, (32, 128)), 'sec', 0, 0, tiled=True)]
    concatenate x2 -> x0, local copies, waits for them, and re-layouts: 2.35 us -> none  [the longest x1 2.31 us: on_device(): packed = jnp.concatenate(rows, 0)]
    convert_element_type x2 -> x0, other arithmetic: 1.44 us -> none  [the longest x1 0.72 us: on_device(): cell_first.astype(F32)]
    ppermute x3 -> x4, starting transfers between devices: 7.83 us -> 8.81 us  [swapped(): return lax.ppermute(block, 'tile', [(i, i ^ 1) for i in range(8)])]
    ppermute x3 -> x4, waiting for transfers between devices: 3.22 us -> 3.26 us  [swapped(): return lax.ppermute(block, 'tile', [(i, i ^ 1) for i in range(8)])]
  transfers between devices with their start and end apart: 13 -> 14, of which waited for: 8 -> 8; matrix products, arithmetic and copies ran while one was open for 0% -> 0% of each run, Pallas kernels for 20% -> 15%
where the time goes in v2:
time: 126 us; the launch traced here: 125 us
  blocking collectives  38.9 us (31%)
  starting transfers between devices  34 us (27%)
  Pallas kernels  24.8 us (20%)
  waiting for transfers between devices  14.4 us (11%)
  local copies, waits for them, and re-layouts  10.9 us (9%)
  other arithmetic  1.44 us (1%)
    all_to_all x1, blocking collectives, on_device(): lax.all_to_all(jnp.broadcast_to(gram, (32, 128)), 'sec', 0, 0, tiled=True)  25.4 us
    ppermute x10, starting transfers between devices, shifted(): return lax.ppermute(block, 'sec', route)  25.2 us
    all_to_all x1, blocking collectives, on_device(): lax.all_to_all(packed, 'tile', 0, 0, tiled=True, axis_index_groups=groups)  13.5 us
    ppermute x10, waiting for transfers between devices, shifted(): return lax.ppermute(block, 'sec', route)  11.1 us
    unnamed x38, local copies, waits for them, and re-layouts  10.1 us
    pallas_call x4, Pallas kernels, on_device(): call(up_kernel, [field, field, ((8, 32, 128), F32)], 8, [wide, wide, wide])  9.18 us
    ppermute x4, starting transfers between devices, swapped(): return lax.ppermute(block, 'tile', [(i, i ^ 1) for i in range(8)])  8.81 us
    pallas_call x4, Pallas kernels, on_device(): call(functools.partial(down_kernel, back=k > 0), [field], 16, [wide, wide...  7.21 us
  transfers between devices with their start and end apart: 14, of which 8 were waited for; matrix products, arithmetic and copies ran while one was open for 0% of the time, Pallas kernels for 15%

profile of v2, /device:TPU:1, one launch (start us, length us, event | category | flops | bytes accessed | tf_op | source)
XLA Modules:
  0.0 125.4 jit_solution(9674475095630268556)
XLA Ops:
  6.4 13.5 %all_to_all.13.same_ref = f32[4,264,128]{2,1,0:T(8,128)S(1)} all-to-all(f32[4,264,128]{2,1,0:T(8,128)S(1)} %shard_map.104), channel_id=1, replica_groups={{0,2,4,6},{1,3,5,7},{8,10,12,14},{9,11,13,15},{16,18,20,22},{17,19,21,2..., dimensions={0} | all-to-all | bytes 1081344 | tf_op jit(solution)/shard_map/all_to_all | solution.py:456
  19.9 1.9 %collective-permute-start = (f32[4,264,128]{2,1,0:T(8,128)S(1)}, f32[4,264,128]{2,1,0:T(8,128)S(1)}, u32[]{:S(2)}, u32[]{:S(2)}) collective-permute-start(f32[4,264,128]{2,1,0:T(8,128)S(1)} %all_to_all.13.same_ref), channel_id=1, source_target_pairs={{0,1},{1,0},{2,3},{3,2},{4,5},{5,4},{6,7},{7,6},{8,9},{9,8},{10,11... | collective-permute-start | bytes 1622024 | tf_op jit(solution)/shard_map/ppermute | solution.py:433
  21.8 1.6 %collective-permute-done.other_ref = f32[4,264,128]{2,1,0:T(8,128)S(1)} collective-permute-done((f32[4,264,128]{2,1,0:T(8,128)S(1)}, f32[4,264,128]{2,1,0:T(8,128)S(1)}, u32[]{:S(2)}, u32[]{:S(2)}) %collective-permute-start) | collective-permute-done | bytes 540704 | tf_op jit(solution)/shard_map/ppermute | solution.py:433
  23.4 3.5 %shard_map.105 = (f32[8,2,8,32,128]{4,3,2,1,0:T(8,128)S(1)}, f32[8,2,8,32,128]{4,3,2,1,0:T(8,128)S(1)}, f32[8,2,32,128]{3,2,1,0:T(8,128)S(1)}, s32[8,2,32,128]{3...) custom-call(s32[1]{0:T(128)} %bitcast.1.comp_ref, ...), custom_call_target="tpu_custom_call" | custom-call | flops 2000000000 | bytes 262144 | tf_op jit(solution)/shard_map/pallas_call | solution.py:465
  28.2 2.3 %shard_map.107 = f32[2,64,256]{2,1,0:T(8,128)S(1)} custom-call(s32[1]{0:T(128)} %bitcast.1.comp_ref, f32[8,2,8,32,128]{4,3,2,1,0:T(8,128)S(1)} %get-tuple-element.29.wx_ref, f32[8,2,8,32,128]{4,3,2,1,0:T(8,128)S(1)} %get-tuple-element.30.wy_ref, f32[8,32,128]{2,1,0:T(8,128)S(1)} %get-tuple-element.33.live_ref, bf16[512,1024]{1,0:T(8,128)(2,1)S(1)} %get-tuple-element.28.ohs_ref), custom_call_target="tpu_custom_call" | custom-call | flops 4000000000 | bytes 262144 | tf_op jit(solution)/shard_map/pallas_call | solution.py:483
  32.0 4.6 %collective-permute-start.2 = (f32[64,256]{1,0:T(8,128)S(1)}, f32[64,256]{1,0:T(8,128)S(1)}, u32[]{:S(2)}, u32[]{:S(2)}) collective-permute-start(f32[64,256]{1,0:T(8,128)S(1)} %sub.27.v_ref.prev_ref.refs_0_.v0), channel_id=1, source_target_pairs={{0,8},{8,16},{16,24},{24,32},{32,40},{40,48},{48,56},{56,64},{64,7... | collective-permute-start | bytes 196616 | tf_op jit(solution)/shard_map/ppermute | solution.py:429
  39.0 1.6 %copy-done.7 = f32[8,2,8,32,128]{4,3,2,1,0:T(8,128)S(1)} copy-done((f32[8,2,8,32,128]{4,3,2,1,0:T(8,128)S(1)}, f32[8,2,8,32,128]{4,3,2,1,0:T(8,128)}, u32[]{:S(2)}) %copy-start.7) | copy-done | bytes 2097176
  44.7 2.3 %shard_map.106 = (f32[64,256]{1,0:T(8,128)S(1)}, f32[64,256]{1,0:T(8,128)S(1)}, f32[8,32,128]{2,1,0:T(8,128)S(1)}) custom-call(f32[64,256]{1,0:T(8,128)S(1)} %sub.27.v_ref.prev_ref.refs_0_.v0, bf16[256,1024]{1,0:T(8,128)(2,1)S(1)} %copy-done.12, bf16[512,1024]{1,0:T(8,128)(2,1)S(1)} %copy-done.10, f32[8,2,8,32,128]{4,3,2,1,0:T(8,128)S(1)} %get-tuple-element.29.wx_ref, ...), custom_call_target="tpu_custom_call" | custom-call | flops 2000000000 | bytes 262144 | tf_op jit(solution)/shard_map/pallas_call | solution.py:494
  48.4 1.8 %shard_map.108 = f32[64,256]{1,0:T(8,128)S(1)} custom-call(s32[1]{0:T(128)} %bitcast.1.comp_ref, f32[64,256]{1,0:T(8,128)S(1)} %sub.27.v_ref.prev_ref.refs_0_.v0, f32[64,256]{1,0:T(8,128)S(1)} %collective-permute-done.2.below_ref, f32[64,256]{1,0:T(8,128)S(1)} %sub.27.v_ref.prev_ref.refs_0_.v0, f32[64,256]{1,0:T(8,128)S(1)} %get-tuple-element.34.part_ref, ...), custom_call_target="tpu_custom_call" | custom-call | flops 2000000000 | bytes 262144 | tf_op jit(solution)/shard_map/pallas_call | solution.py:496
  50.2 2.5 %collective-permute-done.5 = f32[64,256]{1,0:T(8,128)S(1)} collective-permute-done((f32[64,256]{1,0:T(8,128)S(1)}, f32[64,256]{1,0:T(8,128)S(1)}, u32[]{:S(2)}, u32[]{:S(2)}) %collective-permute-start.5) | collective-permute-done | bytes 65568 | tf_op jit(solution)/shard_map/ppermute | solution.py:429
  52.7 3.5 %collective-permute-start.6 = (f32[64,256]{1,0:T(8,128)S(1)}, f32[64,256]{1,0:T(8,128)S(1)}, u32[]{:S(2)}, u32[]{:S(2)}) collective-permute-start(f32[64,256]{1,0:T(8,128)S(1)} %sub.28.v_ref.prev_ref.refs_1_.v1), channel_id=1, source_target_pairs={{0,8},{8,16},{16,24},{24,32},{32,40},{40,48},{48,56},{56,64},{64,7... | collective-permute-start | bytes 196616 | tf_op jit(solution)/shard_map/ppermute | solution.py:429
  56.2 2.3 %shard_map.109 = (f32[64,256]{1,0:T(8,128)S(1)}, f32[64,256]{1,0:T(8,128)S(1)}, f32[8,32,128]{2,1,0:T(8,128)S(1)}) custom-call(f32[64,256]{1,0:T(8,128)S(1)} %sub.28.v_ref.prev_ref.refs_1_.v1, bf16[256,1024]{1,0:T(8,128)(2,1)S(1)} %copy-done.13, bf16[512,1024]{1,0:T(8,128)(2,1)S(1)} %copy-done.10, f32[8,2,8,32,128]{4,3,2,1,0:T(8,128)S(1)} %get-tuple-element.29.wx_ref, ...), custom_call_target="tpu_custom_call" | custom-call | flops 2000000000 | bytes 262144 | tf_op jit(solution)/shard_map/pallas_call | solution.py:494
  59.8 1.8 %shard_map.110 = f32[64,256]{1,0:T(8,128)S(1)} custom-call(s32[1]{0:T(128)} %bitcast.1.comp_ref, f32[64,256]{1,0:T(8,128)S(1)} %sub.28.v_ref.prev_ref.refs_1_.v1, f32[64,256]{1,0:T(8,128)S(1)} %collective-permute-done.6.below_ref, f32[64,256]{1,0:T(8,128)S(1)} %sub.27.v_ref.prev_ref.refs_0_.v0, f32[64,256]{1,0:T(8,128)S(1)} %get-tuple-element.37.part_ref, ...), custom_call_target="tpu_custom_call" | custom-call | flops 2000000000 | bytes 262144 | tf_op jit(solution)/shard_map/pallas_call | solution.py:496
  61.6 3.7 %collective-permute-done.7 = f32[64,256]{1,0:T(8,128)S(1)} collective-permute-done((f32[64,256]{1,0:T(8,128)S(1)}, f32[64,256]{1,0:T(8,128)S(1)}, u32[]{:S(2)}, u32[]{:S(2)}) %collective-permute-start.7) | collective-permute-done | bytes 65568 | tf_op jit(solution)/shard_map/ppermute | solution.py:429
  65.3 5.3 %collective-permute-start.8 = (f32[64,256]{1,0:T(8,128)S(1)}, f32[64,256]{1,0:T(8,128)S(1)}, u32[]{:S(2)}, u32[]{:S(2)}) collective-permute-start(f32[64,256]{1,0:T(8,128)S(1)} %sub.29.v_ref.prev_ref.refs_2_.v2), channel_id=1, source_target_pairs={{0,8},{8,16},{16,24},{24,32},{32,40},{40,48},{48,56},{56,64},{64,7... | collective-permute-start | bytes 196616 | tf_op jit(solution)/shard_map/ppermute | solution.py:429
  70.6 2.3 %shard_map.111 = (f32[64,256]{1,0:T(8,128)S(1)}, f32[64,256]{1,0:T(8,128)S(1)}, f32[8,32,128]{2,1,0:T(8,128)S(1)}) custom-call(f32[64,256]{1,0:T(8,128)S(1)} %sub.29.v_ref.prev_ref.refs_2_.v2, bf16[256,1024]{1,0:T(8,128)(2,1)S(1)} %copy-done.13, bf16[512,1024]{1,0:T(8,128)(2,1)S(1)} %copy-done.10, f32[8,2,8,32,128]{4,3,2,1,0:T(8,128)S(1)} %get-tuple-element.29.wx_ref, ...), custom_call_target="tpu_custom_call" | custom-call | flops 2000000000 | bytes 262144 | tf_op jit(solution)/shard_map/pallas_call | solution.py:494
  74.2 1.8 %shard_map.112 = f32[64,256]{1,0:T(8,128)S(1)} custom-call(s32[1]{0:T(128)} %bitcast.1.comp_ref, f32[64,256]{1,0:T(8,128)S(1)} %sub.29.v_ref.prev_ref.refs_2_.v2, f32[64,256]{1,0:T(8,128)S(1)} %collective-permute-done.8.below_ref, f32[64,256]{1,0:T(8,128)S(1)} %sub.28.v_ref.prev_ref.refs_1_.v1, f32[64,256]{1,0:T(8,128)S(1)} %get-tuple-element.40.part_ref, ...), custom_call_target="tpu_custom_call" | custom-call | flops 2000000000 | bytes 262144 | tf_op jit(solution)/shard_map/pallas_call | solution.py:496
  76.0 1.9 %collective-permute-done.9 = f32[64,256]{1,0:T(8,128)S(1)} collective-permute-done((f32[64,256]{1,0:T(8,128)S(1)}, f32[64,256]{1,0:T(8,128)S(1)}, u32[]{:S(2)}, u32[]{:S(2)}) %collective-permute-start.9) | collective-permute-done | bytes 65568 | tf_op jit(solution)/shard_map/ppermute | solution.py:429
  77.9 4.0 %collective-permute-start.10 = (f32[64,256]{1,0:T(8,128)S(1)}, f32[64,256]{1,0:T(8,128)S(1)}, u32[]{:S(2)}, u32[]{:S(2)}) collective-permute-start(f32[64,256]{1,0:T(8,128)S(1)} %sub.30.v_ref.refs_3_.v3), channel_id=1, source_target_pairs={{0,8},{8,16},{16,24},{24,32},{32,40},{40,48},{48,56},{56,64},{64,7... | collective-permute-start | bytes 196616 | tf_op jit(solution)/shard_map/ppermute | solution.py:429
  82.0 2.3 %shard_map.113 = (f32[64,256]{1,0:T(8,128)S(1)}, f32[64,256]{1,0:T(8,128)S(1)}, f32[8,32,128]{2,1,0:T(8,128)S(1)}) custom-call(f32[64,256]{1,0:T(8,128)S(1)} %sub.30.v_ref.refs_3_.v3, bf16[256,1024]{1,0:T(8,128)(2,1)S(1)} %copy-done.13, bf16[512,1024]{1,0:T(8,128)(2,1)S(1)} %copy-done.10, f32[8,2,8,32,128]{4,3,2,1,0:T(8,128)S(1)} %get-tuple-element.29.wx_ref, ...), custom_call_target="tpu_custom_call" | custom-call | flops 2000000000 | bytes 262144 | tf_op jit(solution)/shard_map/pallas_call | solution.py:494
  85.6 1.8 %shard_map.114 = f32[64,256]{1,0:T(8,128)S(1)} custom-call(s32[1]{0:T(128)} %bitcast.1.comp_ref, f32[64,256]{1,0:T(8,128)S(1)} %sub.30.v_ref.refs_3_.v3, f32[64,256]{1,0:T(8,128)S(1)} %collective-permute-done.10.below_ref, f32[64,256]{1,0:T(8,128)S(1)} %sub.29.v_ref.prev_ref.refs_2_.v2, f32[64,256]{1,0:T(8,128)S(1)} %get-tuple-element.43.part_ref, ...), custom_call_target="tpu_custom_call" | custom-call | flops 2000000000 | bytes 262144 | tf_op jit(solution)/shard_map/pallas_call | solution.py:496
  87.4 1.9 %collective-permute-done.11 = f32[64,256]{1,0:T(8,128)S(1)} collective-permute-done((f32[64,256]{1,0:T(8,128)S(1)}, f32[64,256]{1,0:T(8,128)S(1)}, u32[]{:S(2)}, u32[]{:S(2)}) %collective-permute-start.11) | collective-permute-done | bytes 65568 | tf_op jit(solution)/shard_map/ppermute | solution.py:429
  90.6 25.4 %all_to_all.14 = f32[32,1,128]{2,1,0:T(1,128)S(1)} all-to-all(f32[32,1,128]{2,1,0:T(1,128)S(1)} %broadcast_in_dim.13), channel_id=1, replica_groups=mesh['sec'=32,'tile'=8] {'sec'}, dimensions={0} | all-to-all | bytes 32768 | tf_op jit(solution)/shard_map/all_to_all | solution.py:501
  116.0 5.3 %collective-permute-start.12 = (f32[32,128]{1,0:T(8,128)S(1)}, f32[32,128]{1,0:T(8,128)S(1)}, u32[]{:S(2)}, u32[]{:S(2)}) collective-permute-start(f32[32,128]{1,0:T(8,128)S(1)} %bitcast.20), channel_id=1, source_target_pairs={{0,1},{1,0},{2,3},{3,2},{4,5},{5,4},{6,7},{7,6},{8,9},{9,8},{10,11... | collective-permute-start | bytes 49160 | tf_op jit(solution)/shard_map/ppermute | solution.py:433
  (73 shorter events, 25.7 us)
Async XLA Ops:
  19.9 3.5 %collective-permute-start = (f32[4,264,128]{2,1,0:T(8,128)S(1)}, f32[4,264,128]{2,1,0:T(8,128)S(1)}, u32[]{:S(2)}, u32[]{:S(2)}) collective-permute-start(f32[4,264,128]{2,1,0:T(8,128)S(1)} %all_to_all.13.same_ref), channel_id=1, source_target_pairs={{0,1},{1,0},{2,3},{3,2},{4,5},{5,4},{6,7},{7,6},{8,9},{9,8},{10,11... | collective-permute-start | bytes 1622024 | tf_op jit(solution)/shard_map/ppermute | solution.py:433
  26.9 3.6 %copy-start.6 = (f32[8,2,8,32,128]{4,3,2,1,0:T(8,128)}, f32[8,2,8,32,128]{4,3,2,1,0:T(8,128)S(1)}, u32[]{:S(2)}) copy-start(f32[8,2,8,32,128]{4,3,2,1,0:T(8,128)S(1)} %get-tuple-element.30.wy_ref) | copy-start | bytes 6291460
  26.9 3.6 %copy-start.9 = (bf16[512,1024]{1,0:T(8,128)(2,1)}, bf16[512,1024]{1,0:T(8,128)(2,1)S(1)}, u32[]{:S(2)}) copy-start(bf16[512,1024]{1,0:T(8,128)(2,1)S(1)} %get-tuple-element.28.ohs_ref) | copy-start | bytes 3145732
  26.9 3.6 %copy-start.11 = (bf16[256,1024]{1,0:T(8,128)(2,1)}, bf16[256,1024]{1,0:T(8,128)(2,1)S(1)}, u32[]{:S(2)}) copy-start(bf16[256,1024]{1,0:T(8,128)(2,1)S(1)} %get-tuple-element.27.ohf_ref) | copy-start | bytes 1572868
  26.9 3.6 %copy-start.14 = (f32[8,2,32,128]{3,2,1,0:T(8,128)}, f32[8,2,32,128]{3,2,1,0:T(8,128)S(1)}, u32[]{:S(2)}) copy-start(f32[8,2,32,128]{3,2,1,0:T(8,128)S(1)} %get-tuple-element.31.fx_ref) | copy-start | bytes 786436
  26.9 3.6 %copy-start.17 = (s32[8,2,32,128]{3,2,1,0:T(8,128)}, s32[8,2,32,128]{3,2,1,0:T(8,128)S(1)}, u32[]{:S(2)}) copy-start(s32[8,2,32,128]{3,2,1,0:T(8,128)S(1)} %get-tuple-element.32.col_ref) | copy-start | bytes 786436
  26.9 5.0 %collective-permute-start.1 = (f32[64,256]{1,0:T(8,128)S(1)}, f32[64,256]{1,0:T(8,128)S(1)}, u32[]{:S(2)}, u32[]{:S(2)}) collective-permute-start(f32[64,256]{1,0:T(8,128)S(1)} %get-tuple-element.26), channel_id=1, source_target_pairs={{8,0},{16,8},{24,16},{32,24},{40,32},{48,40},{56,48},{64,56},{72,6... | collective-permute-start | bytes 196616 | tf_op jit(solution)/shard_map/ppermute | solution.py:429
  30.5 7.2 %collective-permute-start.3 = (f32[2,64,256]{2,1,0:T(8,128)S(1)}, f32[2,64,256]{2,1,0:T(8,128)S(1)}, u32[]{:S(2)}, u32[]{:S(2)}) collective-permute-start(f32[2,64,256]{2,1,0:T(8,128)S(1)} %shard_map.107), channel_id=1, source_target_pairs={{8,0},{16,8},{24,16},{32,24},{40,32},{48,40},{56,48},{64,56},{72,6... | collective-permute-start | bytes 393224 | tf_op jit(solution)/shard_map/ppermute | solution.py:429
  32.0 16.3 %collective-permute-start.2 = (f32[64,256]{1,0:T(8,128)S(1)}, f32[64,256]{1,0:T(8,128)S(1)}, u32[]{:S(2)}, u32[]{:S(2)}) collective-permute-start(f32[64,256]{1,0:T(8,128)S(1)} %sub.27.v_ref.prev_ref.refs_0_.v0), channel_id=1, source_target_pairs={{0,8},{8,16},{16,24},{24,32},{32,40},{40,48},{48,56},{56,64},{64,7... | collective-permute-start | bytes 196616 | tf_op jit(solution)/shard_map/ppermute | solution.py:429
  37.8 10.6 %collective-permute-start.4 = (f32[2,64,256]{2,1,0:T(8,128)S(1)}, f32[2,64,256]{2,1,0:T(8,128)S(1)}, u32[]{:S(2)}, u32[]{:S(2)}) collective-permute-start(f32[2,64,256]{2,1,0:T(8,128)S(1)} %collective-permute-done.3.mine_ref), channel_id=1, source_target_pairs={{0,1},{1,0},{2,3},{3,2},{4,5},{5,4},{6,7},{7,6},{8,9},{9,8},{10,11... | collective-permute-start | bytes 393224 | tf_op jit(solution)/shard_map/ppermute | solution.py:433
  39.0 1.6 %copy-start.7 = (f32[8,2,8,32,128]{4,3,2,1,0:T(8,128)S(1)}, f32[8,2,8,32,128]{4,3,2,1,0:T(8,128)}, u32[]{:S(2)}) copy-start(f32[8,2,8,32,128]{4,3,2,1,0:T(8,128)} %copy-done.6) | copy-start | bytes 6291460
  40.6 1.2 copy-start.10
  44.7 3.6 %copy-start.8 = (f32[8,2,8,32,128]{4,3,2,1,0:T(8,128)S(1)}, f32[8,2,8,32,128]{4,3,2,1,0:T(8,128)}, u32[]{:S(2)}) copy-start(f32[8,2,8,32,128]{4,3,2,1,0:T(8,128)} %copy-done.6) | copy-start | bytes 6291460
  44.7 3.6 %copy-start.13 = (bf16[256,1024]{1,0:T(8,128)(2,1)S(1)}, bf16[256,1024]{1,0:T(8,128)(2,1)}, u32[]{:S(2)}) copy-start(bf16[256,1024]{1,0:T(8,128)(2,1)} %copy-done.11) | copy-start | bytes 1572868
  47.0 5.6 %collective-permute-start.5 = (f32[64,256]{1,0:T(8,128)S(1)}, f32[64,256]{1,0:T(8,128)S(1)}, u32[]{:S(2)}, u32[]{:S(2)}) collective-permute-start(f32[64,256]{1,0:T(8,128)S(1)} %get-tuple-element.36), channel_id=1, source_target_pairs={{8,0},{16,8},{24,16},{32,24},{40,32},{48,40},{56,48},{64,56},{72,6... | collective-permute-start | bytes 196616 | tf_op jit(solution)/shard_map/ppermute | solution.py:429
  52.6 7.1 %copy-start.16 = (f32[8,2,32,128]{3,2,1,0:T(8,128)S(1)}, f32[8,2,32,128]{3,2,1,0:T(8,128)}, u32[]{:S(2)}) copy-start(f32[8,2,32,128]{3,2,1,0:T(8,128)} %copy-done.14) | copy-start | bytes 786436
  52.7 7.1 %collective-permute-start.6 = (f32[64,256]{1,0:T(8,128)S(1)}, f32[64,256]{1,0:T(8,128)S(1)}, u32[]{:S(2)}, u32[]{:S(2)}) collective-permute-start(f32[64,256]{1,0:T(8,128)S(1)} %sub.28.v_ref.prev_ref.refs_1_.v1), channel_id=1, source_target_pairs={{0,8},{8,16},{16,24},{24,32},{32,40},{40,48},{48,56},{56,64},{64,7... | collective-permute-start | bytes 196616 | tf_op jit(solution)/shard_map/ppermute | solution.py:429
  58.5 6.8 %collective-permute-start.7 = (f32[64,256]{1,0:T(8,128)S(1)}, f32[64,256]{1,0:T(8,128)S(1)}, u32[]{:S(2)}, u32[]{:S(2)}) collective-permute-start(f32[64,256]{1,0:T(8,128)S(1)} %get-tuple-element.39), channel_id=1, source_target_pairs={{8,0},{16,8},{24,16},{32,24},{40,32},{48,40},{56,48},{64,56},{72,6... | collective-permute-start | bytes 196616 | tf_op jit(solution)/shard_map/ppermute | solution.py:429
  65.3 8.9 %collective-permute-start.8 = (f32[64,256]{1,0:T(8,128)S(1)}, f32[64,256]{1,0:T(8,128)S(1)}, u32[]{:S(2)}, u32[]{:S(2)}) collective-permute-start(f32[64,256]{1,0:T(8,128)S(1)} %sub.29.v_ref.prev_ref.refs_2_.v2), channel_id=1, source_target_pairs={{0,8},{8,16},{16,24},{24,32},{32,40},{40,48},{48,56},{56,64},{64,7... | collective-permute-start | bytes 196616 | tf_op jit(solution)/shard_map/ppermute | solution.py:429
  72.9 5.0 %collective-permute-start.9 = (f32[64,256]{1,0:T(8,128)S(1)}, f32[64,256]{1,0:T(8,128)S(1)}, u32[]{:S(2)}, u32[]{:S(2)}) collective-permute-start(f32[64,256]{1,0:T(8,128)S(1)} %get-tuple-element.42), channel_id=1, source_target_pairs={{8,0},{16,8},{24,16},{32,24},{40,32},{48,40},{56,48},{64,56},{72,6... | collective-permute-start | bytes 196616 | tf_op jit(solution)/shard_map/ppermute | solution.py:429
  77.9 7.6 %collective-permute-start.10 = (f32[64,256]{1,0:T(8,128)S(1)}, f32[64,256]{1,0:T(8,128)S(1)}, u32[]{:S(2)}, u32[]{:S(2)}) collective-permute-start(f32[64,256]{1,0:T(8,128)S(1)} %sub.30.v_ref.refs_3_.v3), channel_id=1, source_target_pairs={{0,8},{8,16},{16,24},{24,32},{32,40},{40,48},{48,56},{56,64},{64,7... | collective-permute-start | bytes 196616 | tf_op jit(solution)/shard_map/ppermute | solution.py:429
  84.3 5.0 %collective-permute-start.11 = (f32[64,256]{1,0:T(8,128)S(1)}, f32[64,256]{1,0:T(8,128)S(1)}, u32[]{:S(2)}, u32[]{:S(2)}) collective-permute-start(f32[64,256]{1,0:T(8,128)S(1)} %get-tuple-element.45), channel_id=1, source_target_pairs={{8,0},{16,8},{24,16},{32,24},{40,32},{48,40},{56,48},{64,56},{72,6... | collective-permute-start | bytes 196616 | tf_op jit(solution)/shard_map/ppermute | solution.py:429
  116.0 6.1 %collective-permute-start.12 = (f32[32,128]{1,0:T(8,128)S(1)}, f32[32,128]{1,0:T(8,128)S(1)}, u32[]{:S(2)}, u32[]{:S(2)}) collective-permute-start(f32[32,128]{1,0:T(8,128)S(1)} %bitcast.20), channel_id=1, source_target_pairs={{0,1},{1,0},{2,3},{3,2},{4,5},{5,4},{6,7},{7,6},{8,9},{9,8},{10,11... | collective-permute-start | bytes 49160 | tf_op jit(solution)/shard_map/ppermute | solution.py:433
  123.4 1.3 %collective-permute-start.13 = (f32[2,32,64]{2,1,0:T(8,128)S(1)}, f32[2,32,64]{2,1,0:T(8,128)S(1)}, u32[]{:S(2)}, u32[]{:S(2)}) collective-permute-start(f32[2,32,64]{2,1,0:T(8,128)S(1)} %get-tuple-element.47), channel_id=1, source_target_pairs={{0,1},{1,0},{2,3},{3,2},{4,5},{5,4},{6,7},{7,6},{8,9},{9,8},{10,11... | collective-permute-start | bytes 49160 | tf_op jit(solution)/shard_map/ppermute | solution.py:433
  (9 other events, 7.3 us)

commit v3 on v2

--- a/solution.py
+++ b/solution.py
@@ -92,30 +92,52 @@
 
 
 def pack_kernel(
-    first_ref, second_ref, count_ref, cell1_ref, cell2_ref, frac1_ref, frac2_ref, target_ref, stiff_ref, out_ref
+    place_ref, first_hbm, second_hbm, count_hbm, cell1_hbm, cell2_hbm, frac1_hbm, frac2_hbm, target_hbm, stiff_hbm,
+    out_ref, ids_ref, stiff_ref, cell_ref, sem, *, sections
 ):
-    for k in range(4):
-        out_ref[k, 0:32, :] = cell1_ref[...].astype(F32)
-        out_ref[k, 32:64, :] = cell2_ref[...].astype(F32)
+    copies = [
+        pltpu.make_async_copy(cell1_hbm, cell_ref.at[0], sem.at[0]),
+        pltpu.make_async_copy(cell2_hbm, cell_ref.at[1], sem.at[1]),
+        pltpu.make_async_copy(first_hbm, ids_ref.at[0], sem.at[2]),
+        pltpu.make_async_copy(second_hbm, ids_ref.at[1], sem.at[3]),
+        pltpu.make_async_copy(count_hbm, ids_ref.at[2], sem.at[4]),
+        pltpu.make_async_copy(stiff_hbm, stiff_ref, sem.at[5]),
+    ]
+    for k, src in enumerate((frac1_hbm, frac2_hbm, target_hbm)):
         for c in range(2):
-            at = slice(32 * c, 32 * c + 32)
-            out_ref[k, 64 + at.start : 64 + at.stop, :] = frac1_ref[c]
-            out_ref[k, 128 + at.start : 128 + at.stop, :] = frac2_ref[c]
-            out_ref[k, 192 + at.start : 192 + at.stop, :] = target_ref[c]
-        rows = [first_ref[...], second_ref[...], count_ref[...]]
-        tail = jnp.concatenate([r.astype(F32) for r in rows] + [stiff_ref[...], jnp.zeros((4, 128), F32)], 0)
-        out_ref[k, 256:264, :] = tail
-
-
-def tables_kernel(
-    comp_ref, same_ref, other_ref,
-    wx_ref, wy_ref, fx_ref, col_ref, live_ref, ohf_ref, ohs_ref, own_ref, down_ref, f_ref
-):
+            at = 64 + 64 * k + 32 * c
+            copies.append(pltpu.make_async_copy(src.at[c], out_ref.at[at : at + 32, :], sem.at[6 + 2 * k + c]))
+    for copy in copies:
+        copy.start()
+    for copy in copies:
+        copy.wait()
+    out_ref[0:32, :] = cell_ref[0].astype(F32)
+    out_ref[32:64, :] = cell_ref[1].astype(F32)
+    shift = sections.bit_length() - 1
+    first = ids_ref[0] >> shift
+    second = ids_ref[1] >> shift
+    second = second + jnp.where((ids_ref[1] & (sections - 1)) == place_ref[0], 0, 256)
+    tile = place_ref[1]
+    stiff = jnp.concatenate([stiff_ref[...], jnp.zeros((1, 96), F32)], 1)
+    stiff = pltpu.roll(jnp.broadcast_to(stiff, (8, 128)), 32 * (tile & 3), 1)
+    row = sublane_ids()
+    tail = jnp.where((row >= 3) & (row - 3 == (tile >> 2)), stiff, 0.0)
+    for k, x in enumerate((first, second, ids_ref[2])):
+        tail = jnp.where(row == k, jnp.broadcast_to(x.astype(F32), (8, 128)), tail)
+    out_ref[256:264, :] = tail
+
+
+def tables_kernel(comp_ref, *refs, blocks, add):
+    datas = refs[:blocks]
+    refs = refs[blocks:]
+    if add:
+        before_own, before_down, before_stiff = refs[:3]
+        refs = refs[3:]
+    wx_ref, wy_ref, fx_ref, col_ref, live_ref, ohf_ref, ohs_ref, own_ref, down_ref, stiff_ref, f_ref = refs
     comp = comp_ref[0]
-
-    def fill(data_ref, at_blk, blk):
-        lanes = lanes_of(blk)
-        count = data_ref[at_blk, 258, :][None, :]
+    for blk, data_ref in enumerate(datas):
+        lanes = slice(128 * blk, 128 * blk + 128)
+        count = data_ref[258, :][None, :]
         goal = []
         for group in range(4):
             ms = slice(8 * group, 8 * group + 8)
@@ -123,15 +145,21 @@
             live = slot < count
             live_ref[blk, ms, :] = jnp.where(live, SCALE, 0.0)
             at = pl.multiple_of(192 + 32 * comp + 8 * group, 8)
-            goal.append(jnp.where(live, data_ref[at_blk, pl.ds(at, 8), :], 0.0))
+            goal.append(jnp.where(live, data_ref[pl.ds(at, 8), :], 0.0))
+        first = data_ref[256, :][None, :].astype(jnp.int32)
+        second = data_ref[257, :][None, :].astype(jnp.int32)
+        ids = lax.broadcasted_iota(jnp.int32, (256, 128), 0)
+        ohf_ref[:, lanes] = jnp.where(ids == first, 1.0, 0.0).astype(jnp.bfloat16)
+        ohs_ref[0:256, lanes] = jnp.where(ids == second, 1.0, 0.0).astype(jnp.bfloat16)
+        ohs_ref[256:512, lanes] = jnp.where(ids + 256 == second, 1.0, 0.0).astype(jnp.bfloat16)
         for side in range(2):
             for group in range(4):
                 ms = slice(8 * group, 8 * group + 8)
                 at = 32 * side + 8 * group
-                cell = data_ref[at_blk, at : at + 8, :].astype(jnp.int32)
+                cell = data_ref[at : at + 8, :].astype(jnp.int32)
                 base = 64 + 64 * side + 8 * group
-                fx = data_ref[at_blk, base : base + 8, :]
-                fy = data_ref[at_blk, base + 32 : base + 40, :]
+                fx = data_ref[base : base + 8, :]
+                fy = data_ref[base + 32 : base + 40, :]
                 row = (cell * 37) >> 8
                 col = cell - 7 * row
                 fx_ref[blk, side, ms, :] = fx
@@ -143,100 +171,114 @@
                     wy_ref[blk, side, k, ms, :] = jnp.where(
                         row == k, 1.0 - fy, jnp.where(row == k - 1, fy, 0.0)
                     )
-        first = data_ref[at_blk, 256, :][None, :].astype(jnp.int32)
-        second = data_ref[at_blk, 257, :][None, :].astype(jnp.int32)
-        ids = lax.broadcasted_iota(jnp.int32, (256, 128), 0)
-        ohf_ref[:, lanes] = jnp.where(ids == first, 1.0, 0.0).astype(jnp.bfloat16)
-        ohs_ref[0:256, lanes] = jnp.where(ids == second, 1.0, 0.0).astype(jnp.bfloat16)
-        ohs_ref[256:512, lanes] = jnp.where(ids + 256 == second, 1.0, 0.0).astype(jnp.bfloat16)
-        for side in range(2):
             tops = load_table(wy_ref, blk, side)
             tops = [[tops[q][g] * goal[g] for g in range(4)] for q in range(8)]
             spread_block(tops, load_table(wx_ref, blk, side), f_ref, lanes, (side,))
-
-    def body(blk, carry):
-        fill(same_ref, blk, blk)
-        fill(other_ref, blk, blk + 4)
-        return carry
-
-    lax.fori_loop(0, 4, body, 0)
     at_first = merge3(lax.dot_general(split3(f_ref[0]), ohf_ref[...], NT, preferred_element_type=F32))
     at_second = merge3(lax.dot_general(split3(f_ref[1]), ohs_ref[...], NT, preferred_element_type=F32))
-    own_ref[...] = at_first - at_second[:, :256]
-    down_ref[...] = at_second[:, 256:]
-
-
-def stencil_kernel(comp_ref, wx_ref, wy_ref, live_ref, ohs_ref, half_ref, f_ref):
+    own = at_first - at_second[:, :256]
+    down = at_second[:, 256:]
+    stiff = jnp.concatenate(
+        [sum(data_ref[row : row + 1, :] for data_ref in datas) for row in (259, 260)], 1
+    )
+    if add:
+        own = own + before_own[...]
+        down = down + before_down[...]
+        stiff = stiff + before_stiff[...]
+    own_ref[...] = own
+    down_ref[...] = down
+    stiff_ref[...] = stiff
+
+
+def stencil_kernel(comp_ref, wx1, wy1, live1, ohs1, wx2, wy2, live2, ohs2, half_ref, f_ref):
     step = comp_ref[0]
-
-    def body(blk, carry):
-        lanes = lanes_of(blk)
-        live = [live_ref[blk, 8 * g : 8 * g + 8, :] for g in range(4)]
-        zero = [jnp.zeros((8, 128), F32)] * 4
-        wy = load_table(wy_ref, blk, 1) + [zero]
-        tops = [
-            [wy[q][g] * jnp.where(step == 0, wy[q][g], wy[q + 1][g]) * live[g] for g in range(4)]
-            for q in range(8)
-        ]
-        for kind in range(2):
-            wx = load_table(wx_ref, blk, 1) + [zero]
-            sides = [[wx[p][g] * wx[p + kind][g] for g in range(4)] for p in range(8)]
-            spread_block(tops, sides, f_ref, lanes, (kind,))
-        return carry
-
-    lax.fori_loop(0, 8, body, 0)
+    for h, (wx_ref, wy_ref, live_ref) in enumerate(((wx1, wy1, live1), (wx2, wy2, live2))):
+
+        def body(blk, carry):
+            lanes = lanes_of(blk + 4 * h)
+            live = [live_ref[blk, 8 * g : 8 * g + 8, :] for g in range(4)]
+            zero = [jnp.zeros((8, 128), F32)] * 4
+            wy = load_table(wy_ref, blk, 1) + [zero]
+            tops = [
+                [wy[q][g] * jnp.where(step == 0, wy[q][g], wy[q + 1][g]) * live[g] for g in range(4)]
+                for q in range(8)
+            ]
+            for kind in range(2):
+                wx = load_table(wx_ref, blk, 1) + [zero]
+                sides = [[wx[p][g] * wx[p + kind][g] for g in range(4)] for p in range(8)]
+                spread_block(tops, sides, f_ref, lanes, (kind,))
+            return carry
+
+        lax.fori_loop(0, 4, body, 0)
     for kind in range(2):
-        half_ref[kind] = merge3(
-            lax.dot_general(split3(f_ref[kind]), ohs_ref[256:512, :], NT, preferred_element_type=F32)
-        )
-
-
-def up_kernel(
-    v_ref, ohf_ref, ohs_ref, wx_ref, wy_ref, fx_ref, col_ref, live_ref,
-    own_ref, down_ref, gap_ref, g_ref, h_ref, f_ref
-):
+        half_ref[kind] = scatter(f_ref[kind], ohs1[256:512, :], ohs2[256:512, :])
+
+
+def gather(parts, hot1, hot2, out_ref):
+    out_ref[:, 0:512] = merge3(jnp.dot(parts, hot1, preferred_element_type=F32))
+    out_ref[:, 512:1024] = merge3(jnp.dot(parts, hot2, preferred_element_type=F32))
+
+
+def scatter(forces, hot1, hot2):
+    parts = split3(forces)
+    return merge3(
+        lax.dot_general(parts[:, 0:512], hot1, NT, preferred_element_type=F32)
+        + lax.dot_general(parts[:, 512:1024], hot2, NT, preferred_element_type=F32)
+    )
+
+
+def up_kernel(v_ref, *refs):
+    halves_of = (refs[:7], refs[7:14])
+    own_ref, down_ref, gap_ref, g_ref, h_ref, f_ref = refs[14:]
     parts = split3(v_ref[...])
-    g_ref[...] = merge3(jnp.dot(parts, ohf_ref[...], preferred_element_type=F32))
-    h_ref[...] = merge3(jnp.dot(parts, ohs_ref[0:256, :], preferred_element_type=F32))
-
-    def body(blk, carry):
-        lanes = lanes_of(blk)
-        got = sample_block(g_ref, lanes, wy_ref, fx_ref, col_ref, blk, 0)
-        less = sample_block(h_ref, lanes, wy_ref, fx_ref, col_ref, blk, 1)
-        gap = [(got[g] - less[g]) * live_ref[blk, 8 * g : 8 * g + 8, :] for g in range(4)]
-        for g in range(4):
-            gap_ref[blk, 8 * g : 8 * g + 8, :] = gap[g]
-        tops = load_table(wy_ref, blk, 1)
-        tops = [[tops[q][g] * gap[g] for g in range(4)] for q in range(8)]
-        spread_block(tops, load_table(wx_ref, blk, 1), f_ref, lanes)
-        return carry
-
-    lax.fori_loop(0, 8, body, 0)
-    forces = merge3(lax.dot_general(split3(f_ref[...]), ohs_ref[...], NT, preferred_element_type=F32))
+    ohf1, ohs1 = refs[0], refs[1]
+    ohf2, ohs2 = refs[7], refs[8]
+    gather(parts, ohf1[...], ohf2[...], g_ref)
+    gather(parts, ohs1[0:256, :], ohs2[0:256, :], h_ref)
+    for h, (_, _, wx_ref, wy_ref, fx_ref, col_ref, live_ref) in enumerate(halves_of):
+
+        def body(blk, carry):
+            lanes = lanes_of(blk + 4 * h)
+            got = sample_block(g_ref, lanes, wy_ref, fx_ref, col_ref, blk, 0)
+            less = sample_block(h_ref, lanes, wy_ref, fx_ref, col_ref, blk, 1)
+            gap = [(got[g] - less[g]) * live_ref[blk, 8 * g : 8 * g + 8, :] for g in range(4)]
+            for g in range(4):
+                gap_ref[blk + 4 * h, 8 * g : 8 * g + 8, :] = gap[g]
+            tops = load_table(wy_ref, blk, 1)
+            tops = [[tops[q][g] * gap[g] for g in range(4)] for q in range(8)]
+            spread_block(tops, load_table(wx_ref, blk, 1), f_ref, lanes)
+            return carry
+
+        lax.fori_loop(0, 4, body, 0)
+    forces = scatter(f_ref[...], ohs1[...], ohs2[...])
     own_ref[...] = forces[:, :256]
     down_ref[...] = forces[:, 256:]
 
 
 def down_kernel(
-    comp_ref, v_ref, below_ref, prev_ref, part_ref, gap_ref, mine_ref, other_ref, stiff_ref,
-    ohf_ref, ohs_ref, wx_ref, wy_ref, fx_ref, col_ref, live_ref, out_ref, g_ref, f_ref, *, back
+    comp_ref, v_ref, below_ref, prev_ref, part_ref, gap_ref, mine_ref, other_ref, stiff_ref, *refs, back
 ):
-    g_ref[...] = merge3(jnp.dot(split3(below_ref[...]), ohs_ref[256:512, :], preferred_element_type=F32))
-
-    def body(blk, carry):
-        lanes = lanes_of(blk)
-        got = sample_block(g_ref, lanes, wy_ref, fx_ref, col_ref, blk, 1)
-        gap = [
-            gap_ref[blk, 8 * g : 8 * g + 8, :] - got[g] * live_ref[blk, 8 * g : 8 * g + 8, :]
-            for g in range(4)
-        ]
-        tops = load_table(wy_ref, blk, 0)
-        tops = [[tops[q][g] * gap[g] for g in range(4)] for q in range(8)]
-        spread_block(tops, load_table(wx_ref, blk, 0), f_ref, lanes)
-        return carry
-
-    lax.fori_loop(0, 8, body, 0)
-    forces = merge3(lax.dot_general(split3(f_ref[...]), ohf_ref[...], NT, preferred_element_type=F32))
+    halves_of = (refs[:7], refs[7:14])
+    out_ref, g_ref, f_ref = refs[14:]
+    ohf1, ohs1 = refs[0], refs[1]
+    ohf2, ohs2 = refs[7], refs[8]
+    gather(split3(below_ref[...]), ohs1[256:512, :], ohs2[256:512, :], g_ref)
+    for h, (_, _, wx_ref, wy_ref, fx_ref, col_ref, live_ref) in enumerate(halves_of):
+
+        def body(blk, carry):
+            lanes = lanes_of(blk + 4 * h)
+            got = sample_block(g_ref, lanes, wy_ref, fx_ref, col_ref, blk, 1)
+            gap = [
+                gap_ref[blk + 4 * h, 8 * g : 8 * g + 8, :] - got[g] * live_ref[blk, 8 * g : 8 * g + 8, :]
+                for g in range(4)
+            ]
+            tops = load_table(wy_ref, blk, 0)
+            tops = [[tops[q][g] * gap[g] for g in range(4)] for q in range(8)]
+            spread_block(tops, load_table(wx_ref, blk, 0), f_ref, lanes)
+            return carry
+
+        lax.fori_loop(0, 4, body, 0)
+    forces = scatter(f_ref[...], ohf1[...], ohf2[...])
     v = v_ref[...]
     up = lambda x, d: pltpu.roll(x, 64 - d, 0)
     dn = lambda x, d: pltpu.roll(x, d, 0)
@@ -411,89 +453,121 @@
         other_ref[k] = both[32:]
 
 
-def call(kernel, outs, n_in, scratch=(), smem=0, us=2.0):
+def call(kernel, outs, n_in, scratch=(), smem=0, us=2.0, hbm=0, grant=8):
     return pl.pallas_call(
         kernel,
         out_shape=[jax.ShapeDtypeStruct(s, d) for s, d in outs],
-        in_specs=[pl.BlockSpec(memory_space=pltpu.SMEM)] * smem + [VMEM] * (n_in - smem),
+        in_specs=[pl.BlockSpec(memory_space=pltpu.SMEM)] * smem
+        + [VMEM] * (n_in - smem - hbm)
+        + [pl.BlockSpec(memory_space=pl.ANY)] * hbm,
         out_specs=[VMEM] * len(outs),
-        scratch_shapes=[pltpu.VMEM(s, d) for s, d in scratch],
-        compiler_params=pltpu.CompilerParams(vmem_limit_bytes=20 * 1024 * 1024),
+        scratch_shapes=list(scratch),
+        compiler_params=pltpu.CompilerParams(vmem_limit_bytes=grant * 1024 * 1024),
         cost_estimate=pl.CostEstimate(flops=int(us * 1e9), bytes_accessed=1 << 18, transcendentals=0),
     )
 
 
+ROW = 4
+
+
+def seat(section):
+    row, col = divmod(section, ROW)
+    return row * ROW + (col if row % 2 == 0 else ROW - 1 - col)
+
+
 def shifted(block, distance):
     devices = range(lax.axis_size("sec"))
-    route = [(i - distance, i) for i in devices if i - distance in devices]
+    route = [(seat(i), seat(i + distance)) for i in devices if i + distance in devices]
     return lax.ppermute(block, "sec", route)
 
 
 def swapped(block):
     return lax.ppermute(block, "tile", [(i, i ^ 1) for i in range(8)])
+
+
+def moved(block, step, flip):
+    route = []
+    for section in range(lax.axis_size("sec")):
+        for tile in range(8):
+            to = ((tile // 2 + step) % 4) * 2 + (tile % 2 ^ flip)
+            route.append((section * 8 + tile, seat(section) * 8 + to))
+    return lax.ppermute(block, ("sec", "tile"), route)
 
 
 def on_device(
     ov_first, ov_second, match_count, cell_first, cell_second, frac_first, frac_second, target, stiffness
 ):
-    sec = lax.axis_index("sec")
     tile = lax.axis_index("tile")
     core = tile % 2
     sections = lax.axis_size("sec")
-    second = ov_second // sections + jnp.where(ov_second % sections == sec, 0, 256)
-    packed = call(pack_kernel, [((4, 264, 128), F32)], 9)(
-        (ov_first // sections).reshape(1, 128),
-        second.reshape(1, 128),
+    dma = pltpu.SemaphoreType.DMA
+    packed = call(
+        functools.partial(pack_kernel, sections=sections),
+        [((264, 128), F32)],
+        10,
+        [
+            pltpu.VMEM((3, 1, 128), jnp.int32),
+            pltpu.VMEM((1, 32), F32),
+            pltpu.VMEM((2, 32, 128), jnp.int32),
+            dma((12,)),
+        ],
+        smem=1,
+        hbm=9,
+        grant=60,
+    )(
+        jnp.stack([lax.axis_index("sec"), tile]),
+        ov_first.reshape(1, 128),
+        ov_second.reshape(1, 128),
         match_count.reshape(1, 128),
         cell_first,
         cell_second,
         frac_first,
         frac_second,
         target,
-        jnp.pad(stiffness.reshape(1, 32), ((0, 0), (0, 96))),
+        stiffness.reshape(1, 32),
     )[0]
-    groups = [[0, 2, 4, 6], [1, 3, 5, 7]]
-    same = lax.all_to_all(packed, "tile", 0, 0, tiled=True, axis_index_groups=groups)
-    other = swapped(same)
-    pair = jnp.stack([same[:, 259, :32], other[:, 259, :32]])
-    pair = jnp.where(core == 0, pair, pair[::-1])
-    stiff = jnp.transpose(pair, (1, 0, 2)).reshape(1, 256)
+    same = [moved(packed, step, 0) for step in (2, 1, 3, 0)]
+    other = swapped(jnp.stack(same))
 
     field = ((64, 256), F32)
     bf16 = jnp.bfloat16
     comp = core.reshape(1)
-    wx, wy, fx, col, live, ohf, ohs, own, down = call(
-        tables_kernel,
-        [
-            ((8, 2, 8, 32, 128), F32),
-            ((8, 2, 8, 32, 128), F32),
-            ((8, 2, 32, 128), F32),
-            ((8, 2, 32, 128), jnp.int32),
-            ((8, 32, 128), F32),
-            ((256, 1024), bf16),
-            ((512, 1024), bf16),
-            field,
-            field,
-        ],
-        3,
-        [((2, 64, 1024), F32)],
-        smem=1,
-    )(comp, same, other)
+    half_tables = [
+        ((4, 2, 8, 32, 128), F32),
+        ((4, 2, 8, 32, 128), F32),
+        ((4, 2, 32, 128), F32),
+        ((4, 2, 32, 128), jnp.int32),
+        ((4, 32, 128), F32),
+        ((256, 512), bf16),
+        ((512, 512), bf16),
+        field,
+        field,
+        ((1, 256), F32),
+    ]
+    work = [pltpu.VMEM((2, 64, 512), F32)]
+    one = call(functools.partial(tables_kernel, blocks=4, add=False), half_tables, 5, work, smem=1)(comp, *same)
+    two = call(functools.partial(tables_kernel, blocks=4, add=True), half_tables, 8, work, smem=1)(
+        comp, other[0], other[1], other[2], other[3], *one[7:]
+    )
+    own, down, stiff = two[7:]
     start_down = shifted(down, -1)
-    half = call(stencil_kernel, [((2, 64, 256), F32)], 5, [((2, 64, 1024), F32)], smem=1, us=4.0)(
-        comp, wx, wy, live, ohs
+    half = call(stencil_kernel, [((2, 64, 256), F32)], 9, [pltpu.VMEM((2, 64, 1024), F32)], smem=1, us=4.0)(
+        comp, one[0], one[1], one[4], one[6], two[0], two[1], two[4], two[6]
     )[0]
+    fields = [own - start_down]
+    half, fields[0] = lax.optimization_barrier((half, fields[0]))
     mine = shifted(half, -1)
     other = swapped(mine)
-    tables = (ohf, ohs, wx, wy, fx, col, live)
-    wide = ((64, 1024), F32)
-    fields = [own - start_down]
+    tables = []
+    for wx, wy, fx, col, live, ohf, ohs in (one[:7], two[:7]):
+        tables += [ohf, ohs, wx, wy, fx, col, live]
+    wide = pltpu.VMEM((64, 1024), F32)
     for k in range(ITERS):
         v = fields[-1]
         below = shifted(v, 1)
-        part, down, gap = call(up_kernel, [field, field, ((8, 32, 128), F32)], 8, [wide, wide, wide])(v, *tables)
+        part, down, gap = call(up_kernel, [field, field, ((8, 32, 128), F32)], 15, [wide, wide, wide])(v, *tables)
         above = shifted(down, -1)
-        partial = call(functools.partial(down_kernel, back=k > 0), [field], 16, [wide, wide], smem=1)(
+        partial = call(functools.partial(down_kernel, back=k > 0), [field], 23, [wide, wide], smem=1)(
             comp, v, below, fields[max(k - 1, 0)], part, gap, mine, other, stiff, *tables
         )[0]
         fields.append(partial - above)
@@ -502,7 +576,8 @@
     mine, other = call(
         finish_kernel, [((2, 32, 64), F32), ((2, 32, 64), F32)], 8, smem=1
     )(tile.reshape(1), gram, swapped(gram), *fields)
-    other = swapped(other)
+    other = moved(other, 0, 1)
+    mine = moved(mine, 0, 0)
     first = jnp.where(core == 0, mine, other)
     last = jnp.where(core == 0, other, mine)
     out = jnp.concatenate([first, last], 2)[:, :, None, :]

time: 126 us -> 116 us (0.921)
  the two profiles are of different devices: /device:TPU:1 before, /device:TPU:33 now
where the time goes in v3:
time: 116 us; the launch traced here: 115 us
  starting transfers between devices  54 us (47%)
  Pallas kernels  26.4 us (23%)
  blocking collectives  18.2 us (16%)
  waiting for transfers between devices  14.1 us (12%)
  other arithmetic  1.46 us (1%)
    ppermute x10, starting transfers between devices, shifted(): return lax.ppermute(block, 'sec', route)  25.2 us
    all_to_all x1, blocking collectives, on_device(): lax.all_to_all(jnp.broadcast_to(gram, (32, 128)), 'sec', 0, 0, tiled=True)  18.2 us
    ppermute x6, starting transfers between devices, moved(): return lax.ppermute(block, ('sec', 'tile'), route)  17.3 us
    ppermute x3, starting transfers between devices, swapped(): return lax.ppermute(block, 'tile', [(i, i ^ 1) for i in range(8)])  11.6 us
    pallas_call x4, Pallas kernels, on_device(): call(up_kernel, [field, field, ((8, 32, 128), F32)], 15, [wide, wide, wide])  9.03 us
    ppermute x6, waiting for transfers between devices, moved(): return lax.ppermute(block, ('sec', 'tile'), route)  7.86 us
    pallas_call x4, Pallas kernels, on_device(): call(functools.partial(down_kernel, back=k > 0), [field], 23, [wide, wide...  7.02 us
    ppermute x10, waiting for transfers between devices, shifted(): return lax.ppermute(block, 'sec', route)  5.44 us
  transfers between devices with their start and end apart: 19, of which 11 were waited for; matrix products, arithmetic and copies ran while one was open for 0% of the time, Pallas kernels for 17%

profile of v3, /device:TPU:33, one launch (start us, length us, event | category | flops | bytes accessed | tf_op | source)
XLA Modules:
  0.0 115.2 jit_solution(9799090189681710313)
XLA Ops:
  1.3 2.4 %shard_map.104 = f32[264,128]{1,0:T(8,128)} custom-call(s32[2]{0:T(128)} %pad_add_fusion.place_ref, s32[1,128]{1,0:T(1,128)} %bitcast.36, s32[1,128]{1,0:T(1,128)} %bitcast.37, s32[1,128]{1,0:T(1,128)} %bitcast.38, s32[32,128]{1,0:T(8,128)} %cell1_hbm.1, s32[32,128]{1,0:T(8,128)} %cell2_hbm.1, f32[2,32,128]{2,1,0:T(8,128)} %frac1_hbm.1, ...), custom_call_target="tpu_custom_call" | custom-call | flops 2000000000 | bytes 262144 | tf_op jit(solution)/shard_map/pallas_call | solution.py:504
  3.7 5.2 %collective-permute-start = (f32[264,128]{1,0:T(8,128)}, f32[264,128]{1,0:T(8,128)S(1)}, u32[]{:S(2)}, u32[]{:S(2)}) collective-permute-start(f32[264,128]{1,0:T(8,128)} %shard_map.104), channel_id=1, source_target_pairs={{0,4},{1,5},{2,6},{3,7},{4,0},{5,1},{6,2},{7,3},{8,12},{9,13},{10,... | collective-permute-start | bytes 405512 | tf_op jit(solution)/shard_map/ppermute | solution.py:494
  9.2 4.5 %collective-permute-start.2 = (f32[264,128]{1,0:T(8,128)}, f32[264,128]{1,0:T(8,128)S(1)}, u32[]{:S(2)}, u32[]{:S(2)}) collective-permute-start(f32[264,128]{1,0:T(8,128)} %shard_map.104), channel_id=1, source_target_pairs={{0,6},{1,7},{2,0},{3,1},{4,2},{5,3},{6,4},{7,5},{8,14},{9,15},{10,... | collective-permute-start | bytes 405512 | tf_op jit(solution)/shard_map/ppermute | solution.py:494
  13.6 2.1 %collective-permute-start.3 = (f32[264,128]{1,0:T(8,128)}, f32[264,128]{1,0:T(8,128)S(1)}, u32[]{:S(2)}, u32[]{:S(2)}) collective-permute-start(f32[264,128]{1,0:T(8,128)} %shard_map.104), channel_id=1, source_target_pairs={{0,0},{1,1},{2,2},{3,3},{4,4},{5,5},{6,6},{7,7},{8,8},{9,9},{10,10... | collective-permute-start | bytes 405512 | tf_op jit(solution)/shard_map/ppermute | solution.py:494
  18.2 2.6 %collective-permute-done.3.refs_3_ = f32[264,128]{1,0:T(8,128)S(1)} collective-permute-done((f32[264,128]{1,0:T(8,128)}, f32[264,128]{1,0:T(8,128)S(1)}, u32[]{:S(2)}, u32[]{:S(2)}) %collective-permute-start.3) | collective-permute-done | bytes 135200 | tf_op jit(solution)/shard_map/ppermute | solution.py:494
  20.9 2.7 %collective-permute-start.4 = (f32[4,264,128]{2,1,0:T(8,128)S(1)}, f32[4,264,128]{2,1,0:T(8,128)S(1)}, u32[]{:S(2)}, u32[]{:S(2)}) collective-permute-start(f32[4,264,128]{2,1,0:T(8,128)S(1)} %pad_maximum_fusion), channel_id=1, source_target_pairs={{0,1},{1,0},{2,3},{3,2},{4,5},{5,4},{6,7},{7,6},{8,9},{9,8},{10,11... | collective-permute-start | bytes 1622024 | tf_op jit(solution)/shard_map/ppermute | solution.py:485
  28.8 2.2 %shard_map.107 = f32[2,64,256]{2,1,0:T(8,128)S(1)} custom-call(s32[1]{0:T(128)} %bitcast.1.comp_ref, f32[4,2,8,32,128]{4,3,2,1,0:T(8,128)S(1)} %get-tuple-element.38.wx1.refs_2_, f32[4,2,8,32,128]{4,3,2,1,0:T(8,128)S(1)} %get-tuple-element.39.wy1.refs_3_, f32[4,32,128]{2,1,0:T(8,128)S(1)} %get-tuple-element.40.live1.refs_6_, ...), custom_call_target="tpu_custom_call" | custom-call | flops 4000000000 | bytes 262144 | tf_op jit(solution)/shard_map/pallas_call | solution.py:554
  31.9 2.5 %collective-permute-start.7 = (f32[2,64,256]{2,1,0:T(8,128)S(1)}, f32[2,64,256]{2,1,0:T(8,128)S(1)}, u32[]{:S(2)}, u32[]{:S(2)}) collective-permute-start(f32[2,64,256]{2,1,0:T(8,128)S(1)} %shard_map.107), channel_id=1, source_target_pairs={{8,0},{16,8},{24,16},{56,24},{48,56},{40,48},{32,40},{64,32},{72,6... | collective-permute-start | bytes 393224 | tf_op jit(solution)/shard_map/ppermute | solution.py:481
  34.4 2.8 %collective-permute-start.6 = (f32[64,256]{1,0:T(8,128)S(1)}, f32[64,256]{1,0:T(8,128)S(1)}, u32[]{:S(2)}, u32[]{:S(2)}) collective-permute-start(f32[64,256]{1,0:T(8,128)S(1)} %sub.15.v_ref.prev_ref.refs_0_.v0), channel_id=1, source_target_pairs={{0,8},{8,16},{16,24},{24,56},{56,48},{48,40},{40,32},{32,64},{64,7... | collective-permute-start | bytes 196616 | tf_op jit(solution)/shard_map/ppermute | solution.py:481
  37.6 2.6 %collective-permute-start.8 = (f32[2,64,256]{2,1,0:T(8,128)S(1)}, f32[2,64,256]{2,1,0:T(8,128)S(1)}, u32[]{:S(2)}, u32[]{:S(2)}) collective-permute-start(f32[2,64,256]{2,1,0:T(8,128)S(1)} %collective-permute-done.7.mine_ref), channel_id=1, source_target_pairs={{0,1},{1,0},{2,3},{3,2},{4,5},{5,4},{6,7},{7,6},{8,9},{9,8},{10,11... | collective-permute-start | bytes 393224 | tf_op jit(solution)/shard_map/ppermute | solution.py:485
  40.2 2.3 %shard_map.108 = (f32[64,256]{1,0:T(8,128)S(1)}, f32[64,256]{1,0:T(8,128)S(1)}, f32[8,32,128]{2,1,0:T(8,128)S(1)}) custom-call(f32[64,256]{1,0:T(8,128)S(1)} %sub.15.v_ref.prev_ref.refs_0_.v0, bf16[256,512]{1,0:T(8,128)(2,1)S(1)} %get-tuple-element.52.refs_0_, bf16[512,512]{1,0:T(8,128)(2,1)S(1)} %get-tuple-element.41.ohs1.refs_1_, ...), custom_call_target="tpu_custom_call" | custom-call | flops 2000000000 | bytes 262144 | tf_op jit(solution)/shard_map/pallas_call | solution.py:568
  50.1 2.3 %shard_map.110 = (f32[64,256]{1,0:T(8,128)S(1)}, f32[64,256]{1,0:T(8,128)S(1)}, f32[8,32,128]{2,1,0:T(8,128)S(1)}) custom-call(f32[64,256]{1,0:T(8,128)S(1)} %sub.16.v_ref.prev_ref.refs_1_.v1, bf16[256,512]{1,0:T(8,128)(2,1)S(1)} %get-tuple-element.52.refs_0_, bf16[512,512]{1,0:T(8,128)(2,1)S(1)} %get-tuple-element.41.ohs1.refs_1_, ...), custom_call_target="tpu_custom_call" | custom-call | flops 2000000000 | bytes 262144 | tf_op jit(solution)/shard_map/pallas_call | solution.py:568
  52.4 3.3 %collective-permute-start.11 = (f32[64,256]{1,0:T(8,128)S(1)}, f32[64,256]{1,0:T(8,128)S(1)}, u32[]{:S(2)}, u32[]{:S(2)}) collective-permute-start(f32[64,256]{1,0:T(8,128)S(1)} %get-tuple-element.65), channel_id=1, source_target_pairs={{8,0},{16,8},{24,16},{56,24},{48,56},{40,48},{32,40},{64,32},{72,6... | collective-permute-start | bytes 196616 | tf_op jit(solution)/shard_map/ppermute | solution.py:481
  57.5 3.2 %collective-permute-start.12 = (f32[64,256]{1,0:T(8,128)S(1)}, f32[64,256]{1,0:T(8,128)S(1)}, u32[]{:S(2)}, u32[]{:S(2)}) collective-permute-start(f32[64,256]{1,0:T(8,128)S(1)} %sub.17.v_ref.prev_ref.refs_2_.v2), channel_id=1, source_target_pairs={{0,8},{8,16},{16,24},{24,56},{56,48},{48,40},{40,32},{32,64},{64,7... | collective-permute-start | bytes 196616 | tf_op jit(solution)/shard_map/ppermute | solution.py:481
  60.7 2.3 %shard_map.112 = (f32[64,256]{1,0:T(8,128)S(1)}, f32[64,256]{1,0:T(8,128)S(1)}, f32[8,32,128]{2,1,0:T(8,128)S(1)}) custom-call(f32[64,256]{1,0:T(8,128)S(1)} %sub.17.v_ref.prev_ref.refs_2_.v2, bf16[256,512]{1,0:T(8,128)(2,1)S(1)} %get-tuple-element.52.refs_0_, bf16[512,512]{1,0:T(8,128)(2,1)S(1)} %get-tuple-element.41.ohs1.refs_1_, ...), custom_call_target="tpu_custom_call" | custom-call | flops 2000000000 | bytes 262144 | tf_op jit(solution)/shard_map/pallas_call | solution.py:568
  63.0 2.0 %collective-permute-start.13 = (f32[64,256]{1,0:T(8,128)S(1)}, f32[64,256]{1,0:T(8,128)S(1)}, u32[]{:S(2)}, u32[]{:S(2)}) collective-permute-start(f32[64,256]{1,0:T(8,128)S(1)} %get-tuple-element.68), channel_id=1, source_target_pairs={{8,0},{16,8},{24,16},{56,24},{48,56},{40,48},{32,40},{64,32},{72,6... | collective-permute-start | bytes 196616 | tf_op jit(solution)/shard_map/ppermute | solution.py:481
  68.0 3.3 %collective-permute-start.14 = (f32[64,256]{1,0:T(8,128)S(1)}, f32[64,256]{1,0:T(8,128)S(1)}, u32[]{:S(2)}, u32[]{:S(2)}) collective-permute-start(f32[64,256]{1,0:T(8,128)S(1)} %sub.18.v_ref.refs_3_.v3), channel_id=1, source_target_pairs={{0,8},{8,16},{16,24},{24,56},{56,48},{48,40},{40,32},{32,64},{64,7... | collective-permute-start | bytes 196616 | tf_op jit(solution)/shard_map/ppermute | solution.py:481
  71.4 2.3 %shard_map.114 = (f32[64,256]{1,0:T(8,128)S(1)}, f32[64,256]{1,0:T(8,128)S(1)}, f32[8,32,128]{2,1,0:T(8,128)S(1)}) custom-call(f32[64,256]{1,0:T(8,128)S(1)} %sub.18.v_ref.refs_3_.v3, bf16[256,512]{1,0:T(8,128)(2,1)S(1)} %get-tuple-element.52.refs_0_, bf16[512,512]{1,0:T(8,128)(2,1)S(1)} %get-tuple-element.41.ohs1.refs_1_, ...), custom_call_target="tpu_custom_call" | custom-call | flops 2000000000 | bytes 262144 | tf_op jit(solution)/shard_map/pallas_call | solution.py:568
  73.6 2.1 %collective-permute-start.15 = (f32[64,256]{1,0:T(8,128)S(1)}, f32[64,256]{1,0:T(8,128)S(1)}, u32[]{:S(2)}, u32[]{:S(2)}) collective-permute-start(f32[64,256]{1,0:T(8,128)S(1)} %get-tuple-element.71), channel_id=1, source_target_pairs={{8,0},{16,8},{24,16},{56,24},{48,56},{40,48},{32,40},{64,32},{72,6... | collective-permute-start | bytes 196616 | tf_op jit(solution)/shard_map/ppermute | solution.py:481
  80.0 18.2 %all_to_all.8 = f32[32,1,128]{2,1,0:T(1,128)S(1)} all-to-all(f32[32,1,128]{2,1,0:T(1,128)S(1)} %broadcast_in_dim.2), channel_id=1, replica_groups=mesh['sec'=32,'tile'=8] {'sec'}, dimensions={0} | all-to-all | bytes 32768 | tf_op jit(solution)/shard_map/all_to_all | solution.py:575
  98.1 6.2 %collective-permute-start.16 = (f32[32,128]{1,0:T(8,128)S(1)}, f32[32,128]{1,0:T(8,128)S(1)}, u32[]{:S(2)}, u32[]{:S(2)}) collective-permute-start(f32[32,128]{1,0:T(8,128)S(1)} %bitcast.31), channel_id=1, source_target_pairs={{0,1},{1,0},{2,3},{3,2},{4,5},{5,4},{6,7},{7,6},{8,9},{9,8},{10,11... | collective-permute-start | bytes 49160 | tf_op jit(solution)/shard_map/ppermute | solution.py:485
  106.5 2.8 %collective-permute-start.17 = (f32[2,32,64]{2,1,0:T(8,128)S(1)}, f32[2,32,64]{2,1,0:T(8,128)S(1)}, u32[]{:S(2)}, u32[]{:S(2)}) collective-permute-start(f32[2,32,64]{2,1,0:T(8,128)S(1)} %get-tuple-element.72), channel_id=1, source_target_pairs={{0,0},{1,1},{2,2},{3,3},{4,4},{5,5},{6,6},{7,7},{8,8},{9,9},{10,10... | collective-permute-start | bytes 49160 | tf_op jit(solution)/shard_map/ppermute | solution.py:494
  109.4 2.3 %collective-permute-start.18 = (f32[2,32,64]{2,1,0:T(8,128)S(1)}, f32[2,32,64]{2,1,0:T(8,128)S(1)}, u32[]{:S(2)}, u32[]{:S(2)}) collective-permute-start(f32[2,32,64]{2,1,0:T(8,128)S(1)} %get-tuple-element.73), channel_id=1, source_target_pairs={{0,1},{1,0},{2,3},{3,2},{4,5},{5,4},{6,7},{7,6},{8,9},{9,8},{10,11... | collective-permute-start | bytes 49160 | tf_op jit(solution)/shard_map/ppermute | solution.py:494
  112.4 2.1 %collective-permute-done.18 = f32[2,32,64]{2,1,0:T(8,128)S(1)} collective-permute-done((f32[2,32,64]{2,1,0:T(8,128)S(1)}, f32[2,32,64]{2,1,0:T(8,128)S(1)}, u32[]{:S(2)}, u32[]{:S(2)}) %collective-permute-start.18) | collective-permute-done | bytes 16416 | tf_op jit(solution)/shard_map/ppermute | solution.py:494
  (40 shorter events, 29.8 us)
Async XLA Ops:
  3.7 12.1 %collective-permute-start = (f32[264,128]{1,0:T(8,128)}, f32[264,128]{1,0:T(8,128)S(1)}, u32[]{:S(2)}, u32[]{:S(2)}) collective-permute-start(f32[264,128]{1,0:T(8,128)} %shard_map.104), channel_id=1, source_target_pairs={{0,4},{1,5},{2,6},{3,7},{4,0},{5,1},{6,2},{7,3},{8,12},{9,13},{10,... | collective-permute-start | bytes 405512 | tf_op jit(solution)/shard_map/ppermute | solution.py:494
  8.9 7.4 %collective-permute-start.1 = (f32[264,128]{1,0:T(8,128)}, f32[264,128]{1,0:T(8,128)S(1)}, u32[]{:S(2)}, u32[]{:S(2)}) collective-permute-start(f32[264,128]{1,0:T(8,128)} %shard_map.104), channel_id=1, source_target_pairs={{0,2},{1,3},{2,4},{3,5},{4,6},{5,7},{6,0},{7,1},{8,10},{9,11},{10,... | collective-permute-start | bytes 405512 | tf_op jit(solution)/shard_map/ppermute | solution.py:494
  9.2 9.0 %collective-permute-start.2 = (f32[264,128]{1,0:T(8,128)}, f32[264,128]{1,0:T(8,128)S(1)}, u32[]{:S(2)}, u32[]{:S(2)}) collective-permute-start(f32[264,128]{1,0:T(8,128)} %shard_map.104), channel_id=1, source_target_pairs={{0,6},{1,7},{2,0},{3,1},{4,2},{5,3},{6,4},{7,5},{8,14},{9,15},{10,... | collective-permute-start | bytes 405512 | tf_op jit(solution)/shard_map/ppermute | solution.py:494
  13.6 7.2 %collective-permute-start.3 = (f32[264,128]{1,0:T(8,128)}, f32[264,128]{1,0:T(8,128)S(1)}, u32[]{:S(2)}, u32[]{:S(2)}) collective-permute-start(f32[264,128]{1,0:T(8,128)} %shard_map.104), channel_id=1, source_target_pairs={{0,0},{1,1},{2,2},{3,3},{4,4},{5,5},{6,6},{7,7},{8,8},{9,9},{10,10... | collective-permute-start | bytes 405512 | tf_op jit(solution)/shard_map/ppermute | solution.py:494
  20.9 4.3 %collective-permute-start.4 = (f32[4,264,128]{2,1,0:T(8,128)S(1)}, f32[4,264,128]{2,1,0:T(8,128)S(1)}, u32[]{:S(2)}, u32[]{:S(2)}) collective-permute-start(f32[4,264,128]{2,1,0:T(8,128)S(1)} %pad_maximum_fusion), channel_id=1, source_target_pairs={{0,1},{1,0},{2,3},{3,2},{4,5},{5,4},{6,7},{7,6},{8,9},{9,8},{10,11... | collective-permute-start | bytes 1622024 | tf_op jit(solution)/shard_map/ppermute | solution.py:485
  26.9 5.0 %collective-permute-start.5 = (f32[64,256]{1,0:T(8,128)S(1)}, f32[64,256]{1,0:T(8,128)S(1)}, u32[]{:S(2)}, u32[]{:S(2)}) collective-permute-start(f32[64,256]{1,0:T(8,128)S(1)} %get-tuple-element.50), channel_id=1, source_target_pairs={{8,0},{16,8},{24,16},{56,24},{48,56},{40,48},{32,40},{64,32},{72,6... | collective-permute-start | bytes 196616 | tf_op jit(solution)/shard_map/ppermute | solution.py:481
  31.9 5.7 %collective-permute-start.7 = (f32[2,64,256]{2,1,0:T(8,128)S(1)}, f32[2,64,256]{2,1,0:T(8,128)S(1)}, u32[]{:S(2)}, u32[]{:S(2)}) collective-permute-start(f32[2,64,256]{2,1,0:T(8,128)S(1)} %shard_map.107), channel_id=1, source_target_pairs={{8,0},{16,8},{24,16},{56,24},{48,56},{40,48},{32,40},{64,32},{72,6... | collective-permute-start | bytes 393224 | tf_op jit(solution)/shard_map/ppermute | solution.py:481
  34.4 10.1 %collective-permute-start.6 = (f32[64,256]{1,0:T(8,128)S(1)}, f32[64,256]{1,0:T(8,128)S(1)}, u32[]{:S(2)}, u32[]{:S(2)}) collective-permute-start(f32[64,256]{1,0:T(8,128)S(1)} %sub.15.v_ref.prev_ref.refs_0_.v0), channel_id=1, source_target_pairs={{0,8},{8,16},{16,24},{24,56},{56,48},{48,40},{40,32},{32,64},{64,7... | collective-permute-start | bytes 196616 | tf_op jit(solution)/shard_map/ppermute | solution.py:481
  37.6 6.8 %collective-permute-start.8 = (f32[2,64,256]{2,1,0:T(8,128)S(1)}, f32[2,64,256]{2,1,0:T(8,128)S(1)}, u32[]{:S(2)}, u32[]{:S(2)}) collective-permute-start(f32[2,64,256]{2,1,0:T(8,128)S(1)} %collective-permute-done.7.mine_ref), channel_id=1, source_target_pairs={{0,1},{1,0},{2,3},{3,2},{4,5},{5,4},{6,7},{7,6},{8,9},{9,8},{10,11... | collective-permute-start | bytes 393224 | tf_op jit(solution)/shard_map/ppermute | solution.py:485
  42.5 5.6 %collective-permute-start.9 = (f32[64,256]{1,0:T(8,128)S(1)}, f32[64,256]{1,0:T(8,128)S(1)}, u32[]{:S(2)}, u32[]{:S(2)}) collective-permute-start(f32[64,256]{1,0:T(8,128)S(1)} %get-tuple-element.62), channel_id=1, source_target_pairs={{8,0},{16,8},{24,16},{56,24},{48,56},{40,48},{32,40},{64,32},{72,6... | collective-permute-start | bytes 196616 | tf_op jit(solution)/shard_map/ppermute | solution.py:481
  48.1 7.6 %collective-permute-start.10 = (f32[64,256]{1,0:T(8,128)S(1)}, f32[64,256]{1,0:T(8,128)S(1)}, u32[]{:S(2)}, u32[]{:S(2)}) collective-permute-start(f32[64,256]{1,0:T(8,128)S(1)} %sub.16.v_ref.prev_ref.refs_1_.v1), channel_id=1, source_target_pairs={{0,8},{8,16},{16,24},{24,56},{56,48},{48,40},{40,32},{32,64},{64,7... | collective-permute-start | bytes 196616 | tf_op jit(solution)/shard_map/ppermute | solution.py:481
  52.4 5.1 %collective-permute-start.11 = (f32[64,256]{1,0:T(8,128)S(1)}, f32[64,256]{1,0:T(8,128)S(1)}, u32[]{:S(2)}, u32[]{:S(2)}) collective-permute-start(f32[64,256]{1,0:T(8,128)S(1)} %get-tuple-element.65), channel_id=1, source_target_pairs={{8,0},{16,8},{24,16},{56,24},{48,56},{40,48},{32,40},{64,32},{72,6... | collective-permute-start | bytes 196616 | tf_op jit(solution)/shard_map/ppermute | solution.py:481
  57.5 7.6 %collective-permute-start.12 = (f32[64,256]{1,0:T(8,128)S(1)}, f32[64,256]{1,0:T(8,128)S(1)}, u32[]{:S(2)}, u32[]{:S(2)}) collective-permute-start(f32[64,256]{1,0:T(8,128)S(1)} %sub.17.v_ref.prev_ref.refs_2_.v2), channel_id=1, source_target_pairs={{0,8},{8,16},{16,24},{24,56},{56,48},{48,40},{40,32},{32,64},{64,7... | collective-permute-start | bytes 196616 | tf_op jit(solution)/shard_map/ppermute | solution.py:481
  63.0 5.0 %collective-permute-start.13 = (f32[64,256]{1,0:T(8,128)S(1)}, f32[64,256]{1,0:T(8,128)S(1)}, u32[]{:S(2)}, u32[]{:S(2)}) collective-permute-start(f32[64,256]{1,0:T(8,128)S(1)} %get-tuple-element.68), channel_id=1, source_target_pairs={{8,0},{16,8},{24,16},{56,24},{48,56},{40,48},{32,40},{64,32},{72,6... | collective-permute-start | bytes 196616 | tf_op jit(solution)/shard_map/ppermute | solution.py:481
  68.0 7.7 %collective-permute-start.14 = (f32[64,256]{1,0:T(8,128)S(1)}, f32[64,256]{1,0:T(8,128)S(1)}, u32[]{:S(2)}, u32[]{:S(2)}) collective-permute-start(f32[64,256]{1,0:T(8,128)S(1)} %sub.18.v_ref.refs_3_.v3), channel_id=1, source_target_pairs={{0,8},{8,16},{16,24},{24,56},{56,48},{48,40},{40,32},{32,64},{64,7... | collective-permute-start | bytes 196616 | tf_op jit(solution)/shard_map/ppermute | solution.py:481
  73.6 5.0 %collective-permute-start.15 = (f32[64,256]{1,0:T(8,128)S(1)}, f32[64,256]{1,0:T(8,128)S(1)}, u32[]{:S(2)}, u32[]{:S(2)}) collective-permute-start(f32[64,256]{1,0:T(8,128)S(1)} %get-tuple-element.71), channel_id=1, source_target_pairs={{8,0},{16,8},{24,16},{56,24},{48,56},{40,48},{32,40},{64,32},{72,6... | collective-permute-start | bytes 196616 | tf_op jit(solution)/shard_map/ppermute | solution.py:481
  98.1 7.1 %collective-permute-start.16 = (f32[32,128]{1,0:T(8,128)S(1)}, f32[32,128]{1,0:T(8,128)S(1)}, u32[]{:S(2)}, u32[]{:S(2)}) collective-permute-start(f32[32,128]{1,0:T(8,128)S(1)} %bitcast.31), channel_id=1, source_target_pairs={{0,1},{1,0},{2,3},{3,2},{4,5},{5,4},{6,7},{7,6},{8,9},{9,8},{10,11... | collective-permute-start | bytes 49160 | tf_op jit(solution)/shard_map/ppermute | solution.py:485
  106.5 5.9 %collective-permute-start.17 = (f32[2,32,64]{2,1,0:T(8,128)S(1)}, f32[2,32,64]{2,1,0:T(8,128)S(1)}, u32[]{:S(2)}, u32[]{:S(2)}) collective-permute-start(f32[2,32,64]{2,1,0:T(8,128)S(1)} %get-tuple-element.72), channel_id=1, source_target_pairs={{0,0},{1,1},{2,2},{3,3},{4,4},{5,5},{6,6},{7,7},{8,8},{9,9},{10,10... | collective-permute-start | bytes 49160 | tf_op jit(solution)/shard_map/ppermute | solution.py:494
  109.4 5.2 %collective-permute-start.18 = (f32[2,32,64]{2,1,0:T(8,128)S(1)}, f32[2,32,64]{2,1,0:T(8,128)S(1)}, u32[]{:S(2)}, u32[]{:S(2)}) collective-permute-start(f32[2,32,64]{2,1,0:T(8,128)S(1)} %get-tuple-element.73), channel_id=1, source_target_pairs={{0,1},{1,0},{2,3},{3,2},{4,5},{5,4},{6,7},{7,6},{8,9},{9,8},{10,11... | collective-permute-start | bytes 49160 | tf_op jit(solution)/shard_map/ppermute | solution.py:494

commit v4 on v3

--- a/solution.py
+++ b/solution.py
@@ -92,7 +92,7 @@
 
 
 def pack_kernel(
-    place_ref, first_hbm, second_hbm, count_hbm, cell1_hbm, cell2_hbm, frac1_hbm, frac2_hbm, target_hbm, stiff_hbm,
+    first_hbm, second_hbm, count_hbm, cell1_hbm, cell2_hbm, frac1_hbm, frac2_hbm, target_hbm, stiff_hbm,
     out_ref, ids_ref, stiff_ref, cell_ref, sem, *, sections
 ):
     copies = [
@@ -116,8 +116,8 @@
     shift = sections.bit_length() - 1
     first = ids_ref[0] >> shift
     second = ids_ref[1] >> shift
-    second = second + jnp.where((ids_ref[1] & (sections - 1)) == place_ref[0], 0, 256)
-    tile = place_ref[1]
+    second = second + jnp.where((ids_ref[1] & (sections - 1)) == lax.axis_index("sec"), 0, 256)
+    tile = lax.axis_index("tile")
     stiff = jnp.concatenate([stiff_ref[...], jnp.zeros((1, 96), F32)], 1)
     stiff = pltpu.roll(jnp.broadcast_to(stiff, (8, 128)), 32 * (tile & 3), 1)
     row = sublane_ids()
@@ -127,14 +127,14 @@
     out_ref[256:264, :] = tail
 
 
-def tables_kernel(comp_ref, *refs, blocks, add):
+def tables_kernel(*refs, blocks, add):
     datas = refs[:blocks]
     refs = refs[blocks:]
     if add:
         before_own, before_down, before_stiff = refs[:3]
         refs = refs[3:]
     wx_ref, wy_ref, fx_ref, col_ref, live_ref, ohf_ref, ohs_ref, own_ref, down_ref, stiff_ref, f_ref = refs
-    comp = comp_ref[0]
+    comp = lax.axis_index("tile") & 1
     for blk, data_ref in enumerate(datas):
         lanes = slice(128 * blk, 128 * blk + 128)
         count = data_ref[258, :][None, :]
@@ -190,8 +190,8 @@
     stiff_ref[...] = stiff
 
 
-def stencil_kernel(comp_ref, wx1, wy1, live1, ohs1, wx2, wy2, live2, ohs2, half_ref, f_ref):
-    step = comp_ref[0]
+def stencil_kernel(wx1, wy1, live1, ohs1, wx2, wy2, live2, ohs2, half_ref, f_ref):
+    step = lax.axis_index("tile") & 1
     for h, (wx_ref, wy_ref, live_ref) in enumerate(((wx1, wy1, live1), (wx2, wy2, live2))):
 
         def body(blk, carry):
@@ -256,7 +256,7 @@
 
 
 def down_kernel(
-    comp_ref, v_ref, below_ref, prev_ref, part_ref, gap_ref, mine_ref, other_ref, stiff_ref, *refs, back
+    v_ref, below_ref, prev_ref, part_ref, gap_ref, mine_ref, other_ref, stiff_ref, *refs, back
 ):
     halves_of = (refs[:7], refs[7:14])
     out_ref, g_ref, f_ref = refs[14:]
@@ -287,7 +287,7 @@
     below = jnp.where(node < 56, up(v, 8) - v, 0.0)
     bend = (dn(right, 1) - right) + (dn(below, 8) - below)
     total = forces - part_ref[...] + (stiff_ref[...] * SCALE) * bend + ((DAMPING - SHIFT) * SCALE) * v
-    first = comp_ref[0] == 0
+    first = (lax.axis_index("tile") & 1) == 0
     band = [jnp.where(first, mine_ref[k], other_ref[k]) for k in range(2)]
     band += [jnp.where(first, other_ref[k], mine_ref[k]) for k in range(2)]
     total = total + band[0] * v
@@ -370,7 +370,7 @@
     out_ref[...] = jnp.sum(row, 0, keepdims=True)
 
 
-def finish_kernel(tile_ref, gram_ref, gram2_ref, v0, v1, v2, v3, v4, mine_ref, other_ref):
+def finish_kernel(gram_ref, gram2_ref, v0, v1, v2, v3, v4, mine_ref, other_ref):
     rows = jnp.concatenate([gram_ref[...], gram2_ref[...]], 0)
     acc = (rows, pltpu.roll(rows, 112, 1))
     n = 64
@@ -440,7 +440,7 @@
             total = term if total is None else total + term
         return total
 
-    tile = tile_ref[0]
+    tile = lax.axis_index("tile")
     ids = lax.broadcasted_iota(jnp.int32, (64, 256), 1)
     want = lax.broadcasted_iota(jnp.int32, (64, 256), 0)
     swap = tile + 1 - 2 * (tile & 1)
@@ -453,12 +453,11 @@
         other_ref[k] = both[32:]
 
 
-def call(kernel, outs, n_in, scratch=(), smem=0, us=2.0, hbm=0, grant=8):
+def call(kernel, outs, n_in, scratch=(), us=2.0, hbm=0, grant=8):
     return pl.pallas_call(
         kernel,
         out_shape=[jax.ShapeDtypeStruct(s, d) for s, d in outs],
-        in_specs=[pl.BlockSpec(memory_space=pltpu.SMEM)] * smem
-        + [VMEM] * (n_in - smem - hbm)
+        in_specs=[VMEM] * (n_in - hbm)
         + [pl.BlockSpec(memory_space=pl.ANY)] * hbm,
         out_specs=[VMEM] * len(outs),
         scratch_shapes=list(scratch),
@@ -468,29 +467,54 @@
 
 
 ROW = 4
-
-
-def seat(section):
+CHIPS = 4
+
+
+def seat(section, y, sections):
     row, col = divmod(section, ROW)
-    return row * ROW + (col if row % 2 == 0 else ROW - 1 - col)
+    col = col if row % 2 == 0 else ROW - 1 - col
+    row = row if y % 2 == 0 else sections // ROW - 1 - row
+    return row * ROW + col
 
 
 def shifted(block, distance):
-    devices = range(lax.axis_size("sec"))
-    route = [(seat(i), seat(i + distance)) for i in devices if i + distance in devices]
-    return lax.ppermute(block, "sec", route)
+    sections = lax.axis_size("sec")
+    route = []
+    for section in range(sections):
+        there = section + distance
+        if not 0 <= there < sections:
+            continue
+        crosses = (section < sections // 2) != (there < sections // 2)
+        for y in range(CHIPS):
+            to = y ^ 1 if crosses else y
+            for core in range(2):
+                route.append(
+                    (seat(section, y, sections) * 8 + 2 * y + core, seat(there, to, sections) * 8 + 2 * to + core)
+                )
+    return lax.ppermute(block, ("sec", "tile"), route)
 
 
 def swapped(block):
     return lax.ppermute(block, "tile", [(i, i ^ 1) for i in range(8)])
 
 
-def moved(block, step, flip):
+def dealt(block, step):
+    sections = lax.axis_size("sec")
     route = []
-    for section in range(lax.axis_size("sec")):
-        for tile in range(8):
-            to = ((tile // 2 + step) % 4) * 2 + (tile % 2 ^ flip)
-            route.append((section * 8 + tile, seat(section) * 8 + to))
+    for section in range(sections):
+        for y in range(CHIPS):
+            to = (y + step) % CHIPS
+            for core in range(2):
+                route.append((section * 8 + 2 * y + core, seat(section, to, sections) * 8 + 2 * to + core))
+    return lax.ppermute(block, ("sec", "tile"), route)
+
+
+def returned(block, flip):
+    sections = lax.axis_size("sec")
+    route = []
+    for section in range(sections):
+        for tile in range(2 * CHIPS):
+            route.append((seat(section, tile // 2, sections) * 8 + tile, section * 8 + (tile ^ flip)))
     return lax.ppermute(block, ("sec", "tile"), route)
 
 
@@ -504,18 +528,16 @@
     packed = call(
         functools.partial(pack_kernel, sections=sections),
         [((264, 128), F32)],
-        10,
+        9,
         [
             pltpu.VMEM((3, 1, 128), jnp.int32),
             pltpu.VMEM((1, 32), F32),
             pltpu.VMEM((2, 32, 128), jnp.int32),
             dma((12,)),
         ],
-        smem=1,
         hbm=9,
         grant=60,
     )(
-        jnp.stack([lax.axis_index("sec"), tile]),
         ov_first.reshape(1, 128),
         ov_second.reshape(1, 128),
         match_count.reshape(1, 128),
@@ -526,12 +548,11 @@
         target,
         stiffness.reshape(1, 32),
     )[0]
-    same = [moved(packed, step, 0) for step in (2, 1, 3, 0)]
+    same = [dealt(packed, step) for step in (2, 1, 3, 0)]
     other = swapped(jnp.stack(same))
 
     field = ((64, 256), F32)
     bf16 = jnp.bfloat16
-    comp = core.reshape(1)
     half_tables = [
         ((4, 2, 8, 32, 128), F32),
         ((4, 2, 8, 32, 128), F32),
@@ -545,14 +566,14 @@
         ((1, 256), F32),
     ]
     work = [pltpu.VMEM((2, 64, 512), F32)]
-    one = call(functools.partial(tables_kernel, blocks=4, add=False), half_tables, 5, work, smem=1)(comp, *same)
-    two = call(functools.partial(tables_kernel, blocks=4, add=True), half_tables, 8, work, smem=1)(
-        comp, other[0], other[1], other[2], other[3], *one[7:]
+    one = call(functools.partial(tables_kernel, blocks=4, add=False), half_tables, 4, work)(*same)
+    two = call(functools.partial(tables_kernel, blocks=4, add=True), half_tables, 7, work)(
+        other[0], other[1], other[2], other[3], *one[7:]
     )
     own, down, stiff = two[7:]
     start_down = shifted(down, -1)
-    half = call(stencil_kernel, [((2, 64, 256), F32)], 9, [pltpu.VMEM((2, 64, 1024), F32)], smem=1, us=4.0)(
-        comp, one[0], one[1], one[4], one[6], two[0], two[1], two[4], two[6]
+    half = call(stencil_kernel, [((2, 64, 256), F32)], 8, [pltpu.VMEM((2, 64, 1024), F32)], us=4.0)(
+        one[0], one[1], one[4], one[6], two[0], two[1], two[4], two[6]
     )[0]
     fields = [own - start_down]
     half, fields[0] = lax.optimization_barrier((half, fields[0]))
@@ -567,17 +588,17 @@
         below = shifted(v, 1)
         part, down, gap = call(up_kernel, [field, field, ((8, 32, 128), F32)], 15, [wide, wide, wide])(v, *tables)
         above = shifted(down, -1)
-        partial = call(functools.partial(down_kernel, back=k > 0), [field], 23, [wide, wide], smem=1)(
-            comp, v, below, fields[max(k - 1, 0)], part, gap, mine, other, stiff, *tables
+        partial = call(functools.partial(down_kernel, back=k > 0), [field], 22, [wide, wide])(
+            v, below, fields[max(k - 1, 0)], part, gap, mine, other, stiff, *tables
         )[0]
         fields.append(partial - above)
     gram = call(dots_kernel, [((1, 128), F32)], 5)(*fields)[0]
     gram = lax.all_to_all(jnp.broadcast_to(gram, (32, 128)), "sec", 0, 0, tiled=True)
     mine, other = call(
-        finish_kernel, [((2, 32, 64), F32), ((2, 32, 64), F32)], 8, smem=1
-    )(tile.reshape(1), gram, swapped(gram), *fields)
-    other = moved(other, 0, 1)
-    mine = moved(mine, 0, 0)
+        finish_kernel, [((2, 32, 64), F32), ((2, 32, 64), F32)], 7
+    )(gram, swapped(gram), *fields)
+    other = returned(other, 1)
+    mine = returned(mine, 0)
     first = jnp.where(core == 0, mine, other)
     last = jnp.where(core == 0, other, mine)
     out = jnp.concatenate([first, last], 2)[:, :, None, :]

time: 116 us -> 120 us (1.034)
  the two profiles are of different devices: /device:TPU:33 before, /device:TPU:41 now
where the time goes in v4:
time: 120 us; the launch traced here: 119 us
  starting transfers between devices  63.8 us (53%)
  Pallas kernels  25.8 us (22%)
  waiting for transfers between devices  14.3 us (12%)
  blocking collectives  13.4 us (11%)
    ppermute x10, starting transfers between devices, shifted(): return lax.ppermute(block, ('sec', 'tile'), route)  29.2 us
    ppermute x4, starting transfers between devices, dealt(): return lax.ppermute(block, ('sec', 'tile'), route)  17 us
    all_to_all x1, blocking collectives, on_device(): lax.all_to_all(jnp.broadcast_to(gram, (32, 128)), 'sec', 0, 0, tiled=True)  13.4 us
    ppermute x3, starting transfers between devices, swapped(): return lax.ppermute(block, 'tile', [(i, i ^ 1) for i in range(8)])  9.93 us
    pallas_call x4, Pallas kernels, on_device(): call(up_kernel, [field, field, ((8, 32, 128), F32)], 15, [wide, wide, wide])  9.03 us
    ppermute x2, starting transfers between devices, returned(): return lax.ppermute(block, ('sec', 'tile'), route)  7.61 us
    pallas_call x4, Pallas kernels, on_device(): call(functools.partial(down_kernel, back=k > 0), [field], 22, [wide, wide])  6.99 us
    ppermute x10, waiting for transfers between devices, shifted(): return lax.ppermute(block, ('sec', 'tile'), route)  5.37 us
  transfers between devices with their start and end apart: 19, of which 10 were waited for; matrix products, arithmetic and copies ran while one was open for 0% of the time, Pallas kernels for 17%

profile of v4, /device:TPU:41, one launch (start us, length us, event | category | flops | bytes accessed | tf_op | source)
XLA Modules:
  0.0 119.1 jit_solution(8023254251878363950)
XLA Ops:
  2.4 9.6 %collective-permute-start = (f32[264,128]{1,0:T(8,128)}, f32[264,128]{1,0:T(8,128)S(1)}, u32[]{:S(2)}, u32[]{:S(2)}) collective-permute-start(f32[264,128]{1,0:T(8,128)} %shard_map.104), channel_id=1, source_target_pairs={{0,4},{1,5},{2,230},{3,231},{4,0},{5,1},{6,226},{7,227},{8,12},{9,... | collective-permute-start | bytes 405512 | tf_op jit(solution)/shard_map/ppermute | solution.py:509
  11.9 7.5 %collective-permute-start.3 = (f32[264,128]{1,0:T(8,128)}, f32[264,128]{1,0:T(8,128)S(1)}, u32[]{:S(2)}, u32[]{:S(2)}) collective-permute-start(f32[264,128]{1,0:T(8,128)} %shard_map.104), channel_id=1, source_target_pairs={{0,0},{1,1},{2,226},{3,227},{4,4},{5,5},{6,230},{7,231},{8,8},{9,9... | collective-permute-start | bytes 405512 | tf_op jit(solution)/shard_map/ppermute | solution.py:509
  20.3 2.7 %collective-permute-done.2.refs_2_ = f32[264,128]{1,0:T(8,128)S(1)} collective-permute-done((f32[264,128]{1,0:T(8,128)}, f32[264,128]{1,0:T(8,128)S(1)}, u32[]{:S(2)}, u32[]{:S(2)}) %collective-permute-start.2) | collective-permute-done | bytes 135200 | tf_op jit(solution)/shard_map/ppermute | solution.py:509
  23.0 2.0 %collective-permute-start.4 = (f32[4,264,128]{2,1,0:T(8,128)S(1)}, f32[4,264,128]{2,1,0:T(8,128)S(1)}, u32[]{:S(2)}, u32[]{:S(2)}) collective-permute-start(f32[4,264,128]{2,1,0:T(8,128)S(1)} %pad_maximum_fusion), channel_id=1, source_target_pairs={{0,1},{1,0},{2,3},{3,2},{4,5},{5,4},{6,7},{7,6},{8,9},{9,8},{10,11... | collective-permute-start | bytes 1622024 | tf_op jit(solution)/shard_map/ppermute | solution.py:498
  28.2 4.5 %collective-permute-start.5 = (f32[64,256]{1,0:T(8,128)S(1)}, f32[64,256]{1,0:T(8,128)S(1)}, u32[]{:S(2)}, u32[]{:S(2)}) collective-permute-start(f32[64,256]{1,0:T(8,128)S(1)} %get-tuple-element.50), channel_id=1, source_target_pairs={{8,0},{9,1},{234,226},{235,227},{12,4},{13,5},{238,230},{239,231},... | collective-permute-start | bytes 196616 | tf_op jit(solution)/shard_map/ppermute | solution.py:494
  32.7 2.3 %shard_map.107 = f32[2,64,256]{2,1,0:T(8,128)S(1)} custom-call(f32[4,2,8,32,128]{4,3,2,1,0:T(8,128)S(1)} %get-tuple-element.38.wx1.refs_2_, f32[4,2,8,32,128]{4,3,2,1,0:T(8,128)S(1)} %get-tuple-element.39.wy1.refs_3_, f32[4,32,128]{2,1,0:T(8,128)S(1)} %get-tuple-element.40.live1.refs_6_, bf16[512,512]{1,0:T(8,128)(2,1)S(1)} %get-tuple-element.41.ohs1.refs_1_, ...), custom_call_target="tpu_custom_call" | custom-call | flops 4000000000 | bytes 262144 | tf_op jit(solution)/shard_map/pallas_call | solution.py:575
  35.0 2.7 %collective-permute-start.7 = (f32[2,64,256]{2,1,0:T(8,128)S(1)}, f32[2,64,256]{2,1,0:T(8,128)S(1)}, u32[]{:S(2)}, u32[]{:S(2)}) collective-permute-start(f32[2,64,256]{2,1,0:T(8,128)S(1)} %shard_map.107), channel_id=1, source_target_pairs={{8,0},{9,1},{234,226},{235,227},{12,4},{13,5},{238,230},{239,231},... | collective-permute-start | bytes 393224 | tf_op jit(solution)/shard_map/ppermute | solution.py:494
  37.8 2.6 %collective-permute-start.6 = (f32[64,256]{1,0:T(8,128)S(1)}, f32[64,256]{1,0:T(8,128)S(1)}, u32[]{:S(2)}, u32[]{:S(2)}) collective-permute-start(f32[64,256]{1,0:T(8,128)S(1)} %sub.15.v_ref.prev_ref.refs_0_.v0), channel_id=1, source_target_pairs={{0,8},{1,9},{226,234},{227,235},{4,12},{5,13},{230,238},{231,239},... | collective-permute-start | bytes 196616 | tf_op jit(solution)/shard_map/ppermute | solution.py:494
  42.8 2.3 %shard_map.108 = (f32[64,256]{1,0:T(8,128)S(1)}, f32[64,256]{1,0:T(8,128)S(1)}, f32[8,32,128]{2,1,0:T(8,128)S(1)}) custom-call(f32[64,256]{1,0:T(8,128)S(1)} %sub.15.v_ref.prev_ref.refs_0_.v0, bf16[256,512]{1,0:T(8,128)(2,1)S(1)} %get-tuple-element.52.refs_0_, bf16[512,512]{1,0:T(8,128)(2,1)S(1)} %get-tuple-element.41.ohs1.refs_1_, ...), custom_call_target="tpu_custom_call" | custom-call | flops 2000000000 | bytes 262144 | tf_op jit(solution)/shard_map/pallas_call | solution.py:589
  45.1 3.3 %collective-permute-start.9 = (f32[64,256]{1,0:T(8,128)S(1)}, f32[64,256]{1,0:T(8,128)S(1)}, u32[]{:S(2)}, u32[]{:S(2)}) collective-permute-start(f32[64,256]{1,0:T(8,128)S(1)} %get-tuple-element.62), channel_id=1, source_target_pairs={{8,0},{9,1},{234,226},{235,227},{12,4},{13,5},{238,230},{239,231},... | collective-permute-start | bytes 196616 | tf_op jit(solution)/shard_map/ppermute | solution.py:494
  50.7 3.5 %collective-permute-start.10 = (f32[64,256]{1,0:T(8,128)S(1)}, f32[64,256]{1,0:T(8,128)S(1)}, u32[]{:S(2)}, u32[]{:S(2)}) collective-permute-start(f32[64,256]{1,0:T(8,128)S(1)} %sub.16.v_ref.prev_ref.refs_1_.v1), channel_id=1, source_target_pairs={{0,8},{1,9},{226,234},{227,235},{4,12},{5,13},{230,238},{231,239},... | collective-permute-start | bytes 196616 | tf_op jit(solution)/shard_map/ppermute | solution.py:494
  54.2 2.3 %shard_map.110 = (f32[64,256]{1,0:T(8,128)S(1)}, f32[64,256]{1,0:T(8,128)S(1)}, f32[8,32,128]{2,1,0:T(8,128)S(1)}) custom-call(f32[64,256]{1,0:T(8,128)S(1)} %sub.16.v_ref.prev_ref.refs_1_.v1, bf16[256,512]{1,0:T(8,128)(2,1)S(1)} %get-tuple-element.52.refs_0_, bf16[512,512]{1,0:T(8,128)(2,1)S(1)} %get-tuple-element.41.ohs1.refs_1_, ...), custom_call_target="tpu_custom_call" | custom-call | flops 2000000000 | bytes 262144 | tf_op jit(solution)/shard_map/pallas_call | solution.py:589
  61.5 3.2 %collective-permute-start.12 = (f32[64,256]{1,0:T(8,128)S(1)}, f32[64,256]{1,0:T(8,128)S(1)}, u32[]{:S(2)}, u32[]{:S(2)}) collective-permute-start(f32[64,256]{1,0:T(8,128)S(1)} %sub.17.v_ref.prev_ref.refs_2_.v2), channel_id=1, source_target_pairs={{0,8},{1,9},{226,234},{227,235},{4,12},{5,13},{230,238},{231,239},... | collective-permute-start | bytes 196616 | tf_op jit(solution)/shard_map/ppermute | solution.py:494
  64.7 2.3 %shard_map.112 = (f32[64,256]{1,0:T(8,128)S(1)}, f32[64,256]{1,0:T(8,128)S(1)}, f32[8,32,128]{2,1,0:T(8,128)S(1)}) custom-call(f32[64,256]{1,0:T(8,128)S(1)} %sub.17.v_ref.prev_ref.refs_2_.v2, bf16[256,512]{1,0:T(8,128)(2,1)S(1)} %get-tuple-element.52.refs_0_, bf16[512,512]{1,0:T(8,128)(2,1)S(1)} %get-tuple-element.41.ohs1.refs_1_, ...), custom_call_target="tpu_custom_call" | custom-call | flops 2000000000 | bytes 262144 | tf_op jit(solution)/shard_map/pallas_call | solution.py:589
  66.9 2.1 %collective-permute-start.13 = (f32[64,256]{1,0:T(8,128)S(1)}, f32[64,256]{1,0:T(8,128)S(1)}, u32[]{:S(2)}, u32[]{:S(2)}) collective-permute-start(f32[64,256]{1,0:T(8,128)S(1)} %get-tuple-element.68), channel_id=1, source_target_pairs={{8,0},{9,1},{234,226},{235,227},{12,4},{13,5},{238,230},{239,231},... | collective-permute-start | bytes 196616 | tf_op jit(solution)/shard_map/ppermute | solution.py:494
  72.0 3.5 %collective-permute-start.14 = (f32[64,256]{1,0:T(8,128)S(1)}, f32[64,256]{1,0:T(8,128)S(1)}, u32[]{:S(2)}, u32[]{:S(2)}) collective-permute-start(f32[64,256]{1,0:T(8,128)S(1)} %sub.18.v_ref.refs_3_.v3), channel_id=1, source_target_pairs={{0,8},{1,9},{226,234},{227,235},{4,12},{5,13},{230,238},{231,239},... | collective-permute-start | bytes 196616 | tf_op jit(solution)/shard_map/ppermute | solution.py:494
  75.5 2.3 %shard_map.114 = (f32[64,256]{1,0:T(8,128)S(1)}, f32[64,256]{1,0:T(8,128)S(1)}, f32[8,32,128]{2,1,0:T(8,128)S(1)}) custom-call(f32[64,256]{1,0:T(8,128)S(1)} %sub.18.v_ref.refs_3_.v3, bf16[256,512]{1,0:T(8,128)(2,1)S(1)} %get-tuple-element.52.refs_0_, bf16[512,512]{1,0:T(8,128)(2,1)S(1)} %get-tuple-element.41.ohs1.refs_1_, ...), custom_call_target="tpu_custom_call" | custom-call | flops 2000000000 | bytes 262144 | tf_op jit(solution)/shard_map/pallas_call | solution.py:589
  77.8 1.9 %collective-permute-start.15 = (f32[64,256]{1,0:T(8,128)S(1)}, f32[64,256]{1,0:T(8,128)S(1)}, u32[]{:S(2)}, u32[]{:S(2)}) collective-permute-start(f32[64,256]{1,0:T(8,128)S(1)} %get-tuple-element.71), channel_id=1, source_target_pairs={{8,0},{9,1},{234,226},{235,227},{12,4},{13,5},{238,230},{239,231},... | collective-permute-start | bytes 196616 | tf_op jit(solution)/shard_map/ppermute | solution.py:494
  84.1 13.4 %all_to_all.8 = f32[32,1,128]{2,1,0:T(1,128)S(1)} all-to-all(f32[32,1,128]{2,1,0:T(1,128)S(1)} %broadcast_in_dim.2), channel_id=1, replica_groups=mesh['sec'=32,'tile'=8] {'sec'}, dimensions={0} | all-to-all | bytes 32768 | tf_op jit(solution)/shard_map/all_to_all | solution.py:596
  97.5 6.5 %collective-permute-start.16 = (f32[32,128]{1,0:T(8,128)S(1)}, f32[32,128]{1,0:T(8,128)S(1)}, u32[]{:S(2)}, u32[]{:S(2)}) collective-permute-start(f32[32,128]{1,0:T(8,128)S(1)} %bitcast.28), channel_id=1, source_target_pairs={{0,1},{1,0},{2,3},{3,2},{4,5},{5,4},{6,7},{7,6},{8,9},{9,8},{10,11... | collective-permute-start | bytes 49160 | tf_op jit(solution)/shard_map/ppermute | solution.py:498
  106.2 3.2 %collective-permute-start.17 = (f32[2,32,64]{2,1,0:T(8,128)S(1)}, f32[2,32,64]{2,1,0:T(8,128)S(1)}, u32[]{:S(2)}, u32[]{:S(2)}) collective-permute-start(f32[2,32,64]{2,1,0:T(8,128)S(1)} %get-tuple-element.72), channel_id=1, source_target_pairs={{0,0},{1,1},{226,2},{227,3},{4,4},{5,5},{230,6},{231,7},{8,8},{9,9... | collective-permute-start | bytes 49160 | tf_op jit(solution)/shard_map/ppermute | solution.py:518
  109.4 4.4 %collective-permute-start.18 = (f32[2,32,64]{2,1,0:T(8,128)S(1)}, f32[2,32,64]{2,1,0:T(8,128)S(1)}, u32[]{:S(2)}, u32[]{:S(2)}) collective-permute-start(f32[2,32,64]{2,1,0:T(8,128)S(1)} %get-tuple-element.73), channel_id=1, source_target_pairs={{0,1},{1,0},{226,3},{227,2},{4,5},{5,4},{230,7},{231,6},{8,9},{9,8... | collective-permute-start | bytes 49160 | tf_op jit(solution)/shard_map/ppermute | solution.py:518
  113.8 2.3 %collective-permute-done.17 = f32[2,32,64]{2,1,0:T(8,128)S(1)} collective-permute-done((f32[2,32,64]{2,1,0:T(8,128)S(1)}, f32[2,32,64]{2,1,0:T(8,128)S(1)}, u32[]{:S(2)}, u32[]{:S(2)}) %collective-permute-start.17) | collective-permute-done | bytes 16416 | tf_op jit(solution)/shard_map/ppermute | solution.py:518
  116.1 2.3 %collective-permute-done.18 = f32[2,32,64]{2,1,0:T(8,128)S(1)} collective-permute-done((f32[2,32,64]{2,1,0:T(8,128)S(1)}, f32[2,32,64]{2,1,0:T(8,128)S(1)}, u32[]{:S(2)}, u32[]{:S(2)}) %collective-permute-start.18) | collective-permute-done | bytes 16416 | tf_op jit(solution)/shard_map/ppermute | solution.py:518
  (39 shorter events, 25.8 us)
Async XLA Ops:
  2.4 17.0 %collective-permute-start = (f32[264,128]{1,0:T(8,128)}, f32[264,128]{1,0:T(8,128)S(1)}, u32[]{:S(2)}, u32[]{:S(2)}) collective-permute-start(f32[264,128]{1,0:T(8,128)} %shard_map.104), channel_id=1, source_target_pairs={{0,4},{1,5},{2,230},{3,231},{4,0},{5,1},{6,226},{7,227},{8,12},{9,... | collective-permute-start | bytes 405512 | tf_op jit(solution)/shard_map/ppermute | solution.py:509
  11.9 8.3 %collective-permute-start.1 = (f32[264,128]{1,0:T(8,128)}, f32[264,128]{1,0:T(8,128)S(1)}, u32[]{:S(2)}, u32[]{:S(2)}) collective-permute-start(f32[264,128]{1,0:T(8,128)} %shard_map.104), channel_id=1, source_target_pairs={{0,226},{1,227},{2,4},{3,5},{4,230},{5,231},{6,0},{7,1},{8,234},{9... | collective-permute-start | bytes 405512 | tf_op jit(solution)/shard_map/ppermute | solution.py:509
  11.9 11.0 %collective-permute-start.2 = (f32[264,128]{1,0:T(8,128)}, f32[264,128]{1,0:T(8,128)S(1)}, u32[]{:S(2)}, u32[]{:S(2)}) collective-permute-start(f32[264,128]{1,0:T(8,128)} %shard_map.104), channel_id=1, source_target_pairs={{0,230},{1,231},{2,0},{3,1},{4,226},{5,227},{6,4},{7,5},{8,238},{9... | collective-permute-start | bytes 405512 | tf_op jit(solution)/shard_map/ppermute | solution.py:509
  11.9 11.0 %collective-permute-start.3 = (f32[264,128]{1,0:T(8,128)}, f32[264,128]{1,0:T(8,128)S(1)}, u32[]{:S(2)}, u32[]{:S(2)}) collective-permute-start(f32[264,128]{1,0:T(8,128)} %shard_map.104), channel_id=1, source_target_pairs={{0,0},{1,1},{2,226},{3,227},{4,4},{5,5},{6,230},{7,231},{8,8},{9,9... | collective-permute-start | bytes 405512 | tf_op jit(solution)/shard_map/ppermute | solution.py:509
  23.0 3.6 %collective-permute-start.4 = (f32[4,264,128]{2,1,0:T(8,128)S(1)}, f32[4,264,128]{2,1,0:T(8,128)S(1)}, u32[]{:S(2)}, u32[]{:S(2)}) collective-permute-start(f32[4,264,128]{2,1,0:T(8,128)S(1)} %pad_maximum_fusion), channel_id=1, source_target_pairs={{0,1},{1,0},{2,3},{3,2},{4,5},{5,4},{6,7},{7,6},{8,9},{9,8},{10,11... | collective-permute-start | bytes 1622024 | tf_op jit(solution)/shard_map/ppermute | solution.py:498
  28.2 6.8 %collective-permute-start.5 = (f32[64,256]{1,0:T(8,128)S(1)}, f32[64,256]{1,0:T(8,128)S(1)}, u32[]{:S(2)}, u32[]{:S(2)}) collective-permute-start(f32[64,256]{1,0:T(8,128)S(1)} %get-tuple-element.50), channel_id=1, source_target_pairs={{8,0},{9,1},{234,226},{235,227},{12,4},{13,5},{238,230},{239,231},... | collective-permute-start | bytes 196616 | tf_op jit(solution)/shard_map/ppermute | solution.py:494
  35.0 6.3 %collective-permute-start.7 = (f32[2,64,256]{2,1,0:T(8,128)S(1)}, f32[2,64,256]{2,1,0:T(8,128)S(1)}, u32[]{:S(2)}, u32[]{:S(2)}) collective-permute-start(f32[2,64,256]{2,1,0:T(8,128)S(1)} %shard_map.107), channel_id=1, source_target_pairs={{8,0},{9,1},{234,226},{235,227},{12,4},{13,5},{238,230},{239,231},... | collective-permute-start | bytes 393224 | tf_op jit(solution)/shard_map/ppermute | solution.py:494
  37.8 10.6 %collective-permute-start.6 = (f32[64,256]{1,0:T(8,128)S(1)}, f32[64,256]{1,0:T(8,128)S(1)}, u32[]{:S(2)}, u32[]{:S(2)}) collective-permute-start(f32[64,256]{1,0:T(8,128)S(1)} %sub.15.v_ref.prev_ref.refs_0_.v0), channel_id=1, source_target_pairs={{0,8},{1,9},{226,234},{227,235},{4,12},{5,13},{230,238},{231,239},... | collective-permute-start | bytes 196616 | tf_op jit(solution)/shard_map/ppermute | solution.py:494
  41.4 7.0 %collective-permute-start.8 = (f32[2,64,256]{2,1,0:T(8,128)S(1)}, f32[2,64,256]{2,1,0:T(8,128)S(1)}, u32[]{:S(2)}, u32[]{:S(2)}) collective-permute-start(f32[2,64,256]{2,1,0:T(8,128)S(1)} %collective-permute-done.7.mine_ref), channel_id=1, source_target_pairs={{0,1},{1,0},{2,3},{3,2},{4,5},{5,4},{6,7},{7,6},{8,9},{9,8},{10,11... | collective-permute-start | bytes 393224 | tf_op jit(solution)/shard_map/ppermute | solution.py:498
  45.1 5.6 %collective-permute-start.9 = (f32[64,256]{1,0:T(8,128)S(1)}, f32[64,256]{1,0:T(8,128)S(1)}, u32[]{:S(2)}, u32[]{:S(2)}) collective-permute-start(f32[64,256]{1,0:T(8,128)S(1)} %get-tuple-element.62), channel_id=1, source_target_pairs={{8,0},{9,1},{234,226},{235,227},{12,4},{13,5},{238,230},{239,231},... | collective-permute-start | bytes 196616 | tf_op jit(solution)/shard_map/ppermute | solution.py:494
  50.7 7.7 %collective-permute-start.10 = (f32[64,256]{1,0:T(8,128)S(1)}, f32[64,256]{1,0:T(8,128)S(1)}, u32[]{:S(2)}, u32[]{:S(2)}) collective-permute-start(f32[64,256]{1,0:T(8,128)S(1)} %sub.16.v_ref.prev_ref.refs_1_.v1), channel_id=1, source_target_pairs={{0,8},{1,9},{226,234},{227,235},{4,12},{5,13},{230,238},{231,239},... | collective-permute-start | bytes 196616 | tf_op jit(solution)/shard_map/ppermute | solution.py:494
  56.5 5.0 %collective-permute-start.11 = (f32[64,256]{1,0:T(8,128)S(1)}, f32[64,256]{1,0:T(8,128)S(1)}, u32[]{:S(2)}, u32[]{:S(2)}) collective-permute-start(f32[64,256]{1,0:T(8,128)S(1)} %get-tuple-element.65), channel_id=1, source_target_pairs={{8,0},{9,1},{234,226},{235,227},{12,4},{13,5},{238,230},{239,231},... | collective-permute-start | bytes 196616 | tf_op jit(solution)/shard_map/ppermute | solution.py:494
  61.5 7.6 %collective-permute-start.12 = (f32[64,256]{1,0:T(8,128)S(1)}, f32[64,256]{1,0:T(8,128)S(1)}, u32[]{:S(2)}, u32[]{:S(2)}) collective-permute-start(f32[64,256]{1,0:T(8,128)S(1)} %sub.17.v_ref.prev_ref.refs_2_.v2), channel_id=1, source_target_pairs={{0,8},{1,9},{226,234},{227,235},{4,12},{5,13},{230,238},{231,239},... | collective-permute-start | bytes 196616 | tf_op jit(solution)/shard_map/ppermute | solution.py:494
  66.9 5.0 %collective-permute-start.13 = (f32[64,256]{1,0:T(8,128)S(1)}, f32[64,256]{1,0:T(8,128)S(1)}, u32[]{:S(2)}, u32[]{:S(2)}) collective-permute-start(f32[64,256]{1,0:T(8,128)S(1)} %get-tuple-element.68), channel_id=1, source_target_pairs={{8,0},{9,1},{234,226},{235,227},{12,4},{13,5},{238,230},{239,231},... | collective-permute-start | bytes 196616 | tf_op jit(solution)/shard_map/ppermute | solution.py:494
  72.0 7.8 %collective-permute-start.14 = (f32[64,256]{1,0:T(8,128)S(1)}, f32[64,256]{1,0:T(8,128)S(1)}, u32[]{:S(2)}, u32[]{:S(2)}) collective-permute-start(f32[64,256]{1,0:T(8,128)S(1)} %sub.18.v_ref.refs_3_.v3), channel_id=1, source_target_pairs={{0,8},{1,9},{226,234},{227,235},{4,12},{5,13},{230,238},{231,239},... | collective-permute-start | bytes 196616 | tf_op jit(solution)/shard_map/ppermute | solution.py:494
  77.8 5.0 %collective-permute-start.15 = (f32[64,256]{1,0:T(8,128)S(1)}, f32[64,256]{1,0:T(8,128)S(1)}, u32[]{:S(2)}, u32[]{:S(2)}) collective-permute-start(f32[64,256]{1,0:T(8,128)S(1)} %get-tuple-element.71), channel_id=1, source_target_pairs={{8,0},{9,1},{234,226},{235,227},{12,4},{13,5},{238,230},{239,231},... | collective-permute-start | bytes 196616 | tf_op jit(solution)/shard_map/ppermute | solution.py:494
  97.5 7.3 %collective-permute-start.16 = (f32[32,128]{1,0:T(8,128)S(1)}, f32[32,128]{1,0:T(8,128)S(1)}, u32[]{:S(2)}, u32[]{:S(2)}) collective-permute-start(f32[32,128]{1,0:T(8,128)S(1)} %bitcast.28), channel_id=1, source_target_pairs={{0,1},{1,0},{2,3},{3,2},{4,5},{5,4},{6,7},{7,6},{8,9},{9,8},{10,11... | collective-permute-start | bytes 49160 | tf_op jit(solution)/shard_map/ppermute | solution.py:498
  106.2 9.9 %collective-permute-start.17 = (f32[2,32,64]{2,1,0:T(8,128)S(1)}, f32[2,32,64]{2,1,0:T(8,128)S(1)}, u32[]{:S(2)}, u32[]{:S(2)}) collective-permute-start(f32[2,32,64]{2,1,0:T(8,128)S(1)} %get-tuple-element.72), channel_id=1, source_target_pairs={{0,0},{1,1},{226,2},{227,3},{4,4},{5,5},{230,6},{231,7},{8,8},{9,9... | collective-permute-start | bytes 49160 | tf_op jit(solution)/shard_map/ppermute | solution.py:518
  109.4 9.0 %collective-permute-start.18 = (f32[2,32,64]{2,1,0:T(8,128)S(1)}, f32[2,32,64]{2,1,0:T(8,128)S(1)}, u32[]{:S(2)}, u32[]{:S(2)}) collective-permute-start(f32[2,32,64]{2,1,0:T(8,128)S(1)} %get-tuple-element.73), channel_id=1, source_target_pairs={{0,1},{1,0},{226,3},{227,2},{4,5},{5,4},{230,7},{231,6},{8,9},{9,8... | collective-permute-start | bytes 49160 | tf_op jit(solution)/shard_map/ppermute | solution.py:518

commit v5 on v4

--- a/solution.py
+++ b/solution.py
@@ -256,13 +256,13 @@
 
 
 def down_kernel(
-    v_ref, below_ref, prev_ref, part_ref, gap_ref, mine_ref, other_ref, stiff_ref, *refs, back
+    v_ref, raw_ref, sent_ref, prev_ref, part_ref, gap_ref, mine_ref, other_ref, stiff_ref, *refs, back
 ):
     halves_of = (refs[:7], refs[7:14])
     out_ref, g_ref, f_ref = refs[14:]
     ohf1, ohs1 = refs[0], refs[1]
     ohf2, ohs2 = refs[7], refs[8]
-    gather(split3(below_ref[...]), ohs1[256:512, :], ohs2[256:512, :], g_ref)
+    gather(split3(raw_ref[...] - sent_ref[...]), ohs1[256:512, :], ohs2[256:512, :], g_ref)
     for h, (_, _, wx_ref, wy_ref, fx_ref, col_ref, live_ref) in enumerate(halves_of):
 
         def body(blk, carry):
@@ -571,11 +571,12 @@
         other[0], other[1], other[2], other[3], *one[7:]
     )
     own, down, stiff = two[7:]
-    start_down = shifted(down, -1)
+    above = shifted(down, -1)
+    raw = shifted(own, 1)
     half = call(stencil_kernel, [((2, 64, 256), F32)], 8, [pltpu.VMEM((2, 64, 1024), F32)], us=4.0)(
         one[0], one[1], one[4], one[6], two[0], two[1], two[4], two[6]
     )[0]
-    fields = [own - start_down]
+    fields = [own - above]
     half, fields[0] = lax.optimization_barrier((half, fields[0]))
     mine = shifted(half, -1)
     other = swapped(mine)
@@ -585,12 +586,14 @@
     wide = pltpu.VMEM((64, 1024), F32)
     for k in range(ITERS):
         v = fields[-1]
-        below = shifted(v, 1)
+        sent = down
         part, down, gap = call(up_kernel, [field, field, ((8, 32, 128), F32)], 15, [wide, wide, wide])(v, *tables)
         above = shifted(down, -1)
-        partial = call(functools.partial(down_kernel, back=k > 0), [field], 22, [wide, wide])(
-            v, below, fields[max(k - 1, 0)], part, gap, mine, other, stiff, *tables
+        partial = call(functools.partial(down_kernel, back=k > 0), [field], 23, [wide, wide])(
+            v, raw, sent, fields[max(k - 1, 0)], part, gap, mine, other, stiff, *tables
         )[0]
+        if k < ITERS - 1:
+            raw = shifted(partial, 1)
         fields.append(partial - above)
     gram = call(dots_kernel, [((1, 128), F32)], 5)(*fields)[0]
     gram = lax.all_to_all(jnp.broadcast_to(gram, (32, 128)), "sec", 0, 0, tiled=True)

time: 120 us -> 114 us (0.950)
  the two profiles are of different devices: /device:TPU:41 before, /device:TPU:40 now
where the time goes in v5:
time: 114 us
  starting transfers between devices  57.6 us (51%)
  Pallas kernels  25.8 us (23%)
  blocking collectives  16.3 us (14%)
  waiting for transfers between devices  12.2 us (11%)
    ppermute x10, starting transfers between devices, shifted(): return lax.ppermute(block, ('sec', 'tile'), route)  31.9 us
    ppermute x4, starting transfers between devices, dealt(): return lax.ppermute(block, ('sec', 'tile'), route)  18.2 us
    all_to_all x1, blocking collectives, on_device(): lax.all_to_all(jnp.broadcast_to(gram, (32, 128)), 'sec', 0, 0, tiled=True)  16.3 us
    pallas_call x4, Pallas kernels, on_device(): call(up_kernel, [field, field, ((8, 32, 128), F32)], 15, [wide, wide, wide])  9.04 us
    ppermute x2, starting transfers between devices, returned(): return lax.ppermute(block, ('sec', 'tile'), route)  7.42 us
    pallas_call x4, Pallas kernels, on_device(): call(functools.partial(down_kernel, back=k > 0), [field], 23, [wide, wide])  7 us
    ppermute x2, waiting for transfers between devices, returned(): return lax.ppermute(block, ('sec', 'tile'), route)  4.85 us
    ppermute x4, waiting for transfers between devices, dealt(): return lax.ppermute(block, ('sec', 'tile'), route)  3.61 us
  transfers between devices with their start and end apart: 19, of which 8 were waited for; matrix products, arithmetic and copies ran while one was open for 0% of the time, Pallas kernels for 17%

profile of v5, /device:TPU:40, one launch (start us, length us, event | category | flops | bytes accessed | tf_op | source)
XLA Modules:
  0.0 113.7 jit_solution(16958927669864051320)
XLA Ops:
  2.4 9.8 %collective-permute-start = (f32[264,128]{1,0:T(8,128)}, f32[264,128]{1,0:T(8,128)S(1)}, u32[]{:S(2)}, u32[]{:S(2)}) collective-permute-start(f32[264,128]{1,0:T(8,128)} %shard_map.104), channel_id=1, source_target_pairs={{0,4},{1,5},{2,230},{3,231},{4,0},{5,1},{6,226},{7,227},{8,12},{9,... | collective-permute-start | bytes 405512 | tf_op jit(solution)/shard_map/ppermute | solution.py:509
  12.8 7.7 %collective-permute-start.3 = (f32[264,128]{1,0:T(8,128)}, f32[264,128]{1,0:T(8,128)S(1)}, u32[]{:S(2)}, u32[]{:S(2)}) collective-permute-start(f32[264,128]{1,0:T(8,128)} %shard_map.104), channel_id=1, source_target_pairs={{0,0},{1,1},{2,226},{3,227},{4,4},{5,5},{6,230},{7,231},{8,8},{9,9... | collective-permute-start | bytes 405512 | tf_op jit(solution)/shard_map/ppermute | solution.py:509
  20.5 2.4 %collective-permute-done.1.refs_1_ = f32[264,128]{1,0:T(8,128)S(1)} collective-permute-done((f32[264,128]{1,0:T(8,128)}, f32[264,128]{1,0:T(8,128)S(1)}, u32[]{:S(2)}, u32[]{:S(2)}) %collective-permute-start.1) | collective-permute-done | bytes 135200 | tf_op jit(solution)/shard_map/ppermute | solution.py:509
  27.9 4.8 %collective-permute-start.5 = (f32[64,256]{1,0:T(8,128)S(1)}, f32[64,256]{1,0:T(8,128)S(1)}, u32[]{:S(2)}, u32[]{:S(2)}) collective-permute-start(f32[64,256]{1,0:T(8,128)S(1)} %get-tuple-element.50.sent_ref), channel_id=1, source_target_pairs={{8,0},{9,1},{234,226},{235,227},{12,4},{13,5},{238,230},{239,231},... | collective-permute-start | bytes 196616 | tf_op jit(solution)/shard_map/ppermute | solution.py:494
  32.7 2.3 %shard_map.107 = f32[2,64,256]{2,1,0:T(8,128)S(1)} custom-call(f32[4,2,8,32,128]{4,3,2,1,0:T(8,128)S(1)} %get-tuple-element.38.wx1.refs_2_, f32[4,2,8,32,128]{4,3,2,1,0:T(8,128)S(1)} %get-tuple-element.39.wy1.refs_3_, f32[4,32,128]{2,1,0:T(8,128)S(1)} %get-tuple-element.40.live1.refs_6_, bf16[512,512]{1,0:T(8,128)(2,1)S(1)} %get-tuple-element.41.ohs1.refs_1_, ...), custom_call_target="tpu_custom_call" | custom-call | flops 4000000000 | bytes 262144 | tf_op jit(solution)/shard_map/pallas_call | solution.py:576
  35.0 3.9 %collective-permute-start.7 = (f32[2,64,256]{2,1,0:T(8,128)S(1)}, f32[2,64,256]{2,1,0:T(8,128)S(1)}, u32[]{:S(2)}, u32[]{:S(2)}) collective-permute-start(f32[2,64,256]{2,1,0:T(8,128)S(1)} %shard_map.107), channel_id=1, source_target_pairs={{8,0},{9,1},{234,226},{235,227},{12,4},{13,5},{238,230},{239,231},... | collective-permute-start | bytes 393224 | tf_op jit(solution)/shard_map/ppermute | solution.py:494
  38.9 2.0 %collective-permute-start.6 = (f32[64,256]{1,0:T(8,128)S(1)}, f32[64,256]{1,0:T(8,128)S(1)}, u32[]{:S(2)}, u32[]{:S(2)}) collective-permute-start(f32[64,256]{1,0:T(8,128)S(1)} %get-tuple-element.49), channel_id=1, source_target_pairs={{0,8},{1,9},{226,234},{227,235},{4,12},{5,13},{230,238},{231,239},... | collective-permute-start | bytes 196616 | tf_op jit(solution)/shard_map/ppermute | solution.py:494
  42.2 2.3 %shard_map.108 = (f32[64,256]{1,0:T(8,128)S(1)}, f32[64,256]{1,0:T(8,128)S(1)}, f32[8,32,128]{2,1,0:T(8,128)S(1)}) custom-call(f32[64,256]{1,0:T(8,128)S(1)} %sub.15.v_ref.prev_ref.refs_0_.v0, bf16[256,512]{1,0:T(8,128)(2,1)S(1)} %get-tuple-element.52.refs_0_, bf16[512,512]{1,0:T(8,128)(2,1)S(1)} %get-tuple-element.41.ohs1.refs_1_, ...), custom_call_target="tpu_custom_call" | custom-call | flops 2000000000 | bytes 262144 | tf_op jit(solution)/shard_map/pallas_call | solution.py:590
  44.4 3.5 %collective-permute-start.9 = (f32[64,256]{1,0:T(8,128)S(1)}, f32[64,256]{1,0:T(8,128)S(1)}, u32[]{:S(2)}, u32[]{:S(2)}) collective-permute-start(f32[64,256]{1,0:T(8,128)S(1)} %get-tuple-element.62.sent_ref), channel_id=1, source_target_pairs={{8,0},{9,1},{234,226},{235,227},{12,4},{13,5},{238,230},{239,231},... | collective-permute-start | bytes 196616 | tf_op jit(solution)/shard_map/ppermute | solution.py:494
  49.8 2.3 %collective-permute-start.10 = (f32[64,256]{1,0:T(8,128)S(1)}, f32[64,256]{1,0:T(8,128)S(1)}, u32[]{:S(2)}, u32[]{:S(2)}) collective-permute-start(f32[64,256]{1,0:T(8,128)S(1)} %shard_map.109), channel_id=1, source_target_pairs={{0,8},{1,9},{226,234},{227,235},{4,12},{5,13},{230,238},{231,239},... | collective-permute-start | bytes 196616 | tf_op jit(solution)/shard_map/ppermute | solution.py:494
  52.1 2.3 %shard_map.110 = (f32[64,256]{1,0:T(8,128)S(1)}, f32[64,256]{1,0:T(8,128)S(1)}, f32[8,32,128]{2,1,0:T(8,128)S(1)}) custom-call(f32[64,256]{1,0:T(8,128)S(1)} %sub.16.v_ref.prev_ref.refs_1_.v1, bf16[256,512]{1,0:T(8,128)(2,1)S(1)} %get-tuple-element.52.refs_0_, bf16[512,512]{1,0:T(8,128)(2,1)S(1)} %get-tuple-element.41.ohs1.refs_1_, ...), custom_call_target="tpu_custom_call" | custom-call | flops 2000000000 | bytes 262144 | tf_op jit(solution)/shard_map/pallas_call | solution.py:590
  54.4 3.5 %collective-permute-start.11 = (f32[64,256]{1,0:T(8,128)S(1)}, f32[64,256]{1,0:T(8,128)S(1)}, u32[]{:S(2)}, u32[]{:S(2)}) collective-permute-start(f32[64,256]{1,0:T(8,128)S(1)} %get-tuple-element.65.sent_ref), channel_id=1, source_target_pairs={{8,0},{9,1},{234,226},{235,227},{12,4},{13,5},{238,230},{239,231},... | collective-permute-start | bytes 196616 | tf_op jit(solution)/shard_map/ppermute | solution.py:494
  57.9 1.8 %shard_map.111 = f32[64,256]{1,0:T(8,128)S(1)} custom-call(f32[64,256]{1,0:T(8,128)S(1)} %sub.16.v_ref.prev_ref.refs_1_.v1, f32[64,256]{1,0:T(8,128)S(1)} %collective-permute-done.10.raw_ref, f32[64,256]{1,0:T(8,128)S(1)} %get-tuple-element.62.sent_ref, f32[64,256]{1,0:T(8,128)S(1)} %sub.15.v_ref.prev_ref.refs_0_.v0, ...), custom_call_target="tpu_custom_call" | custom-call | flops 2000000000 | bytes 262144 | tf_op jit(solution)/shard_map/pallas_call | solution.py:592
  59.7 2.3 %collective-permute-start.12 = (f32[64,256]{1,0:T(8,128)S(1)}, f32[64,256]{1,0:T(8,128)S(1)}, u32[]{:S(2)}, u32[]{:S(2)}) collective-permute-start(f32[64,256]{1,0:T(8,128)S(1)} %shard_map.111), channel_id=1, source_target_pairs={{0,8},{1,9},{226,234},{227,235},{4,12},{5,13},{230,238},{231,239},... | collective-permute-start | bytes 196616 | tf_op jit(solution)/shard_map/ppermute | solution.py:494
  62.0 2.3 %shard_map.112 = (f32[64,256]{1,0:T(8,128)S(1)}, f32[64,256]{1,0:T(8,128)S(1)}, f32[8,32,128]{2,1,0:T(8,128)S(1)}) custom-call(f32[64,256]{1,0:T(8,128)S(1)} %sub.17.v_ref.prev_ref.refs_2_.v2, bf16[256,512]{1,0:T(8,128)(2,1)S(1)} %get-tuple-element.52.refs_0_, bf16[512,512]{1,0:T(8,128)(2,1)S(1)} %get-tuple-element.41.ohs1.refs_1_, ...), custom_call_target="tpu_custom_call" | custom-call | flops 2000000000 | bytes 262144 | tf_op jit(solution)/shard_map/pallas_call | solution.py:590
  64.3 3.5 %collective-permute-start.13 = (f32[64,256]{1,0:T(8,128)S(1)}, f32[64,256]{1,0:T(8,128)S(1)}, u32[]{:S(2)}, u32[]{:S(2)}) collective-permute-start(f32[64,256]{1,0:T(8,128)S(1)} %get-tuple-element.68.sent_ref), channel_id=1, source_target_pairs={{8,0},{9,1},{234,226},{235,227},{12,4},{13,5},{238,230},{239,231},... | collective-permute-start | bytes 196616 | tf_op jit(solution)/shard_map/ppermute | solution.py:494
  67.8 1.8 %shard_map.113 = f32[64,256]{1,0:T(8,128)S(1)} custom-call(f32[64,256]{1,0:T(8,128)S(1)} %sub.17.v_ref.prev_ref.refs_2_.v2, f32[64,256]{1,0:T(8,128)S(1)} %collective-permute-done.12.raw_ref, f32[64,256]{1,0:T(8,128)S(1)} %get-tuple-element.65.sent_ref, f32[64,256]{1,0:T(8,128)S(1)} %sub.16.v_ref.prev_ref.refs_1_.v1, ...), custom_call_target="tpu_custom_call" | custom-call | flops 2000000000 | bytes 262144 | tf_op jit(solution)/shard_map/pallas_call | solution.py:592
  69.6 2.5 %collective-permute-start.14 = (f32[64,256]{1,0:T(8,128)S(1)}, f32[64,256]{1,0:T(8,128)S(1)}, u32[]{:S(2)}, u32[]{:S(2)}) collective-permute-start(f32[64,256]{1,0:T(8,128)S(1)} %shard_map.113), channel_id=1, source_target_pairs={{0,8},{1,9},{226,234},{227,235},{4,12},{5,13},{230,238},{231,239},... | collective-permute-start | bytes 196616 | tf_op jit(solution)/shard_map/ppermute | solution.py:494
  72.1 2.3 %shard_map.114 = (f32[64,256]{1,0:T(8,128)S(1)}, f32[64,256]{1,0:T(8,128)S(1)}, f32[8,32,128]{2,1,0:T(8,128)S(1)}) custom-call(f32[64,256]{1,0:T(8,128)S(1)} %sub.18.v_ref.refs_3_.v3, bf16[256,512]{1,0:T(8,128)(2,1)S(1)} %get-tuple-element.52.refs_0_, bf16[512,512]{1,0:T(8,128)(2,1)S(1)} %get-tuple-element.41.ohs1.refs_1_, ...), custom_call_target="tpu_custom_call" | custom-call | flops 2000000000 | bytes 262144 | tf_op jit(solution)/shard_map/pallas_call | solution.py:590
  74.4 3.5 %collective-permute-start.15 = (f32[64,256]{1,0:T(8,128)S(1)}, f32[64,256]{1,0:T(8,128)S(1)}, u32[]{:S(2)}, u32[]{:S(2)}) collective-permute-start(f32[64,256]{1,0:T(8,128)S(1)} %get-tuple-element.71), channel_id=1, source_target_pairs={{8,0},{9,1},{234,226},{235,227},{12,4},{13,5},{238,230},{239,231},... | collective-permute-start | bytes 196616 | tf_op jit(solution)/shard_map/ppermute | solution.py:494
  78.0 1.8 %shard_map.115 = f32[64,256]{1,0:T(8,128)S(1)} custom-call(f32[64,256]{1,0:T(8,128)S(1)} %sub.18.v_ref.refs_3_.v3, f32[64,256]{1,0:T(8,128)S(1)} %collective-permute-done.14.raw_ref, f32[64,256]{1,0:T(8,128)S(1)} %get-tuple-element.68.sent_ref, f32[64,256]{1,0:T(8,128)S(1)} %sub.17.v_ref.prev_ref.refs_2_.v2, f32[64,256]{1,0:T(8,128)S(1)} %get-tuple-element.69.part_ref, ...), custom_call_target="tpu_custom_call" | custom-call | flops 2000000000 | bytes 262144 | tf_op jit(solution)/shard_map/pallas_call | solution.py:592
  81.9 16.3 %all_to_all.8 = f32[32,1,128]{2,1,0:T(1,128)S(1)} all-to-all(f32[32,1,128]{2,1,0:T(1,128)S(1)} %broadcast_in_dim.2), channel_id=1, replica_groups=mesh['sec'=32,'tile'=8] {'sec'}, dimensions={0} | all-to-all | bytes 32768 | tf_op jit(solution)/shard_map/all_to_all | solution.py:599
  102.1 6.0 %collective-permute-start.17 = (f32[2,32,64]{2,1,0:T(8,128)S(1)}, f32[2,32,64]{2,1,0:T(8,128)S(1)}, u32[]{:S(2)}, u32[]{:S(2)}) collective-permute-start(f32[2,32,64]{2,1,0:T(8,128)S(1)} %get-tuple-element.72), channel_id=1, source_target_pairs={{0,0},{1,1},{226,2},{227,3},{4,4},{5,5},{230,6},{231,7},{8,8},{9,9... | collective-permute-start | bytes 49160 | tf_op jit(solution)/shard_map/ppermute | solution.py:518
  109.2 3.8 %collective-permute-done.17 = f32[2,32,64]{2,1,0:T(8,128)S(1)} collective-permute-done((f32[2,32,64]{2,1,0:T(8,128)S(1)}, f32[2,32,64]{2,1,0:T(8,128)S(1)}, u32[]{:S(2)}, u32[]{:S(2)}) %collective-permute-start.17) | collective-permute-done | bytes 16416 | tf_op jit(solution)/shard_map/ppermute | solution.py:518
  (39 shorter events, 18.2 us)
Async XLA Ops:
  2.4 18.2 %collective-permute-start = (f32[264,128]{1,0:T(8,128)}, f32[264,128]{1,0:T(8,128)S(1)}, u32[]{:S(2)}, u32[]{:S(2)}) collective-permute-start(f32[264,128]{1,0:T(8,128)} %shard_map.104), channel_id=1, source_target_pairs={{0,4},{1,5},{2,230},{3,231},{4,0},{5,1},{6,226},{7,227},{8,12},{9,... | collective-permute-start | bytes 405512 | tf_op jit(solution)/shard_map/ppermute | solution.py:509
  12.2 10.7 %collective-permute-start.1 = (f32[264,128]{1,0:T(8,128)}, f32[264,128]{1,0:T(8,128)S(1)}, u32[]{:S(2)}, u32[]{:S(2)}) collective-permute-start(f32[264,128]{1,0:T(8,128)} %shard_map.104), channel_id=1, source_target_pairs={{0,226},{1,227},{2,4},{3,5},{4,230},{5,231},{6,0},{7,1},{8,234},{9... | collective-permute-start | bytes 405512 | tf_op jit(solution)/shard_map/ppermute | solution.py:509
  12.2 11.9 %collective-permute-start.2 = (f32[264,128]{1,0:T(8,128)}, f32[264,128]{1,0:T(8,128)S(1)}, u32[]{:S(2)}, u32[]{:S(2)}) collective-permute-start(f32[264,128]{1,0:T(8,128)} %shard_map.104), channel_id=1, source_target_pairs={{0,230},{1,231},{2,0},{3,1},{4,226},{5,227},{6,4},{7,5},{8,238},{9... | collective-permute-start | bytes 405512 | tf_op jit(solution)/shard_map/ppermute | solution.py:509
  12.8 11.4 %collective-permute-start.3 = (f32[264,128]{1,0:T(8,128)}, f32[264,128]{1,0:T(8,128)S(1)}, u32[]{:S(2)}, u32[]{:S(2)}) collective-permute-start(f32[264,128]{1,0:T(8,128)} %shard_map.104), channel_id=1, source_target_pairs={{0,0},{1,1},{2,226},{3,227},{4,4},{5,5},{6,230},{7,231},{8,8},{9,9... | collective-permute-start | bytes 405512 | tf_op jit(solution)/shard_map/ppermute | solution.py:509
  24.2 2.0 %collective-permute-start.4 = (f32[4,264,128]{2,1,0:T(8,128)S(1)}, f32[4,264,128]{2,1,0:T(8,128)S(1)}, u32[]{:S(2)}, u32[]{:S(2)}) collective-permute-start(f32[4,264,128]{2,1,0:T(8,128)S(1)} %pad_maximum_fusion), channel_id=1, source_target_pairs={{0,1},{1,0},{2,3},{3,2},{4,5},{5,4},{6,7},{7,6},{8,9},{9,8},{10,11... | collective-permute-start | bytes 1622024 | tf_op jit(solution)/shard_map/ppermute | solution.py:498
  27.9 7.1 %collective-permute-start.5 = (f32[64,256]{1,0:T(8,128)S(1)}, f32[64,256]{1,0:T(8,128)S(1)}, u32[]{:S(2)}, u32[]{:S(2)}) collective-permute-start(f32[64,256]{1,0:T(8,128)S(1)} %get-tuple-element.50.sent_ref), channel_id=1, source_target_pairs={{8,0},{9,1},{234,226},{235,227},{12,4},{13,5},{238,230},{239,231},... | collective-permute-start | bytes 196616 | tf_op jit(solution)/shard_map/ppermute | solution.py:494
  35.0 7.2 %collective-permute-start.7 = (f32[2,64,256]{2,1,0:T(8,128)S(1)}, f32[2,64,256]{2,1,0:T(8,128)S(1)}, u32[]{:S(2)}, u32[]{:S(2)}) collective-permute-start(f32[2,64,256]{2,1,0:T(8,128)S(1)} %shard_map.107), channel_id=1, source_target_pairs={{8,0},{9,1},{234,226},{235,227},{12,4},{13,5},{238,230},{239,231},... | collective-permute-start | bytes 393224 | tf_op jit(solution)/shard_map/ppermute | solution.py:494
  38.9 9.1 %collective-permute-start.6 = (f32[64,256]{1,0:T(8,128)S(1)}, f32[64,256]{1,0:T(8,128)S(1)}, u32[]{:S(2)}, u32[]{:S(2)}) collective-permute-start(f32[64,256]{1,0:T(8,128)S(1)} %get-tuple-element.49), channel_id=1, source_target_pairs={{0,8},{1,9},{226,234},{227,235},{4,12},{5,13},{230,238},{231,239},... | collective-permute-start | bytes 196616 | tf_op jit(solution)/shard_map/ppermute | solution.py:494
  42.2 5.8 %collective-permute-start.8 = (f32[2,64,256]{2,1,0:T(8,128)S(1)}, f32[2,64,256]{2,1,0:T(8,128)S(1)}, u32[]{:S(2)}, u32[]{:S(2)}) collective-permute-start(f32[2,64,256]{2,1,0:T(8,128)S(1)} %collective-permute-done.7.mine_ref), channel_id=1, source_target_pairs={{0,1},{1,0},{2,3},{3,2},{4,5},{5,4},{6,7},{7,6},{8,9},{9,8},{10,11... | collective-permute-start | bytes 393224 | tf_op jit(solution)/shard_map/ppermute | solution.py:498
  44.4 7.6 %collective-permute-start.9 = (f32[64,256]{1,0:T(8,128)S(1)}, f32[64,256]{1,0:T(8,128)S(1)}, u32[]{:S(2)}, u32[]{:S(2)}) collective-permute-start(f32[64,256]{1,0:T(8,128)S(1)} %get-tuple-element.62.sent_ref), channel_id=1, source_target_pairs={{8,0},{9,1},{234,226},{235,227},{12,4},{13,5},{238,230},{239,231},... | collective-permute-start | bytes 196616 | tf_op jit(solution)/shard_map/ppermute | solution.py:494
  49.8 8.2 %collective-permute-start.10 = (f32[64,256]{1,0:T(8,128)S(1)}, f32[64,256]{1,0:T(8,128)S(1)}, u32[]{:S(2)}, u32[]{:S(2)}) collective-permute-start(f32[64,256]{1,0:T(8,128)S(1)} %shard_map.109), channel_id=1, source_target_pairs={{0,8},{1,9},{226,234},{227,235},{4,12},{5,13},{230,238},{231,239},... | collective-permute-start | bytes 196616 | tf_op jit(solution)/shard_map/ppermute | solution.py:494
  54.4 7.6 %collective-permute-start.11 = (f32[64,256]{1,0:T(8,128)S(1)}, f32[64,256]{1,0:T(8,128)S(1)}, u32[]{:S(2)}, u32[]{:S(2)}) collective-permute-start(f32[64,256]{1,0:T(8,128)S(1)} %get-tuple-element.65.sent_ref), channel_id=1, source_target_pairs={{8,0},{9,1},{234,226},{235,227},{12,4},{13,5},{238,230},{239,231},... | collective-permute-start | bytes 196616 | tf_op jit(solution)/shard_map/ppermute | solution.py:494
  59.7 8.2 %collective-permute-start.12 = (f32[64,256]{1,0:T(8,128)S(1)}, f32[64,256]{1,0:T(8,128)S(1)}, u32[]{:S(2)}, u32[]{:S(2)}) collective-permute-start(f32[64,256]{1,0:T(8,128)S(1)} %shard_map.111), channel_id=1, source_target_pairs={{0,8},{1,9},{226,234},{227,235},{4,12},{5,13},{230,238},{231,239},... | collective-permute-start | bytes 196616 | tf_op jit(solution)/shard_map/ppermute | solution.py:494
  64.3 7.8 %collective-permute-start.13 = (f32[64,256]{1,0:T(8,128)S(1)}, f32[64,256]{1,0:T(8,128)S(1)}, u32[]{:S(2)}, u32[]{:S(2)}) collective-permute-start(f32[64,256]{1,0:T(8,128)S(1)} %get-tuple-element.68.sent_ref), channel_id=1, source_target_pairs={{8,0},{9,1},{234,226},{235,227},{12,4},{13,5},{238,230},{239,231},... | collective-permute-start | bytes 196616 | tf_op jit(solution)/shard_map/ppermute | solution.py:494
  69.6 8.3 %collective-permute-start.14 = (f32[64,256]{1,0:T(8,128)S(1)}, f32[64,256]{1,0:T(8,128)S(1)}, u32[]{:S(2)}, u32[]{:S(2)}) collective-permute-start(f32[64,256]{1,0:T(8,128)S(1)} %shard_map.113), channel_id=1, source_target_pairs={{0,8},{1,9},{226,234},{227,235},{4,12},{5,13},{230,238},{231,239},... | collective-permute-start | bytes 196616 | tf_op jit(solution)/shard_map/ppermute | solution.py:494
  74.4 6.2 %collective-permute-start.15 = (f32[64,256]{1,0:T(8,128)S(1)}, f32[64,256]{1,0:T(8,128)S(1)}, u32[]{:S(2)}, u32[]{:S(2)}) collective-permute-start(f32[64,256]{1,0:T(8,128)S(1)} %get-tuple-element.71), channel_id=1, source_target_pairs={{8,0},{9,1},{234,226},{235,227},{12,4},{13,5},{238,230},{239,231},... | collective-permute-start | bytes 196616 | tf_op jit(solution)/shard_map/ppermute | solution.py:494
  98.2 1.2 %collective-permute-start.16 = (f32[32,128]{1,0:T(8,128)S(1)}, f32[32,128]{1,0:T(8,128)S(1)}, u32[]{:S(2)}, u32[]{:S(2)}) collective-permute-start(f32[32,128]{1,0:T(8,128)S(1)} %bitcast.28), channel_id=1, source_target_pairs={{0,1},{1,0},{2,3},{3,2},{4,5},{5,4},{6,7},{7,6},{8,9},{9,8},{10,11... | collective-permute-start | bytes 49160 | tf_op jit(solution)/shard_map/ppermute | solution.py:498
  100.7 8.5 %collective-permute-start.18 = (f32[2,32,64]{2,1,0:T(8,128)S(1)}, f32[2,32,64]{2,1,0:T(8,128)S(1)}, u32[]{:S(2)}, u32[]{:S(2)}) collective-permute-start(f32[2,32,64]{2,1,0:T(8,128)S(1)} %get-tuple-element.73), channel_id=1, source_target_pairs={{0,1},{1,0},{226,3},{227,2},{4,5},{5,4},{230,7},{231,6},{8,9},{9,8... | collective-permute-start | bytes 49160 | tf_op jit(solution)/shard_map/ppermute | solution.py:518
  102.1 10.9 %collective-permute-start.17 = (f32[2,32,64]{2,1,0:T(8,128)S(1)}, f32[2,32,64]{2,1,0:T(8,128)S(1)}, u32[]{:S(2)}, u32[]{:S(2)}) collective-permute-start(f32[2,32,64]{2,1,0:T(8,128)S(1)} %get-tuple-element.72), channel_id=1, source_target_pairs={{0,0},{1,1},{226,2},{227,3},{4,4},{5,5},{230,6},{231,7},{8,8},{9,9... | collective-permute-start | bytes 49160 | tf_op jit(solution)/shard_map/ppermute | solution.py:518

commit v6 on v5

--- a/solution.py
+++ b/solution.py
@@ -190,8 +190,9 @@
     stiff_ref[...] = stiff
 
 
-def stencil_kernel(wx1, wy1, live1, ohs1, wx2, wy2, live2, ohs2, half_ref, f_ref):
+def stencil_kernel(down_ref, wx1, wy1, live1, ohs1, wx2, wy2, live2, ohs2, send_ref, keep_ref, f_ref):
     step = lax.axis_index("tile") & 1
+    send_ref[0] = down_ref[...]
     for h, (wx_ref, wy_ref, live_ref) in enumerate(((wx1, wy1, live1), (wx2, wy2, live2))):
 
         def body(blk, carry):
@@ -211,7 +212,9 @@
 
         lax.fori_loop(0, 4, body, 0)
     for kind in range(2):
-        half_ref[kind] = scatter(f_ref[kind], ohs1[256:512, :], ohs2[256:512, :])
+        both = scatter(f_ref[kind], ohs1[...], ohs2[...])
+        keep_ref[kind] = both[:, :256]
+        send_ref[kind + 1] = both[:, 256:]
 
 
 def gather(parts, hot1, hot2, out_ref):
@@ -229,19 +232,16 @@
 
 def up_kernel(v_ref, *refs):
     halves_of = (refs[:7], refs[7:14])
-    own_ref, down_ref, gap_ref, g_ref, h_ref, f_ref = refs[14:]
-    parts = split3(v_ref[...])
+    own_ref, down_ref, gap_ref, g_ref, f_ref = refs[14:]
     ohf1, ohs1 = refs[0], refs[1]
     ohf2, ohs2 = refs[7], refs[8]
-    gather(parts, ohf1[...], ohf2[...], g_ref)
-    gather(parts, ohs1[0:256, :], ohs2[0:256, :], h_ref)
+    gather(split3(v_ref[...]), ohf1[...], ohf2[...], g_ref)
     for h, (_, _, wx_ref, wy_ref, fx_ref, col_ref, live_ref) in enumerate(halves_of):
 
         def body(blk, carry):
             lanes = lanes_of(blk + 4 * h)
             got = sample_block(g_ref, lanes, wy_ref, fx_ref, col_ref, blk, 0)
-            less = sample_block(h_ref, lanes, wy_ref, fx_ref, col_ref, blk, 1)
-            gap = [(got[g] - less[g]) * live_ref[blk, 8 * g : 8 * g + 8, :] for g in range(4)]
+            gap = [got[g] * live_ref[blk, 8 * g : 8 * g + 8, :] for g in range(4)]
             for g in range(4):
                 gap_ref[blk + 4 * h, 8 * g : 8 * g + 8, :] = gap[g]
             tops = load_table(wy_ref, blk, 1)
@@ -249,7 +249,7 @@
             spread_block(tops, load_table(wx_ref, blk, 1), f_ref, lanes)
             return carry
 
-        lax.fori_loop(0, 4, body, 0)
+        lax.fori_loop(0, 4, body, 0, unroll=2)
     forces = scatter(f_ref[...], ohs1[...], ohs2[...])
     own_ref[...] = forces[:, :256]
     down_ref[...] = forces[:, 256:]
@@ -262,7 +262,9 @@
     out_ref, g_ref, f_ref = refs[14:]
     ohf1, ohs1 = refs[0], refs[1]
     ohf2, ohs2 = refs[7], refs[8]
-    gather(split3(raw_ref[...] - sent_ref[...]), ohs1[256:512, :], ohs2[256:512, :], g_ref)
+    v = v_ref[...]
+    parts = jnp.concatenate([split3(v), split3(raw_ref[...] - sent_ref[...])], 1)
+    gather(parts, ohs1[...], ohs2[...], g_ref)
     for h, (_, _, wx_ref, wy_ref, fx_ref, col_ref, live_ref) in enumerate(halves_of):
 
         def body(blk, carry):
@@ -277,9 +279,8 @@
             spread_block(tops, load_table(wx_ref, blk, 0), f_ref, lanes)
             return carry
 
-        lax.fori_loop(0, 4, body, 0)
+        lax.fori_loop(0, 4, body, 0, unroll=2)
     forces = scatter(f_ref[...], ohf1[...], ohf2[...])
-    v = v_ref[...]
     up = lambda x, d: pltpu.roll(x, 64 - d, 0)
     dn = lambda x, d: pltpu.roll(x, d, 0)
     node = lax.broadcasted_iota(jnp.int32, (64, 256), 0)
@@ -344,14 +345,12 @@
     return quick(q, rest[0] / y[0])
 
 
-def dots_kernel(*refs):
-    out_ref = refs[5]
-    fields = [r[...] for r in refs[:5]]
+def dots(fields, pairs):
     sub = lax.broadcasted_iota(jnp.int32, (16, 128), 0)
     lane = lax.broadcasted_iota(jnp.int32, (16, 128), 1)
     high = jnp.zeros((16, 128), F32)
     low = jnp.zeros((16, 128), F32)
-    for k, (i, j) in enumerate(PAIRS):
+    for i, j in pairs:
         acc = two_prod(fields[i], fields[j])
         acc = dd_add((acc[0][:, :128], acc[1][:, :128]), (acc[0][:, 128:], acc[1][:, 128:]))
         n = 64
@@ -361,19 +360,42 @@
         for d in (4, 2, 1):
             acc = dd_add(acc, (pltpu.roll(acc[0], d, 0), pltpu.roll(acc[1], d, 0)))
         wide = [jnp.concatenate([a, a], 0) for a in acc]
-        high = jnp.where(sub == k, wide[0], high)
-        low = jnp.where(sub == k, wide[1], low)
+        here = sub == PAIRS.index((i, j))
+        high = jnp.where(here, wide[0], high)
+        low = jnp.where(here, wide[1], low)
     acc = (high, low)
     for d in (64, 32, 16, 8, 4, 2, 1):
         acc = dd_add(acc, (pltpu.roll(acc[0], d, 1), pltpu.roll(acc[1], d, 1)))
     row = jnp.where(lane == sub, acc[0], 0.0) + jnp.where(lane == sub + 16, acc[1], 0.0)
-    out_ref[...] = jnp.sum(row, 0, keepdims=True)
-
-
-def finish_kernel(gram_ref, gram2_ref, v0, v1, v2, v3, v4, mine_ref, other_ref):
-    rows = jnp.concatenate([gram_ref[...], gram2_ref[...]], 0)
-    acc = (rows, pltpu.roll(rows, 112, 1))
-    n = 64
+    return jnp.sum(row, 0, keepdims=True)
+
+
+def dots_kernel(v0, v1, v2, v3, out_ref):
+    out_ref[...] = dots([r[...] for r in (v0, v1, v2, v3)], [p for p in PAIRS if p[1] < 4])
+
+
+def last_kernel(row_ref, v0, v1, v2, v3, v4, out_ref, slice_ref):
+    fields = [r[...] for r in (v0, v1, v2, v3, v4)]
+    y = lax.axis_index("tile") >> 1
+    for k in range(3):
+        sides = []
+        for m in (2 * k, 2 * k + 1):
+            if m < 5:
+                x = jnp.where(y >= 2, fields[m][:, 128:], fields[m][:, :128])
+                sides.append((x, pltpu.roll(x, 64, 1)))
+            else:
+                sides.append((jnp.zeros((64, 128), F32),) * 2)
+        left = jnp.where((y & 1) == 0, sides[0][0], sides[0][1])
+        right = jnp.where((y & 1) == 0, sides[1][1], sides[1][0])
+        lane = lax.broadcasted_iota(jnp.int32, (64, 128), 1)
+        slice_ref[k] = jnp.where(lane < 64, left, right)
+    out_ref[...] = row_ref[...] + dots(fields, [p for p in PAIRS if p[1] == 4])
+
+
+def finish_kernel(gram_ref, slice_ref, mine_ref, other_ref):
+    rows = gram_ref[...]
+    acc = dd_add((rows, pltpu.roll(rows, 112, 1)), (pltpu.roll(rows, 96, 1), pltpu.roll(rows, 80, 1)))
+    n = 32
     while n > 8:
         n //= 2
         acc = dd_add((acc[0][:n], acc[1][:n]), (acc[0][n:], acc[1][n:]))
@@ -431,21 +453,19 @@
             new = form(res, res)
             direc = axpy(dd_div(new, norm), direc, res)
             norm = new
-    fields = [r[...] for r in (v0, v1, v2, v3, v4)]
+    lane = lax.broadcasted_iota(jnp.int32, (64, 128), 1)
 
     def combine(coefs):
-        total = None
-        for c, f in zip(coefs, fields):
-            term = c[0][0:1, 0:1] * f
-            total = term if total is None else total + term
-        return total
-
-    tile = lax.axis_index("tile")
-    ids = lax.broadcasted_iota(jnp.int32, (64, 256), 1)
-    want = lax.broadcasted_iota(jnp.int32, (64, 256), 0)
-    swap = tile + 1 - 2 * (tile & 1)
-    want = jnp.where(want < 32, tile * 32 + want, swap * 32 + want - 32)
-    pick = jnp.where(ids == want, 1.0, 0.0).astype(jnp.bfloat16)
+        total = jnp.zeros((64, 128), F32)
+        flat = [c[0][0:1, 0:1] for c in coefs] + [jnp.zeros((1, 1), F32)] * (6 - len(coefs))
+        for k in range(3):
+            total = total + jnp.where(lane < 64, flat[2 * k], flat[2 * k + 1]) * slice_ref[k]
+        return total + pltpu.roll(total, 64, 1)
+
+    core = lax.axis_index("tile") & 1
+    want = lax.broadcasted_iota(jnp.int32, (64, 128), 0)
+    want = jnp.where(want < 32, want + 32 * core, want - 32 * core)
+    pick = jnp.where(lane == want, 1.0, 0.0).astype(jnp.bfloat16)
     for k, coefs in enumerate((sol, res)):
         parts = lax.dot_general(pick, split3(combine(coefs)), NT, preferred_element_type=F32)
         both = parts[:, :64] + (parts[:, 64:128] + parts[:, 128:192])
@@ -509,12 +529,12 @@
     return lax.ppermute(block, ("sec", "tile"), route)
 
 
-def returned(block, flip):
+def returned(block):
     sections = lax.axis_size("sec")
     route = []
     for section in range(sections):
         for tile in range(2 * CHIPS):
-            route.append((seat(section, tile // 2, sections) * 8 + tile, section * 8 + (tile ^ flip)))
+            route.append((seat(section, tile // 2, sections) * 8 + tile, section * 8 + tile))
     return lax.ppermute(block, ("sec", "tile"), route)
 
 
@@ -571,14 +591,13 @@
         other[0], other[1], other[2], other[3], *one[7:]
     )
     own, down, stiff = two[7:]
-    above = shifted(down, -1)
+    send, keep = call(
+        stencil_kernel, [((3, 64, 256), F32), ((2, 64, 256), F32)], 9, [pltpu.VMEM((2, 64, 1024), F32)], us=4.0
+    )(down, one[0], one[1], one[4], one[6], two[0], two[1], two[4], two[6])
+    above = shifted(send, -1)
     raw = shifted(own, 1)
-    half = call(stencil_kernel, [((2, 64, 256), F32)], 8, [pltpu.VMEM((2, 64, 1024), F32)], us=4.0)(
-        one[0], one[1], one[4], one[6], two[0], two[1], two[4], two[6]
-    )[0]
-    fields = [own - above]
-    half, fields[0] = lax.optimization_barrier((half, fields[0]))
-    mine = shifted(half, -1)
+    fields = [own - above[0]]
+    mine = keep + above[1:]
     other = swapped(mine)
     tables = []
     for wx, wy, fx, col, live, ohf, ohs in (one[:7], two[:7]):
@@ -587,7 +606,7 @@
     for k in range(ITERS):
         v = fields[-1]
         sent = down
-        part, down, gap = call(up_kernel, [field, field, ((8, 32, 128), F32)], 15, [wide, wide, wide])(v, *tables)
+        part, down, gap = call(up_kernel, [field, field, ((8, 32, 128), F32)], 15, [wide, wide])(v, *tables)
         above = shifted(down, -1)
         partial = call(functools.partial(down_kernel, back=k > 0), [field], 23, [wide, wide])(
             v, raw, sent, fields[max(k - 1, 0)], part, gap, mine, other, stiff, *tables
@@ -595,13 +614,13 @@
         if k < ITERS - 1:
             raw = shifted(partial, 1)
         fields.append(partial - above)
-    gram = call(dots_kernel, [((1, 128), F32)], 5)(*fields)[0]
-    gram = lax.all_to_all(jnp.broadcast_to(gram, (32, 128)), "sec", 0, 0, tiled=True)
-    mine, other = call(
-        finish_kernel, [((2, 32, 64), F32), ((2, 32, 64), F32)], 7
-    )(gram, swapped(gram), *fields)
-    other = returned(other, 1)
-    mine = returned(mine, 0)
+    row = call(dots_kernel, [((1, 128), F32)], 4, us=1.0)(*fields[:4])[0]
+    row, slices = call(last_kernel, [((1, 128), F32), ((3, 64, 128), F32)], 6, us=1.0)(row, *fields)
+    slices = returned(slices)
+    row = row + jnp.roll(swapped(row), 32, 1)
+    gram = lax.all_to_all(jnp.broadcast_to(row, (32, 128)), "sec", 0, 0, tiled=True)
+    mine, other = call(finish_kernel, [((2, 32, 64), F32), ((2, 32, 64), F32)], 2)(gram, slices)
+    other = swapped(other)
     first = jnp.where(core == 0, mine, other)
     last = jnp.where(core == 0, other, mine)
     out = jnp.concatenate([first, last], 2)[:, :, None, :]

time: 114 us -> 108 us (0.947)
  the two profiles are of different devices: /device:TPU:40 before, /device:TPU:25 now
where the time goes in v6:
time: 108 us; the launch traced here: 107 us
  starting transfers between devices  51.7 us (48%)
  Pallas kernels  25.6 us (24%)
  blocking collectives  14.8 us (14%)
  waiting for transfers between devices  13.3 us (12%)
    ppermute x9, starting transfers between devices, shifted(): return lax.ppermute(block, ('sec', 'tile'), route)  23.8 us
    all_to_all x1, blocking collectives, on_device(): lax.all_to_all(jnp.broadcast_to(row, (32, 128)), 'sec', 0, 0, tiled=True)  14.8 us
    ppermute x4, starting transfers between devices, dealt(): return lax.ppermute(block, ('sec', 'tile'), route)  14.2 us
    ppermute x4, waiting for transfers between devices, dealt(): return lax.ppermute(block, ('sec', 'tile'), route)  9.78 us
    pallas_call x4, Pallas kernels, on_device(): call(up_kernel, [field, field, ((8, 32, 128), F32)], 15, [wide, wide])  7.46 us
    pallas_call x4, Pallas kernels, on_device(): call(functools.partial(down_kernel, back=k > 0), [field], 23, [wide, wide])  7.39 us
    ppermute x4, starting transfers between devices, swapped(): return lax.ppermute(block, 'tile', [(i, i ^ 1) for i in range(8)])  7.26 us
    ppermute x1, starting transfers between devices, returned(): return lax.ppermute(block, ('sec', 'tile'), route)  6.5 us
  transfers between devices with their start and end apart: 18, of which 5 were waited for; matrix products, arithmetic and copies ran while one was open for 0% of the time, Pallas kernels for 16%

profile of v6, /device:TPU:25, one launch (start us, length us, event | category | flops | bytes accessed | tf_op | source)
XLA Modules:
  0.0 107.4 jit_solution(1455725554885862378)
XLA Ops:
  2.3 7.5 %collective-permute-start.3 = (f32[264,128]{1,0:T(8,128)}, f32[264,128]{1,0:T(8,128)S(1)}, u32[]{:S(2)}, u32[]{:S(2)}) collective-permute-start(f32[264,128]{1,0:T(8,128)} %shard_map.104), channel_id=1, source_target_pairs={{0,0},{1,1},{2,226},{3,227},{4,4},{5,5},{6,230},{7,231},{8,8},{9,9... | collective-permute-start | bytes 405512 | tf_op jit(solution)/shard_map/ppermute | solution.py:529
  9.9 2.4 %collective-permute-start.1 = (f32[264,128]{1,0:T(8,128)}, f32[264,128]{1,0:T(8,128)S(1)}, u32[]{:S(2)}, u32[]{:S(2)}) collective-permute-start(f32[264,128]{1,0:T(8,128)} %shard_map.104), channel_id=1, source_target_pairs={{0,226},{1,227},{2,4},{3,5},{4,230},{5,231},{6,0},{7,1},{8,234},{9... | collective-permute-start | bytes 405512 | tf_op jit(solution)/shard_map/ppermute | solution.py:529
  12.3 4.2 %collective-permute-start = (f32[264,128]{1,0:T(8,128)}, f32[264,128]{1,0:T(8,128)S(1)}, u32[]{:S(2)}, u32[]{:S(2)}) collective-permute-start(f32[264,128]{1,0:T(8,128)} %shard_map.104), channel_id=1, source_target_pairs={{0,4},{1,5},{2,230},{3,231},{4,0},{5,1},{6,226},{7,227},{8,12},{9,... | collective-permute-start | bytes 405512 | tf_op jit(solution)/shard_map/ppermute | solution.py:529
  16.5 2.2 %collective-permute-done.3.refs_3_ = f32[264,128]{1,0:T(8,128)S(1)} collective-permute-done((f32[264,128]{1,0:T(8,128)}, f32[264,128]{1,0:T(8,128)S(1)}, u32[]{:S(2)}, u32[]{:S(2)}) %collective-permute-start.3) | collective-permute-done | bytes 135200 | tf_op jit(solution)/shard_map/ppermute | solution.py:529
  19.4 6.9 %collective-permute-done.1.refs_1_ = f32[264,128]{1,0:T(8,128)S(1)} collective-permute-done((f32[264,128]{1,0:T(8,128)}, f32[264,128]{1,0:T(8,128)S(1)}, u32[]{:S(2)}, u32[]{:S(2)}) %collective-permute-start.1) | collective-permute-done | bytes 135200 | tf_op jit(solution)/shard_map/ppermute | solution.py:529
  26.4 2.6 %collective-permute-start.4 = (f32[4,264,128]{2,1,0:T(8,128)S(1)}, f32[4,264,128]{2,1,0:T(8,128)S(1)}, u32[]{:S(2)}, u32[]{:S(2)}) collective-permute-start(f32[4,264,128]{2,1,0:T(8,128)S(1)} %pad_maximum_fusion), channel_id=1, source_target_pairs={{0,1},{1,0},{2,3},{3,2},{4,5},{5,4},{6,7},{7,6},{8,9},{9,8},{10,11... | collective-permute-start | bytes 1622024 | tf_op jit(solution)/shard_map/ppermute | solution.py:518
  32.2 2.6 %shard_map.107 = (f32[3,64,256]{2,1,0:T(8,128)S(1)}, f32[2,64,256]{2,1,0:T(8,128)S(1)}) custom-call(f32[64,256]{1,0:T(8,128)S(1)} %get-tuple-element.44.down_ref.sent_ref, f32[4,2,8,32,128]{4,3,2,1,0:T(8,128)S(1)} %get-tuple-element.45.wx1.refs_2_, f32[4,2,8,32,128]{4,3,2,1,0:T(8,128)S(1)} %get-tuple-element.46.wy1.refs_3_, ...), custom_call_target="tpu_custom_call" | custom-call | flops 4000000000 | bytes 262144 | tf_op jit(solution)/shard_map/pallas_call | solution.py:594
  34.8 1.9 %collective-permute-start.5 = (f32[3,64,256]{2,1,0:T(8,128)S(1)}, f32[3,64,256]{2,1,0:T(8,128)S(1)}, u32[]{:S(2)}, u32[]{:S(2)}) collective-permute-start(f32[3,64,256]{2,1,0:T(8,128)S(1)} %get-tuple-element.53), channel_id=1, source_target_pairs={{8,0},{9,1},{234,226},{235,227},{12,4},{13,5},{238,230},{239,231},... | collective-permute-start | bytes 589832 | tf_op jit(solution)/shard_map/ppermute | solution.py:514
  38.0 2.6 %collective-permute-done.5 = f32[3,64,256]{2,1,0:T(8,128)S(1)} collective-permute-done((f32[3,64,256]{2,1,0:T(8,128)S(1)}, f32[3,64,256]{2,1,0:T(8,128)S(1)}, u32[]{:S(2)}, u32[]{:S(2)}) %collective-permute-start.5) | collective-permute-done | bytes 196640 | tf_op jit(solution)/shard_map/ppermute | solution.py:514
  41.9 1.9 %shard_map.108 = (f32[64,256]{1,0:T(8,128)S(1)}, f32[64,256]{1,0:T(8,128)S(1)}, f32[8,32,128]{2,1,0:T(8,128)S(1)}) custom-call(f32[64,256]{1,0:T(8,128)S(1)} %fusion.v_ref.prev_ref.v0, bf16[256,512]{1,0:T(8,128)(2,1)S(1)} %get-tuple-element.54.refs_0_, bf16[512,512]{1,0:T(8,128)(2,1)S(1)} %get-tuple-element.48.ohs1.refs_1_, ...), custom_call_target="tpu_custom_call" | custom-call | flops 2000000000 | bytes 262144 | tf_op jit(solution)/shard_map/pallas_call | solution.py:609
  43.8 4.1 %collective-permute-start.8 = (f32[64,256]{1,0:T(8,128)S(1)}, f32[64,256]{1,0:T(8,128)S(1)}, u32[]{:S(2)}, u32[]{:S(2)}) collective-permute-start(f32[64,256]{1,0:T(8,128)S(1)} %get-tuple-element.64.sent_ref), channel_id=1, source_target_pairs={{8,0},{9,1},{234,226},{235,227},{12,4},{13,5},{238,230},{239,231},... | collective-permute-start | bytes 196616 | tf_op jit(solution)/shard_map/ppermute | solution.py:514
  47.9 1.8 %shard_map.109 = f32[64,256]{1,0:T(8,128)S(1)} custom-call(f32[64,256]{1,0:T(8,128)S(1)} %fusion.v_ref.prev_ref.v0, f32[64,256]{1,0:T(8,128)S(1)} %collective-permute-done.6.raw_ref, f32[64,256]{1,0:T(8,128)S(1)} %get-tuple-element.44.down_ref.sent_ref, f32[64,256]{1,0:T(8,128)S(1)} %fusion.v_ref.prev_ref.v0, f32[64,256]{1,0:T(8,128)S(1)} %get-tuple-element.60.part_ref, ...), custom_call_target="tpu_custom_call" | custom-call | flops 2000000000 | bytes 262144 | tf_op jit(solution)/shard_map/pallas_call | solution.py:611
  51.1 1.9 %shard_map.110 = (f32[64,256]{1,0:T(8,128)S(1)}, f32[64,256]{1,0:T(8,128)S(1)}, f32[8,32,128]{2,1,0:T(8,128)S(1)}) custom-call(f32[64,256]{1,0:T(8,128)S(1)} %sub.16.v_ref.prev_ref.v1, bf16[256,512]{1,0:T(8,128)(2,1)S(1)} %get-tuple-element.54.refs_0_, bf16[512,512]{1,0:T(8,128)(2,1)S(1)} %get-tuple-element.48.ohs1.refs_1_, ...), custom_call_target="tpu_custom_call" | custom-call | flops 2000000000 | bytes 262144 | tf_op jit(solution)/shard_map/pallas_call | solution.py:609
  53.0 4.0 %collective-permute-start.10 = (f32[64,256]{1,0:T(8,128)S(1)}, f32[64,256]{1,0:T(8,128)S(1)}, u32[]{:S(2)}, u32[]{:S(2)}) collective-permute-start(f32[64,256]{1,0:T(8,128)S(1)} %get-tuple-element.67.sent_ref), channel_id=1, source_target_pairs={{8,0},{9,1},{234,226},{235,227},{12,4},{13,5},{238,230},{239,231},... | collective-permute-start | bytes 196616 | tf_op jit(solution)/shard_map/ppermute | solution.py:514
  57.0 1.8 %shard_map.111 = f32[64,256]{1,0:T(8,128)S(1)} custom-call(f32[64,256]{1,0:T(8,128)S(1)} %sub.16.v_ref.prev_ref.v1, f32[64,256]{1,0:T(8,128)S(1)} %collective-permute-done.9.raw_ref, f32[64,256]{1,0:T(8,128)S(1)} %get-tuple-element.64.sent_ref, f32[64,256]{1,0:T(8,128)S(1)} %fusion.v_ref.prev_ref.v0, f32[64,256]{1,0:T(8,128)S(1)} %get-tuple-element.65.part_ref, ...), custom_call_target="tpu_custom_call" | custom-call | flops 2000000000 | bytes 262144 | tf_op jit(solution)/shard_map/pallas_call | solution.py:611
  60.4 1.9 %shard_map.112 = (f32[64,256]{1,0:T(8,128)S(1)}, f32[64,256]{1,0:T(8,128)S(1)}, f32[8,32,128]{2,1,0:T(8,128)S(1)}) custom-call(f32[64,256]{1,0:T(8,128)S(1)} %sub.17.v_ref.v2.prev_ref, bf16[256,512]{1,0:T(8,128)(2,1)S(1)} %get-tuple-element.54.refs_0_, bf16[512,512]{1,0:T(8,128)(2,1)S(1)} %get-tuple-element.48.ohs1.refs_1_, ...), custom_call_target="tpu_custom_call" | custom-call | flops 2000000000 | bytes 262144 | tf_op jit(solution)/shard_map/pallas_call | solution.py:609
  62.2 4.4 %collective-permute-start.12 = (f32[64,256]{1,0:T(8,128)S(1)}, f32[64,256]{1,0:T(8,128)S(1)}, u32[]{:S(2)}, u32[]{:S(2)}) collective-permute-start(f32[64,256]{1,0:T(8,128)S(1)} %get-tuple-element.70.sent_ref), channel_id=1, source_target_pairs={{8,0},{9,1},{234,226},{235,227},{12,4},{13,5},{238,230},{239,231},... | collective-permute-start | bytes 196616 | tf_op jit(solution)/shard_map/ppermute | solution.py:514
  66.7 1.8 %shard_map.113 = f32[64,256]{1,0:T(8,128)S(1)} custom-call(f32[64,256]{1,0:T(8,128)S(1)} %sub.17.v_ref.v2.prev_ref, f32[64,256]{1,0:T(8,128)S(1)} %collective-permute-done.11.raw_ref, f32[64,256]{1,0:T(8,128)S(1)} %get-tuple-element.67.sent_ref, f32[64,256]{1,0:T(8,128)S(1)} %sub.16.v_ref.prev_ref.v1, f32[64,256]{1,0:T(8,128)S(1)} %get-tuple-element.68.part_ref, ...), custom_call_target="tpu_custom_call" | custom-call | flops 2000000000 | bytes 262144 | tf_op jit(solution)/shard_map/pallas_call | solution.py:611
  69.8 1.9 %shard_map.115 = (f32[64,256]{1,0:T(8,128)S(1)}, f32[64,256]{1,0:T(8,128)S(1)}, f32[8,32,128]{2,1,0:T(8,128)S(1)}) custom-call(f32[64,256]{1,0:T(8,128)S(1)} %sub.18.v3.v_ref, bf16[256,512]{1,0:T(8,128)(2,1)S(1)} %get-tuple-element.54.refs_0_, bf16[512,512]{1,0:T(8,128)(2,1)S(1)} %get-tuple-element.48.ohs1.refs_1_, ...), custom_call_target="tpu_custom_call" | custom-call | flops 2000000000 | bytes 262144 | tf_op jit(solution)/shard_map/pallas_call | solution.py:609
  71.7 4.0 %collective-permute-start.14 = (f32[64,256]{1,0:T(8,128)S(1)}, f32[64,256]{1,0:T(8,128)S(1)}, u32[]{:S(2)}, u32[]{:S(2)}) collective-permute-start(f32[64,256]{1,0:T(8,128)S(1)} %get-tuple-element.73), channel_id=1, source_target_pairs={{8,0},{9,1},{234,226},{235,227},{12,4},{13,5},{238,230},{239,231},... | collective-permute-start | bytes 196616 | tf_op jit(solution)/shard_map/ppermute | solution.py:514
  76.8 1.8 %shard_map.116 = f32[64,256]{1,0:T(8,128)S(1)} custom-call(f32[64,256]{1,0:T(8,128)S(1)} %sub.18.v3.v_ref, f32[64,256]{1,0:T(8,128)S(1)} %collective-permute-done.13.raw_ref, f32[64,256]{1,0:T(8,128)S(1)} %get-tuple-element.70.sent_ref, f32[64,256]{1,0:T(8,128)S(1)} %sub.17.v_ref.v2.prev_ref, f32[64,256]{1,0:T(8,128)S(1)} %get-tuple-element.71.part_ref, ...), custom_call_target="tpu_custom_call" | custom-call | flops 2000000000 | bytes 262144 | tf_op jit(solution)/shard_map/pallas_call | solution.py:611
  81.2 6.5 %collective-permute-start.16 = (f32[3,64,128]{2,1,0:T(8,128)S(1)}, f32[3,64,128]{2,1,0:T(8,128)S(1)}, u32[]{:S(2)}, u32[]{:S(2)}) collective-permute-start(f32[3,64,128]{2,1,0:T(8,128)S(1)} %get-tuple-element.75), channel_id=1, source_target_pairs={{0,0},{1,1},{226,2},{227,3},{4,4},{5,5},{230,6},{231,7},{8,8},{9,9... | collective-permute-start | bytes 294920 | tf_op jit(solution)/shard_map/ppermute | solution.py:538
  87.8 14.8 %all_to_all.8 = f32[32,1,128]{2,1,0:T(1,128)S(1)} all-to-all(f32[32,1,128]{2,1,0:T(1,128)S(1)} %broadcast_in_dim.2), channel_id=1, replica_groups=mesh['sec'=32,'tile'=8] {'sec'}, dimensions={0} | all-to-all | bytes 32768 | tf_op jit(solution)/shard_map/all_to_all | solution.py:621
  104.0 1.8 %collective-permute-start.17 = (f32[2,32,64]{2,1,0:T(8,128)S(1)}, f32[2,32,64]{2,1,0:T(8,128)S(1)}, u32[]{:S(2)}, u32[]{:S(2)}) collective-permute-start(f32[2,32,64]{2,1,0:T(8,128)S(1)} %get-tuple-element.77), channel_id=1, source_target_pairs={{0,1},{1,0},{2,3},{3,2},{4,5},{5,4},{6,7},{7,6},{8,9},{9,8},{10,11... | collective-permute-start | bytes 49160 | tf_op jit(solution)/shard_map/ppermute | solution.py:518
  (41 shorter events, 19.0 us)
Async XLA Ops:
  2.3 16.4 %collective-permute-start.3 = (f32[264,128]{1,0:T(8,128)}, f32[264,128]{1,0:T(8,128)S(1)}, u32[]{:S(2)}, u32[]{:S(2)}) collective-permute-start(f32[264,128]{1,0:T(8,128)} %shard_map.104), channel_id=1, source_target_pairs={{0,0},{1,1},{2,226},{3,227},{4,4},{5,5},{6,230},{7,231},{8,8},{9,9... | collective-permute-start | bytes 405512 | tf_op jit(solution)/shard_map/ppermute | solution.py:529
  9.8 9.6 %collective-permute-start.2 = (f32[264,128]{1,0:T(8,128)}, f32[264,128]{1,0:T(8,128)S(1)}, u32[]{:S(2)}, u32[]{:S(2)}) collective-permute-start(f32[264,128]{1,0:T(8,128)} %shard_map.104), channel_id=1, source_target_pairs={{0,230},{1,231},{2,0},{3,1},{4,226},{5,227},{6,4},{7,5},{8,238},{9... | collective-permute-start | bytes 405512 | tf_op jit(solution)/shard_map/ppermute | solution.py:529
  9.9 16.4 %collective-permute-start.1 = (f32[264,128]{1,0:T(8,128)}, f32[264,128]{1,0:T(8,128)S(1)}, u32[]{:S(2)}, u32[]{:S(2)}) collective-permute-start(f32[264,128]{1,0:T(8,128)} %shard_map.104), channel_id=1, source_target_pairs={{0,226},{1,227},{2,4},{3,5},{4,230},{5,231},{6,0},{7,1},{8,234},{9... | collective-permute-start | bytes 405512 | tf_op jit(solution)/shard_map/ppermute | solution.py:529
  12.3 14.0 %collective-permute-start = (f32[264,128]{1,0:T(8,128)}, f32[264,128]{1,0:T(8,128)S(1)}, u32[]{:S(2)}, u32[]{:S(2)}) collective-permute-start(f32[264,128]{1,0:T(8,128)} %shard_map.104), channel_id=1, source_target_pairs={{0,4},{1,5},{2,230},{3,231},{4,0},{5,1},{6,226},{7,227},{8,12},{9,... | collective-permute-start | bytes 405512 | tf_op jit(solution)/shard_map/ppermute | solution.py:529
  26.4 4.1 %collective-permute-start.4 = (f32[4,264,128]{2,1,0:T(8,128)S(1)}, f32[4,264,128]{2,1,0:T(8,128)S(1)}, u32[]{:S(2)}, u32[]{:S(2)}) collective-permute-start(f32[4,264,128]{2,1,0:T(8,128)S(1)} %pad_maximum_fusion), channel_id=1, source_target_pairs={{0,1},{1,0},{2,3},{3,2},{4,5},{5,4},{6,7},{7,6},{8,9},{9,8},{10,11... | collective-permute-start | bytes 1622024 | tf_op jit(solution)/shard_map/ppermute | solution.py:518
  34.8 5.9 %collective-permute-start.5 = (f32[3,64,256]{2,1,0:T(8,128)S(1)}, f32[3,64,256]{2,1,0:T(8,128)S(1)}, u32[]{:S(2)}, u32[]{:S(2)}) collective-permute-start(f32[3,64,256]{2,1,0:T(8,128)S(1)} %get-tuple-element.53), channel_id=1, source_target_pairs={{8,0},{9,1},{234,226},{235,227},{12,4},{13,5},{238,230},{239,231},... | collective-permute-start | bytes 589832 | tf_op jit(solution)/shard_map/ppermute | solution.py:514
  36.7 11.2 %collective-permute-start.6 = (f32[64,256]{1,0:T(8,128)S(1)}, f32[64,256]{1,0:T(8,128)S(1)}, u32[]{:S(2)}, u32[]{:S(2)}) collective-permute-start(f32[64,256]{1,0:T(8,128)S(1)} %get-tuple-element.43), channel_id=1, source_target_pairs={{0,8},{1,9},{226,234},{227,235},{4,12},{5,13},{230,238},{231,239},... | collective-permute-start | bytes 196616 | tf_op jit(solution)/shard_map/ppermute | solution.py:514
  40.7 7.3 %collective-permute-start.7 = (f32[2,64,256]{2,1,0:T(8,128)S(1)}, f32[2,64,256]{2,1,0:T(8,128)S(1)}, u32[]{:S(2)}, u32[]{:S(2)}) collective-permute-start(f32[2,64,256]{2,1,0:T(8,128)S(1)} %slice_add_fusion.mine_ref), channel_id=1, source_target_pairs={{0,1},{1,0},{2,3},{3,2},{4,5},{5,4},{6,7},{7,6},{8,9},{9,8},{10,11... | collective-permute-start | bytes 393224 | tf_op jit(solution)/shard_map/ppermute | solution.py:518
  43.8 7.3 %collective-permute-start.8 = (f32[64,256]{1,0:T(8,128)S(1)}, f32[64,256]{1,0:T(8,128)S(1)}, u32[]{:S(2)}, u32[]{:S(2)}) collective-permute-start(f32[64,256]{1,0:T(8,128)S(1)} %get-tuple-element.64.sent_ref), channel_id=1, source_target_pairs={{8,0},{9,1},{234,226},{235,227},{12,4},{13,5},{238,230},{239,231},... | collective-permute-start | bytes 196616 | tf_op jit(solution)/shard_map/ppermute | solution.py:514
  49.8 7.2 %collective-permute-start.9 = (f32[64,256]{1,0:T(8,128)S(1)}, f32[64,256]{1,0:T(8,128)S(1)}, u32[]{:S(2)}, u32[]{:S(2)}) collective-permute-start(f32[64,256]{1,0:T(8,128)S(1)} %shard_map.109), channel_id=1, source_target_pairs={{0,8},{1,9},{226,234},{227,235},{4,12},{5,13},{230,238},{231,239},... | collective-permute-start | bytes 196616 | tf_op jit(solution)/shard_map/ppermute | solution.py:514
  53.0 7.3 %collective-permute-start.10 = (f32[64,256]{1,0:T(8,128)S(1)}, f32[64,256]{1,0:T(8,128)S(1)}, u32[]{:S(2)}, u32[]{:S(2)}) collective-permute-start(f32[64,256]{1,0:T(8,128)S(1)} %get-tuple-element.67.sent_ref), channel_id=1, source_target_pairs={{8,0},{9,1},{234,226},{235,227},{12,4},{13,5},{238,230},{239,231},... | collective-permute-start | bytes 196616 | tf_op jit(solution)/shard_map/ppermute | solution.py:514
  58.8 7.8 %collective-permute-start.11 = (f32[64,256]{1,0:T(8,128)S(1)}, f32[64,256]{1,0:T(8,128)S(1)}, u32[]{:S(2)}, u32[]{:S(2)}) collective-permute-start(f32[64,256]{1,0:T(8,128)S(1)} %shard_map.111), channel_id=1, source_target_pairs={{0,8},{1,9},{226,234},{227,235},{4,12},{5,13},{230,238},{231,239},... | collective-permute-start | bytes 196616 | tf_op jit(solution)/shard_map/ppermute | solution.py:514
  62.2 7.6 %collective-permute-start.12 = (f32[64,256]{1,0:T(8,128)S(1)}, f32[64,256]{1,0:T(8,128)S(1)}, u32[]{:S(2)}, u32[]{:S(2)}) collective-permute-start(f32[64,256]{1,0:T(8,128)S(1)} %get-tuple-element.70.sent_ref), channel_id=1, source_target_pairs={{8,0},{9,1},{234,226},{235,227},{12,4},{13,5},{238,230},{239,231},... | collective-permute-start | bytes 196616 | tf_op jit(solution)/shard_map/ppermute | solution.py:514
  68.5 8.3 %collective-permute-start.13 = (f32[64,256]{1,0:T(8,128)S(1)}, f32[64,256]{1,0:T(8,128)S(1)}, u32[]{:S(2)}, u32[]{:S(2)}) collective-permute-start(f32[64,256]{1,0:T(8,128)S(1)} %shard_map.113), channel_id=1, source_target_pairs={{0,8},{1,9},{226,234},{227,235},{4,12},{5,13},{230,238},{231,239},... | collective-permute-start | bytes 196616 | tf_op jit(solution)/shard_map/ppermute | solution.py:514
  71.7 7.0 %collective-permute-start.14 = (f32[64,256]{1,0:T(8,128)S(1)}, f32[64,256]{1,0:T(8,128)S(1)}, u32[]{:S(2)}, u32[]{:S(2)}) collective-permute-start(f32[64,256]{1,0:T(8,128)S(1)} %get-tuple-element.73), channel_id=1, source_target_pairs={{8,0},{9,1},{234,226},{235,227},{12,4},{13,5},{238,230},{239,231},... | collective-permute-start | bytes 196616 | tf_op jit(solution)/shard_map/ppermute | solution.py:514
  79.5 8.2 %collective-permute-start.15 = (f32[1,128]{1,0:T(1,128)S(1)}, f32[1,128]{1,0:T(1,128)S(1)}, u32[]{:S(2)}, u32[]{:S(2)}) collective-permute-start(f32[1,128]{1,0:T(1,128)S(1)} %get-tuple-element.74), channel_id=1, source_target_pairs={{0,1},{1,0},{2,3},{3,2},{4,5},{5,4},{6,7},{7,6},{8,9},{9,8},{10,11... | collective-permute-start | bytes 1544 | tf_op jit(solution)/shard_map/ppermute | solution.py:518
  81.2 21.5 %collective-permute-start.16 = (f32[3,64,128]{2,1,0:T(8,128)S(1)}, f32[3,64,128]{2,1,0:T(8,128)S(1)}, u32[]{:S(2)}, u32[]{:S(2)}) collective-permute-start(f32[3,64,128]{2,1,0:T(8,128)S(1)} %get-tuple-element.75), channel_id=1, source_target_pairs={{0,0},{1,1},{226,2},{227,3},{4,4},{5,5},{230,6},{231,7},{8,8},{9,9... | collective-permute-start | bytes 294920 | tf_op jit(solution)/shard_map/ppermute | solution.py:538
  104.0 2.7 %collective-permute-start.17 = (f32[2,32,64]{2,1,0:T(8,128)S(1)}, f32[2,32,64]{2,1,0:T(8,128)S(1)}, u32[]{:S(2)}, u32[]{:S(2)}) collective-permute-start(f32[2,32,64]{2,1,0:T(8,128)S(1)} %get-tuple-element.77), channel_id=1, source_target_pairs={{0,1},{1,0},{2,3},{3,2},{4,5},{5,4},{6,7},{7,6},{8,9},{9,8},{10,11... | collective-permute-start | bytes 49160 | tf_op jit(solution)/shard_map/ppermute | solution.py:518

commit v7 on v6

--- a/solution.py
+++ b/solution.py
@@ -54,7 +54,8 @@
     )
 
 
-def spread_block(tops, sides, out_ref, lanes, lead=()):
+def spread_rows(tops, sides):
+    rows = []
     for q in range(8):
         parts = []
         for p in range(8):
@@ -62,10 +63,11 @@
             for group in range(1, 4):
                 acc = acc + tops[q][group] * sides[p][group]
             parts.append(acc)
-        out_ref[lead + (slice(8 * q, 8 * q + 8), lanes)] = fold_rows(parts)
-
-
-def sample_block(rows_ref, lanes, wy_ref, fx_ref, col_ref, blk, side):
+        rows.append(fold_rows(parts))
+    return jnp.concatenate(rows, 0)
+
+
+def sample_block(rows, wy_ref, fx_ref, col_ref, blk, side):
     out = []
     for group in range(4):
         ms = slice(8 * group, 8 * group + 8)
@@ -74,7 +76,7 @@
         fx = fx_ref[blk, side, ms, :]
         acc = None
         for q in range(8):
-            row = rows_ref[8 * q : 8 * q + 8, lanes]
+            row = rows[8 * q : 8 * q + 8]
             left = jnp.take_along_axis(row, col, axis=0, mode="promise_in_bounds")
             right = jnp.take_along_axis(row, nxt, axis=0, mode="promise_in_bounds")
             term = wy_ref[blk, side, q, ms, :] * (left + fx * (right - left))
@@ -133,8 +135,9 @@
     if add:
         before_own, before_down, before_stiff = refs[:3]
         refs = refs[3:]
-    wx_ref, wy_ref, fx_ref, col_ref, live_ref, ohf_ref, ohs_ref, own_ref, down_ref, stiff_ref, f_ref = refs
+    wx_ref, wy_ref, fx_ref, col_ref, live_ref, ohf_ref, ohs_ref, own_ref, down_ref, stiff_ref = refs
     comp = lax.axis_index("tile") & 1
+    columns = [[], []]
     for blk, data_ref in enumerate(datas):
         lanes = slice(128 * blk, 128 * blk + 128)
         count = data_ref[258, :][None, :]
@@ -173,9 +176,10 @@
                     )
             tops = load_table(wy_ref, blk, side)
             tops = [[tops[q][g] * goal[g] for g in range(4)] for q in range(8)]
-            spread_block(tops, load_table(wx_ref, blk, side), f_ref, lanes, (side,))
-    at_first = merge3(lax.dot_general(split3(f_ref[0]), ohf_ref[...], NT, preferred_element_type=F32))
-    at_second = merge3(lax.dot_general(split3(f_ref[1]), ohs_ref[...], NT, preferred_element_type=F32))
+            columns[side].append(spread_rows(tops, load_table(wx_ref, blk, side)))
+    spreads = [jnp.concatenate(c, 1) for c in columns]
+    at_first = merge3(lax.dot_general(split3(spreads[0]), ohf_ref[...], NT, preferred_element_type=F32))
+    at_second = merge3(lax.dot_general(split3(spreads[1]), ohs_ref[...], NT, preferred_element_type=F32))
     own = at_first - at_second[:, :256]
     down = at_second[:, 256:]
     stiff = jnp.concatenate(
@@ -190,36 +194,27 @@
     stiff_ref[...] = stiff
 
 
-def stencil_kernel(down_ref, wx1, wy1, live1, ohs1, wx2, wy2, live2, ohs2, send_ref, keep_ref, f_ref):
+def stencil_kernel(down_ref, wx1, wy1, live1, ohs1, wx2, wy2, live2, ohs2, send_ref, keep_ref):
     step = lax.axis_index("tile") & 1
     send_ref[0] = down_ref[...]
-    for h, (wx_ref, wy_ref, live_ref) in enumerate(((wx1, wy1, live1), (wx2, wy2, live2))):
-
-        def body(blk, carry):
-            lanes = lanes_of(blk + 4 * h)
+    zero = [jnp.zeros((8, 128), F32)] * 4
+    columns = [[], []]
+    for wx_ref, wy_ref, live_ref in ((wx1, wy1, live1), (wx2, wy2, live2)):
+        for blk in range(4):
             live = [live_ref[blk, 8 * g : 8 * g + 8, :] for g in range(4)]
-            zero = [jnp.zeros((8, 128), F32)] * 4
             wy = load_table(wy_ref, blk, 1) + [zero]
             tops = [
                 [wy[q][g] * jnp.where(step == 0, wy[q][g], wy[q + 1][g]) * live[g] for g in range(4)]
                 for q in range(8)
             ]
+            wx = load_table(wx_ref, blk, 1) + [zero]
             for kind in range(2):
-                wx = load_table(wx_ref, blk, 1) + [zero]
                 sides = [[wx[p][g] * wx[p + kind][g] for g in range(4)] for p in range(8)]
-                spread_block(tops, sides, f_ref, lanes, (kind,))
-            return carry
-
-        lax.fori_loop(0, 4, body, 0)
+                columns[kind].append(spread_rows(tops, sides))
     for kind in range(2):
-        both = scatter(f_ref[kind], ohs1[...], ohs2[...])
+        both = scatter(jnp.concatenate(columns[kind], 1), ohs1[...], ohs2[...])
         keep_ref[kind] = both[:, :256]
         send_ref[kind + 1] = both[:, 256:]
-
-
-def gather(parts, hot1, hot2, out_ref):
-    out_ref[:, 0:512] = merge3(jnp.dot(parts, hot1, preferred_element_type=F32))
-    out_ref[:, 512:1024] = merge3(jnp.dot(parts, hot2, preferred_element_type=F32))
 
 
 def scatter(forces, hot1, hot2):
@@ -230,27 +225,38 @@
     )
 
 
+def passed(parts, hot_in, hot_out, tables, side_in, side_out, scale):
+    terms = []
+    for h in range(2):
+        wx_ref, wy_ref, fx_ref, col_ref = tables[h][2:6]
+        columns = []
+        for pair in range(2):
+            at = slice(256 * pair, 256 * pair + 256)
+            rows = merge3(jnp.dot(parts, hot_in[h][:, at], preferred_element_type=F32))
+            for sub in range(2):
+                blk = 2 * pair + sub
+                got = sample_block(rows[:, 128 * sub : 128 * sub + 128], wy_ref, fx_ref, col_ref, blk, side_in)
+                gap = scale(h, blk, got)
+                tops = load_table(wy_ref, blk, side_out)
+                tops = [[tops[q][g] * gap[g] for g in range(4)] for q in range(8)]
+                columns.append(spread_rows(tops, load_table(wx_ref, blk, side_out)))
+        terms.append(jnp.concatenate(columns, 1))
+    return scatter(jnp.concatenate(terms, 1), hot_out[0][...], hot_out[1][...])
+
+
 def up_kernel(v_ref, *refs):
-    halves_of = (refs[:7], refs[7:14])
-    own_ref, down_ref, gap_ref, g_ref, f_ref = refs[14:]
-    ohf1, ohs1 = refs[0], refs[1]
-    ohf2, ohs2 = refs[7], refs[8]
-    gather(split3(v_ref[...]), ohf1[...], ohf2[...], g_ref)
-    for h, (_, _, wx_ref, wy_ref, fx_ref, col_ref, live_ref) in enumerate(halves_of):
-
-        def body(blk, carry):
-            lanes = lanes_of(blk + 4 * h)
-            got = sample_block(g_ref, lanes, wy_ref, fx_ref, col_ref, blk, 0)
-            gap = [got[g] * live_ref[blk, 8 * g : 8 * g + 8, :] for g in range(4)]
-            for g in range(4):
-                gap_ref[blk + 4 * h, 8 * g : 8 * g + 8, :] = gap[g]
-            tops = load_table(wy_ref, blk, 1)
-            tops = [[tops[q][g] * gap[g] for g in range(4)] for q in range(8)]
-            spread_block(tops, load_table(wx_ref, blk, 1), f_ref, lanes)
-            return carry
-
-        lax.fori_loop(0, 4, body, 0, unroll=2)
-    forces = scatter(f_ref[...], ohs1[...], ohs2[...])
+    tables = (refs[:7], refs[7:14])
+    own_ref, down_ref, gap_ref = refs[14:]
+
+    def scale(h, blk, got):
+        gap = []
+        for g in range(4):
+            ms = slice(8 * g, 8 * g + 8)
+            gap.append(got[g] * tables[h][6][blk, ms, :])
+            gap_ref[blk + 4 * h, ms, :] = gap[g]
+        return gap
+
+    forces = passed(split3(v_ref[...]), [t[0] for t in tables], [t[1] for t in tables], tables, 0, 1, scale)
     own_ref[...] = forces[:, :256]
     down_ref[...] = forces[:, 256:]
 
@@ -258,29 +264,18 @@
 def down_kernel(
     v_ref, raw_ref, sent_ref, prev_ref, part_ref, gap_ref, mine_ref, other_ref, stiff_ref, *refs, back
 ):
-    halves_of = (refs[:7], refs[7:14])
-    out_ref, g_ref, f_ref = refs[14:]
-    ohf1, ohs1 = refs[0], refs[1]
-    ohf2, ohs2 = refs[7], refs[8]
+    tables = (refs[:7], refs[7:14])
+    (out_ref,) = refs[14:]
     v = v_ref[...]
     parts = jnp.concatenate([split3(v), split3(raw_ref[...] - sent_ref[...])], 1)
-    gather(parts, ohs1[...], ohs2[...], g_ref)
-    for h, (_, _, wx_ref, wy_ref, fx_ref, col_ref, live_ref) in enumerate(halves_of):
-
-        def body(blk, carry):
-            lanes = lanes_of(blk + 4 * h)
-            got = sample_block(g_ref, lanes, wy_ref, fx_ref, col_ref, blk, 1)
-            gap = [
-                gap_ref[blk + 4 * h, 8 * g : 8 * g + 8, :] - got[g] * live_ref[blk, 8 * g : 8 * g + 8, :]
-                for g in range(4)
-            ]
-            tops = load_table(wy_ref, blk, 0)
-            tops = [[tops[q][g] * gap[g] for g in range(4)] for q in range(8)]
-            spread_block(tops, load_table(wx_ref, blk, 0), f_ref, lanes)
-            return carry
-
-        lax.fori_loop(0, 4, body, 0, unroll=2)
-    forces = scatter(f_ref[...], ohf1[...], ohf2[...])
+
+    def scale(h, blk, got):
+        return [
+            gap_ref[blk + 4 * h, 8 * g : 8 * g + 8, :] - got[g] * tables[h][6][blk, 8 * g : 8 * g + 8, :]
+            for g in range(4)
+        ]
+
+    forces = passed(parts, [t[1] for t in tables], [t[0] for t in tables], tables, 1, 0, scale)
     up = lambda x, d: pltpu.roll(x, 64 - d, 0)
     dn = lambda x, d: pltpu.roll(x, d, 0)
     node = lax.broadcasted_iota(jnp.int32, (64, 256), 0)
@@ -409,16 +404,13 @@
     zero = jnp.zeros((8, 128), F32)
     const = lambda c: (jnp.full((8, 128), c, F32), zero)
 
+    def tree(terms):
+        while len(terms) > 1:
+            terms = [dd_add(*terms[k : k + 2]) if k + 1 < len(terms) else terms[k] for k in range(0, len(terms), 2)]
+        return terms[0]
+
     def form(a, b):
-        total = None
-        for j, bj in enumerate(b):
-            inner = None
-            for i, ai in enumerate(a):
-                term = dd_mul(ai, gram[(i, j)])
-                inner = term if inner is None else dd_add(inner, term)
-            inner = dd_mul(inner, bj)
-            total = inner if total is None else dd_add(total, inner)
-        return total
+        return tree([dd_mul(bj, tree([dd_mul(ai, gram[(i, j)]) for i, ai in enumerate(a)])) for j, bj in enumerate(b)])
 
     def apply(p):
         out = [const(0.0) for _ in range(len(p) + 1)]
@@ -501,9 +493,7 @@
     sections = lax.axis_size("sec")
     route = []
     for section in range(sections):
-        there = section + distance
-        if not 0 <= there < sections:
-            continue
+        there = (section + distance) % sections
         crosses = (section < sections // 2) != (there < sections // 2)
         for y in range(CHIPS):
             to = y ^ 1 if crosses else y
@@ -585,14 +575,13 @@
         field,
         ((1, 256), F32),
     ]
-    work = [pltpu.VMEM((2, 64, 512), F32)]
-    one = call(functools.partial(tables_kernel, blocks=4, add=False), half_tables, 4, work)(*same)
-    two = call(functools.partial(tables_kernel, blocks=4, add=True), half_tables, 7, work)(
+    one = call(functools.partial(tables_kernel, blocks=4, add=False), half_tables, 4)(*same)
+    two = call(functools.partial(tables_kernel, blocks=4, add=True), half_tables, 7)(
         other[0], other[1], other[2], other[3], *one[7:]
     )
     own, down, stiff = two[7:]
     send, keep = call(
-        stencil_kernel, [((3, 64, 256), F32), ((2, 64, 256), F32)], 9, [pltpu.VMEM((2, 64, 1024), F32)], us=4.0
+        stencil_kernel, [((3, 64, 256), F32), ((2, 64, 256), F32)], 9, us=4.0
     )(down, one[0], one[1], one[4], one[6], two[0], two[1], two[4], two[6])
     above = shifted(send, -1)
     raw = shifted(own, 1)
@@ -602,13 +591,12 @@
     tables = []
     for wx, wy, fx, col, live, ohf, ohs in (one[:7], two[:7]):
         tables += [ohf, ohs, wx, wy, fx, col, live]
-    wide = pltpu.VMEM((64, 1024), F32)
     for k in range(ITERS):
         v = fields[-1]
         sent = down
-        part, down, gap = call(up_kernel, [field, field, ((8, 32, 128), F32)], 15, [wide, wide])(v, *tables)
+        part, down, gap = call(up_kernel, [field, field, ((8, 32, 128), F32)], 15)(v, *tables)
         above = shifted(down, -1)
-        partial = call(functools.partial(down_kernel, back=k > 0), [field], 23, [wide, wide])(
+        partial = call(functools.partial(down_kernel, back=k > 0), [field], 23)(
             v, raw, sent, fields[max(k - 1, 0)], part, gap, mine, other, stiff, *tables
         )[0]
         if k < ITERS - 1:

time: 108 us -> 92.2 us (0.85)
  the two profiles are of different devices: /device:TPU:25 before, /device:TPU:1 now
where the time goes in v7:
time: 92.2 us; the launch traced here: 90.5 us
  starting transfers between devices  38.2 us (41%)
  Pallas kernels  22.9 us (25%)
  blocking collectives  15.4 us (17%)
  waiting for transfers between devices  12.1 us (13%)
    all_to_all x1, blocking collectives, on_device(): lax.all_to_all(jnp.broadcast_to(row, (32, 128)), 'sec', 0, 0, tiled=True)  15.4 us
    ppermute x4, starting transfers between devices, dealt(): return lax.ppermute(block, ('sec', 'tile'), route)  14.9 us
    ppermute x9, starting transfers between devices, shifted(): return lax.ppermute(block, ('sec', 'tile'), route)  14.7 us
    ppermute x4, starting transfers between devices, swapped(): return lax.ppermute(block, 'tile', [(i, i ^ 1) for i in range(8)])  7.98 us
    ppermute x4, waiting for transfers between devices, dealt(): return lax.ppermute(block, ('sec', 'tile'), route)  7.09 us
    pallas_call x4, Pallas kernels, on_device(): call(functools.partial(down_kernel, back=k > 0), [field], 23)  6.46 us
    pallas_call x4, Pallas kernels, on_device(): call(up_kernel, [field, field, ((8, 32, 128), F32)], 15)(v, *tables)  6.18 us
    ppermute x9, waiting for transfers between devices, shifted(): return lax.ppermute(block, ('sec', 'tile'), route)  3.98 us
  transfers between devices with their start and end apart: 18, of which 4 were waited for; matrix products, arithmetic and copies ran while one was open for 0% of the time, Pallas kernels for 17%

profile of v7, /device:TPU:1, one launch (start us, length us, event | category | flops | bytes accessed | tf_op | source)
XLA Modules:
  0.0 90.5 jit_solution(1729020537255867616)
XLA Ops:
  0.6 1.7 %shard_map.104 = f32[264,128]{1,0:T(8,128)} custom-call(s32[1,128]{1,0:T(1,128)} %bitcast.38, s32[1,128]{1,0:T(1,128)} %bitcast.39, s32[1,128]{1,0:T(1,128)} %bitcast.40, s32[32,128]{1,0:T(8,128)} %cell1_hbm.1, s32[32,128]{1,0:T(8,128)} %cell2_hbm.1, f32[2,32,128]{2,1,0:T(8,128)} %frac1_hbm.1, f32[2,32,128]{2,1,0:T(8,128)} %frac2_hbm.1, ...), custom_call_target="tpu_custom_call" | custom-call | flops 2000000000 | bytes 262144 | tf_op jit(solution)/shard_map/pallas_call | solution.py:538
  2.3 1.6 %collective-permute-start.3 = (f32[264,128]{1,0:T(8,128)}, f32[264,128]{1,0:T(8,128)S(1)}, u32[]{:S(2)}, u32[]{:S(2)}) collective-permute-start(f32[264,128]{1,0:T(8,128)} %shard_map.104), channel_id=1, source_target_pairs={{0,0},{1,1},{2,226},{3,227},{4,4},{5,5},{6,230},{7,231},{8,8},{9,9... | collective-permute-start | bytes 405512 | tf_op jit(solution)/shard_map/ppermute | solution.py:519
  3.9 9.3 %collective-permute-start.2 = (f32[264,128]{1,0:T(8,128)}, f32[264,128]{1,0:T(8,128)S(1)}, u32[]{:S(2)}, u32[]{:S(2)}) collective-permute-start(f32[264,128]{1,0:T(8,128)} %shard_map.104), channel_id=1, source_target_pairs={{0,230},{1,231},{2,0},{3,1},{4,226},{5,227},{6,4},{7,5},{8,238},{9... | collective-permute-start | bytes 405512 | tf_op jit(solution)/shard_map/ppermute | solution.py:519
  14.3 2.9 %collective-permute-start = (f32[264,128]{1,0:T(8,128)}, f32[264,128]{1,0:T(8,128)S(1)}, u32[]{:S(2)}, u32[]{:S(2)}) collective-permute-start(f32[264,128]{1,0:T(8,128)} %shard_map.104), channel_id=1, source_target_pairs={{0,4},{1,5},{2,230},{3,231},{4,0},{5,1},{6,226},{7,227},{8,12},{9,... | collective-permute-start | bytes 405512 | tf_op jit(solution)/shard_map/ppermute | solution.py:519
  17.2 7.1 %collective-permute-done.1.refs_1_ = f32[264,128]{1,0:T(8,128)S(1)} collective-permute-done((f32[264,128]{1,0:T(8,128)}, f32[264,128]{1,0:T(8,128)S(1)}, u32[]{:S(2)}, u32[]{:S(2)}) %collective-permute-start.1) | collective-permute-done | bytes 135200 | tf_op jit(solution)/shard_map/ppermute | solution.py:519
  24.4 1.8 %collective-permute-start.4 = (f32[4,264,128]{2,1,0:T(8,128)S(1)}, f32[4,264,128]{2,1,0:T(8,128)S(1)}, u32[]{:S(2)}, u32[]{:S(2)}) collective-permute-start(f32[4,264,128]{2,1,0:T(8,128)S(1)} %pad_maximum_fusion), channel_id=1, source_target_pairs={{0,1},{1,0},{2,3},{3,2},{4,5},{5,4},{6,7},{7,6},{8,9},{9,8},{10,11... | collective-permute-start | bytes 1622024 | tf_op jit(solution)/shard_map/ppermute | solution.py:508
  26.1 1.6 %shard_map.105 = (f32[4,2,8,32,128]{4,3,2,1,0:T(8,128)S(1)}, f32[4,2,8,32,128]{4,3,2,1,0:T(8,128)S(1)}, f32[4,2,32,128]{3,2,1,0:T(8,128)S(1)}, s32[4,2,32,128]{3...) custom-call(f32[264,128]{1,0:T(8,128)S(1)} %collective-permute-done., ...), custom_call_target="tpu_custom_call" | custom-call | flops 2000000000 | bytes 262144 | tf_op jit(solution)/shard_map/pallas_call | solution.py:578
  27.8 1.6 %shard_map.106 = (f32[4,2,8,32,128]{4,3,2,1,0:T(8,128)S(1)}, f32[4,2,8,32,128]{4,3,2,1,0:T(8,128)S(1)}, f32[4,2,32,128]{3,2,1,0:T(8,128)S(1)}, s32[4,2,32,128]{3...) custom-call(f32[264,128]{1,0:T(8,128)S(1)} %get-tuple-element.85.ref, ...), custom_call_target="tpu_custom_call" | custom-call | flops 2000000000 | bytes 262144 | tf_op jit(solution)/shard_map/pallas_call | solution.py:579
  29.4 2.2 %shard_map.107 = (f32[3,64,256]{2,1,0:T(8,128)S(1)}, f32[2,64,256]{2,1,0:T(8,128)S(1)}) custom-call(f32[64,256]{1,0:T(8,128)S(1)} %get-tuple-element.44.down_ref.sent_ref, f32[4,2,8,32,128]{4,3,2,1,0:T(8,128)S(1)} %get-tuple-element.45.wx1.refs_2_, f32[4,2,8,32,128]{4,3,2,1,0:T(8,128)S(1)} %get-tuple-element.46.wy1.refs_3_, ...), custom_call_target="tpu_custom_call" | custom-call | flops 4000000000 | bytes 262144 | tf_op jit(solution)/shard_map/pallas_call | solution.py:583
  31.6 6.7 %collective-permute-start.5 = (f32[3,64,256]{2,1,0:T(8,128)S(1)}, f32[3,64,256]{2,1,0:T(8,128)S(1)}, u32[]{:S(2)}, u32[]{:S(2)}) collective-permute-start(f32[3,64,256]{2,1,0:T(8,128)S(1)} %get-tuple-element.53), channel_id=1, source_target_pairs={{0,2},{1,3},{226,224},{227,225},{4,6},{5,7},{230,228},{231,229},{8... | collective-permute-start | bytes 589832 | tf_op jit(solution)/shard_map/ppermute | solution.py:504
  38.2 4.0 %collective-permute-done.5 = f32[3,64,256]{2,1,0:T(8,128)S(1)} collective-permute-done((f32[3,64,256]{2,1,0:T(8,128)S(1)}, f32[3,64,256]{2,1,0:T(8,128)S(1)}, u32[]{:S(2)}, u32[]{:S(2)}) %collective-permute-start.5) | collective-permute-done | bytes 196640 | tf_op jit(solution)/shard_map/ppermute | solution.py:504
  43.5 1.5 %shard_map.108 = (f32[64,256]{1,0:T(8,128)S(1)}, f32[64,256]{1,0:T(8,128)S(1)}, f32[8,32,128]{2,1,0:T(8,128)S(1)}) custom-call(f32[64,256]{1,0:T(8,128)S(1)} %fusion.v_ref.prev_ref.v0, bf16[256,512]{1,0:T(8,128)(2,1)S(1)} %get-tuple-element.54.refs_0_, bf16[512,512]{1,0:T(8,128)(2,1)S(1)} %get-tuple-element.48.ohs1.refs_1_, ...), custom_call_target="tpu_custom_call" | custom-call | flops 2000000000 | bytes 262144 | tf_op jit(solution)/shard_map/pallas_call | solution.py:597
  45.0 2.5 %collective-permute-start.8 = (f32[64,256]{1,0:T(8,128)S(1)}, f32[64,256]{1,0:T(8,128)S(1)}, u32[]{:S(2)}, u32[]{:S(2)}) collective-permute-start(f32[64,256]{1,0:T(8,128)S(1)} %get-tuple-element.64.sent_ref), channel_id=1, source_target_pairs={{0,2},{1,3},{226,224},{227,225},{4,6},{5,7},{230,228},{231,229},{8... | collective-permute-start | bytes 196616 | tf_op jit(solution)/shard_map/ppermute | solution.py:504
  47.5 1.6 %shard_map.109 = f32[64,256]{1,0:T(8,128)S(1)} custom-call(f32[64,256]{1,0:T(8,128)S(1)} %fusion.v_ref.prev_ref.v0, f32[64,256]{1,0:T(8,128)S(1)} %collective-permute-done.6.raw_ref, f32[64,256]{1,0:T(8,128)S(1)} %get-tuple-element.44.down_ref.sent_ref, f32[64,256]{1,0:T(8,128)S(1)} %fusion.v_ref.prev_ref.v0, f32[64,256]{1,0:T(8,128)S(1)} %get-tuple-element.60.part_ref, ...), custom_call_target="tpu_custom_call" | custom-call | flops 2000000000 | bytes 262144 | tf_op jit(solution)/shard_map/pallas_call | solution.py:599
  49.2 1.5 %shard_map.110 = (f32[64,256]{1,0:T(8,128)S(1)}, f32[64,256]{1,0:T(8,128)S(1)}, f32[8,32,128]{2,1,0:T(8,128)S(1)}) custom-call(f32[64,256]{1,0:T(8,128)S(1)} %sub.16.v_ref.prev_ref.v1, bf16[256,512]{1,0:T(8,128)(2,1)S(1)} %get-tuple-element.54.refs_0_, bf16[512,512]{1,0:T(8,128)(2,1)S(1)} %get-tuple-element.48.ohs1.refs_1_, ...), custom_call_target="tpu_custom_call" | custom-call | flops 2000000000 | bytes 262144 | tf_op jit(solution)/shard_map/pallas_call | solution.py:597
  50.8 2.1 %collective-permute-start.10 = (f32[64,256]{1,0:T(8,128)S(1)}, f32[64,256]{1,0:T(8,128)S(1)}, u32[]{:S(2)}, u32[]{:S(2)}) collective-permute-start(f32[64,256]{1,0:T(8,128)S(1)} %get-tuple-element.67.sent_ref), channel_id=1, source_target_pairs={{0,2},{1,3},{226,224},{227,225},{4,6},{5,7},{230,228},{231,229},{8... | collective-permute-start | bytes 196616 | tf_op jit(solution)/shard_map/ppermute | solution.py:504
  52.8 1.6 %shard_map.111 = f32[64,256]{1,0:T(8,128)S(1)} custom-call(f32[64,256]{1,0:T(8,128)S(1)} %sub.16.v_ref.prev_ref.v1, f32[64,256]{1,0:T(8,128)S(1)} %collective-permute-done.9.raw_ref, f32[64,256]{1,0:T(8,128)S(1)} %get-tuple-element.64.sent_ref, f32[64,256]{1,0:T(8,128)S(1)} %fusion.v_ref.prev_ref.v0, f32[64,256]{1,0:T(8,128)S(1)} %get-tuple-element.65.part_ref, ...), custom_call_target="tpu_custom_call" | custom-call | flops 2000000000 | bytes 262144 | tf_op jit(solution)/shard_map/pallas_call | solution.py:599
  54.6 1.5 %shard_map.112 = (f32[64,256]{1,0:T(8,128)S(1)}, f32[64,256]{1,0:T(8,128)S(1)}, f32[8,32,128]{2,1,0:T(8,128)S(1)}) custom-call(f32[64,256]{1,0:T(8,128)S(1)} %sub.17.v_ref.v2.prev_ref, bf16[256,512]{1,0:T(8,128)(2,1)S(1)} %get-tuple-element.54.refs_0_, bf16[512,512]{1,0:T(8,128)(2,1)S(1)} %get-tuple-element.48.ohs1.refs_1_, ...), custom_call_target="tpu_custom_call" | custom-call | flops 2000000000 | bytes 262144 | tf_op jit(solution)/shard_map/pallas_call | solution.py:597
  57.6 1.6 %shard_map.113 = f32[64,256]{1,0:T(8,128)S(1)} custom-call(f32[64,256]{1,0:T(8,128)S(1)} %sub.17.v_ref.v2.prev_ref, f32[64,256]{1,0:T(8,128)S(1)} %collective-permute-done.11.raw_ref, f32[64,256]{1,0:T(8,128)S(1)} %get-tuple-element.67.sent_ref, f32[64,256]{1,0:T(8,128)S(1)} %sub.16.v_ref.prev_ref.v1, f32[64,256]{1,0:T(8,128)S(1)} %get-tuple-element.68.part_ref, ...), custom_call_target="tpu_custom_call" | custom-call | flops 2000000000 | bytes 262144 | tf_op jit(solution)/shard_map/pallas_call | solution.py:599
  59.6 1.5 %shard_map.115 = (f32[64,256]{1,0:T(8,128)S(1)}, f32[64,256]{1,0:T(8,128)S(1)}, f32[8,32,128]{2,1,0:T(8,128)S(1)}) custom-call(f32[64,256]{1,0:T(8,128)S(1)} %sub.18.v3.v_ref, bf16[256,512]{1,0:T(8,128)(2,1)S(1)} %get-tuple-element.54.refs_0_, bf16[512,512]{1,0:T(8,128)(2,1)S(1)} %get-tuple-element.48.ohs1.refs_1_, ...), custom_call_target="tpu_custom_call" | custom-call | flops 2000000000 | bytes 262144 | tf_op jit(solution)/shard_map/pallas_call | solution.py:597
  63.8 1.6 %shard_map.116 = f32[64,256]{1,0:T(8,128)S(1)} custom-call(f32[64,256]{1,0:T(8,128)S(1)} %sub.18.v3.v_ref, f32[64,256]{1,0:T(8,128)S(1)} %collective-permute-done.13.raw_ref, f32[64,256]{1,0:T(8,128)S(1)} %get-tuple-element.70.sent_ref, f32[64,256]{1,0:T(8,128)S(1)} %sub.17.v_ref.v2.prev_ref, f32[64,256]{1,0:T(8,128)S(1)} %get-tuple-element.71.part_ref, ...), custom_call_target="tpu_custom_call" | custom-call | flops 2000000000 | bytes 262144 | tf_op jit(solution)/shard_map/pallas_call | solution.py:599
  66.2 3.1 %collective-permute-start.15 = (f32[1,128]{1,0:T(1,128)S(1)}, f32[1,128]{1,0:T(1,128)S(1)}, u32[]{:S(2)}, u32[]{:S(2)}) collective-permute-start(f32[1,128]{1,0:T(1,128)S(1)} %get-tuple-element.74), channel_id=1, source_target_pairs={{0,1},{1,0},{2,3},{3,2},{4,5},{5,4},{6,7},{7,6},{8,9},{9,8},{10,11... | collective-permute-start | bytes 1544 | tf_op jit(solution)/shard_map/ppermute | solution.py:508
  70.4 15.4 %all_to_all.8 = f32[32,1,128]{2,1,0:T(1,128)S(1)} all-to-all(f32[32,1,128]{2,1,0:T(1,128)S(1)} %broadcast_in_dim.2), channel_id=1, replica_groups=mesh['sec'=32,'tile'=8] {'sec'}, dimensions={0} | all-to-all | bytes 32768 | tf_op jit(solution)/shard_map/all_to_all | solution.py:609
  87.1 1.8 %collective-permute-start.17 = (f32[2,32,64]{2,1,0:T(8,128)S(1)}, f32[2,32,64]{2,1,0:T(8,128)S(1)}, u32[]{:S(2)}, u32[]{:S(2)}) collective-permute-start(f32[2,32,64]{2,1,0:T(8,128)S(1)} %get-tuple-element.77), channel_id=1, source_target_pairs={{0,1},{1,0},{2,3},{3,2},{4,5},{5,4},{6,7},{7,6},{8,9},{9,8},{10,11... | collective-permute-start | bytes 49160 | tf_op jit(solution)/shard_map/ppermute | solution.py:508
  (41 shorter events, 11.9 us)
Async XLA Ops:
  2.3 14.9 %collective-permute-start.3 = (f32[264,128]{1,0:T(8,128)}, f32[264,128]{1,0:T(8,128)S(1)}, u32[]{:S(2)}, u32[]{:S(2)}) collective-permute-start(f32[264,128]{1,0:T(8,128)} %shard_map.104), channel_id=1, source_target_pairs={{0,0},{1,1},{2,226},{3,227},{4,4},{5,5},{6,230},{7,231},{8,8},{9,9... | collective-permute-start | bytes 405512 | tf_op jit(solution)/shard_map/ppermute | solution.py:519
  3.9 13.3 %collective-permute-start.2 = (f32[264,128]{1,0:T(8,128)}, f32[264,128]{1,0:T(8,128)S(1)}, u32[]{:S(2)}, u32[]{:S(2)}) collective-permute-start(f32[264,128]{1,0:T(8,128)} %shard_map.104), channel_id=1, source_target_pairs={{0,230},{1,231},{2,0},{3,1},{4,226},{5,227},{6,4},{7,5},{8,238},{9... | collective-permute-start | bytes 405512 | tf_op jit(solution)/shard_map/ppermute | solution.py:519
  13.2 11.1 %collective-permute-start.1 = (f32[264,128]{1,0:T(8,128)}, f32[264,128]{1,0:T(8,128)S(1)}, u32[]{:S(2)}, u32[]{:S(2)}) collective-permute-start(f32[264,128]{1,0:T(8,128)} %shard_map.104), channel_id=1, source_target_pairs={{0,226},{1,227},{2,4},{3,5},{4,230},{5,231},{6,0},{7,1},{8,234},{9... | collective-permute-start | bytes 405512 | tf_op jit(solution)/shard_map/ppermute | solution.py:519
  14.3 10.0 %collective-permute-start = (f32[264,128]{1,0:T(8,128)}, f32[264,128]{1,0:T(8,128)S(1)}, u32[]{:S(2)}, u32[]{:S(2)}) collective-permute-start(f32[264,128]{1,0:T(8,128)} %shard_map.104), channel_id=1, source_target_pairs={{0,4},{1,5},{2,230},{3,231},{4,0},{5,1},{6,226},{7,227},{8,12},{9,... | collective-permute-start | bytes 405512 | tf_op jit(solution)/shard_map/ppermute | solution.py:519
  24.4 3.4 %collective-permute-start.4 = (f32[4,264,128]{2,1,0:T(8,128)S(1)}, f32[4,264,128]{2,1,0:T(8,128)S(1)}, u32[]{:S(2)}, u32[]{:S(2)}) collective-permute-start(f32[4,264,128]{2,1,0:T(8,128)S(1)} %pad_maximum_fusion), channel_id=1, source_target_pairs={{0,1},{1,0},{2,3},{3,2},{4,5},{5,4},{6,7},{7,6},{8,9},{9,8},{10,11... | collective-permute-start | bytes 1622024 | tf_op jit(solution)/shard_map/ppermute | solution.py:508
  31.6 10.6 %collective-permute-start.5 = (f32[3,64,256]{2,1,0:T(8,128)S(1)}, f32[3,64,256]{2,1,0:T(8,128)S(1)}, u32[]{:S(2)}, u32[]{:S(2)}) collective-permute-start(f32[3,64,256]{2,1,0:T(8,128)S(1)} %get-tuple-element.53), channel_id=1, source_target_pairs={{0,2},{1,3},{226,224},{227,225},{4,6},{5,7},{230,228},{231,229},{8... | collective-permute-start | bytes 589832 | tf_op jit(solution)/shard_map/ppermute | solution.py:504
  38.2 9.3 %collective-permute-start.6 = (f32[64,256]{1,0:T(8,128)S(1)}, f32[64,256]{1,0:T(8,128)S(1)}, u32[]{:S(2)}, u32[]{:S(2)}) collective-permute-start(f32[64,256]{1,0:T(8,128)S(1)} %get-tuple-element.43), channel_id=1, source_target_pairs={{0,8},{1,9},{226,234},{227,235},{4,12},{5,13},{230,238},{231,239},... | collective-permute-start | bytes 196616 | tf_op jit(solution)/shard_map/ppermute | solution.py:504
  42.2 5.3 %collective-permute-start.7 = (f32[2,64,256]{2,1,0:T(8,128)S(1)}, f32[2,64,256]{2,1,0:T(8,128)S(1)}, u32[]{:S(2)}, u32[]{:S(2)}) collective-permute-start(f32[2,64,256]{2,1,0:T(8,128)S(1)} %slice_add_fusion.mine_ref), channel_id=1, source_target_pairs={{0,1},{1,0},{2,3},{3,2},{4,5},{5,4},{6,7},{7,6},{8,9},{9,8},{10,11... | collective-permute-start | bytes 393224 | tf_op jit(solution)/shard_map/ppermute | solution.py:508
  45.0 4.2 %collective-permute-start.8 = (f32[64,256]{1,0:T(8,128)S(1)}, f32[64,256]{1,0:T(8,128)S(1)}, u32[]{:S(2)}, u32[]{:S(2)}) collective-permute-start(f32[64,256]{1,0:T(8,128)S(1)} %get-tuple-element.64.sent_ref), channel_id=1, source_target_pairs={{0,2},{1,3},{226,224},{227,225},{4,6},{5,7},{230,228},{231,229},{8... | collective-permute-start | bytes 196616 | tf_op jit(solution)/shard_map/ppermute | solution.py:504
  49.1 3.7 %collective-permute-start.9 = (f32[64,256]{1,0:T(8,128)S(1)}, f32[64,256]{1,0:T(8,128)S(1)}, u32[]{:S(2)}, u32[]{:S(2)}) collective-permute-start(f32[64,256]{1,0:T(8,128)S(1)} %shard_map.109), channel_id=1, source_target_pairs={{0,8},{1,9},{226,234},{227,235},{4,12},{5,13},{230,238},{231,239},... | collective-permute-start | bytes 196616 | tf_op jit(solution)/shard_map/ppermute | solution.py:504
  50.8 3.8 %collective-permute-start.10 = (f32[64,256]{1,0:T(8,128)S(1)}, f32[64,256]{1,0:T(8,128)S(1)}, u32[]{:S(2)}, u32[]{:S(2)}) collective-permute-start(f32[64,256]{1,0:T(8,128)S(1)} %get-tuple-element.67.sent_ref), channel_id=1, source_target_pairs={{0,2},{1,3},{226,224},{227,225},{4,6},{5,7},{230,228},{231,229},{8... | collective-permute-start | bytes 196616 | tf_op jit(solution)/shard_map/ppermute | solution.py:504
  54.4 3.2 %collective-permute-start.11 = (f32[64,256]{1,0:T(8,128)S(1)}, f32[64,256]{1,0:T(8,128)S(1)}, u32[]{:S(2)}, u32[]{:S(2)}) collective-permute-start(f32[64,256]{1,0:T(8,128)S(1)} %shard_map.111), channel_id=1, source_target_pairs={{0,8},{1,9},{226,234},{227,235},{4,12},{5,13},{230,238},{231,239},... | collective-permute-start | bytes 196616 | tf_op jit(solution)/shard_map/ppermute | solution.py:504
  56.2 3.5 %collective-permute-start.12 = (f32[64,256]{1,0:T(8,128)S(1)}, f32[64,256]{1,0:T(8,128)S(1)}, u32[]{:S(2)}, u32[]{:S(2)}) collective-permute-start(f32[64,256]{1,0:T(8,128)S(1)} %get-tuple-element.70.sent_ref), channel_id=1, source_target_pairs={{0,2},{1,3},{226,224},{227,225},{4,6},{5,7},{230,228},{231,229},{8... | collective-permute-start | bytes 196616 | tf_op jit(solution)/shard_map/ppermute | solution.py:504
  59.3 4.5 %collective-permute-start.13 = (f32[64,256]{1,0:T(8,128)S(1)}, f32[64,256]{1,0:T(8,128)S(1)}, u32[]{:S(2)}, u32[]{:S(2)}) collective-permute-start(f32[64,256]{1,0:T(8,128)S(1)} %shard_map.113), channel_id=1, source_target_pairs={{0,8},{1,9},{226,234},{227,235},{4,12},{5,13},{230,238},{231,239},... | collective-permute-start | bytes 196616 | tf_op jit(solution)/shard_map/ppermute | solution.py:504
  61.2 4.2 %collective-permute-start.14 = (f32[64,256]{1,0:T(8,128)S(1)}, f32[64,256]{1,0:T(8,128)S(1)}, u32[]{:S(2)}, u32[]{:S(2)}) collective-permute-start(f32[64,256]{1,0:T(8,128)S(1)} %get-tuple-element.73), channel_id=1, source_target_pairs={{0,2},{1,3},{226,224},{227,225},{4,6},{5,7},{230,228},{231,229},{8... | collective-permute-start | bytes 196616 | tf_op jit(solution)/shard_map/ppermute | solution.py:504
  66.2 4.0 %collective-permute-start.15 = (f32[1,128]{1,0:T(1,128)S(1)}, f32[1,128]{1,0:T(1,128)S(1)}, u32[]{:S(2)}, u32[]{:S(2)}) collective-permute-start(f32[1,128]{1,0:T(1,128)S(1)} %get-tuple-element.74), channel_id=1, source_target_pairs={{0,1},{1,0},{2,3},{3,2},{4,5},{5,4},{6,7},{7,6},{8,9},{9,8},{10,11... | collective-permute-start | bytes 1544 | tf_op jit(solution)/shard_map/ppermute | solution.py:508
  69.4 16.3 %collective-permute-start.16 = (f32[3,64,128]{2,1,0:T(8,128)S(1)}, f32[3,64,128]{2,1,0:T(8,128)S(1)}, u32[]{:S(2)}, u32[]{:S(2)}) collective-permute-start(f32[3,64,128]{2,1,0:T(8,128)S(1)} %get-tuple-element.75), channel_id=1, source_target_pairs={{0,0},{1,1},{226,2},{227,3},{4,4},{5,5},{230,6},{231,7},{8,8},{9,9... | collective-permute-start | bytes 294920 | tf_op jit(solution)/shard_map/ppermute | solution.py:528
  87.1 2.7 %collective-permute-start.17 = (f32[2,32,64]{2,1,0:T(8,128)S(1)}, f32[2,32,64]{2,1,0:T(8,128)S(1)}, u32[]{:S(2)}, u32[]{:S(2)}) collective-permute-start(f32[2,32,64]{2,1,0:T(8,128)S(1)} %get-tuple-element.77), channel_id=1, source_target_pairs={{0,1},{1,0},{2,3},{3,2},{4,5},{5,4},{6,7},{7,6},{8,9},{9,8},{10,11... | collective-permute-start | bytes 49160 | tf_op jit(solution)/shard_map/ppermute | solution.py:508

commit v8 on v7

--- a/solution.py
+++ b/solution.py
@@ -194,13 +194,16 @@
     stiff_ref[...] = stiff
 
 
-def stencil_kernel(down_ref, wx1, wy1, live1, ohs1, wx2, wy2, live2, ohs2, send_ref, keep_ref):
+def stencil_kernel(down_ref, *refs):
     step = lax.axis_index("tile") & 1
+    send_ref, keep_ref = refs[12:]
     send_ref[0] = down_ref[...]
     zero = [jnp.zeros((8, 128), F32)] * 4
-    columns = [[], []]
-    for wx_ref, wy_ref, live_ref in ((wx1, wy1, live1), (wx2, wy2, live2)):
-        for blk in range(4):
+    terms = [[], []]
+    for h, blocks in enumerate(BLOCKS):
+        wx_ref, wy_ref, live_ref = refs[4 * h : 4 * h + 3]
+        columns = [[], []]
+        for blk in range(blocks):
             live = [live_ref[blk, 8 * g : 8 * g + 8, :] for g in range(4)]
             wy = load_table(wy_ref, blk, 1) + [zero]
             tops = [
@@ -211,49 +214,55 @@
             for kind in range(2):
                 sides = [[wx[p][g] * wx[p + kind][g] for g in range(4)] for p in range(8)]
                 columns[kind].append(spread_rows(tops, sides))
+        for kind in range(2):
+            terms[kind].append(split3(jnp.concatenate(columns[kind], 1)))
     for kind in range(2):
-        both = scatter(jnp.concatenate(columns[kind], 1), ohs1[...], ohs2[...])
+        both = scatter(terms[kind], refs[3:12:4])
         keep_ref[kind] = both[:, :256]
         send_ref[kind + 1] = both[:, 256:]
 
 
-def scatter(forces, hot1, hot2):
-    parts = split3(forces)
-    return merge3(
-        lax.dot_general(parts[:, 0:512], hot1, NT, preferred_element_type=F32)
-        + lax.dot_general(parts[:, 512:1024], hot2, NT, preferred_element_type=F32)
-    )
+def scatter(terms, hots):
+    total = None
+    for parts, hot in zip(terms, hots):
+        term = lax.dot_general(parts, hot[...], NT, preferred_element_type=F32)
+        total = term if total is None else total + term
+    return merge3(total)
+
+
+BLOCKS = (2, 3, 3)
+AT = (0, 2, 5)
 
 
 def passed(parts, hot_in, hot_out, tables, side_in, side_out, scale):
     terms = []
-    for h in range(2):
+    for h, blocks in enumerate(BLOCKS):
         wx_ref, wy_ref, fx_ref, col_ref = tables[h][2:6]
         columns = []
-        for pair in range(2):
-            at = slice(256 * pair, 256 * pair + 256)
-            rows = merge3(jnp.dot(parts, hot_in[h][:, at], preferred_element_type=F32))
-            for sub in range(2):
-                blk = 2 * pair + sub
-                got = sample_block(rows[:, 128 * sub : 128 * sub + 128], wy_ref, fx_ref, col_ref, blk, side_in)
+        for start in range(0, blocks, 2):
+            stop = min(start + 2, blocks)
+            rows = merge3(jnp.dot(parts, hot_in[h][:, 128 * start : 128 * stop], preferred_element_type=F32))
+            for blk in range(start, stop):
+                at = 128 * (blk - start)
+                got = sample_block(rows[:, at : at + 128], wy_ref, fx_ref, col_ref, blk, side_in)
                 gap = scale(h, blk, got)
                 tops = load_table(wy_ref, blk, side_out)
                 tops = [[tops[q][g] * gap[g] for g in range(4)] for q in range(8)]
                 columns.append(spread_rows(tops, load_table(wx_ref, blk, side_out)))
-        terms.append(jnp.concatenate(columns, 1))
-    return scatter(jnp.concatenate(terms, 1), hot_out[0][...], hot_out[1][...])
+        terms.append(split3(jnp.concatenate(columns, 1)))
+    return scatter(terms, hot_out)
 
 
 def up_kernel(v_ref, *refs):
-    tables = (refs[:7], refs[7:14])
-    own_ref, down_ref, gap_ref = refs[14:]
+    tables = (refs[:7], refs[7:14], refs[14:21])
+    own_ref, down_ref, gap_ref = refs[21:]
 
     def scale(h, blk, got):
         gap = []
         for g in range(4):
             ms = slice(8 * g, 8 * g + 8)
             gap.append(got[g] * tables[h][6][blk, ms, :])
-            gap_ref[blk + 4 * h, ms, :] = gap[g]
+            gap_ref[blk + AT[h], ms, :] = gap[g]
         return gap
 
     forces = passed(split3(v_ref[...]), [t[0] for t in tables], [t[1] for t in tables], tables, 0, 1, scale)
@@ -264,14 +273,14 @@
 def down_kernel(
     v_ref, raw_ref, sent_ref, prev_ref, part_ref, gap_ref, mine_ref, other_ref, stiff_ref, *refs, back
 ):
-    tables = (refs[:7], refs[7:14])
-    (out_ref,) = refs[14:]
+    tables = (refs[:7], refs[7:14], refs[14:21])
+    (out_ref,) = refs[21:]
     v = v_ref[...]
     parts = jnp.concatenate([split3(v), split3(raw_ref[...] - sent_ref[...])], 1)
 
     def scale(h, blk, got):
         return [
-            gap_ref[blk + 4 * h, 8 * g : 8 * g + 8, :] - got[g] * tables[h][6][blk, 8 * g : 8 * g + 8, :]
+            gap_ref[blk + AT[h], 8 * g : 8 * g + 8, :] - got[g] * tables[h][6][blk, 8 * g : 8 * g + 8, :]
             for g in range(4)
         ]
 
@@ -369,25 +378,12 @@
     out_ref[...] = dots([r[...] for r in (v0, v1, v2, v3)], [p for p in PAIRS if p[1] < 4])
 
 
-def last_kernel(row_ref, v0, v1, v2, v3, v4, out_ref, slice_ref):
+def last_kernel(row_ref, v0, v1, v2, v3, v4, out_ref):
     fields = [r[...] for r in (v0, v1, v2, v3, v4)]
-    y = lax.axis_index("tile") >> 1
-    for k in range(3):
-        sides = []
-        for m in (2 * k, 2 * k + 1):
-            if m < 5:
-                x = jnp.where(y >= 2, fields[m][:, 128:], fields[m][:, :128])
-                sides.append((x, pltpu.roll(x, 64, 1)))
-            else:
-                sides.append((jnp.zeros((64, 128), F32),) * 2)
-        left = jnp.where((y & 1) == 0, sides[0][0], sides[0][1])
-        right = jnp.where((y & 1) == 0, sides[1][1], sides[1][0])
-        lane = lax.broadcasted_iota(jnp.int32, (64, 128), 1)
-        slice_ref[k] = jnp.where(lane < 64, left, right)
     out_ref[...] = row_ref[...] + dots(fields, [p for p in PAIRS if p[1] == 4])
 
 
-def finish_kernel(gram_ref, slice_ref, mine_ref, other_ref):
+def finish_kernel(gram_ref, v0, v1, v2, v3, v4, mine_ref, other_ref):
     rows = gram_ref[...]
     acc = dd_add((rows, pltpu.roll(rows, 112, 1)), (pltpu.roll(rows, 96, 1), pltpu.roll(rows, 80, 1)))
     n = 32
@@ -445,19 +441,20 @@
             new = form(res, res)
             direc = axpy(dd_div(new, norm), direc, res)
             norm = new
-    lane = lax.broadcasted_iota(jnp.int32, (64, 128), 1)
+    fields = [r[...] for r in (v0, v1, v2, v3, v4)]
 
     def combine(coefs):
-        total = jnp.zeros((64, 128), F32)
-        flat = [c[0][0:1, 0:1] for c in coefs] + [jnp.zeros((1, 1), F32)] * (6 - len(coefs))
-        for k in range(3):
-            total = total + jnp.where(lane < 64, flat[2 * k], flat[2 * k + 1]) * slice_ref[k]
-        return total + pltpu.roll(total, 64, 1)
-
-    core = lax.axis_index("tile") & 1
-    want = lax.broadcasted_iota(jnp.int32, (64, 128), 0)
-    want = jnp.where(want < 32, want + 32 * core, want - 32 * core)
-    pick = jnp.where(lane == want, 1.0, 0.0).astype(jnp.bfloat16)
+        total = None
+        for c, f in zip(coefs, fields):
+            term = c[0][0:1, 0:1] * f
+            total = term if total is None else total + term
+        return total
+
+    tile = lax.axis_index("tile")
+    ids = lax.broadcasted_iota(jnp.int32, (64, 256), 1)
+    want = lax.broadcasted_iota(jnp.int32, (64, 256), 0)
+    want = jnp.where(want < 32, tile * 32 + want, (tile ^ 1) * 32 + want - 32)
+    pick = jnp.where(ids == want, 1.0, 0.0).astype(jnp.bfloat16)
     for k, coefs in enumerate((sol, res)):
         parts = lax.dot_general(pick, split3(combine(coefs)), NT, preferred_element_type=F32)
         both = parts[:, :64] + (parts[:, 64:128] + parts[:, 128:192])
@@ -478,30 +475,9 @@
     )
 
 
-ROW = 4
-CHIPS = 4
-
-
-def seat(section, y, sections):
-    row, col = divmod(section, ROW)
-    col = col if row % 2 == 0 else ROW - 1 - col
-    row = row if y % 2 == 0 else sections // ROW - 1 - row
-    return row * ROW + col
-
-
 def shifted(block, distance):
     sections = lax.axis_size("sec")
-    route = []
-    for section in range(sections):
-        there = (section + distance) % sections
-        crosses = (section < sections // 2) != (there < sections // 2)
-        for y in range(CHIPS):
-            to = y ^ 1 if crosses else y
-            for core in range(2):
-                route.append(
-                    (seat(section, y, sections) * 8 + 2 * y + core, seat(there, to, sections) * 8 + 2 * to + core)
-                )
-    return lax.ppermute(block, ("sec", "tile"), route)
+    return lax.ppermute(block, "sec", [(i, (i + distance) % sections) for i in range(sections)])
 
 
 def swapped(block):
@@ -509,23 +485,7 @@
 
 
 def dealt(block, step):
-    sections = lax.axis_size("sec")
-    route = []
-    for section in range(sections):
-        for y in range(CHIPS):
-            to = (y + step) % CHIPS
-            for core in range(2):
-                route.append((section * 8 + 2 * y + core, seat(section, to, sections) * 8 + 2 * to + core))
-    return lax.ppermute(block, ("sec", "tile"), route)
-
-
-def returned(block):
-    sections = lax.axis_size("sec")
-    route = []
-    for section in range(sections):
-        for tile in range(2 * CHIPS):
-            route.append((seat(section, tile // 2, sections) * 8 + tile, section * 8 + tile))
-    return lax.ppermute(block, ("sec", "tile"), route)
+    return lax.ppermute(block, "tile", [(i, (i + 2 * step) % 8) for i in range(8)])
 
 
 def on_device(
@@ -558,56 +518,67 @@
         target,
         stiffness.reshape(1, 32),
     )[0]
-    same = [dealt(packed, step) for step in (2, 1, 3, 0)]
-    other = swapped(jnp.stack(same))
-
+    far = [dealt(packed, step) for step in (2, 1, 3)]
+    near = swapped(packed)
     field = ((64, 256), F32)
     bf16 = jnp.bfloat16
-    half_tables = [
-        ((4, 2, 8, 32, 128), F32),
-        ((4, 2, 8, 32, 128), F32),
-        ((4, 2, 32, 128), F32),
-        ((4, 2, 32, 128), jnp.int32),
-        ((4, 32, 128), F32),
-        ((256, 512), bf16),
-        ((512, 512), bf16),
-        field,
-        field,
-        ((1, 256), F32),
-    ]
-    one = call(functools.partial(tables_kernel, blocks=4, add=False), half_tables, 4)(*same)
-    two = call(functools.partial(tables_kernel, blocks=4, add=True), half_tables, 7)(
-        other[0], other[1], other[2], other[3], *one[7:]
-    )
-    own, down, stiff = two[7:]
-    send, keep = call(
-        stencil_kernel, [((3, 64, 256), F32), ((2, 64, 256), F32)], 9, us=4.0
-    )(down, one[0], one[1], one[4], one[6], two[0], two[1], two[4], two[6])
+    groups = []
+    sums = ()
+    for blocks in BLOCKS:
+        if not groups:
+            datas = (packed, near)
+        elif len(groups) == 1:
+            far, sums = lax.optimization_barrier((far, sums))
+            far_other = swapped(jnp.stack(far))
+            datas = far
+        else:
+            datas = [far_other[k] for k in range(3)]
+        outs = call(
+            functools.partial(tables_kernel, blocks=blocks, add=len(sums) > 0),
+            [
+                ((blocks, 2, 8, 32, 128), F32),
+                ((blocks, 2, 8, 32, 128), F32),
+                ((blocks, 2, 32, 128), F32),
+                ((blocks, 2, 32, 128), jnp.int32),
+                ((blocks, 32, 128), F32),
+                ((256, 128 * blocks), bf16),
+                ((512, 128 * blocks), bf16),
+                field,
+                field,
+                ((1, 256), F32),
+            ],
+            blocks + len(sums),
+            us=0.4 * blocks,
+        )(*datas, *sums)
+        groups.append(outs[:7])
+        sums = tuple(outs[7:])
+    own, down, stiff = sums
+    parts = [x for g in groups for x in (g[0], g[1], g[4], g[6])]
+    send, keep = call(stencil_kernel, [((3, 64, 256), F32), ((2, 64, 256), F32)], 13, us=4.0)(down, *parts)
     above = shifted(send, -1)
     raw = shifted(own, 1)
     fields = [own - above[0]]
     mine = keep + above[1:]
     other = swapped(mine)
     tables = []
-    for wx, wy, fx, col, live, ohf, ohs in (one[:7], two[:7]):
+    for wx, wy, fx, col, live, ohf, ohs in groups:
         tables += [ohf, ohs, wx, wy, fx, col, live]
     for k in range(ITERS):
         v = fields[-1]
         sent = down
-        part, down, gap = call(up_kernel, [field, field, ((8, 32, 128), F32)], 15)(v, *tables)
+        part, down, gap = call(up_kernel, [field, field, ((8, 32, 128), F32)], 22)(v, *tables)
         above = shifted(down, -1)
-        partial = call(functools.partial(down_kernel, back=k > 0), [field], 23)(
+        partial = call(functools.partial(down_kernel, back=k > 0), [field], 30)(
             v, raw, sent, fields[max(k - 1, 0)], part, gap, mine, other, stiff, *tables
         )[0]
         if k < ITERS - 1:
             raw = shifted(partial, 1)
         fields.append(partial - above)
     row = call(dots_kernel, [((1, 128), F32)], 4, us=1.0)(*fields[:4])[0]
-    row, slices = call(last_kernel, [((1, 128), F32), ((3, 64, 128), F32)], 6, us=1.0)(row, *fields)
-    slices = returned(slices)
+    row = call(last_kernel, [((1, 128), F32)], 6, us=1.0)(row, *fields)[0]
     row = row + jnp.roll(swapped(row), 32, 1)
     gram = lax.all_to_all(jnp.broadcast_to(row, (32, 128)), "sec", 0, 0, tiled=True)
-    mine, other = call(finish_kernel, [((2, 32, 64), F32), ((2, 32, 64), F32)], 2)(gram, slices)
+    mine, other = call(finish_kernel, [((2, 32, 64), F32), ((2, 32, 64), F32)], 6)(gram, *fields)
     other = swapped(other)
     first = jnp.where(core == 0, mine, other)
     last = jnp.where(core == 0, other, mine)

time: 92.2 us -> 93.3 us (1.012); the launches traced: 90.5 us -> 93 us
  starting transfers between devices: 38.2 us -> 41.5 us
  waiting for transfers between devices: 12.1 us -> 10.2 us
  Pallas kernels: 22.9 us -> 24.1 us
    ppermute x14 -> x12, waiting for transfers between devices: 11.1 us -> 8.4 us  [the longest x3 4.48 us: dealt(): lax.ppermute(block, 'tile', [(i, (i + 2 * step) % 8) for i in range(8)])]
    ppermute x4 -> x5, starting transfers between devices: 7.98 us -> 9.95 us  [swapped(): return lax.ppermute(block, 'tile', [(i, i ^ 1) for i in range(8)])]
    ppermute x14 -> x12, starting transfers between devices: 30.3 us -> 31.5 us  [the longest x9 27.6 us: shifted(): lax.ppermute(block, 'sec', [(i, (i + distance) % sections) for i in range...]
    pallas_call x13 -> x14, Pallas kernels: 20.2 us -> 21.3 us  [the longest x4 6.87 us: on_device(): call(functools.partial(down_kernel, back=k > 0), [field], 30)]
    unnamed x0 -> x2, local copies, waits for them, and re-layouts: none -> 0.94 us
  transfers between devices with their start and end apart: 18 -> 17, of which waited for: 4 -> 6; matrix products, arithmetic and copies ran while one was open for 0% -> 0% of each run, Pallas kernels for 17% -> 18%
where the time goes in v8:
time: 93.3 us; the launch traced here: 93 us
  starting transfers between devices  41.5 us (44%)
  Pallas kernels  24.1 us (26%)
  blocking collectives  14.5 us (16%)
  waiting for transfers between devices  10.2 us (11%)
  local copies, waits for them, and re-layouts  1.05 us (1%)
    ppermute x9, starting transfers between devices, shifted(): lax.ppermute(block, 'sec', [(i, (i + distance) % sections) for i in range...  27.6 us
    all_to_all x1, blocking collectives, on_device(): lax.all_to_all(jnp.broadcast_to(row, (32, 128)), 'sec', 0, 0, tiled=True)  14.5 us
    ppermute x5, starting transfers between devices, swapped(): return lax.ppermute(block, 'tile', [(i, i ^ 1) for i in range(8)])  9.95 us
    pallas_call x4, Pallas kernels, on_device(): call(functools.partial(down_kernel, back=k > 0), [field], 30)  6.87 us
    pallas_call x4, Pallas kernels, on_device(): call(up_kernel, [field, field, ((8, 32, 128), F32)], 22)(v, *tables)  6.65 us
    ppermute x3, waiting for transfers between devices, dealt(): lax.ppermute(block, 'tile', [(i, (i + 2 * step) % 8) for i in range(8)])  4.48 us
    ppermute x9, waiting for transfers between devices, shifted(): lax.ppermute(block, 'sec', [(i, (i + distance) % sections) for i in range...  3.93 us
    ppermute x3, starting transfers between devices, dealt(): lax.ppermute(block, 'tile', [(i, (i + 2 * step) % 8) for i in range(8)])  3.87 us
  transfers between devices with their start and end apart: 17, of which 6 were waited for; matrix products, arithmetic and copies ran while one was open for 0% of the time, Pallas kernels for 18%

profile of v8, /device:TPU:1, one launch (start us, length us, event | category | flops | bytes accessed | tf_op | source)
XLA Modules:
  0.0 93.0 jit_solution(14604464744778246822)
XLA Ops:
  0.6 1.7 %shard_map.104.refs_0_ = f32[264,128]{1,0:T(8,128)} custom-call(s32[1,128]{1,0:T(1,128)} %bitcast.34, s32[1,128]{1,0:T(1,128)} %bitcast.35, s32[1,128]{1,0:T(1,128)} %bitcast.36, s32[32,128]{1,0:T(8,128)} %cell1_hbm.1, s32[32,128]{1,0:T(8,128)} %cell2_hbm.1, f32[2,32,128]{2,1,0:T(8,128)} %frac1_hbm.1, f32[2,32,128]{2,1,0:T(8,128)} %frac2_hbm.1, ...), custom_call_target="tpu_custom_call" | custom-call | flops 2000000000 | bytes 262144 | tf_op jit(solution)/shard_map/pallas_call | solution.py:498
  2.3 3.3 %collective-permute-start.3 = (f32[264,128]{1,0:T(8,128)}, f32[264,128]{1,0:T(8,128)S(1)}, u32[]{:S(2)}, u32[]{:S(2)}) collective-permute-start(f32[264,128]{1,0:T(8,128)} %shard_map.104.refs_0_), channel_id=1, source_target_pairs={{0,1},{1,0},{2,3},{3,2},{4,5},{5,4},{6,7},{7,6},{8,9},{9,8},{10,11... | collective-permute-start | bytes 405512 | tf_op jit(solution)/shard_map/ppermute | solution.py:484
  7.3 2.3 %collective-permute-start.2 = (f32[264,128]{1,0:T(8,128)}, f32[264,128]{1,0:T(8,128)S(1)}, u32[]{:S(2)}, u32[]{:S(2)}) collective-permute-start(f32[264,128]{1,0:T(8,128)} %shard_map.104.refs_0_), channel_id=1, source_target_pairs={{0,6},{1,7},{2,0},{3,1},{4,2},{5,3},{6,4},{7,5},{8,14},{9,15},{10,... | collective-permute-start | bytes 405512 | tf_op jit(solution)/shard_map/ppermute | solution.py:488
  12.5 3.3 %collective-permute-done.1.refs_1_ = f32[264,128]{1,0:T(8,128)S(1)} collective-permute-done((f32[264,128]{1,0:T(8,128)}, f32[264,128]{1,0:T(8,128)S(1)}, u32[]{:S(2)}, u32[]{:S(2)}) %collective-permute-start.1) | collective-permute-done | bytes 135200 | tf_op jit(solution)/shard_map/ppermute | solution.py:488
  17.8 1.3 %shard_map.107 = (f32[3,2,8,32,128]{4,3,2,1,0:T(8,128)S(1)}, f32[3,2,8,32,128]{4,3,2,1,0:T(8,128)S(1)}, f32[3,2,32,128]{3,2,1,0:T(8,128)S(1)}, s32[3,2,32,128]{3...) custom-call(f32[264,128]{1,0:T(8,128)S(1)} %get-tuple-element.112.re, ...), custom_call_target="tpu_custom_call" | custom-call | flops 1200000000 | bytes 262144 | tf_op jit(solution)/shard_map/pallas_call | solution.py:536
  19.1 2.2 %shard_map.108 = (f32[3,64,256]{2,1,0:T(8,128)S(1)}, f32[2,64,256]{2,1,0:T(8,128)S(1)}) custom-call(f32[64,256]{1,0:T(8,128)S(1)} %get-tuple-element.67.down_ref.sent_ref, f32[2,2,8,32,128]{4,3,2,1,0:T(8,128)S(1)} %get-tuple-element.68.refs_0_.refs_2_, f32[2,2,8,32,128]{4,3,2,1,0:T(8,128)S(1)} %get-tuple-element.69.refs_1_.refs_3_, ...), custom_call_target="tpu_custom_call" | custom-call | flops 4000000000 | bytes 262144 | tf_op jit(solution)/shard_map/pallas_call | solution.py:557
  21.4 6.4 %collective-permute-start.5 = (f32[3,64,256]{2,1,0:T(8,128)S(1)}, f32[3,64,256]{2,1,0:T(8,128)S(1)}, u32[]{:S(2)}, u32[]{:S(2)}) collective-permute-start(f32[3,64,256]{2,1,0:T(8,128)S(1)} %get-tuple-element.80), channel_id=1, source_target_pairs={{0,248},{8,0},{16,8},{24,16},{32,24},{40,32},{48,40},{56,48},{64,5... | collective-permute-start | bytes 589832 | tf_op jit(solution)/shard_map/ppermute | solution.py:480
  27.8 3.9 %collective-permute-done.5 = f32[3,64,256]{2,1,0:T(8,128)S(1)} collective-permute-done((f32[3,64,256]{2,1,0:T(8,128)S(1)}, f32[3,64,256]{2,1,0:T(8,128)S(1)}, u32[]{:S(2)}, u32[]{:S(2)}) %collective-permute-start.5) | collective-permute-done | bytes 196640 | tf_op jit(solution)/shard_map/ppermute | solution.py:480
  33.0 1.7 %shard_map.109 = (f32[64,256]{1,0:T(8,128)S(1)}, f32[64,256]{1,0:T(8,128)S(1)}, f32[8,32,128]{2,1,0:T(8,128)S(1)}) custom-call(f32[64,256]{1,0:T(8,128)S(1)} %fusion.v_ref.prev_ref.v0, bf16[256,256]{1,0:T(8,128)(2,1)S(1)} %get-tuple-element.81.refs_0_, bf16[512,256]{1,0:T(8,128)(2,1)S(1)} %get-tuple-element.71.refs_3_.refs_1_, ...), custom_call_target="tpu_custom_call" | custom-call | flops 2000000000 | bytes 262144 | tf_op jit(solution)/shard_map/pallas_call | solution.py:569
  34.7 5.8 %collective-permute-start.8 = (f32[64,256]{1,0:T(8,128)S(1)}, f32[64,256]{1,0:T(8,128)S(1)}, u32[]{:S(2)}, u32[]{:S(2)}) collective-permute-start(f32[64,256]{1,0:T(8,128)S(1)} %get-tuple-element.94.sent_ref), channel_id=1, source_target_pairs={{0,248},{8,0},{16,8},{24,16},{32,24},{40,32},{48,40},{56,48},{64,5... | collective-permute-start | bytes 196616 | tf_op jit(solution)/shard_map/ppermute | solution.py:480
  40.5 1.7 %shard_map.110 = f32[64,256]{1,0:T(8,128)S(1)} custom-call(f32[64,256]{1,0:T(8,128)S(1)} %fusion.v_ref.prev_ref.v0, f32[64,256]{1,0:T(8,128)S(1)} %collective-permute-done.6.raw_ref, f32[64,256]{1,0:T(8,128)S(1)} %get-tuple-element.67.down_ref.sent_ref, f32[64,256]{1,0:T(8,128)S(1)} %fusion.v_ref.prev_ref.v0, f32[64,256]{1,0:T(8,128)S(1)} %get-tuple-element.90.part_ref, ...), custom_call_target="tpu_custom_call" | custom-call | flops 2000000000 | bytes 262144 | tf_op jit(solution)/shard_map/pallas_call | solution.py:571
  42.3 1.7 %shard_map.111 = (f32[64,256]{1,0:T(8,128)S(1)}, f32[64,256]{1,0:T(8,128)S(1)}, f32[8,32,128]{2,1,0:T(8,128)S(1)}) custom-call(f32[64,256]{1,0:T(8,128)S(1)} %sub.16.v_ref.prev_ref.v1, bf16[256,256]{1,0:T(8,128)(2,1)S(1)} %get-tuple-element.81.refs_0_, bf16[512,256]{1,0:T(8,128)(2,1)S(1)} %get-tuple-element.71.refs_3_.refs_1_, ...), custom_call_target="tpu_custom_call" | custom-call | flops 2000000000 | bytes 262144 | tf_op jit(solution)/shard_map/pallas_call | solution.py:569
  44.0 5.3 %collective-permute-start.10 = (f32[64,256]{1,0:T(8,128)S(1)}, f32[64,256]{1,0:T(8,128)S(1)}, u32[]{:S(2)}, u32[]{:S(2)}) collective-permute-start(f32[64,256]{1,0:T(8,128)S(1)} %get-tuple-element.97.sent_ref), channel_id=1, source_target_pairs={{0,248},{8,0},{16,8},{24,16},{32,24},{40,32},{48,40},{56,48},{64,5... | collective-permute-start | bytes 196616 | tf_op jit(solution)/shard_map/ppermute | solution.py:480
  49.3 1.7 %shard_map.112 = f32[64,256]{1,0:T(8,128)S(1)} custom-call(f32[64,256]{1,0:T(8,128)S(1)} %sub.16.v_ref.prev_ref.v1, f32[64,256]{1,0:T(8,128)S(1)} %collective-permute-done.9.raw_ref, f32[64,256]{1,0:T(8,128)S(1)} %get-tuple-element.94.sent_ref, f32[64,256]{1,0:T(8,128)S(1)} %fusion.v_ref.prev_ref.v0, f32[64,256]{1,0:T(8,128)S(1)} %get-tuple-element.95.part_ref, ...), custom_call_target="tpu_custom_call" | custom-call | flops 2000000000 | bytes 262144 | tf_op jit(solution)/shard_map/pallas_call | solution.py:571
  51.1 1.7 %shard_map.113 = (f32[64,256]{1,0:T(8,128)S(1)}, f32[64,256]{1,0:T(8,128)S(1)}, f32[8,32,128]{2,1,0:T(8,128)S(1)}) custom-call(f32[64,256]{1,0:T(8,128)S(1)} %sub.17.v_ref.v2.prev_ref, bf16[256,256]{1,0:T(8,128)(2,1)S(1)} %get-tuple-element.81.refs_0_, bf16[512,256]{1,0:T(8,128)(2,1)S(1)} %get-tuple-element.71.refs_3_.refs_1_, ...), custom_call_target="tpu_custom_call" | custom-call | flops 2000000000 | bytes 262144 | tf_op jit(solution)/shard_map/pallas_call | solution.py:569
  52.8 4.8 %collective-permute-start.12 = (f32[64,256]{1,0:T(8,128)S(1)}, f32[64,256]{1,0:T(8,128)S(1)}, u32[]{:S(2)}, u32[]{:S(2)}) collective-permute-start(f32[64,256]{1,0:T(8,128)S(1)} %get-tuple-element.100.sent_ref), channel_id=1, source_target_pairs={{0,248},{8,0},{16,8},{24,16},{32,24},{40,32},{48,40},{56,48},{64,5... | collective-permute-start | bytes 196616 | tf_op jit(solution)/shard_map/ppermute | solution.py:480
  57.6 1.7 %shard_map.114 = f32[64,256]{1,0:T(8,128)S(1)} custom-call(f32[64,256]{1,0:T(8,128)S(1)} %sub.17.v_ref.v2.prev_ref, f32[64,256]{1,0:T(8,128)S(1)} %collective-permute-done.11.raw_ref, f32[64,256]{1,0:T(8,128)S(1)} %get-tuple-element.97.sent_ref, f32[64,256]{1,0:T(8,128)S(1)} %sub.16.v_ref.prev_ref.v1, f32[64,256]{1,0:T(8,128)S(1)} %get-tuple-element.98.part_ref, ...), custom_call_target="tpu_custom_call" | custom-call | flops 2000000000 | bytes 262144 | tf_op jit(solution)/shard_map/pallas_call | solution.py:571
  59.7 1.7 %shard_map.116 = (f32[64,256]{1,0:T(8,128)S(1)}, f32[64,256]{1,0:T(8,128)S(1)}, f32[8,32,128]{2,1,0:T(8,128)S(1)}) custom-call(f32[64,256]{1,0:T(8,128)S(1)} %sub.18.v3.v_ref, bf16[256,256]{1,0:T(8,128)(2,1)S(1)} %get-tuple-element.81.refs_0_, bf16[512,256]{1,0:T(8,128)(2,1)S(1)} %get-tuple-element.71.refs_3_.refs_1_, ...), custom_call_target="tpu_custom_call" | custom-call | flops 2000000000 | bytes 262144 | tf_op jit(solution)/shard_map/pallas_call | solution.py:569
  61.3 4.8 %collective-permute-start.14 = (f32[64,256]{1,0:T(8,128)S(1)}, f32[64,256]{1,0:T(8,128)S(1)}, u32[]{:S(2)}, u32[]{:S(2)}) collective-permute-start(f32[64,256]{1,0:T(8,128)S(1)} %get-tuple-element.103), channel_id=1, source_target_pairs={{0,248},{8,0},{16,8},{24,16},{32,24},{40,32},{48,40},{56,48},{64,5... | collective-permute-start | bytes 196616 | tf_op jit(solution)/shard_map/ppermute | solution.py:480
  67.3 1.7 %shard_map.117 = f32[64,256]{1,0:T(8,128)S(1)} custom-call(f32[64,256]{1,0:T(8,128)S(1)} %sub.18.v3.v_ref, f32[64,256]{1,0:T(8,128)S(1)} %collective-permute-done.13.raw_ref, f32[64,256]{1,0:T(8,128)S(1)} %get-tuple-element.100.sent_ref, f32[64,256]{1,0:T(8,128)S(1)} %sub.17.v_ref.v2.prev_ref, f32[64,256]{1,0:T(8,128)S(1)} %get-tuple-element.101.part_ref, ...), custom_call_target="tpu_custom_call" | custom-call | flops 2000000000 | bytes 262144 | tf_op jit(solution)/shard_map/pallas_call | solution.py:571
  69.8 3.0 %collective-permute-start.15 = (f32[1,128]{1,0:T(1,128)S(1)}, f32[1,128]{1,0:T(1,128)S(1)}, u32[]{:S(2)}, u32[]{:S(2)}) collective-permute-start(f32[1,128]{1,0:T(1,128)S(1)} %shard_map.118), channel_id=1, source_target_pairs={{0,1},{1,0},{2,3},{3,2},{4,5},{5,4},{6,7},{7,6},{8,9},{9,8},{10,11... | collective-permute-start | bytes 1544 | tf_op jit(solution)/shard_map/ppermute | solution.py:484
  73.8 14.5 %all_to_all.8 = f32[32,1,128]{2,1,0:T(1,128)S(1)} all-to-all(f32[32,1,128]{2,1,0:T(1,128)S(1)} %broadcast_in_dim.2), channel_id=1, replica_groups=mesh['sec'=32,'tile'=8] {'sec'}, dimensions={0} | all-to-all | bytes 32768 | tf_op jit(solution)/shard_map/all_to_all | solution.py:580
  88.3 1.3 %shard_map.119 = (f32[2,32,64]{2,1,0:T(8,128)S(1)}, f32[2,32,64]{2,1,0:T(8,128)S(1)}) custom-call(f32[32,128]{1,0:T(8,128)S(1)} %bitcast.30, f32[64,256]{1,0:T(8,128)S(1)} %fusion.v_ref.prev_ref.v0, f32[64,256]{1,0:T(8,128)S(1)} %sub.16.v_ref.prev_ref.v1, f32[64,256]{1,0:T(8,128)S(1)} %sub.17.v_ref.v2.prev_ref, f32[64,256]{1,0:T(8,128)S(1)} %sub.18.v3.v_ref, ...), custom_call_target="tpu_custom_call" | custom-call | flops 2000000000 | bytes 262144 | tf_op jit(solution)/shard_map/pallas_call | solution.py:581
  89.6 1.8 %collective-permute-start.16 = (f32[2,32,64]{2,1,0:T(8,128)S(1)}, f32[2,32,64]{2,1,0:T(8,128)S(1)}, u32[]{:S(2)}, u32[]{:S(2)}) collective-permute-start(f32[2,32,64]{2,1,0:T(8,128)S(1)} %get-tuple-element.105), channel_id=1, source_target_pairs={{0,1},{1,0},{2,3},{3,2},{4,5},{5,4},{6,7},{7,6},{8,9},{9,8},{10,11... | collective-permute-start | bytes 49160 | tf_op jit(solution)/shard_map/ppermute | solution.py:484
  (42 shorter events, 12.9 us)
Async XLA Ops:
  2.3 7.2 %collective-permute-start.3 = (f32[264,128]{1,0:T(8,128)}, f32[264,128]{1,0:T(8,128)S(1)}, u32[]{:S(2)}, u32[]{:S(2)}) collective-permute-start(f32[264,128]{1,0:T(8,128)} %shard_map.104.refs_0_), channel_id=1, source_target_pairs={{0,1},{1,0},{2,3},{3,2},{4,5},{5,4},{6,7},{7,6},{8,9},{9,8},{10,11... | collective-permute-start | bytes 405512 | tf_op jit(solution)/shard_map/ppermute | solution.py:484
  5.7 6.9 %collective-permute-start = (f32[264,128]{1,0:T(8,128)}, f32[264,128]{1,0:T(8,128)S(1)}, u32[]{:S(2)}, u32[]{:S(2)}) collective-permute-start(f32[264,128]{1,0:T(8,128)} %shard_map.104.refs_0_), channel_id=1, source_target_pairs={{0,4},{1,5},{2,6},{3,7},{4,0},{5,1},{6,2},{7,3},{8,12},{9,13},{10,... | collective-permute-start | bytes 405512 | tf_op jit(solution)/shard_map/ppermute | solution.py:488
  6.9 9.0 %collective-permute-start.1 = (f32[264,128]{1,0:T(8,128)}, f32[264,128]{1,0:T(8,128)S(1)}, u32[]{:S(2)}, u32[]{:S(2)}) collective-permute-start(f32[264,128]{1,0:T(8,128)} %shard_map.104.refs_0_), channel_id=1, source_target_pairs={{0,2},{1,3},{2,4},{3,5},{4,6},{5,7},{6,0},{7,1},{8,10},{9,11},{10,... | collective-permute-start | bytes 405512 | tf_op jit(solution)/shard_map/ppermute | solution.py:488
  7.3 8.6 %collective-permute-start.2 = (f32[264,128]{1,0:T(8,128)}, f32[264,128]{1,0:T(8,128)S(1)}, u32[]{:S(2)}, u32[]{:S(2)}) collective-permute-start(f32[264,128]{1,0:T(8,128)} %shard_map.104.refs_0_), channel_id=1, source_target_pairs={{0,6},{1,7},{2,0},{3,1},{4,2},{5,3},{6,4},{7,5},{8,14},{9,15},{10,... | collective-permute-start | bytes 405512 | tf_op jit(solution)/shard_map/ppermute | solution.py:488
  9.5 0.9 %copy-start = (f32[264,128]{1,0:T(8,128)S(1)}, f32[264,128]{1,0:T(8,128)}, u32[]{:S(2)}) copy-start(f32[264,128]{1,0:T(8,128)} %shard_map.104.refs_0_) | copy-start | bytes 405508
  15.9 1.9 %collective-permute-start.4 = (f32[3,264,128]{2,1,0:T(8,128)S(1)}, f32[3,264,128]{2,1,0:T(8,128)S(1)}, u32[]{:S(2)}, u32[]{:S(2)}) collective-permute-start(f32[3,264,128]{2,1,0:T(8,128)S(1)} %pad_maximum_fusion), channel_id=1, source_target_pairs={{0,1},{1,0},{2,3},{3,2},{4,5},{5,4},{6,7},{7,6},{8,9},{9,8},{10,11... | collective-permute-start | bytes 1216520 | tf_op jit(solution)/shard_map/ppermute | solution.py:484
  21.4 10.4 %collective-permute-start.5 = (f32[3,64,256]{2,1,0:T(8,128)S(1)}, f32[3,64,256]{2,1,0:T(8,128)S(1)}, u32[]{:S(2)}, u32[]{:S(2)}) collective-permute-start(f32[3,64,256]{2,1,0:T(8,128)S(1)} %get-tuple-element.80), channel_id=1, source_target_pairs={{0,248},{8,0},{16,8},{24,16},{32,24},{40,32},{48,40},{56,48},{64,5... | collective-permute-start | bytes 589832 | tf_op jit(solution)/shard_map/ppermute | solution.py:480
  27.8 12.7 %collective-permute-start.6 = (f32[64,256]{1,0:T(8,128)S(1)}, f32[64,256]{1,0:T(8,128)S(1)}, u32[]{:S(2)}, u32[]{:S(2)}) collective-permute-start(f32[64,256]{1,0:T(8,128)S(1)} %get-tuple-element.66), channel_id=1, source_target_pairs={{0,8},{8,16},{16,24},{24,32},{32,40},{40,48},{48,56},{56,64},{64,7... | collective-permute-start | bytes 196616 | tf_op jit(solution)/shard_map/ppermute | solution.py:480
  31.7 8.8 %collective-permute-start.7 = (f32[2,64,256]{2,1,0:T(8,128)S(1)}, f32[2,64,256]{2,1,0:T(8,128)S(1)}, u32[]{:S(2)}, u32[]{:S(2)}) collective-permute-start(f32[2,64,256]{2,1,0:T(8,128)S(1)} %slice_add_fusion.mine_ref), channel_id=1, source_target_pairs={{0,1},{1,0},{2,3},{3,2},{4,5},{5,4},{6,7},{7,6},{8,9},{9,8},{10,11... | collective-permute-start | bytes 393224 | tf_op jit(solution)/shard_map/ppermute | solution.py:484
  34.7 7.6 %collective-permute-start.8 = (f32[64,256]{1,0:T(8,128)S(1)}, f32[64,256]{1,0:T(8,128)S(1)}, u32[]{:S(2)}, u32[]{:S(2)}) collective-permute-start(f32[64,256]{1,0:T(8,128)S(1)} %get-tuple-element.94.sent_ref), channel_id=1, source_target_pairs={{0,248},{8,0},{16,8},{24,16},{32,24},{40,32},{48,40},{56,48},{64,5... | collective-permute-start | bytes 196616 | tf_op jit(solution)/shard_map/ppermute | solution.py:480
  42.2 7.1 %collective-permute-start.9 = (f32[64,256]{1,0:T(8,128)S(1)}, f32[64,256]{1,0:T(8,128)S(1)}, u32[]{:S(2)}, u32[]{:S(2)}) collective-permute-start(f32[64,256]{1,0:T(8,128)S(1)} %shard_map.110), channel_id=1, source_target_pairs={{0,8},{8,16},{16,24},{24,32},{32,40},{40,48},{48,56},{56,64},{64,7... | collective-permute-start | bytes 196616 | tf_op jit(solution)/shard_map/ppermute | solution.py:480
  44.0 7.1 %collective-permute-start.10 = (f32[64,256]{1,0:T(8,128)S(1)}, f32[64,256]{1,0:T(8,128)S(1)}, u32[]{:S(2)}, u32[]{:S(2)}) collective-permute-start(f32[64,256]{1,0:T(8,128)S(1)} %get-tuple-element.97.sent_ref), channel_id=1, source_target_pairs={{0,248},{8,0},{16,8},{24,16},{32,24},{40,32},{48,40},{56,48},{64,5... | collective-permute-start | bytes 196616 | tf_op jit(solution)/shard_map/ppermute | solution.py:480
  51.0 6.6 %collective-permute-start.11 = (f32[64,256]{1,0:T(8,128)S(1)}, f32[64,256]{1,0:T(8,128)S(1)}, u32[]{:S(2)}, u32[]{:S(2)}) collective-permute-start(f32[64,256]{1,0:T(8,128)S(1)} %shard_map.112), channel_id=1, source_target_pairs={{0,8},{8,16},{16,24},{24,32},{32,40},{40,48},{48,56},{56,64},{64,7... | collective-permute-start | bytes 196616 | tf_op jit(solution)/shard_map/ppermute | solution.py:480
  52.8 6.9 %collective-permute-start.12 = (f32[64,256]{1,0:T(8,128)S(1)}, f32[64,256]{1,0:T(8,128)S(1)}, u32[]{:S(2)}, u32[]{:S(2)}) collective-permute-start(f32[64,256]{1,0:T(8,128)S(1)} %get-tuple-element.100.sent_ref), channel_id=1, source_target_pairs={{0,248},{8,0},{16,8},{24,16},{32,24},{40,32},{48,40},{56,48},{64,5... | collective-permute-start | bytes 196616 | tf_op jit(solution)/shard_map/ppermute | solution.py:480
  59.3 7.9 %collective-permute-start.13 = (f32[64,256]{1,0:T(8,128)S(1)}, f32[64,256]{1,0:T(8,128)S(1)}, u32[]{:S(2)}, u32[]{:S(2)}) collective-permute-start(f32[64,256]{1,0:T(8,128)S(1)} %shard_map.114), channel_id=1, source_target_pairs={{0,8},{8,16},{16,24},{24,32},{32,40},{40,48},{48,56},{56,64},{64,7... | collective-permute-start | bytes 196616 | tf_op jit(solution)/shard_map/ppermute | solution.py:480
  61.3 7.7 %collective-permute-start.14 = (f32[64,256]{1,0:T(8,128)S(1)}, f32[64,256]{1,0:T(8,128)S(1)}, u32[]{:S(2)}, u32[]{:S(2)}) collective-permute-start(f32[64,256]{1,0:T(8,128)S(1)} %get-tuple-element.103), channel_id=1, source_target_pairs={{0,248},{8,0},{16,8},{24,16},{32,24},{40,32},{48,40},{56,48},{64,5... | collective-permute-start | bytes 196616 | tf_op jit(solution)/shard_map/ppermute | solution.py:480
  69.8 3.8 %collective-permute-start.15 = (f32[1,128]{1,0:T(1,128)S(1)}, f32[1,128]{1,0:T(1,128)S(1)}, u32[]{:S(2)}, u32[]{:S(2)}) collective-permute-start(f32[1,128]{1,0:T(1,128)S(1)} %shard_map.118), channel_id=1, source_target_pairs={{0,1},{1,0},{2,3},{3,2},{4,5},{5,4},{6,7},{7,6},{8,9},{9,8},{10,11... | collective-permute-start | bytes 1544 | tf_op jit(solution)/shard_map/ppermute | solution.py:484
  89.6 2.7 %collective-permute-start.16 = (f32[2,32,64]{2,1,0:T(8,128)S(1)}, f32[2,32,64]{2,1,0:T(8,128)S(1)}, u32[]{:S(2)}, u32[]{:S(2)}) collective-permute-start(f32[2,32,64]{2,1,0:T(8,128)S(1)} %get-tuple-element.105), channel_id=1, source_target_pairs={{0,1},{1,0},{2,3},{3,2},{4,5},{5,4},{6,7},{7,6},{8,9},{9,8},{10,11... | collective-permute-start | bytes 49160 | tf_op jit(solution)/shard_map/ppermute | solution.py:484

commit v9 on v8

--- a/solution.py
+++ b/solution.py
@@ -194,10 +194,9 @@
     stiff_ref[...] = stiff
 
 
-def stencil_kernel(down_ref, *refs):
+def stencil_kernel(*refs):
     step = lax.axis_index("tile") & 1
-    send_ref, keep_ref = refs[12:]
-    send_ref[0] = down_ref[...]
+    send_ref, keep_ref = refs[4 * len(BLOCKS) :]
     zero = [jnp.zeros((8, 128), F32)] * 4
     terms = [[], []]
     for h, blocks in enumerate(BLOCKS):
@@ -217,9 +216,9 @@
         for kind in range(2):
             terms[kind].append(split3(jnp.concatenate(columns[kind], 1)))
     for kind in range(2):
-        both = scatter(terms[kind], refs[3:12:4])
+        both = scatter(terms[kind], refs[3 : 4 * len(BLOCKS) : 4])
         keep_ref[kind] = both[:, :256]
-        send_ref[kind + 1] = both[:, 256:]
+        send_ref[kind] = both[:, 256:]
 
 
 def scatter(terms, hots):
@@ -230,8 +229,8 @@
     return merge3(total)
 
 
-BLOCKS = (2, 3, 3)
-AT = (0, 2, 5)
+BLOCKS = (2, 4, 2)
+AT = (0, 2, 6)
 
 
 def passed(parts, hot_in, hot_out, tables, side_in, side_out, scale):
@@ -254,8 +253,8 @@
 
 
 def up_kernel(v_ref, *refs):
-    tables = (refs[:7], refs[7:14], refs[14:21])
-    own_ref, down_ref, gap_ref = refs[21:]
+    tables = [refs[7 * h : 7 * h + 7] for h in range(len(BLOCKS))]
+    own_ref, down_ref, gap_ref = refs[7 * len(BLOCKS) :]
 
     def scale(h, blk, got):
         gap = []
@@ -270,11 +269,37 @@
     down_ref[...] = forces[:, 256:]
 
 
+def up(x, d):
+    return pltpu.roll(x, 64 - d, 0)
+
+
+def dn(x, d):
+    return pltpu.roll(x, d, 0)
+
+
+def banded(v, mine_ref, other_ref):
+    first = (lax.axis_index("tile") & 1) == 0
+    band = [jnp.where(first, mine_ref[k], other_ref[k]) for k in range(2)]
+    band += [jnp.where(first, other_ref[k], mine_ref[k]) for k in range(2)]
+    total = band[0] * v
+    total = total + band[1] * up(v, 1) + dn(band[1] * v, 1)
+    total = total + band[2] * up(v, 8) + dn(band[2] * v, 8)
+    total = total + band[3] * up(v, 9) + dn(band[3] * v, 9)
+    return total + dn(band[3] * up(v, 8), 1) + dn(band[3] * up(v, 1), 8)
+
+
+def band_kernel(part_ref, v_ref, mine_ref, other_ref, out_ref):
+    out_ref[...] = part_ref[...] + banded(v_ref[...], mine_ref, other_ref)
+
+
 def down_kernel(
-    v_ref, raw_ref, sent_ref, prev_ref, part_ref, gap_ref, mine_ref, other_ref, stiff_ref, *refs, back
+    v_ref, raw_ref, sent_ref, part_ref, gap_ref, stiff_ref, *refs, back
 ):
-    tables = (refs[:7], refs[7:14], refs[14:21])
-    (out_ref,) = refs[21:]
+    if back:
+        prev_ref, mine_ref, other_ref = refs[:3]
+        refs = refs[3:]
+    tables = [refs[7 * h : 7 * h + 7] for h in range(len(BLOCKS))]
+    (out_ref,) = refs[7 * len(BLOCKS) :]
     v = v_ref[...]
     parts = jnp.concatenate([split3(v), split3(raw_ref[...] - sent_ref[...])], 1)
 
@@ -285,22 +310,13 @@
         ]
 
     forces = passed(parts, [t[1] for t in tables], [t[0] for t in tables], tables, 1, 0, scale)
-    up = lambda x, d: pltpu.roll(x, 64 - d, 0)
-    dn = lambda x, d: pltpu.roll(x, d, 0)
     node = lax.broadcasted_iota(jnp.int32, (64, 256), 0)
     right = jnp.where((node & 7) < 7, up(v, 1) - v, 0.0)
     below = jnp.where(node < 56, up(v, 8) - v, 0.0)
     bend = (dn(right, 1) - right) + (dn(below, 8) - below)
     total = forces - part_ref[...] + (stiff_ref[...] * SCALE) * bend + ((DAMPING - SHIFT) * SCALE) * v
-    first = (lax.axis_index("tile") & 1) == 0
-    band = [jnp.where(first, mine_ref[k], other_ref[k]) for k in range(2)]
-    band += [jnp.where(first, other_ref[k], mine_ref[k]) for k in range(2)]
-    total = total + band[0] * v
-    total = total + band[1] * up(v, 1) + dn(band[1] * v, 1)
-    total = total + band[2] * up(v, 8) + dn(band[2] * v, 8)
-    total = total + band[3] * up(v, 9) + dn(band[3] * v, 9)
-    total = total + dn(band[3] * up(v, 8), 1) + dn(band[3] * up(v, 1), 8)
     if back:
+        total = total + banded(v, mine_ref, other_ref)
         total = total - BACK * prev_ref[...]
     out_ref[...] = total
 
@@ -378,12 +394,25 @@
     out_ref[...] = dots([r[...] for r in (v0, v1, v2, v3)], [p for p in PAIRS if p[1] < 4])
 
 
-def last_kernel(row_ref, v0, v1, v2, v3, v4, out_ref):
+def last_kernel(row_ref, v0, v1, v2, v3, v4, out_ref, slice_ref):
     fields = [r[...] for r in (v0, v1, v2, v3, v4)]
+    y = lax.axis_index("tile") >> 1
+    for k in range(3):
+        sides = []
+        for m in (2 * k, 2 * k + 1):
+            if m < 5:
+                x = jnp.where(y >= 2, fields[m][:, 128:], fields[m][:, :128])
+                sides.append((x, pltpu.roll(x, 64, 1)))
+            else:
+                sides.append((jnp.zeros((64, 128), F32),) * 2)
+        left = jnp.where((y & 1) == 0, sides[0][0], sides[0][1])
+        right = jnp.where((y & 1) == 0, sides[1][1], sides[1][0])
+        lane = lax.broadcasted_iota(jnp.int32, (64, 128), 1)
+        slice_ref[k] = jnp.where(lane < 64, left, right)
     out_ref[...] = row_ref[...] + dots(fields, [p for p in PAIRS if p[1] == 4])
 
 
-def finish_kernel(gram_ref, v0, v1, v2, v3, v4, mine_ref, other_ref):
+def finish_kernel(gram_ref, slice_ref, mine_ref, other_ref):
     rows = gram_ref[...]
     acc = dd_add((rows, pltpu.roll(rows, 112, 1)), (pltpu.roll(rows, 96, 1), pltpu.roll(rows, 80, 1)))
     n = 32
@@ -441,20 +470,19 @@
             new = form(res, res)
             direc = axpy(dd_div(new, norm), direc, res)
             norm = new
-    fields = [r[...] for r in (v0, v1, v2, v3, v4)]
+    lane = lax.broadcasted_iota(jnp.int32, (64, 128), 1)
 
     def combine(coefs):
-        total = None
-        for c, f in zip(coefs, fields):
-            term = c[0][0:1, 0:1] * f
-            total = term if total is None else total + term
-        return total
-
-    tile = lax.axis_index("tile")
-    ids = lax.broadcasted_iota(jnp.int32, (64, 256), 1)
-    want = lax.broadcasted_iota(jnp.int32, (64, 256), 0)
-    want = jnp.where(want < 32, tile * 32 + want, (tile ^ 1) * 32 + want - 32)
-    pick = jnp.where(ids == want, 1.0, 0.0).astype(jnp.bfloat16)
+        total = jnp.zeros((64, 128), F32)
+        flat = [c[0][0:1, 0:1] for c in coefs] + [jnp.zeros((1, 1), F32)] * (6 - len(coefs))
+        for k in range(3):
+            total = total + jnp.where(lane < 64, flat[2 * k], flat[2 * k + 1]) * slice_ref[k]
+        return total + pltpu.roll(total, 64, 1)
+
+    core = lax.axis_index("tile") & 1
+    want = lax.broadcasted_iota(jnp.int32, (64, 128), 0)
+    want = jnp.where(want < 32, want + 32 * core, want - 32 * core)
+    pick = jnp.where(lane == want, 1.0, 0.0).astype(jnp.bfloat16)
     for k, coefs in enumerate((sol, res)):
         parts = lax.dot_general(pick, split3(combine(coefs)), NT, preferred_element_type=F32)
         both = parts[:, :64] + (parts[:, 64:128] + parts[:, 128:192])
@@ -475,9 +503,30 @@
     )
 
 
+ROW = 4
+CHIPS = 4
+
+
+def seat(section, y, sections):
+    row, col = divmod(section, ROW)
+    col = col if row % 2 == 0 else ROW - 1 - col
+    row = row if y % 2 == 0 else sections // ROW - 1 - row
+    return row * ROW + col
+
+
 def shifted(block, distance):
     sections = lax.axis_size("sec")
-    return lax.ppermute(block, "sec", [(i, (i + distance) % sections) for i in range(sections)])
+    route = []
+    for section in range(sections):
+        there = (section + distance) % sections
+        crosses = (section < sections // 2) != (there < sections // 2)
+        for y in range(CHIPS):
+            to = y ^ 1 if crosses else y
+            for core in range(2):
+                route.append(
+                    (seat(section, y, sections) * 8 + 2 * y + core, seat(there, to, sections) * 8 + 2 * to + core)
+                )
+    return lax.ppermute(block, ("sec", "tile"), route)
 
 
 def swapped(block):
@@ -485,7 +534,23 @@
 
 
 def dealt(block, step):
-    return lax.ppermute(block, "tile", [(i, (i + 2 * step) % 8) for i in range(8)])
+    sections = lax.axis_size("sec")
+    route = []
+    for section in range(sections):
+        for y in range(CHIPS):
+            to = (y + step) % CHIPS
+            for core in range(2):
+                route.append((section * 8 + 2 * y + core, seat(section, to, sections) * 8 + 2 * to + core))
+    return lax.ppermute(block, ("sec", "tile"), route)
+
+
+def returned(block):
+    sections = lax.axis_size("sec")
+    route = []
+    for section in range(sections):
+        for tile in range(2 * CHIPS):
+            route.append((seat(section, tile // 2, sections) * 8 + tile, section * 8 + tile))
+    return lax.ppermute(block, ("sec", "tile"), route)
 
 
 def on_device(
@@ -518,21 +583,21 @@
         target,
         stiffness.reshape(1, 32),
     )[0]
-    far = [dealt(packed, step) for step in (2, 1, 3)]
-    near = swapped(packed)
+    far = [dealt(packed, step) for step in (0, 3, 1, 2)]
     field = ((64, 256), F32)
     bf16 = jnp.bfloat16
     groups = []
     sums = ()
-    for blocks in BLOCKS:
-        if not groups:
-            datas = (packed, near)
-        elif len(groups) == 1:
-            far, sums = lax.optimization_barrier((far, sums))
-            far_other = swapped(jnp.stack(far))
-            datas = far
+    for k, blocks in enumerate(BLOCKS):
+        if k == 0:
+            datas = far[:2]
+            near = [swapped(x) for x in datas]
+        elif k == 1:
+            late, sums = lax.optimization_barrier((far[2:], sums))
+            datas = near + late
+            near = [swapped(x) for x in late]
         else:
-            datas = [far_other[k] for k in range(3)]
+            datas = near
         outs = call(
             functools.partial(tables_kernel, blocks=blocks, add=len(sums) > 0),
             [
@@ -554,31 +619,37 @@
         sums = tuple(outs[7:])
     own, down, stiff = sums
     parts = [x for g in groups for x in (g[0], g[1], g[4], g[6])]
-    send, keep = call(stencil_kernel, [((3, 64, 256), F32), ((2, 64, 256), F32)], 13, us=4.0)(down, *parts)
-    above = shifted(send, -1)
+    above = shifted(down, -1)
     raw = shifted(own, 1)
-    fields = [own - above[0]]
-    mine = keep + above[1:]
-    other = swapped(mine)
+    send, keep = call(stencil_kernel, [((2, 64, 256), F32)] * 2, len(parts), us=4.0)(*parts)
+    above, send = lax.optimization_barrier((above, send))
+    got = shifted(send, -1)
+    fields = [own - above]
     tables = []
     for wx, wy, fx, col, live, ohf, ohs in groups:
         tables += [ohf, ohs, wx, wy, fx, col, live]
     for k in range(ITERS):
         v = fields[-1]
         sent = down
-        part, down, gap = call(up_kernel, [field, field, ((8, 32, 128), F32)], 22)(v, *tables)
+        part, down, gap = call(up_kernel, [field, field, ((8, 32, 128), F32)], 1 + len(tables))(v, *tables)
         above = shifted(down, -1)
-        partial = call(functools.partial(down_kernel, back=k > 0), [field], 30)(
-            v, raw, sent, fields[max(k - 1, 0)], part, gap, mine, other, stiff, *tables
+        more = (fields[k - 1], mine, other) if k else ()
+        partial = call(functools.partial(down_kernel, back=k > 0), [field], 6 + len(more) + len(tables))(
+            v, raw, sent, part, gap, stiff, *more, *tables
         )[0]
+        if k == 0:
+            mine = keep + got
+            other = swapped(mine)
+            partial = call(band_kernel, [field], 4, us=0.3)(partial, v, mine, other)[0]
         if k < ITERS - 1:
             raw = shifted(partial, 1)
         fields.append(partial - above)
     row = call(dots_kernel, [((1, 128), F32)], 4, us=1.0)(*fields[:4])[0]
-    row = call(last_kernel, [((1, 128), F32)], 6, us=1.0)(row, *fields)[0]
+    row, slices = call(last_kernel, [((1, 128), F32), ((3, 64, 128), F32)], 6, us=1.0)(row, *fields)
+    slices = returned(slices)
     row = row + jnp.roll(swapped(row), 32, 1)
     gram = lax.all_to_all(jnp.broadcast_to(row, (32, 128)), "sec", 0, 0, tiled=True)
-    mine, other = call(finish_kernel, [((2, 32, 64), F32), ((2, 32, 64), F32)], 6)(gram, *fields)
+    mine, other = call(finish_kernel, [((2, 32, 64), F32), ((2, 32, 64), F32)], 2)(gram, slices)
     other = swapped(other)
     first = jnp.where(core == 0, mine, other)
     last = jnp.where(core == 0, other, mine)

time: 93.3 us -> 89.4 us (0.958)
  waiting for transfers between devices: 10.2 us -> 2.83 us
  starting transfers between devices: 41.5 us -> 43.8 us
  blocking collectives: 14.5 us -> 16.5 us
  local copies, waits for them, and re-layouts: 1.05 us -> 0.08 us
    ppermute x12 -> x15, waiting for transfers between devices: 8.4 us -> 1.8 us  [the longest x10 1.78 us: shifted(): return lax.ppermute(block, ('sec', 'tile'), route)]
    ppermute x5 -> x7, starting transfers between devices: 9.95 us -> 13.9 us  [swapped(): return lax.ppermute(block, 'tile', [(i, i ^ 1) for i in range(8)])]
    all_to_all x1, blocking collectives: 14.5 us -> 16.5 us  [on_device(): lax.all_to_all(jnp.broadcast_to(row, (32, 128)), 'sec', 0, 0, tiled=True)]
    ppermute x12 -> x15, starting transfers between devices: 31.5 us -> 29.9 us  [the longest x4 14.9 us: dealt(): return lax.ppermute(block, ('sec', 'tile'), route)]
    unnamed x2 -> x0, local copies, waits for them, and re-layouts: 0.94 us -> none
    pallas_call x11 -> x12, Pallas kernels: 17.9 us -> 17.2 us  [the longest x4 6.46 us: on_device(): call(functools.partial(down_kernel, back=k > 0), [field], 6 + len(more) +...]
  transfers between devices with their start and end apart: 17 -> 22, of which waited for: 6 -> 4; matrix products, arithmetic and copies ran while one was open for 0% -> 0% of each run, Pallas kernels for 18% -> 21%
where the time goes in v9:
time: 89.4 us; the launch traced here: 88.2 us
  starting transfers between devices  43.8 us (49%)
  Pallas kernels  23.3 us (26%)
  blocking collectives  16.5 us (18%)
  waiting for transfers between devices  2.83 us (3%)
    all_to_all x1, blocking collectives, on_device(): lax.all_to_all(jnp.broadcast_to(row, (32, 128)), 'sec', 0, 0, tiled=True)  16.5 us
    ppermute x4, starting transfers between devices, dealt(): return lax.ppermute(block, ('sec', 'tile'), route)  14.9 us
    ppermute x10, starting transfers between devices, shifted(): return lax.ppermute(block, ('sec', 'tile'), route)  14.4 us
    ppermute x7, starting transfers between devices, swapped(): return lax.ppermute(block, 'tile', [(i, i ^ 1) for i in range(8)])  13.9 us
    pallas_call x4, Pallas kernels, on_device(): call(functools.partial(down_kernel, back=k > 0), [field], 6 + len(more) +...  6.46 us
    pallas_call x4, Pallas kernels, on_device(): call(up_kernel, [field, field, ((8, 32, 128), F32)], 1 + len(tables))  6.3 us
    pallas_call x3, Pallas kernels, on_device(): call(functools.partial(tables_kernel, blocks=blocks, add=len(sums) > 0),...  3.32 us
    pallas_call x1, Pallas kernels, on_device(): call(stencil_kernel, [((2, 64, 256), F32)] * 2, len(parts), us=4.0)(*parts)  2.18 us
  transfers between devices with their start and end apart: 22, of which 4 were waited for; matrix products, arithmetic and copies ran while one was open for 0% of the time, Pallas kernels for 21%

profile of v9, /device:TPU:1, one launch (start us, length us, event | category | flops | bytes accessed | tf_op | source)
XLA Modules:
  0.0 88.2 jit_solution(14048739225975449407)
XLA Ops:
  0.6 1.7 %shard_map.104 = f32[264,128]{1,0:T(8,128)} custom-call(s32[1,128]{1,0:T(1,128)} %bitcast.18, s32[1,128]{1,0:T(1,128)} %bitcast.19, s32[1,128]{1,0:T(1,128)} %bitcast.20, s32[32,128]{1,0:T(8,128)} %cell1_hbm.1, s32[32,128]{1,0:T(8,128)} %cell2_hbm.1, f32[2,32,128]{2,1,0:T(8,128)} %frac1_hbm.1, f32[2,32,128]{2,1,0:T(8,128)} %frac2_hbm.1, ...), custom_call_target="tpu_custom_call" | custom-call | flops 2000000000 | bytes 262144 | tf_op jit(solution)/shard_map/pallas_call | solution.py:563
  2.3 1.6 %collective-permute-start.2 = (f32[264,128]{1,0:T(8,128)}, f32[264,128]{1,0:T(8,128)S(1)}, u32[]{:S(2)}, u32[]{:S(2)}) collective-permute-start(f32[264,128]{1,0:T(8,128)} %shard_map.104), channel_id=1, source_target_pairs={{0,0},{1,1},{2,226},{3,227},{4,4},{5,5},{6,230},{7,231},{8,8},{9,9... | collective-permute-start | bytes 405512 | tf_op jit(solution)/shard_map/ppermute | solution.py:544
  3.9 9.3 %collective-permute-start.3 = (f32[264,128]{1,0:T(8,128)}, f32[264,128]{1,0:T(8,128)S(1)}, u32[]{:S(2)}, u32[]{:S(2)}) collective-permute-start(f32[264,128]{1,0:T(8,128)} %shard_map.104), channel_id=1, source_target_pairs={{0,230},{1,231},{2,0},{3,1},{4,226},{5,227},{6,4},{7,5},{8,238},{9... | collective-permute-start | bytes 405512 | tf_op jit(solution)/shard_map/ppermute | solution.py:544
  14.3 2.9 %collective-permute-start.1 = (f32[264,128]{1,0:T(8,128)}, f32[264,128]{1,0:T(8,128)S(1)}, u32[]{:S(2)}, u32[]{:S(2)}) collective-permute-start(f32[264,128]{1,0:T(8,128)} %shard_map.104), channel_id=1, source_target_pairs={{0,4},{1,5},{2,230},{3,231},{4,0},{5,1},{6,226},{7,227},{8,12},{9,... | collective-permute-start | bytes 405512 | tf_op jit(solution)/shard_map/ppermute | solution.py:544
  17.2 1.8 %collective-permute-start.6 = (f32[264,128]{1,0:T(8,128)S(1)}, f32[264,128]{1,0:T(8,128)S(1)}, u32[]{:S(2)}, u32[]{:S(2)}) collective-permute-start(f32[264,128]{1,0:T(8,128)S(1)} %collective-permute-done.2.refs_0_), channel_id=1, source_target_pairs={{0,1},{1,0},{2,3},{3,2},{4,5},{5,4},{6,7},{7,6},{8,9},{9,8},{10,11... | collective-permute-start | bytes 405512 | tf_op jit(solution)/shard_map/ppermute | solution.py:533
  19.0 5.1 %collective-permute-start.7 = (f32[264,128]{1,0:T(8,128)S(1)}, f32[264,128]{1,0:T(8,128)S(1)}, u32[]{:S(2)}, u32[]{:S(2)}) collective-permute-start(f32[264,128]{1,0:T(8,128)S(1)} %collective-permute-done.3.refs_1_), channel_id=1, source_target_pairs={{0,1},{1,0},{2,3},{3,2},{4,5},{5,4},{6,7},{7,6},{8,9},{9,8},{10,11... | collective-permute-start | bytes 405512 | tf_op jit(solution)/shard_map/ppermute | solution.py:533
  26.0 1.6 %shard_map.106 = (f32[4,2,8,32,128]{4,3,2,1,0:T(8,128)S(1)}, f32[4,2,8,32,128]{4,3,2,1,0:T(8,128)S(1)}, f32[4,2,32,128]{3,2,1,0:T(8,128)S(1)}, s32[4,2,32,128]{3...) custom-call(f32[264,128]{1,0:T(8,128)S(1)} %collective-permute-done., ...), custom_call_target="tpu_custom_call" | custom-call | flops 1600000000 | bytes 262144 | tf_op jit(solution)/shard_map/pallas_call | solution.py:601
  28.5 6.7 %collective-permute-start.8 = (f32[64,256]{1,0:T(8,128)S(1)}, f32[64,256]{1,0:T(8,128)S(1)}, u32[]{:S(2)}, u32[]{:S(2)}) collective-permute-start(f32[64,256]{1,0:T(8,128)S(1)} %get-tuple-element.69.sent_ref), channel_id=1, source_target_pairs={{0,2},{1,3},{226,224},{227,225},{4,6},{5,7},{230,228},{231,229},{8... | collective-permute-start | bytes 196616 | tf_op jit(solution)/shard_map/ppermute | solution.py:529
  35.2 2.2 %shard_map.108 = (f32[2,64,256]{2,1,0:T(8,128)S(1)}, f32[2,64,256]{2,1,0:T(8,128)S(1)}) custom-call(f32[2,2,8,32,128]{4,3,2,1,0:T(8,128)S(1)} %get-tuple-element.70.refs_0_.refs_2_.refs_5_, f32[2,2,8,32,128]{4,3,2,1,0:T(8,128)S(1)} %get-tuple-element.71.refs_1_.refs_3_.refs_6_, f32[2,32,128]{2,1,0:T(8,128)S(1)} %get-tuple-element.72.refs_2_.refs_6_.refs_9_, ...), custom_call_target="tpu_custom_call" | custom-call | flops 4000000000 | bytes 262144 | tf_op jit(solution)/shard_map/pallas_call | solution.py:624
  37.4 1.7 %collective-permute-start.10 = (f32[2,64,256]{2,1,0:T(8,128)S(1)}, f32[2,64,256]{2,1,0:T(8,128)S(1)}, u32[]{:S(2)}, u32[]{:S(2)}) collective-permute-start(f32[2,64,256]{2,1,0:T(8,128)S(1)} %get-tuple-element.97), channel_id=1, source_target_pairs={{0,2},{1,3},{226,224},{227,225},{4,6},{5,7},{230,228},{231,229},{8... | collective-permute-start | bytes 393224 | tf_op jit(solution)/shard_map/ppermute | solution.py:529
  39.1 1.6 %shard_map.109 = (f32[64,256]{1,0:T(8,128)S(1)}, f32[64,256]{1,0:T(8,128)S(1)}, f32[8,32,128]{2,1,0:T(8,128)S(1)}) custom-call(f32[64,256]{1,0:T(8,128)S(1)} %sub.15.v_ref.refs_0_.v0, bf16[256,256]{1,0:T(8,128)(2,1)S(1)} %get-tuple-element.84.refs_0_.refs_3_, bf16[512,256]{1,0:T(8,128)(2,1)S(1)} %get-tuple-element.73.refs_3_.refs_1_.refs_4_, ...), custom_call_target="tpu_custom_call" | custom-call | flops 2000000000 | bytes 262144 | tf_op jit(solution)/shard_map/pallas_call | solution.py:634
  41.9 1.9 %collective-permute-start.11 = (f32[2,64,256]{2,1,0:T(8,128)S(1)}, f32[2,64,256]{2,1,0:T(8,128)S(1)}, u32[]{:S(2)}, u32[]{:S(2)}) collective-permute-start(f32[2,64,256]{2,1,0:T(8,128)S(1)} %add.13.mine_ref.refs_1_), channel_id=1, source_target_pairs={{0,1},{1,0},{2,3},{3,2},{4,5},{5,4},{6,7},{7,6},{8,9},{9,8},{10,11... | collective-permute-start | bytes 393224 | tf_op jit(solution)/shard_map/ppermute | solution.py:533
  43.8 1.6 %shard_map.110.part_ref = f32[64,256]{1,0:T(8,128)S(1)} custom-call(f32[64,256]{1,0:T(8,128)S(1)} %sub.15.v_ref.refs_0_.v0, f32[64,256]{1,0:T(8,128)S(1)} %collective-permute-done.9.raw_ref, f32[64,256]{1,0:T(8,128)S(1)} %get-tuple-element.69.sent_ref, f32[64,256]{1,0:T(8,128)S(1)} %get-tuple-element.93.part_ref, ...), custom_call_target="tpu_custom_call" | custom-call | flops 2000000000 | bytes 262144 | tf_op jit(solution)/shard_map/pallas_call | solution.py:637
  45.8 1.6 %shard_map.112 = (f32[64,256]{1,0:T(8,128)S(1)}, f32[64,256]{1,0:T(8,128)S(1)}, f32[8,32,128]{2,1,0:T(8,128)S(1)}) custom-call(f32[64,256]{1,0:T(8,128)S(1)} %sub.16.v_ref.refs_0_.v1, bf16[256,256]{1,0:T(8,128)(2,1)S(1)} %get-tuple-element.84.refs_0_.refs_3_, bf16[512,256]{1,0:T(8,128)(2,1)S(1)} %get-tuple-element.73.refs_3_.refs_1_.refs_4_, ...), custom_call_target="tpu_custom_call" | custom-call | flops 2000000000 | bytes 262144 | tf_op jit(solution)/shard_map/pallas_call | solution.py:634
  47.4 2.1 %collective-permute-start.14 = (f32[64,256]{1,0:T(8,128)S(1)}, f32[64,256]{1,0:T(8,128)S(1)}, u32[]{:S(2)}, u32[]{:S(2)}) collective-permute-start(f32[64,256]{1,0:T(8,128)S(1)} %get-tuple-element.101.sent_ref), channel_id=1, source_target_pairs={{0,2},{1,3},{226,224},{227,225},{4,6},{5,7},{230,228},{231,229},{8... | collective-permute-start | bytes 196616 | tf_op jit(solution)/shard_map/ppermute | solution.py:529
  50.2 1.6 %shard_map.113 = f32[64,256]{1,0:T(8,128)S(1)} custom-call(f32[64,256]{1,0:T(8,128)S(1)} %sub.16.v_ref.refs_0_.v1, f32[64,256]{1,0:T(8,128)S(1)} %collective-permute-done.13.raw_ref, f32[64,256]{1,0:T(8,128)S(1)} %get-tuple-element.98.sent_ref, f32[64,256]{1,0:T(8,128)S(1)} %get-tuple-element.99.part_ref, f32[8,32,128]{2,1,0:T(8,128)S(1)} %get-tuple-element.100.gap_ref, ...), custom_call_target="tpu_custom_call" | custom-call | flops 2000000000 | bytes 262144 | tf_op jit(solution)/shard_map/pallas_call | solution.py:637
  52.0 1.6 %shard_map.114 = (f32[64,256]{1,0:T(8,128)S(1)}, f32[64,256]{1,0:T(8,128)S(1)}, f32[8,32,128]{2,1,0:T(8,128)S(1)}) custom-call(f32[64,256]{1,0:T(8,128)S(1)} %sub.17.v_ref.v2.refs_0_, bf16[256,256]{1,0:T(8,128)(2,1)S(1)} %get-tuple-element.84.refs_0_.refs_3_, bf16[512,256]{1,0:T(8,128)(2,1)S(1)} %get-tuple-element.73.refs_3_.refs_1_.refs_4_, ...), custom_call_target="tpu_custom_call" | custom-call | flops 2000000000 | bytes 262144 | tf_op jit(solution)/shard_map/pallas_call | solution.py:634
  53.5 1.7 %collective-permute-start.16 = (f32[64,256]{1,0:T(8,128)S(1)}, f32[64,256]{1,0:T(8,128)S(1)}, u32[]{:S(2)}, u32[]{:S(2)}) collective-permute-start(f32[64,256]{1,0:T(8,128)S(1)} %get-tuple-element.104.sent_ref), channel_id=1, source_target_pairs={{0,2},{1,3},{226,224},{227,225},{4,6},{5,7},{230,228},{231,229},{8... | collective-permute-start | bytes 196616 | tf_op jit(solution)/shard_map/ppermute | solution.py:529
  55.3 1.6 %shard_map.115 = f32[64,256]{1,0:T(8,128)S(1)} custom-call(f32[64,256]{1,0:T(8,128)S(1)} %sub.17.v_ref.v2.refs_0_, f32[64,256]{1,0:T(8,128)S(1)} %collective-permute-done.15.raw_ref, f32[64,256]{1,0:T(8,128)S(1)} %get-tuple-element.101.sent_ref, f32[64,256]{1,0:T(8,128)S(1)} %get-tuple-element.102.part_ref, f32[8,32,128]{2,1,0:T(8,128)S(1)} %get-tuple-element.103.gap_ref, ...), custom_call_target="tpu_custom_call" | custom-call | flops 2000000000 | bytes 262144 | tf_op jit(solution)/shard_map/pallas_call | solution.py:637
  57.0 1.6 %shard_map.117 = (f32[64,256]{1,0:T(8,128)S(1)}, f32[64,256]{1,0:T(8,128)S(1)}, f32[8,32,128]{2,1,0:T(8,128)S(1)}) custom-call(f32[64,256]{1,0:T(8,128)S(1)} %sub.18.v3.v_ref, bf16[256,256]{1,0:T(8,128)(2,1)S(1)} %get-tuple-element.84.refs_0_.refs_3_, bf16[512,256]{1,0:T(8,128)(2,1)S(1)} %get-tuple-element.73.refs_3_.refs_1_.refs_4_, ...), custom_call_target="tpu_custom_call" | custom-call | flops 2000000000 | bytes 262144 | tf_op jit(solution)/shard_map/pallas_call | solution.py:634
  61.2 1.6 %shard_map.118 = f32[64,256]{1,0:T(8,128)S(1)} custom-call(f32[64,256]{1,0:T(8,128)S(1)} %sub.18.v3.v_ref, f32[64,256]{1,0:T(8,128)S(1)} %collective-permute-done.17.raw_ref, f32[64,256]{1,0:T(8,128)S(1)} %get-tuple-element.104.sent_ref, f32[64,256]{1,0:T(8,128)S(1)} %get-tuple-element.105.part_ref, f32[8,32,128]{2,1,0:T(8,128)S(1)} %get-tuple-element.106.gap_ref, ...), custom_call_target="tpu_custom_call" | custom-call | flops 2000000000 | bytes 262144 | tf_op jit(solution)/shard_map/pallas_call | solution.py:637
  63.7 2.3 %collective-permute-start.19 = (f32[1,128]{1,0:T(1,128)S(1)}, f32[1,128]{1,0:T(1,128)S(1)}, u32[]{:S(2)}, u32[]{:S(2)}) collective-permute-start(f32[1,128]{1,0:T(1,128)S(1)} %get-tuple-element.108), channel_id=1, source_target_pairs={{0,1},{1,0},{2,3},{3,2},{4,5},{5,4},{6,7},{7,6},{8,9},{9,8},{10,11... | collective-permute-start | bytes 1544 | tf_op jit(solution)/shard_map/ppermute | solution.py:533
  67.0 16.5 %all_to_all.8 = f32[32,1,128]{2,1,0:T(1,128)S(1)} all-to-all(f32[32,1,128]{2,1,0:T(1,128)S(1)} %broadcast_in_dim.2), channel_id=1, replica_groups=mesh['sec'=32,'tile'=8] {'sec'}, dimensions={0} | all-to-all | bytes 32768 | tf_op jit(solution)/shard_map/all_to_all | solution.py:651
  84.9 1.8 %collective-permute-start.21 = (f32[2,32,64]{2,1,0:T(8,128)S(1)}, f32[2,32,64]{2,1,0:T(8,128)S(1)}, u32[]{:S(2)}, u32[]{:S(2)}) collective-permute-start(f32[2,32,64]{2,1,0:T(8,128)S(1)} %get-tuple-element.111), channel_id=1, source_target_pairs={{0,1},{1,0},{2,3},{3,2},{4,5},{5,4},{6,7},{7,6},{8,9},{9,8},{10,11... | collective-permute-start | bytes 49160 | tf_op jit(solution)/shard_map/ppermute | solution.py:533
  (49 shorter events, 13.8 us)
Async XLA Ops:
  2.3 14.9 %collective-permute-start.2 = (f32[264,128]{1,0:T(8,128)}, f32[264,128]{1,0:T(8,128)S(1)}, u32[]{:S(2)}, u32[]{:S(2)}) collective-permute-start(f32[264,128]{1,0:T(8,128)} %shard_map.104), channel_id=1, source_target_pairs={{0,0},{1,1},{2,226},{3,227},{4,4},{5,5},{6,230},{7,231},{8,8},{9,9... | collective-permute-start | bytes 405512 | tf_op jit(solution)/shard_map/ppermute | solution.py:544
  3.9 15.1 %collective-permute-start.3 = (f32[264,128]{1,0:T(8,128)}, f32[264,128]{1,0:T(8,128)S(1)}, u32[]{:S(2)}, u32[]{:S(2)}) collective-permute-start(f32[264,128]{1,0:T(8,128)} %shard_map.104), channel_id=1, source_target_pairs={{0,230},{1,231},{2,0},{3,1},{4,226},{5,227},{6,4},{7,5},{8,238},{9... | collective-permute-start | bytes 405512 | tf_op jit(solution)/shard_map/ppermute | solution.py:544
  13.2 11.8 %collective-permute-start = (f32[264,128]{1,0:T(8,128)}, f32[264,128]{1,0:T(8,128)S(1)}, u32[]{:S(2)}, u32[]{:S(2)}) collective-permute-start(f32[264,128]{1,0:T(8,128)} %shard_map.104), channel_id=1, source_target_pairs={{0,226},{1,227},{2,4},{3,5},{4,230},{5,231},{6,0},{7,1},{8,234},{9... | collective-permute-start | bytes 405512 | tf_op jit(solution)/shard_map/ppermute | solution.py:544
  14.3 10.7 %collective-permute-start.1 = (f32[264,128]{1,0:T(8,128)}, f32[264,128]{1,0:T(8,128)S(1)}, u32[]{:S(2)}, u32[]{:S(2)}) collective-permute-start(f32[264,128]{1,0:T(8,128)} %shard_map.104), channel_id=1, source_target_pairs={{0,4},{1,5},{2,230},{3,231},{4,0},{5,1},{6,226},{7,227},{8,12},{9,... | collective-permute-start | bytes 405512 | tf_op jit(solution)/shard_map/ppermute | solution.py:544
  17.2 8.8 %collective-permute-start.6 = (f32[264,128]{1,0:T(8,128)S(1)}, f32[264,128]{1,0:T(8,128)S(1)}, u32[]{:S(2)}, u32[]{:S(2)}) collective-permute-start(f32[264,128]{1,0:T(8,128)S(1)} %collective-permute-done.2.refs_0_), channel_id=1, source_target_pairs={{0,1},{1,0},{2,3},{3,2},{4,5},{5,4},{6,7},{7,6},{8,9},{9,8},{10,11... | collective-permute-start | bytes 405512 | tf_op jit(solution)/shard_map/ppermute | solution.py:533
  19.0 7.0 %collective-permute-start.7 = (f32[264,128]{1,0:T(8,128)S(1)}, f32[264,128]{1,0:T(8,128)S(1)}, u32[]{:S(2)}, u32[]{:S(2)}) collective-permute-start(f32[264,128]{1,0:T(8,128)S(1)} %collective-permute-done.3.refs_1_), channel_id=1, source_target_pairs={{0,1},{1,0},{2,3},{3,2},{4,5},{5,4},{6,7},{7,6},{8,9},{9,8},{10,11... | collective-permute-start | bytes 405512 | tf_op jit(solution)/shard_map/ppermute | solution.py:533
  25.0 2.6 %collective-permute-start.4 = (f32[264,128]{1,0:T(8,128)S(1)}, f32[264,128]{1,0:T(8,128)S(1)}, u32[]{:S(2)}, u32[]{:S(2)}) collective-permute-start(f32[264,128]{1,0:T(8,128)S(1)} %collective-permute-done.refs_2_), channel_id=1, source_target_pairs={{0,1},{1,0},{2,3},{3,2},{4,5},{5,4},{6,7},{7,6},{8,9},{9,8},{10,11... | collective-permute-start | bytes 405512 | tf_op jit(solution)/shard_map/ppermute | solution.py:533
  26.0 1.6 %collective-permute-start.5 = (f32[264,128]{1,0:T(8,128)S(1)}, f32[264,128]{1,0:T(8,128)S(1)}, u32[]{:S(2)}, u32[]{:S(2)}) collective-permute-start(f32[264,128]{1,0:T(8,128)S(1)} %collective-permute-done.1.refs_3_), channel_id=1, source_target_pairs={{0,1},{1,0},{2,3},{3,2},{4,5},{5,4},{6,7},{7,6},{8,9},{9,8},{10,11... | collective-permute-start | bytes 405512 | tf_op jit(solution)/shard_map/ppermute | solution.py:533
  28.5 8.9 %collective-permute-start.8 = (f32[64,256]{1,0:T(8,128)S(1)}, f32[64,256]{1,0:T(8,128)S(1)}, u32[]{:S(2)}, u32[]{:S(2)}) collective-permute-start(f32[64,256]{1,0:T(8,128)S(1)} %get-tuple-element.69.sent_ref), channel_id=1, source_target_pairs={{0,2},{1,3},{226,224},{227,225},{4,6},{5,7},{230,228},{231,229},{8... | collective-permute-start | bytes 196616 | tf_op jit(solution)/shard_map/ppermute | solution.py:529
  35.2 8.6 %collective-permute-start.9 = (f32[64,256]{1,0:T(8,128)S(1)}, f32[64,256]{1,0:T(8,128)S(1)}, u32[]{:S(2)}, u32[]{:S(2)}) collective-permute-start(f32[64,256]{1,0:T(8,128)S(1)} %get-tuple-element.68), channel_id=1, source_target_pairs={{0,8},{1,9},{226,234},{227,235},{4,12},{5,13},{230,238},{231,239},... | collective-permute-start | bytes 196616 | tf_op jit(solution)/shard_map/ppermute | solution.py:529
  37.4 4.5 %collective-permute-start.10 = (f32[2,64,256]{2,1,0:T(8,128)S(1)}, f32[2,64,256]{2,1,0:T(8,128)S(1)}, u32[]{:S(2)}, u32[]{:S(2)}) collective-permute-start(f32[2,64,256]{2,1,0:T(8,128)S(1)} %get-tuple-element.97), channel_id=1, source_target_pairs={{0,2},{1,3},{226,224},{227,225},{4,6},{5,7},{230,228},{231,229},{8... | collective-permute-start | bytes 393224 | tf_op jit(solution)/shard_map/ppermute | solution.py:529
  40.7 5.1 %collective-permute-start.12 = (f32[64,256]{1,0:T(8,128)S(1)}, f32[64,256]{1,0:T(8,128)S(1)}, u32[]{:S(2)}, u32[]{:S(2)}) collective-permute-start(f32[64,256]{1,0:T(8,128)S(1)} %get-tuple-element.98.sent_ref), channel_id=1, source_target_pairs={{0,2},{1,3},{226,224},{227,225},{4,6},{5,7},{230,228},{231,229},{8... | collective-permute-start | bytes 196616 | tf_op jit(solution)/shard_map/ppermute | solution.py:529
  41.9 3.5 %collective-permute-start.11 = (f32[2,64,256]{2,1,0:T(8,128)S(1)}, f32[2,64,256]{2,1,0:T(8,128)S(1)}, u32[]{:S(2)}, u32[]{:S(2)}) collective-permute-start(f32[2,64,256]{2,1,0:T(8,128)S(1)} %add.13.mine_ref.refs_1_), channel_id=1, source_target_pairs={{0,1},{1,0},{2,3},{3,2},{4,5},{5,4},{6,7},{7,6},{8,9},{9,8},{10,11... | collective-permute-start | bytes 393224 | tf_op jit(solution)/shard_map/ppermute | solution.py:533
  45.5 4.7 %collective-permute-start.13 = (f32[64,256]{1,0:T(8,128)S(1)}, f32[64,256]{1,0:T(8,128)S(1)}, u32[]{:S(2)}, u32[]{:S(2)}) collective-permute-start(f32[64,256]{1,0:T(8,128)S(1)} %shard_map.111), channel_id=1, source_target_pairs={{0,8},{1,9},{226,234},{227,235},{4,12},{5,13},{230,238},{231,239},... | collective-permute-start | bytes 196616 | tf_op jit(solution)/shard_map/ppermute | solution.py:529
  47.4 4.5 %collective-permute-start.14 = (f32[64,256]{1,0:T(8,128)S(1)}, f32[64,256]{1,0:T(8,128)S(1)}, u32[]{:S(2)}, u32[]{:S(2)}) collective-permute-start(f32[64,256]{1,0:T(8,128)S(1)} %get-tuple-element.101.sent_ref), channel_id=1, source_target_pairs={{0,2},{1,3},{226,224},{227,225},{4,6},{5,7},{230,228},{231,229},{8... | collective-permute-start | bytes 196616 | tf_op jit(solution)/shard_map/ppermute | solution.py:529
  51.8 3.4 %collective-permute-start.15 = (f32[64,256]{1,0:T(8,128)S(1)}, f32[64,256]{1,0:T(8,128)S(1)}, u32[]{:S(2)}, u32[]{:S(2)}) collective-permute-start(f32[64,256]{1,0:T(8,128)S(1)} %shard_map.113), channel_id=1, source_target_pairs={{0,8},{1,9},{226,234},{227,235},{4,12},{5,13},{230,238},{231,239},... | collective-permute-start | bytes 196616 | tf_op jit(solution)/shard_map/ppermute | solution.py:529
  53.5 3.5 %collective-permute-start.16 = (f32[64,256]{1,0:T(8,128)S(1)}, f32[64,256]{1,0:T(8,128)S(1)}, u32[]{:S(2)}, u32[]{:S(2)}) collective-permute-start(f32[64,256]{1,0:T(8,128)S(1)} %get-tuple-element.104.sent_ref), channel_id=1, source_target_pairs={{0,2},{1,3},{226,224},{227,225},{4,6},{5,7},{230,228},{231,229},{8... | collective-permute-start | bytes 196616 | tf_op jit(solution)/shard_map/ppermute | solution.py:529
  56.9 4.3 %collective-permute-start.17 = (f32[64,256]{1,0:T(8,128)S(1)}, f32[64,256]{1,0:T(8,128)S(1)}, u32[]{:S(2)}, u32[]{:S(2)}) collective-permute-start(f32[64,256]{1,0:T(8,128)S(1)} %shard_map.115), channel_id=1, source_target_pairs={{0,8},{1,9},{226,234},{227,235},{4,12},{5,13},{230,238},{231,239},... | collective-permute-start | bytes 196616 | tf_op jit(solution)/shard_map/ppermute | solution.py:529
  58.6 4.3 %collective-permute-start.18 = (f32[64,256]{1,0:T(8,128)S(1)}, f32[64,256]{1,0:T(8,128)S(1)}, u32[]{:S(2)}, u32[]{:S(2)}) collective-permute-start(f32[64,256]{1,0:T(8,128)S(1)} %get-tuple-element.107), channel_id=1, source_target_pairs={{0,2},{1,3},{226,224},{227,225},{4,6},{5,7},{230,228},{231,229},{8... | collective-permute-start | bytes 196616 | tf_op jit(solution)/shard_map/ppermute | solution.py:529
  63.7 3.1 %collective-permute-start.19 = (f32[1,128]{1,0:T(1,128)S(1)}, f32[1,128]{1,0:T(1,128)S(1)}, u32[]{:S(2)}, u32[]{:S(2)}) collective-permute-start(f32[1,128]{1,0:T(1,128)S(1)} %get-tuple-element.108), channel_id=1, source_target_pairs={{0,1},{1,0},{2,3},{3,2},{4,5},{5,4},{6,7},{7,6},{8,9},{9,8},{10,11... | collective-permute-start | bytes 1544 | tf_op jit(solution)/shard_map/ppermute | solution.py:533
  66.0 17.4 %collective-permute-start.20 = (f32[3,64,128]{2,1,0:T(8,128)S(1)}, f32[3,64,128]{2,1,0:T(8,128)S(1)}, u32[]{:S(2)}, u32[]{:S(2)}) collective-permute-start(f32[3,64,128]{2,1,0:T(8,128)S(1)} %get-tuple-element.109), channel_id=1, source_target_pairs={{0,0},{1,1},{226,2},{227,3},{4,4},{5,5},{230,6},{231,7},{8,8},{9,9... | collective-permute-start | bytes 294920 | tf_op jit(solution)/shard_map/ppermute | solution.py:553
  84.9 2.7 %collective-permute-start.21 = (f32[2,32,64]{2,1,0:T(8,128)S(1)}, f32[2,32,64]{2,1,0:T(8,128)S(1)}, u32[]{:S(2)}, u32[]{:S(2)}) collective-permute-start(f32[2,32,64]{2,1,0:T(8,128)S(1)} %get-tuple-element.111), channel_id=1, source_target_pairs={{0,1},{1,0},{2,3},{3,2},{4,5},{5,4},{6,7},{7,6},{8,9},{9,8},{10,11... | collective-permute-start | bytes 49160 | tf_op jit(solution)/shard_map/ppermute | solution.py:533

commit v10 on v9

--- a/solution.py
+++ b/solution.py
@@ -334,9 +334,13 @@
 
 
 def two_prod(a, b):
+    return split_prod(a, b, halves(a), halves(b))
+
+
+def split_prod(a, b, a_halves, b_halves):
     p = a * b
-    ah, al = halves(a)
-    bh, bl = halves(b)
+    ah, al = a_halves
+    bh, bl = b_halves
     return p, ((ah * bh - p) + ah * bl + al * bh) + al * bl
 
 
@@ -370,8 +374,9 @@
     lane = lax.broadcasted_iota(jnp.int32, (16, 128), 1)
     high = jnp.zeros((16, 128), F32)
     low = jnp.zeros((16, 128), F32)
+    cut = [halves(f) for f in fields]
     for i, j in pairs:
-        acc = two_prod(fields[i], fields[j])
+        acc = split_prod(fields[i], fields[j], cut[i], cut[j])
         acc = dd_add((acc[0][:, :128], acc[1][:, :128]), (acc[0][:, 128:], acc[1][:, 128:]))
         n = 64
         while n > 8:
@@ -583,7 +588,7 @@
         target,
         stiffness.reshape(1, 32),
     )[0]
-    far = [dealt(packed, step) for step in (0, 3, 1, 2)]
+    far = [dealt(packed, step) for step in (3, 2, 1, 0)]
     field = ((64, 256), F32)
     bf16 = jnp.bfloat16
     groups = []

time: 89.4 us -> 86.9 us (0.972)
  starting transfers between devices: 43.8 us -> 39 us
  blocking collectives: 16.5 us -> 19 us
    ppermute x4, starting transfers between devices: 14.9 us -> 11.4 us  [dealt(): return lax.ppermute(block, ('sec', 'tile'), route)]
    ppermute x10, starting transfers between devices: 14.4 us -> 11.6 us  [shifted(): return lax.ppermute(block, ('sec', 'tile'), route)]
    all_to_all x1, blocking collectives: 16.5 us -> 19 us  [on_device(): lax.all_to_all(jnp.broadcast_to(row, (32, 128)), 'sec', 0, 0, tiled=True)]
    ppermute x7, starting transfers between devices: 13.9 us -> 15.4 us  [swapped(): return lax.ppermute(block, 'tile', [(i, i ^ 1) for i in range(8)])]
  transfers between devices with their start and end apart: 22 -> 22, of which waited for: 4 -> 5; matrix products, arithmetic and copies ran while one was open for 0% -> 0% of each run, Pallas kernels for 21% -> 22%
where the time goes in v10:
time: 86.9 us; the launch traced here: 86 us
  starting transfers between devices  39 us (45%)
  Pallas kernels  23.3 us (27%)
  blocking collectives  19 us (22%)
  waiting for transfers between devices  2.91 us (3%)
  between operations  0.88 us (1%)
    all_to_all x1, blocking collectives, on_device(): lax.all_to_all(jnp.broadcast_to(row, (32, 128)), 'sec', 0, 0, tiled=True)  19 us
    ppermute x7, starting transfers between devices, swapped(): return lax.ppermute(block, 'tile', [(i, i ^ 1) for i in range(8)])  15.4 us
    ppermute x10, starting transfers between devices, shifted(): return lax.ppermute(block, ('sec', 'tile'), route)  11.6 us
    ppermute x4, starting transfers between devices, dealt(): return lax.ppermute(block, ('sec', 'tile'), route)  11.4 us
    pallas_call x4, Pallas kernels, on_device(): call(functools.partial(down_kernel, back=k > 0), [field], 6 + len(more) +...  6.46 us
    pallas_call x4, Pallas kernels, on_device(): call(up_kernel, [field, field, ((8, 32, 128), F32)], 1 + len(tables))  6.3 us
    pallas_call x3, Pallas kernels, on_device(): call(functools.partial(tables_kernel, blocks=blocks, add=len(sums) > 0),...  3.32 us
    pallas_call x1, Pallas kernels, on_device(): call(stencil_kernel, [((2, 64, 256), F32)] * 2, len(parts), us=4.0)(*parts)  2.18 us
  transfers between devices with their start and end apart: 22, of which 5 were waited for; matrix products, arithmetic and copies ran while one was open for 0% of the time, Pallas kernels for 22%

profile of v10, /device:TPU:1, one launch (start us, length us, event | category | flops | bytes accessed | tf_op | source)
XLA Modules:
  0.0 86.0 jit_solution(822162276035916481)
XLA Ops:
  0.6 1.7 %shard_map.104 = f32[264,128]{1,0:T(8,128)} custom-call(s32[1,128]{1,0:T(1,128)} %bitcast.18, s32[1,128]{1,0:T(1,128)} %bitcast.19, s32[1,128]{1,0:T(1,128)} %bitcast.20, s32[32,128]{1,0:T(8,128)} %cell1_hbm.1, s32[32,128]{1,0:T(8,128)} %cell2_hbm.1, f32[2,32,128]{2,1,0:T(8,128)} %frac1_hbm.1, f32[2,32,128]{2,1,0:T(8,128)} %frac2_hbm.1, ...), custom_call_target="tpu_custom_call" | custom-call | flops 2000000000 | bytes 262144 | tf_op jit(solution)/shard_map/pallas_call | solution.py:568
  2.3 8.9 %collective-permute-start.2 = (f32[264,128]{1,0:T(8,128)}, f32[264,128]{1,0:T(8,128)S(1)}, u32[]{:S(2)}, u32[]{:S(2)}) collective-permute-start(f32[264,128]{1,0:T(8,128)} %shard_map.104), channel_id=1, source_target_pairs={{0,230},{1,231},{2,0},{3,1},{4,226},{5,227},{6,4},{7,5},{8,238},{9... | collective-permute-start | bytes 405512 | tf_op jit(solution)/shard_map/ppermute | solution.py:549
  12.2 1.6 %collective-permute-start.1 = (f32[264,128]{1,0:T(8,128)}, f32[264,128]{1,0:T(8,128)S(1)}, u32[]{:S(2)}, u32[]{:S(2)}) collective-permute-start(f32[264,128]{1,0:T(8,128)} %shard_map.104), channel_id=1, source_target_pairs={{0,0},{1,1},{2,226},{3,227},{4,4},{5,5},{6,230},{7,231},{8,8},{9,9... | collective-permute-start | bytes 405512 | tf_op jit(solution)/shard_map/ppermute | solution.py:549
  13.8 8.3 %collective-permute-start.6 = (f32[264,128]{1,0:T(8,128)S(1)}, f32[264,128]{1,0:T(8,128)S(1)}, u32[]{:S(2)}, u32[]{:S(2)}) collective-permute-start(f32[264,128]{1,0:T(8,128)S(1)} %collective-permute-done.2.refs_0_), channel_id=1, source_target_pairs={{0,1},{1,0},{2,3},{3,2},{4,5},{5,4},{6,7},{7,6},{8,9},{9,8},{10,11... | collective-permute-start | bytes 405512 | tf_op jit(solution)/shard_map/ppermute | solution.py:538
  24.1 1.6 %shard_map.106 = (f32[4,2,8,32,128]{4,3,2,1,0:T(8,128)S(1)}, f32[4,2,8,32,128]{4,3,2,1,0:T(8,128)S(1)}, f32[4,2,32,128]{3,2,1,0:T(8,128)S(1)}, s32[4,2,32,128]{3...) custom-call(f32[264,128]{1,0:T(8,128)S(1)} %collective-permute-done., ...), custom_call_target="tpu_custom_call" | custom-call | flops 1600000000 | bytes 262144 | tf_op jit(solution)/shard_map/pallas_call | solution.py:606
  26.6 3.8 %collective-permute-start.8 = (f32[64,256]{1,0:T(8,128)S(1)}, f32[64,256]{1,0:T(8,128)S(1)}, u32[]{:S(2)}, u32[]{:S(2)}) collective-permute-start(f32[64,256]{1,0:T(8,128)S(1)} %get-tuple-element.69.sent_ref), channel_id=1, source_target_pairs={{0,2},{1,3},{226,224},{227,225},{4,6},{5,7},{230,228},{231,229},{8... | collective-permute-start | bytes 196616 | tf_op jit(solution)/shard_map/ppermute | solution.py:534
  30.4 2.2 %shard_map.108 = (f32[2,64,256]{2,1,0:T(8,128)S(1)}, f32[2,64,256]{2,1,0:T(8,128)S(1)}) custom-call(f32[2,2,8,32,128]{4,3,2,1,0:T(8,128)S(1)} %get-tuple-element.70.refs_0_.refs_2_.refs_5_, f32[2,2,8,32,128]{4,3,2,1,0:T(8,128)S(1)} %get-tuple-element.71.refs_1_.refs_3_.refs_6_, f32[2,32,128]{2,1,0:T(8,128)S(1)} %get-tuple-element.72.refs_2_.refs_6_.refs_9_, ...), custom_call_target="tpu_custom_call" | custom-call | flops 4000000000 | bytes 262144 | tf_op jit(solution)/shard_map/pallas_call | solution.py:629
  32.7 1.7 %collective-permute-start.10 = (f32[2,64,256]{2,1,0:T(8,128)S(1)}, f32[2,64,256]{2,1,0:T(8,128)S(1)}, u32[]{:S(2)}, u32[]{:S(2)}) collective-permute-start(f32[2,64,256]{2,1,0:T(8,128)S(1)} %get-tuple-element.97), channel_id=1, source_target_pairs={{0,2},{1,3},{226,224},{227,225},{4,6},{5,7},{230,228},{231,229},{8... | collective-permute-start | bytes 393224 | tf_op jit(solution)/shard_map/ppermute | solution.py:534
  34.4 1.6 %shard_map.109 = (f32[64,256]{1,0:T(8,128)S(1)}, f32[64,256]{1,0:T(8,128)S(1)}, f32[8,32,128]{2,1,0:T(8,128)S(1)}) custom-call(f32[64,256]{1,0:T(8,128)S(1)} %sub.15.v_ref.refs_0_.v0, bf16[256,256]{1,0:T(8,128)(2,1)S(1)} %get-tuple-element.84.refs_0_.refs_3_, bf16[512,256]{1,0:T(8,128)(2,1)S(1)} %get-tuple-element.73.refs_3_.refs_1_.refs_4_, ...), custom_call_target="tpu_custom_call" | custom-call | flops 2000000000 | bytes 262144 | tf_op jit(solution)/shard_map/pallas_call | solution.py:639
  37.2 1.9 %collective-permute-start.11 = (f32[2,64,256]{2,1,0:T(8,128)S(1)}, f32[2,64,256]{2,1,0:T(8,128)S(1)}, u32[]{:S(2)}, u32[]{:S(2)}) collective-permute-start(f32[2,64,256]{2,1,0:T(8,128)S(1)} %add.13.mine_ref.refs_1_), channel_id=1, source_target_pairs={{0,1},{1,0},{2,3},{3,2},{4,5},{5,4},{6,7},{7,6},{8,9},{9,8},{10,11... | collective-permute-start | bytes 393224 | tf_op jit(solution)/shard_map/ppermute | solution.py:538
  39.1 1.6 %shard_map.110.part_ref = f32[64,256]{1,0:T(8,128)S(1)} custom-call(f32[64,256]{1,0:T(8,128)S(1)} %sub.15.v_ref.refs_0_.v0, f32[64,256]{1,0:T(8,128)S(1)} %collective-permute-done.9.raw_ref, f32[64,256]{1,0:T(8,128)S(1)} %get-tuple-element.69.sent_ref, f32[64,256]{1,0:T(8,128)S(1)} %get-tuple-element.93.part_ref, ...), custom_call_target="tpu_custom_call" | custom-call | flops 2000000000 | bytes 262144 | tf_op jit(solution)/shard_map/pallas_call | solution.py:642
  41.1 1.6 %shard_map.112 = (f32[64,256]{1,0:T(8,128)S(1)}, f32[64,256]{1,0:T(8,128)S(1)}, f32[8,32,128]{2,1,0:T(8,128)S(1)}) custom-call(f32[64,256]{1,0:T(8,128)S(1)} %sub.16.v_ref.refs_0_.v1, bf16[256,256]{1,0:T(8,128)(2,1)S(1)} %get-tuple-element.84.refs_0_.refs_3_, bf16[512,256]{1,0:T(8,128)(2,1)S(1)} %get-tuple-element.73.refs_3_.refs_1_.refs_4_, ...), custom_call_target="tpu_custom_call" | custom-call | flops 2000000000 | bytes 262144 | tf_op jit(solution)/shard_map/pallas_call | solution.py:639
  42.6 2.1 %collective-permute-start.14 = (f32[64,256]{1,0:T(8,128)S(1)}, f32[64,256]{1,0:T(8,128)S(1)}, u32[]{:S(2)}, u32[]{:S(2)}) collective-permute-start(f32[64,256]{1,0:T(8,128)S(1)} %get-tuple-element.101.sent_ref), channel_id=1, source_target_pairs={{0,2},{1,3},{226,224},{227,225},{4,6},{5,7},{230,228},{231,229},{8... | collective-permute-start | bytes 196616 | tf_op jit(solution)/shard_map/ppermute | solution.py:534
  45.4 1.6 %shard_map.113 = f32[64,256]{1,0:T(8,128)S(1)} custom-call(f32[64,256]{1,0:T(8,128)S(1)} %sub.16.v_ref.refs_0_.v1, f32[64,256]{1,0:T(8,128)S(1)} %collective-permute-done.13.raw_ref, f32[64,256]{1,0:T(8,128)S(1)} %get-tuple-element.98.sent_ref, f32[64,256]{1,0:T(8,128)S(1)} %get-tuple-element.99.part_ref, f32[8,32,128]{2,1,0:T(8,128)S(1)} %get-tuple-element.100.gap_ref, ...), custom_call_target="tpu_custom_call" | custom-call | flops 2000000000 | bytes 262144 | tf_op jit(solution)/shard_map/pallas_call | solution.py:642
  47.2 1.6 %shard_map.114 = (f32[64,256]{1,0:T(8,128)S(1)}, f32[64,256]{1,0:T(8,128)S(1)}, f32[8,32,128]{2,1,0:T(8,128)S(1)}) custom-call(f32[64,256]{1,0:T(8,128)S(1)} %sub.17.v_ref.v2.refs_0_, bf16[256,256]{1,0:T(8,128)(2,1)S(1)} %get-tuple-element.84.refs_0_.refs_3_, bf16[512,256]{1,0:T(8,128)(2,1)S(1)} %get-tuple-element.73.refs_3_.refs_1_.refs_4_, ...), custom_call_target="tpu_custom_call" | custom-call | flops 2000000000 | bytes 262144 | tf_op jit(solution)/shard_map/pallas_call | solution.py:639
  48.8 1.7 %collective-permute-start.16 = (f32[64,256]{1,0:T(8,128)S(1)}, f32[64,256]{1,0:T(8,128)S(1)}, u32[]{:S(2)}, u32[]{:S(2)}) collective-permute-start(f32[64,256]{1,0:T(8,128)S(1)} %get-tuple-element.104.sent_ref), channel_id=1, source_target_pairs={{0,2},{1,3},{226,224},{227,225},{4,6},{5,7},{230,228},{231,229},{8... | collective-permute-start | bytes 196616 | tf_op jit(solution)/shard_map/ppermute | solution.py:534
  50.5 1.6 %shard_map.115 = f32[64,256]{1,0:T(8,128)S(1)} custom-call(f32[64,256]{1,0:T(8,128)S(1)} %sub.17.v_ref.v2.refs_0_, f32[64,256]{1,0:T(8,128)S(1)} %collective-permute-done.15.raw_ref, f32[64,256]{1,0:T(8,128)S(1)} %get-tuple-element.101.sent_ref, f32[64,256]{1,0:T(8,128)S(1)} %get-tuple-element.102.part_ref, f32[8,32,128]{2,1,0:T(8,128)S(1)} %get-tuple-element.103.gap_ref, ...), custom_call_target="tpu_custom_call" | custom-call | flops 2000000000 | bytes 262144 | tf_op jit(solution)/shard_map/pallas_call | solution.py:642
  52.3 1.6 %shard_map.117 = (f32[64,256]{1,0:T(8,128)S(1)}, f32[64,256]{1,0:T(8,128)S(1)}, f32[8,32,128]{2,1,0:T(8,128)S(1)}) custom-call(f32[64,256]{1,0:T(8,128)S(1)} %sub.18.v3.v_ref, bf16[256,256]{1,0:T(8,128)(2,1)S(1)} %get-tuple-element.84.refs_0_.refs_3_, bf16[512,256]{1,0:T(8,128)(2,1)S(1)} %get-tuple-element.73.refs_3_.refs_1_.refs_4_, ...), custom_call_target="tpu_custom_call" | custom-call | flops 2000000000 | bytes 262144 | tf_op jit(solution)/shard_map/pallas_call | solution.py:639
  53.9 1.5 %collective-permute-start.18 = (f32[64,256]{1,0:T(8,128)S(1)}, f32[64,256]{1,0:T(8,128)S(1)}, u32[]{:S(2)}, u32[]{:S(2)}) collective-permute-start(f32[64,256]{1,0:T(8,128)S(1)} %get-tuple-element.107), channel_id=1, source_target_pairs={{0,2},{1,3},{226,224},{227,225},{4,6},{5,7},{230,228},{231,229},{8... | collective-permute-start | bytes 196616 | tf_op jit(solution)/shard_map/ppermute | solution.py:534
  56.5 1.6 %shard_map.118 = f32[64,256]{1,0:T(8,128)S(1)} custom-call(f32[64,256]{1,0:T(8,128)S(1)} %sub.18.v3.v_ref, f32[64,256]{1,0:T(8,128)S(1)} %collective-permute-done.17.raw_ref, f32[64,256]{1,0:T(8,128)S(1)} %get-tuple-element.104.sent_ref, f32[64,256]{1,0:T(8,128)S(1)} %get-tuple-element.105.part_ref, f32[8,32,128]{2,1,0:T(8,128)S(1)} %get-tuple-element.106.gap_ref, ...), custom_call_target="tpu_custom_call" | custom-call | flops 2000000000 | bytes 262144 | tf_op jit(solution)/shard_map/pallas_call | solution.py:642
  59.0 2.3 %collective-permute-start.19 = (f32[1,128]{1,0:T(1,128)S(1)}, f32[1,128]{1,0:T(1,128)S(1)}, u32[]{:S(2)}, u32[]{:S(2)}) collective-permute-start(f32[1,128]{1,0:T(1,128)S(1)} %get-tuple-element.108), channel_id=1, source_target_pairs={{0,1},{1,0},{2,3},{3,2},{4,5},{5,4},{6,7},{7,6},{8,9},{9,8},{10,11... | collective-permute-start | bytes 1544 | tf_op jit(solution)/shard_map/ppermute | solution.py:538
  62.3 19.0 %all_to_all.8 = f32[32,1,128]{2,1,0:T(1,128)S(1)} all-to-all(f32[32,1,128]{2,1,0:T(1,128)S(1)} %broadcast_in_dim.2), channel_id=1, replica_groups=mesh['sec'=32,'tile'=8] {'sec'}, dimensions={0} | all-to-all | bytes 32768 | tf_op jit(solution)/shard_map/all_to_all | solution.py:656
  81.3 1.4 %shard_map.120 = (f32[2,32,64]{2,1,0:T(8,128)S(1)}, f32[2,32,64]{2,1,0:T(8,128)S(1)}) custom-call(f32[32,128]{1,0:T(8,128)S(1)} %bitcast.14, f32[3,64,128]{2,1,0:T(8,128)S(1)} %collective-permute-done.20.slice_ref), custom_call_target="tpu_custom_call" | custom-call | flops 2000000000 | bytes 262144 | tf_op jit(solution)/shard_map/pallas_call | solution.py:657
  82.6 1.8 %collective-permute-start.21 = (f32[2,32,64]{2,1,0:T(8,128)S(1)}, f32[2,32,64]{2,1,0:T(8,128)S(1)}, u32[]{:S(2)}, u32[]{:S(2)}) collective-permute-start(f32[2,32,64]{2,1,0:T(8,128)S(1)} %get-tuple-element.111), channel_id=1, source_target_pairs={{0,1},{1,0},{2,3},{3,2},{4,5},{5,4},{6,7},{7,6},{8,9},{9,8},{10,11... | collective-permute-start | bytes 49160 | tf_op jit(solution)/shard_map/ppermute | solution.py:538
  (49 shorter events, 10.8 us)
Async XLA Ops:
  2.3 11.5 %collective-permute-start.2 = (f32[264,128]{1,0:T(8,128)}, f32[264,128]{1,0:T(8,128)S(1)}, u32[]{:S(2)}, u32[]{:S(2)}) collective-permute-start(f32[264,128]{1,0:T(8,128)} %shard_map.104), channel_id=1, source_target_pairs={{0,230},{1,231},{2,0},{3,1},{4,226},{5,227},{6,4},{7,5},{8,238},{9... | collective-permute-start | bytes 405512 | tf_op jit(solution)/shard_map/ppermute | solution.py:549
  11.3 10.9 %collective-permute-start.3 = (f32[264,128]{1,0:T(8,128)}, f32[264,128]{1,0:T(8,128)S(1)}, u32[]{:S(2)}, u32[]{:S(2)}) collective-permute-start(f32[264,128]{1,0:T(8,128)} %shard_map.104), channel_id=1, source_target_pairs={{0,4},{1,5},{2,230},{3,231},{4,0},{5,1},{6,226},{7,227},{8,12},{9,... | collective-permute-start | bytes 405512 | tf_op jit(solution)/shard_map/ppermute | solution.py:549
  11.6 11.4 %collective-permute-start = (f32[264,128]{1,0:T(8,128)}, f32[264,128]{1,0:T(8,128)S(1)}, u32[]{:S(2)}, u32[]{:S(2)}) collective-permute-start(f32[264,128]{1,0:T(8,128)} %shard_map.104), channel_id=1, source_target_pairs={{0,226},{1,227},{2,4},{3,5},{4,230},{5,231},{6,0},{7,1},{8,234},{9... | collective-permute-start | bytes 405512 | tf_op jit(solution)/shard_map/ppermute | solution.py:549
  12.2 10.9 %collective-permute-start.1 = (f32[264,128]{1,0:T(8,128)}, f32[264,128]{1,0:T(8,128)S(1)}, u32[]{:S(2)}, u32[]{:S(2)}) collective-permute-start(f32[264,128]{1,0:T(8,128)} %shard_map.104), channel_id=1, source_target_pairs={{0,0},{1,1},{2,226},{3,227},{4,4},{5,5},{6,230},{7,231},{8,8},{9,9... | collective-permute-start | bytes 405512 | tf_op jit(solution)/shard_map/ppermute | solution.py:549
  13.8 10.2 %collective-permute-start.6 = (f32[264,128]{1,0:T(8,128)S(1)}, f32[264,128]{1,0:T(8,128)S(1)}, u32[]{:S(2)}, u32[]{:S(2)}) collective-permute-start(f32[264,128]{1,0:T(8,128)S(1)} %collective-permute-done.2.refs_0_), channel_id=1, source_target_pairs={{0,1},{1,0},{2,3},{3,2},{4,5},{5,4},{6,7},{7,6},{8,9},{9,8},{10,11... | collective-permute-start | bytes 405512 | tf_op jit(solution)/shard_map/ppermute | solution.py:538
  22.2 1.9 %collective-permute-start.7 = (f32[264,128]{1,0:T(8,128)S(1)}, f32[264,128]{1,0:T(8,128)S(1)}, u32[]{:S(2)}, u32[]{:S(2)}) collective-permute-start(f32[264,128]{1,0:T(8,128)S(1)} %collective-permute-done.3.refs_1_), channel_id=1, source_target_pairs={{0,1},{1,0},{2,3},{3,2},{4,5},{5,4},{6,7},{7,6},{8,9},{9,8},{10,11... | collective-permute-start | bytes 405512 | tf_op jit(solution)/shard_map/ppermute | solution.py:538
  23.1 2.6 %collective-permute-start.4 = (f32[264,128]{1,0:T(8,128)S(1)}, f32[264,128]{1,0:T(8,128)S(1)}, u32[]{:S(2)}, u32[]{:S(2)}) collective-permute-start(f32[264,128]{1,0:T(8,128)S(1)} %collective-permute-done.refs_2_), channel_id=1, source_target_pairs={{0,1},{1,0},{2,3},{3,2},{4,5},{5,4},{6,7},{7,6},{8,9},{9,8},{10,11... | collective-permute-start | bytes 405512 | tf_op jit(solution)/shard_map/ppermute | solution.py:538
  24.1 1.6 %collective-permute-start.5 = (f32[264,128]{1,0:T(8,128)S(1)}, f32[264,128]{1,0:T(8,128)S(1)}, u32[]{:S(2)}, u32[]{:S(2)}) collective-permute-start(f32[264,128]{1,0:T(8,128)S(1)} %collective-permute-done.1.refs_3_), channel_id=1, source_target_pairs={{0,1},{1,0},{2,3},{3,2},{4,5},{5,4},{6,7},{7,6},{8,9},{9,8},{10,11... | collective-permute-start | bytes 405512 | tf_op jit(solution)/shard_map/ppermute | solution.py:538
  26.6 6.0 %collective-permute-start.8 = (f32[64,256]{1,0:T(8,128)S(1)}, f32[64,256]{1,0:T(8,128)S(1)}, u32[]{:S(2)}, u32[]{:S(2)}) collective-permute-start(f32[64,256]{1,0:T(8,128)S(1)} %get-tuple-element.69.sent_ref), channel_id=1, source_target_pairs={{0,2},{1,3},{226,224},{227,225},{4,6},{5,7},{230,228},{231,229},{8... | collective-permute-start | bytes 196616 | tf_op jit(solution)/shard_map/ppermute | solution.py:534
  30.4 8.6 %collective-permute-start.9 = (f32[64,256]{1,0:T(8,128)S(1)}, f32[64,256]{1,0:T(8,128)S(1)}, u32[]{:S(2)}, u32[]{:S(2)}) collective-permute-start(f32[64,256]{1,0:T(8,128)S(1)} %get-tuple-element.68), channel_id=1, source_target_pairs={{0,8},{1,9},{226,234},{227,235},{4,12},{5,13},{230,238},{231,239},... | collective-permute-start | bytes 196616 | tf_op jit(solution)/shard_map/ppermute | solution.py:534
  32.7 4.5 %collective-permute-start.10 = (f32[2,64,256]{2,1,0:T(8,128)S(1)}, f32[2,64,256]{2,1,0:T(8,128)S(1)}, u32[]{:S(2)}, u32[]{:S(2)}) collective-permute-start(f32[2,64,256]{2,1,0:T(8,128)S(1)} %get-tuple-element.97), channel_id=1, source_target_pairs={{0,2},{1,3},{226,224},{227,225},{4,6},{5,7},{230,228},{231,229},{8... | collective-permute-start | bytes 393224 | tf_op jit(solution)/shard_map/ppermute | solution.py:534
  36.0 5.1 %collective-permute-start.12 = (f32[64,256]{1,0:T(8,128)S(1)}, f32[64,256]{1,0:T(8,128)S(1)}, u32[]{:S(2)}, u32[]{:S(2)}) collective-permute-start(f32[64,256]{1,0:T(8,128)S(1)} %get-tuple-element.98.sent_ref), channel_id=1, source_target_pairs={{0,2},{1,3},{226,224},{227,225},{4,6},{5,7},{230,228},{231,229},{8... | collective-permute-start | bytes 196616 | tf_op jit(solution)/shard_map/ppermute | solution.py:534
  37.2 3.5 %collective-permute-start.11 = (f32[2,64,256]{2,1,0:T(8,128)S(1)}, f32[2,64,256]{2,1,0:T(8,128)S(1)}, u32[]{:S(2)}, u32[]{:S(2)}) collective-permute-start(f32[2,64,256]{2,1,0:T(8,128)S(1)} %add.13.mine_ref.refs_1_), channel_id=1, source_target_pairs={{0,1},{1,0},{2,3},{3,2},{4,5},{5,4},{6,7},{7,6},{8,9},{9,8},{10,11... | collective-permute-start | bytes 393224 | tf_op jit(solution)/shard_map/ppermute | solution.py:538
  40.7 4.7 %collective-permute-start.13 = (f32[64,256]{1,0:T(8,128)S(1)}, f32[64,256]{1,0:T(8,128)S(1)}, u32[]{:S(2)}, u32[]{:S(2)}) collective-permute-start(f32[64,256]{1,0:T(8,128)S(1)} %shard_map.111), channel_id=1, source_target_pairs={{0,8},{1,9},{226,234},{227,235},{4,12},{5,13},{230,238},{231,239},... | collective-permute-start | bytes 196616 | tf_op jit(solution)/shard_map/ppermute | solution.py:534
  42.6 4.5 %collective-permute-start.14 = (f32[64,256]{1,0:T(8,128)S(1)}, f32[64,256]{1,0:T(8,128)S(1)}, u32[]{:S(2)}, u32[]{:S(2)}) collective-permute-start(f32[64,256]{1,0:T(8,128)S(1)} %get-tuple-element.101.sent_ref), channel_id=1, source_target_pairs={{0,2},{1,3},{226,224},{227,225},{4,6},{5,7},{230,228},{231,229},{8... | collective-permute-start | bytes 196616 | tf_op jit(solution)/shard_map/ppermute | solution.py:534
  47.1 3.4 %collective-permute-start.15 = (f32[64,256]{1,0:T(8,128)S(1)}, f32[64,256]{1,0:T(8,128)S(1)}, u32[]{:S(2)}, u32[]{:S(2)}) collective-permute-start(f32[64,256]{1,0:T(8,128)S(1)} %shard_map.113), channel_id=1, source_target_pairs={{0,8},{1,9},{226,234},{227,235},{4,12},{5,13},{230,238},{231,239},... | collective-permute-start | bytes 196616 | tf_op jit(solution)/shard_map/ppermute | solution.py:534
  48.8 3.5 %collective-permute-start.16 = (f32[64,256]{1,0:T(8,128)S(1)}, f32[64,256]{1,0:T(8,128)S(1)}, u32[]{:S(2)}, u32[]{:S(2)}) collective-permute-start(f32[64,256]{1,0:T(8,128)S(1)} %get-tuple-element.104.sent_ref), channel_id=1, source_target_pairs={{0,2},{1,3},{226,224},{227,225},{4,6},{5,7},{230,228},{231,229},{8... | collective-permute-start | bytes 196616 | tf_op jit(solution)/shard_map/ppermute | solution.py:534
  52.1 4.3 %collective-permute-start.17 = (f32[64,256]{1,0:T(8,128)S(1)}, f32[64,256]{1,0:T(8,128)S(1)}, u32[]{:S(2)}, u32[]{:S(2)}) collective-permute-start(f32[64,256]{1,0:T(8,128)S(1)} %shard_map.115), channel_id=1, source_target_pairs={{0,8},{1,9},{226,234},{227,235},{4,12},{5,13},{230,238},{231,239},... | collective-permute-start | bytes 196616 | tf_op jit(solution)/shard_map/ppermute | solution.py:534
  53.9 4.3 %collective-permute-start.18 = (f32[64,256]{1,0:T(8,128)S(1)}, f32[64,256]{1,0:T(8,128)S(1)}, u32[]{:S(2)}, u32[]{:S(2)}) collective-permute-start(f32[64,256]{1,0:T(8,128)S(1)} %get-tuple-element.107), channel_id=1, source_target_pairs={{0,2},{1,3},{226,224},{227,225},{4,6},{5,7},{230,228},{231,229},{8... | collective-permute-start | bytes 196616 | tf_op jit(solution)/shard_map/ppermute | solution.py:534
  59.0 3.2 %collective-permute-start.19 = (f32[1,128]{1,0:T(1,128)S(1)}, f32[1,128]{1,0:T(1,128)S(1)}, u32[]{:S(2)}, u32[]{:S(2)}) collective-permute-start(f32[1,128]{1,0:T(1,128)S(1)} %get-tuple-element.108), channel_id=1, source_target_pairs={{0,1},{1,0},{2,3},{3,2},{4,5},{5,4},{6,7},{7,6},{8,9},{9,8},{10,11... | collective-permute-start | bytes 1544 | tf_op jit(solution)/shard_map/ppermute | solution.py:538
  61.3 20.0 %collective-permute-start.20 = (f32[3,64,128]{2,1,0:T(8,128)S(1)}, f32[3,64,128]{2,1,0:T(8,128)S(1)}, u32[]{:S(2)}, u32[]{:S(2)}) collective-permute-start(f32[3,64,128]{2,1,0:T(8,128)S(1)} %get-tuple-element.109), channel_id=1, source_target_pairs={{0,0},{1,1},{226,2},{227,3},{4,4},{5,5},{230,6},{231,7},{8,8},{9,9... | collective-permute-start | bytes 294920 | tf_op jit(solution)/shard_map/ppermute | solution.py:558
  82.6 2.7 %collective-permute-start.21 = (f32[2,32,64]{2,1,0:T(8,128)S(1)}, f32[2,32,64]{2,1,0:T(8,128)S(1)}, u32[]{:S(2)}, u32[]{:S(2)}) collective-permute-start(f32[2,32,64]{2,1,0:T(8,128)S(1)} %get-tuple-element.111), channel_id=1, source_target_pairs={{0,1},{1,0},{2,3},{3,2},{4,5},{5,4},{6,7},{7,6},{8,9},{9,8},{10,11... | collective-permute-start | bytes 49160 | tf_op jit(solution)/shard_map/ppermute | solution.py:538

commit v11 on v10

--- a/solution.py
+++ b/solution.py
@@ -399,25 +399,25 @@
     out_ref[...] = dots([r[...] for r in (v0, v1, v2, v3)], [p for p in PAIRS if p[1] < 4])
 
 
-def last_kernel(row_ref, v0, v1, v2, v3, v4, out_ref, slice_ref):
+def slice_kernel(v0, v1, v2, v3, v4, even_ref, odd_ref):
     fields = [r[...] for r in (v0, v1, v2, v3, v4)]
     y = lax.axis_index("tile") >> 1
+    low = lax.broadcasted_iota(jnp.int32, (64, 128), 1) < 64
     for k in range(3):
-        sides = []
-        for m in (2 * k, 2 * k + 1):
-            if m < 5:
-                x = jnp.where(y >= 2, fields[m][:, 128:], fields[m][:, :128])
-                sides.append((x, pltpu.roll(x, 64, 1)))
-            else:
-                sides.append((jnp.zeros((64, 128), F32),) * 2)
-        left = jnp.where((y & 1) == 0, sides[0][0], sides[0][1])
-        right = jnp.where((y & 1) == 0, sides[1][1], sides[1][0])
-        lane = lax.broadcasted_iota(jnp.int32, (64, 128), 1)
-        slice_ref[k] = jnp.where(lane < 64, left, right)
-    out_ref[...] = row_ref[...] + dots(fields, [p for p in PAIRS if p[1] == 4])
-
-
-def finish_kernel(gram_ref, slice_ref, mine_ref, other_ref):
+        left = jnp.where(y >= 2, fields[2 * k][:, 128:], fields[2 * k][:, :128])
+        if k < 2:
+            right = jnp.where(y >= 2, fields[2 * k + 1][:, 128:], fields[2 * k + 1][:, :128])
+        else:
+            right = jnp.zeros((64, 128), F32)
+        even_ref[k] = jnp.where(low, left, pltpu.roll(right, 64, 1))
+        odd_ref[k] = jnp.where(low, pltpu.roll(left, 64, 1), right)
+
+
+def last_kernel(row_ref, v0, v1, v2, v3, v4, out_ref):
+    out_ref[...] = row_ref[...] + dots([r[...] for r in (v0, v1, v2, v3, v4)], [p for p in PAIRS if p[1] == 4])
+
+
+def finish_kernel(gram_ref, even_ref, odd_ref, mine_ref, other_ref):
     rows = gram_ref[...]
     acc = dd_add((rows, pltpu.roll(rows, 112, 1)), (pltpu.roll(rows, 96, 1), pltpu.roll(rows, 80, 1)))
     n = 32
@@ -477,11 +477,13 @@
             norm = new
     lane = lax.broadcasted_iota(jnp.int32, (64, 128), 1)
 
+    odd = ((lax.axis_index("tile") >> 1) & 1) == 1
+
     def combine(coefs):
         total = jnp.zeros((64, 128), F32)
         flat = [c[0][0:1, 0:1] for c in coefs] + [jnp.zeros((1, 1), F32)] * (6 - len(coefs))
         for k in range(3):
-            total = total + jnp.where(lane < 64, flat[2 * k], flat[2 * k + 1]) * slice_ref[k]
+            total = total + jnp.where(lane < 64, flat[2 * k], flat[2 * k + 1]) * jnp.where(odd, odd_ref[k], even_ref[k])
         return total + pltpu.roll(total, 64, 1)
 
     core = lax.axis_index("tile") & 1
@@ -549,12 +551,16 @@
     return lax.ppermute(block, ("sec", "tile"), route)
 
 
-def returned(block):
+def returned(block, up):
     sections = lax.axis_size("sec")
     route = []
     for section in range(sections):
-        for tile in range(2 * CHIPS):
-            route.append((seat(section, tile // 2, sections) * 8 + tile, section * 8 + tile))
+        for y in range(CHIPS):
+            for core in range(2):
+                if y % 2 == 0:
+                    route.append((seat(section, y, sections) * 8 + 2 * y + core, section * 8 + 2 * (y + up) + core))
+                else:
+                    route.append((section * 8 + 2 * y + core, section * 8 + 2 * (y - up) + core))
     return lax.ppermute(block, ("sec", "tile"), route)
 
 
@@ -650,11 +656,13 @@
             raw = shifted(partial, 1)
         fields.append(partial - above)
     row = call(dots_kernel, [((1, 128), F32)], 4, us=1.0)(*fields[:4])[0]
-    row, slices = call(last_kernel, [((1, 128), F32), ((3, 64, 128), F32)], 6, us=1.0)(row, *fields)
-    slices = returned(slices)
+    even, odd = call(slice_kernel, [((3, 64, 128), F32)] * 2, 5, us=0.1)(*fields)
+    even = returned(even, 0)
+    odd = returned(odd, 1)
+    row = call(last_kernel, [((1, 128), F32)], 6, us=1.0)(row, *fields)[0]
     row = row + jnp.roll(swapped(row), 32, 1)
     gram = lax.all_to_all(jnp.broadcast_to(row, (32, 128)), "sec", 0, 0, tiled=True)
-    mine, other = call(finish_kernel, [((2, 32, 64), F32), ((2, 32, 64), F32)], 2)(gram, slices)
+    mine, other = call(finish_kernel, [((2, 32, 64), F32), ((2, 32, 64), F32)], 3)(gram, even, odd)
     other = swapped(other)
     first = jnp.where(core == 0, mine, other)
     last = jnp.where(core == 0, other, mine)

time: 86.9 us -> 86.6 us (level)
  starting transfers between devices: 39 us -> 40.6 us
  blocking collectives: 19 us -> 17.7 us
    ppermute x1 -> x2, starting transfers between devices: 0.65 us -> 2.21 us  [returned(): return lax.ppermute(block, ('sec', 'tile'), route)]
    all_to_all x1, blocking collectives: 19 us -> 17.7 us  [on_device(): lax.all_to_all(jnp.broadcast_to(row, (32, 128)), 'sec', 0, 0, tiled=True)]
    pallas_call x2 -> x3, Pallas kernels: 2.18 us -> 2.3 us  [the longest x1 1.36 us: on_device(): call(finish_kernel, [((2, 32, 64), F32), ((2, 32, 64), F32)], 3)]
  transfers between devices with their start and end apart: 22 -> 23, of which waited for: 5 -> 4; matrix products, arithmetic and copies ran while one was open for 0% -> 0% of each run, Pallas kernels for 22% -> 22%
where the time goes in v11:
time: 86.6 us; the launch traced here: 86.2 us
  starting transfers between devices  40.6 us (47%)
  Pallas kernels  23.4 us (27%)
  blocking collectives  17.7 us (20%)
  waiting for transfers between devices  2.76 us (3%)
  between operations  0.88 us (1%)
    all_to_all x1, blocking collectives, on_device(): lax.all_to_all(jnp.broadcast_to(row, (32, 128)), 'sec', 0, 0, tiled=True)  17.7 us
    ppermute x7, starting transfers between devices, swapped(): return lax.ppermute(block, 'tile', [(i, i ^ 1) for i in range(8)])  15.4 us
    ppermute x10, starting transfers between devices, shifted(): return lax.ppermute(block, ('sec', 'tile'), route)  11.6 us
    ppermute x4, starting transfers between devices, dealt(): return lax.ppermute(block, ('sec', 'tile'), route)  11.4 us
    pallas_call x4, Pallas kernels, on_device(): call(functools.partial(down_kernel, back=k > 0), [field], 6 + len(more) +...  6.45 us
    pallas_call x4, Pallas kernels, on_device(): call(up_kernel, [field, field, ((8, 32, 128), F32)], 1 + len(tables))  6.3 us
    pallas_call x3, Pallas kernels, on_device(): call(functools.partial(tables_kernel, blocks=blocks, add=len(sums) > 0),...  3.33 us
    ppermute x2, starting transfers between devices, returned(): return lax.ppermute(block, ('sec', 'tile'), route)  2.21 us
  transfers between devices with their start and end apart: 23, of which 4 were waited for; matrix products, arithmetic and copies ran while one was open for 0% of the time, Pallas kernels for 22%

profile of v11, /device:TPU:1, one launch (start us, length us, event | category | flops | bytes accessed | tf_op | source)
XLA Modules:
  0.0 86.2 jit_solution(13886554171321276274)
XLA Ops:
  0.6 1.7 %shard_map.104 = f32[264,128]{1,0:T(8,128)} custom-call(s32[1,128]{1,0:T(1,128)} %bitcast.18, s32[1,128]{1,0:T(1,128)} %bitcast.19, s32[1,128]{1,0:T(1,128)} %bitcast.20, s32[32,128]{1,0:T(8,128)} %cell1_hbm.1, s32[32,128]{1,0:T(8,128)} %cell2_hbm.1, f32[2,32,128]{2,1,0:T(8,128)} %frac1_hbm.1, f32[2,32,128]{2,1,0:T(8,128)} %frac2_hbm.1, ...), custom_call_target="tpu_custom_call" | custom-call | flops 2000000000 | bytes 262144 | tf_op jit(solution)/shard_map/pallas_call | solution.py:574
  2.3 8.9 %collective-permute-start.2 = (f32[264,128]{1,0:T(8,128)}, f32[264,128]{1,0:T(8,128)S(1)}, u32[]{:S(2)}, u32[]{:S(2)}) collective-permute-start(f32[264,128]{1,0:T(8,128)} %shard_map.104), channel_id=1, source_target_pairs={{0,230},{1,231},{2,0},{3,1},{4,226},{5,227},{6,4},{7,5},{8,238},{9... | collective-permute-start | bytes 405512 | tf_op jit(solution)/shard_map/ppermute | solution.py:551
  12.2 1.6 %collective-permute-start.1 = (f32[264,128]{1,0:T(8,128)}, f32[264,128]{1,0:T(8,128)S(1)}, u32[]{:S(2)}, u32[]{:S(2)}) collective-permute-start(f32[264,128]{1,0:T(8,128)} %shard_map.104), channel_id=1, source_target_pairs={{0,0},{1,1},{2,226},{3,227},{4,4},{5,5},{6,230},{7,231},{8,8},{9,9... | collective-permute-start | bytes 405512 | tf_op jit(solution)/shard_map/ppermute | solution.py:551
  13.8 8.3 %collective-permute-start.6 = (f32[264,128]{1,0:T(8,128)S(1)}, f32[264,128]{1,0:T(8,128)S(1)}, u32[]{:S(2)}, u32[]{:S(2)}) collective-permute-start(f32[264,128]{1,0:T(8,128)S(1)} %collective-permute-done.2.refs_0_), channel_id=1, source_target_pairs={{0,1},{1,0},{2,3},{3,2},{4,5},{5,4},{6,7},{7,6},{8,9},{9,8},{10,11... | collective-permute-start | bytes 405512 | tf_op jit(solution)/shard_map/ppermute | solution.py:540
  24.1 1.6 %shard_map.106 = (f32[4,2,8,32,128]{4,3,2,1,0:T(8,128)S(1)}, f32[4,2,8,32,128]{4,3,2,1,0:T(8,128)S(1)}, f32[4,2,32,128]{3,2,1,0:T(8,128)S(1)}, s32[4,2,32,128]{3...) custom-call(f32[264,128]{1,0:T(8,128)S(1)} %collective-permute-done., ...), custom_call_target="tpu_custom_call" | custom-call | flops 1600000000 | bytes 262144 | tf_op jit(solution)/shard_map/pallas_call | solution.py:612
  26.6 3.8 %collective-permute-start.8 = (f32[64,256]{1,0:T(8,128)S(1)}, f32[64,256]{1,0:T(8,128)S(1)}, u32[]{:S(2)}, u32[]{:S(2)}) collective-permute-start(f32[64,256]{1,0:T(8,128)S(1)} %get-tuple-element.69.sent_ref), channel_id=1, source_target_pairs={{0,2},{1,3},{226,224},{227,225},{4,6},{5,7},{230,228},{231,229},{8... | collective-permute-start | bytes 196616 | tf_op jit(solution)/shard_map/ppermute | solution.py:536
  30.4 2.2 %shard_map.108 = (f32[2,64,256]{2,1,0:T(8,128)S(1)}, f32[2,64,256]{2,1,0:T(8,128)S(1)}) custom-call(f32[2,2,8,32,128]{4,3,2,1,0:T(8,128)S(1)} %get-tuple-element.70.refs_0_.refs_2_.refs_5_, f32[2,2,8,32,128]{4,3,2,1,0:T(8,128)S(1)} %get-tuple-element.71.refs_1_.refs_3_.refs_6_, f32[2,32,128]{2,1,0:T(8,128)S(1)} %get-tuple-element.72.refs_2_.refs_6_.refs_9_, ...), custom_call_target="tpu_custom_call" | custom-call | flops 4000000000 | bytes 262144 | tf_op jit(solution)/shard_map/pallas_call | solution.py:635
  32.7 1.7 %collective-permute-start.10 = (f32[2,64,256]{2,1,0:T(8,128)S(1)}, f32[2,64,256]{2,1,0:T(8,128)S(1)}, u32[]{:S(2)}, u32[]{:S(2)}) collective-permute-start(f32[2,64,256]{2,1,0:T(8,128)S(1)} %get-tuple-element.97), channel_id=1, source_target_pairs={{0,2},{1,3},{226,224},{227,225},{4,6},{5,7},{230,228},{231,229},{8... | collective-permute-start | bytes 393224 | tf_op jit(solution)/shard_map/ppermute | solution.py:536
  34.4 1.6 %shard_map.109 = (f32[64,256]{1,0:T(8,128)S(1)}, f32[64,256]{1,0:T(8,128)S(1)}, f32[8,32,128]{2,1,0:T(8,128)S(1)}) custom-call(f32[64,256]{1,0:T(8,128)S(1)} %sub.15.v_ref.refs_0_.v0, bf16[256,256]{1,0:T(8,128)(2,1)S(1)} %get-tuple-element.84.refs_0_.refs_3_, bf16[512,256]{1,0:T(8,128)(2,1)S(1)} %get-tuple-element.73.refs_3_.refs_1_.refs_4_, ...), custom_call_target="tpu_custom_call" | custom-call | flops 2000000000 | bytes 262144 | tf_op jit(solution)/shard_map/pallas_call | solution.py:645
  37.2 1.9 %collective-permute-start.11 = (f32[2,64,256]{2,1,0:T(8,128)S(1)}, f32[2,64,256]{2,1,0:T(8,128)S(1)}, u32[]{:S(2)}, u32[]{:S(2)}) collective-permute-start(f32[2,64,256]{2,1,0:T(8,128)S(1)} %add.13.mine_ref.refs_1_), channel_id=1, source_target_pairs={{0,1},{1,0},{2,3},{3,2},{4,5},{5,4},{6,7},{7,6},{8,9},{9,8},{10,11... | collective-permute-start | bytes 393224 | tf_op jit(solution)/shard_map/ppermute | solution.py:540
  39.1 1.6 %shard_map.110.part_ref = f32[64,256]{1,0:T(8,128)S(1)} custom-call(f32[64,256]{1,0:T(8,128)S(1)} %sub.15.v_ref.refs_0_.v0, f32[64,256]{1,0:T(8,128)S(1)} %collective-permute-done.9.raw_ref, f32[64,256]{1,0:T(8,128)S(1)} %get-tuple-element.69.sent_ref, f32[64,256]{1,0:T(8,128)S(1)} %get-tuple-element.93.part_ref, ...), custom_call_target="tpu_custom_call" | custom-call | flops 2000000000 | bytes 262144 | tf_op jit(solution)/shard_map/pallas_call | solution.py:648
  41.1 1.6 %shard_map.112 = (f32[64,256]{1,0:T(8,128)S(1)}, f32[64,256]{1,0:T(8,128)S(1)}, f32[8,32,128]{2,1,0:T(8,128)S(1)}) custom-call(f32[64,256]{1,0:T(8,128)S(1)} %sub.16.v_ref.refs_0_.v1, bf16[256,256]{1,0:T(8,128)(2,1)S(1)} %get-tuple-element.84.refs_0_.refs_3_, bf16[512,256]{1,0:T(8,128)(2,1)S(1)} %get-tuple-element.73.refs_3_.refs_1_.refs_4_, ...), custom_call_target="tpu_custom_call" | custom-call | flops 2000000000 | bytes 262144 | tf_op jit(solution)/shard_map/pallas_call | solution.py:645
  42.6 2.1 %collective-permute-start.14 = (f32[64,256]{1,0:T(8,128)S(1)}, f32[64,256]{1,0:T(8,128)S(1)}, u32[]{:S(2)}, u32[]{:S(2)}) collective-permute-start(f32[64,256]{1,0:T(8,128)S(1)} %get-tuple-element.101.sent_ref), channel_id=1, source_target_pairs={{0,2},{1,3},{226,224},{227,225},{4,6},{5,7},{230,228},{231,229},{8... | collective-permute-start | bytes 196616 | tf_op jit(solution)/shard_map/ppermute | solution.py:536
  45.5 1.6 %shard_map.113 = f32[64,256]{1,0:T(8,128)S(1)} custom-call(f32[64,256]{1,0:T(8,128)S(1)} %sub.16.v_ref.refs_0_.v1, f32[64,256]{1,0:T(8,128)S(1)} %collective-permute-done.13.raw_ref, f32[64,256]{1,0:T(8,128)S(1)} %get-tuple-element.98.sent_ref, f32[64,256]{1,0:T(8,128)S(1)} %get-tuple-element.99.part_ref, f32[8,32,128]{2,1,0:T(8,128)S(1)} %get-tuple-element.100.gap_ref, ...), custom_call_target="tpu_custom_call" | custom-call | flops 2000000000 | bytes 262144 | tf_op jit(solution)/shard_map/pallas_call | solution.py:648
  47.2 1.6 %shard_map.114 = (f32[64,256]{1,0:T(8,128)S(1)}, f32[64,256]{1,0:T(8,128)S(1)}, f32[8,32,128]{2,1,0:T(8,128)S(1)}) custom-call(f32[64,256]{1,0:T(8,128)S(1)} %sub.17.v_ref.v2.refs_0_, bf16[256,256]{1,0:T(8,128)(2,1)S(1)} %get-tuple-element.84.refs_0_.refs_3_, bf16[512,256]{1,0:T(8,128)(2,1)S(1)} %get-tuple-element.73.refs_3_.refs_1_.refs_4_, ...), custom_call_target="tpu_custom_call" | custom-call | flops 2000000000 | bytes 262144 | tf_op jit(solution)/shard_map/pallas_call | solution.py:645
  48.8 1.7 %collective-permute-start.16 = (f32[64,256]{1,0:T(8,128)S(1)}, f32[64,256]{1,0:T(8,128)S(1)}, u32[]{:S(2)}, u32[]{:S(2)}) collective-permute-start(f32[64,256]{1,0:T(8,128)S(1)} %get-tuple-element.104.sent_ref), channel_id=1, source_target_pairs={{0,2},{1,3},{226,224},{227,225},{4,6},{5,7},{230,228},{231,229},{8... | collective-permute-start | bytes 196616 | tf_op jit(solution)/shard_map/ppermute | solution.py:536
  50.5 1.6 %shard_map.115 = f32[64,256]{1,0:T(8,128)S(1)} custom-call(f32[64,256]{1,0:T(8,128)S(1)} %sub.17.v_ref.v2.refs_0_, f32[64,256]{1,0:T(8,128)S(1)} %collective-permute-done.15.raw_ref, f32[64,256]{1,0:T(8,128)S(1)} %get-tuple-element.101.sent_ref, f32[64,256]{1,0:T(8,128)S(1)} %get-tuple-element.102.part_ref, f32[8,32,128]{2,1,0:T(8,128)S(1)} %get-tuple-element.103.gap_ref, ...), custom_call_target="tpu_custom_call" | custom-call | flops 2000000000 | bytes 262144 | tf_op jit(solution)/shard_map/pallas_call | solution.py:648
  52.3 1.6 %shard_map.117 = (f32[64,256]{1,0:T(8,128)S(1)}, f32[64,256]{1,0:T(8,128)S(1)}, f32[8,32,128]{2,1,0:T(8,128)S(1)}) custom-call(f32[64,256]{1,0:T(8,128)S(1)} %sub.18.v3.v_ref, bf16[256,256]{1,0:T(8,128)(2,1)S(1)} %get-tuple-element.84.refs_0_.refs_3_, bf16[512,256]{1,0:T(8,128)(2,1)S(1)} %get-tuple-element.73.refs_3_.refs_1_.refs_4_, ...), custom_call_target="tpu_custom_call" | custom-call | flops 2000000000 | bytes 262144 | tf_op jit(solution)/shard_map/pallas_call | solution.py:645
  53.9 1.5 %collective-permute-start.18 = (f32[64,256]{1,0:T(8,128)S(1)}, f32[64,256]{1,0:T(8,128)S(1)}, u32[]{:S(2)}, u32[]{:S(2)}) collective-permute-start(f32[64,256]{1,0:T(8,128)S(1)} %get-tuple-element.107), channel_id=1, source_target_pairs={{0,2},{1,3},{226,224},{227,225},{4,6},{5,7},{230,228},{231,229},{8... | collective-permute-start | bytes 196616 | tf_op jit(solution)/shard_map/ppermute | solution.py:536
  56.5 1.6 %shard_map.118 = f32[64,256]{1,0:T(8,128)S(1)} custom-call(f32[64,256]{1,0:T(8,128)S(1)} %sub.18.v3.v_ref, f32[64,256]{1,0:T(8,128)S(1)} %collective-permute-done.17.raw_ref, f32[64,256]{1,0:T(8,128)S(1)} %get-tuple-element.104.sent_ref, f32[64,256]{1,0:T(8,128)S(1)} %get-tuple-element.105.part_ref, f32[8,32,128]{2,1,0:T(8,128)S(1)} %get-tuple-element.106.gap_ref, ...), custom_call_target="tpu_custom_call" | custom-call | flops 2000000000 | bytes 262144 | tf_op jit(solution)/shard_map/pallas_call | solution.py:648
  59.0 2.3 %collective-permute-start.19 = (f32[1,128]{1,0:T(1,128)S(1)}, f32[1,128]{1,0:T(1,128)S(1)}, u32[]{:S(2)}, u32[]{:S(2)}) collective-permute-start(f32[1,128]{1,0:T(1,128)S(1)} %shard_map.119), channel_id=1, source_target_pairs={{0,1},{1,0},{2,3},{3,2},{4,5},{5,4},{6,7},{7,6},{8,9},{9,8},{10,11... | collective-permute-start | bytes 1544 | tf_op jit(solution)/shard_map/ppermute | solution.py:540
  62.1 1.5 %collective-permute-start.21 = (f32[3,64,128]{2,1,0:T(8,128)S(1)}, f32[3,64,128]{2,1,0:T(8,128)S(1)}, u32[]{:S(2)}, u32[]{:S(2)}) collective-permute-start(f32[3,64,128]{2,1,0:T(8,128)S(1)} %get-tuple-element.109), channel_id=1, source_target_pairs={{0,2},{1,3},{2,0},{3,1},{4,6},{5,7},{6,4},{7,5},{8,10},{9,11},{10,... | collective-permute-start | bytes 294920 | tf_op jit(solution)/shard_map/ppermute | solution.py:564
  63.8 17.7 %all_to_all.8 = f32[32,1,128]{2,1,0:T(1,128)S(1)} all-to-all(f32[32,1,128]{2,1,0:T(1,128)S(1)} %broadcast_in_dim.2), channel_id=1, replica_groups=mesh['sec'=32,'tile'=8] {'sec'}, dimensions={0} | all-to-all | bytes 32768 | tf_op jit(solution)/shard_map/all_to_all | solution.py:664
  82.9 1.8 %collective-permute-start.22 = (f32[2,32,64]{2,1,0:T(8,128)S(1)}, f32[2,32,64]{2,1,0:T(8,128)S(1)}, u32[]{:S(2)}, u32[]{:S(2)}) collective-permute-start(f32[2,32,64]{2,1,0:T(8,128)S(1)} %get-tuple-element.111), channel_id=1, source_target_pairs={{0,1},{1,0},{2,3},{3,2},{4,5},{5,4},{6,7},{7,6},{8,9},{9,8},{10,11... | collective-permute-start | bytes 49160 | tf_op jit(solution)/shard_map/ppermute | solution.py:540
  (52 shorter events, 12.2 us)
Async XLA Ops:
  2.3 11.5 %collective-permute-start.2 = (f32[264,128]{1,0:T(8,128)}, f32[264,128]{1,0:T(8,128)S(1)}, u32[]{:S(2)}, u32[]{:S(2)}) collective-permute-start(f32[264,128]{1,0:T(8,128)} %shard_map.104), channel_id=1, source_target_pairs={{0,230},{1,231},{2,0},{3,1},{4,226},{5,227},{6,4},{7,5},{8,238},{9... | collective-permute-start | bytes 405512 | tf_op jit(solution)/shard_map/ppermute | solution.py:551
  11.3 10.9 %collective-permute-start.3 = (f32[264,128]{1,0:T(8,128)}, f32[264,128]{1,0:T(8,128)S(1)}, u32[]{:S(2)}, u32[]{:S(2)}) collective-permute-start(f32[264,128]{1,0:T(8,128)} %shard_map.104), channel_id=1, source_target_pairs={{0,4},{1,5},{2,230},{3,231},{4,0},{5,1},{6,226},{7,227},{8,12},{9,... | collective-permute-start | bytes 405512 | tf_op jit(solution)/shard_map/ppermute | solution.py:551
  11.6 11.4 %collective-permute-start = (f32[264,128]{1,0:T(8,128)}, f32[264,128]{1,0:T(8,128)S(1)}, u32[]{:S(2)}, u32[]{:S(2)}) collective-permute-start(f32[264,128]{1,0:T(8,128)} %shard_map.104), channel_id=1, source_target_pairs={{0,226},{1,227},{2,4},{3,5},{4,230},{5,231},{6,0},{7,1},{8,234},{9... | collective-permute-start | bytes 405512 | tf_op jit(solution)/shard_map/ppermute | solution.py:551
  12.2 10.9 %collective-permute-start.1 = (f32[264,128]{1,0:T(8,128)}, f32[264,128]{1,0:T(8,128)S(1)}, u32[]{:S(2)}, u32[]{:S(2)}) collective-permute-start(f32[264,128]{1,0:T(8,128)} %shard_map.104), channel_id=1, source_target_pairs={{0,0},{1,1},{2,226},{3,227},{4,4},{5,5},{6,230},{7,231},{8,8},{9,9... | collective-permute-start | bytes 405512 | tf_op jit(solution)/shard_map/ppermute | solution.py:551
  13.8 10.2 %collective-permute-start.6 = (f32[264,128]{1,0:T(8,128)S(1)}, f32[264,128]{1,0:T(8,128)S(1)}, u32[]{:S(2)}, u32[]{:S(2)}) collective-permute-start(f32[264,128]{1,0:T(8,128)S(1)} %collective-permute-done.2.refs_0_), channel_id=1, source_target_pairs={{0,1},{1,0},{2,3},{3,2},{4,5},{5,4},{6,7},{7,6},{8,9},{9,8},{10,11... | collective-permute-start | bytes 405512 | tf_op jit(solution)/shard_map/ppermute | solution.py:540
  22.2 1.9 %collective-permute-start.7 = (f32[264,128]{1,0:T(8,128)S(1)}, f32[264,128]{1,0:T(8,128)S(1)}, u32[]{:S(2)}, u32[]{:S(2)}) collective-permute-start(f32[264,128]{1,0:T(8,128)S(1)} %collective-permute-done.3.refs_1_), channel_id=1, source_target_pairs={{0,1},{1,0},{2,3},{3,2},{4,5},{5,4},{6,7},{7,6},{8,9},{9,8},{10,11... | collective-permute-start | bytes 405512 | tf_op jit(solution)/shard_map/ppermute | solution.py:540
  23.1 2.6 %collective-permute-start.4 = (f32[264,128]{1,0:T(8,128)S(1)}, f32[264,128]{1,0:T(8,128)S(1)}, u32[]{:S(2)}, u32[]{:S(2)}) collective-permute-start(f32[264,128]{1,0:T(8,128)S(1)} %collective-permute-done.refs_2_), channel_id=1, source_target_pairs={{0,1},{1,0},{2,3},{3,2},{4,5},{5,4},{6,7},{7,6},{8,9},{9,8},{10,11... | collective-permute-start | bytes 405512 | tf_op jit(solution)/shard_map/ppermute | solution.py:540
  24.1 1.6 %collective-permute-start.5 = (f32[264,128]{1,0:T(8,128)S(1)}, f32[264,128]{1,0:T(8,128)S(1)}, u32[]{:S(2)}, u32[]{:S(2)}) collective-permute-start(f32[264,128]{1,0:T(8,128)S(1)} %collective-permute-done.1.refs_3_), channel_id=1, source_target_pairs={{0,1},{1,0},{2,3},{3,2},{4,5},{5,4},{6,7},{7,6},{8,9},{9,8},{10,11... | collective-permute-start | bytes 405512 | tf_op jit(solution)/shard_map/ppermute | solution.py:540
  26.6 6.0 %collective-permute-start.8 = (f32[64,256]{1,0:T(8,128)S(1)}, f32[64,256]{1,0:T(8,128)S(1)}, u32[]{:S(2)}, u32[]{:S(2)}) collective-permute-start(f32[64,256]{1,0:T(8,128)S(1)} %get-tuple-element.69.sent_ref), channel_id=1, source_target_pairs={{0,2},{1,3},{226,224},{227,225},{4,6},{5,7},{230,228},{231,229},{8... | collective-permute-start | bytes 196616 | tf_op jit(solution)/shard_map/ppermute | solution.py:536
  30.4 8.6 %collective-permute-start.9 = (f32[64,256]{1,0:T(8,128)S(1)}, f32[64,256]{1,0:T(8,128)S(1)}, u32[]{:S(2)}, u32[]{:S(2)}) collective-permute-start(f32[64,256]{1,0:T(8,128)S(1)} %get-tuple-element.68), channel_id=1, source_target_pairs={{0,8},{1,9},{226,234},{227,235},{4,12},{5,13},{230,238},{231,239},... | collective-permute-start | bytes 196616 | tf_op jit(solution)/shard_map/ppermute | solution.py:536
  32.7 4.5 %collective-permute-start.10 = (f32[2,64,256]{2,1,0:T(8,128)S(1)}, f32[2,64,256]{2,1,0:T(8,128)S(1)}, u32[]{:S(2)}, u32[]{:S(2)}) collective-permute-start(f32[2,64,256]{2,1,0:T(8,128)S(1)} %get-tuple-element.97), channel_id=1, source_target_pairs={{0,2},{1,3},{226,224},{227,225},{4,6},{5,7},{230,228},{231,229},{8... | collective-permute-start | bytes 393224 | tf_op jit(solution)/shard_map/ppermute | solution.py:536
  36.0 5.1 %collective-permute-start.12 = (f32[64,256]{1,0:T(8,128)S(1)}, f32[64,256]{1,0:T(8,128)S(1)}, u32[]{:S(2)}, u32[]{:S(2)}) collective-permute-start(f32[64,256]{1,0:T(8,128)S(1)} %get-tuple-element.98.sent_ref), channel_id=1, source_target_pairs={{0,2},{1,3},{226,224},{227,225},{4,6},{5,7},{230,228},{231,229},{8... | collective-permute-start | bytes 196616 | tf_op jit(solution)/shard_map/ppermute | solution.py:536
  37.2 3.5 %collective-permute-start.11 = (f32[2,64,256]{2,1,0:T(8,128)S(1)}, f32[2,64,256]{2,1,0:T(8,128)S(1)}, u32[]{:S(2)}, u32[]{:S(2)}) collective-permute-start(f32[2,64,256]{2,1,0:T(8,128)S(1)} %add.13.mine_ref.refs_1_), channel_id=1, source_target_pairs={{0,1},{1,0},{2,3},{3,2},{4,5},{5,4},{6,7},{7,6},{8,9},{9,8},{10,11... | collective-permute-start | bytes 393224 | tf_op jit(solution)/shard_map/ppermute | solution.py:540
  40.7 4.7 %collective-permute-start.13 = (f32[64,256]{1,0:T(8,128)S(1)}, f32[64,256]{1,0:T(8,128)S(1)}, u32[]{:S(2)}, u32[]{:S(2)}) collective-permute-start(f32[64,256]{1,0:T(8,128)S(1)} %shard_map.111), channel_id=1, source_target_pairs={{0,8},{1,9},{226,234},{227,235},{4,12},{5,13},{230,238},{231,239},... | collective-permute-start | bytes 196616 | tf_op jit(solution)/shard_map/ppermute | solution.py:536
  42.6 4.5 %collective-permute-start.14 = (f32[64,256]{1,0:T(8,128)S(1)}, f32[64,256]{1,0:T(8,128)S(1)}, u32[]{:S(2)}, u32[]{:S(2)}) collective-permute-start(f32[64,256]{1,0:T(8,128)S(1)} %get-tuple-element.101.sent_ref), channel_id=1, source_target_pairs={{0,2},{1,3},{226,224},{227,225},{4,6},{5,7},{230,228},{231,229},{8... | collective-permute-start | bytes 196616 | tf_op jit(solution)/shard_map/ppermute | solution.py:536
  47.1 3.4 %collective-permute-start.15 = (f32[64,256]{1,0:T(8,128)S(1)}, f32[64,256]{1,0:T(8,128)S(1)}, u32[]{:S(2)}, u32[]{:S(2)}) collective-permute-start(f32[64,256]{1,0:T(8,128)S(1)} %shard_map.113), channel_id=1, source_target_pairs={{0,8},{1,9},{226,234},{227,235},{4,12},{5,13},{230,238},{231,239},... | collective-permute-start | bytes 196616 | tf_op jit(solution)/shard_map/ppermute | solution.py:536
  48.8 3.5 %collective-permute-start.16 = (f32[64,256]{1,0:T(8,128)S(1)}, f32[64,256]{1,0:T(8,128)S(1)}, u32[]{:S(2)}, u32[]{:S(2)}) collective-permute-start(f32[64,256]{1,0:T(8,128)S(1)} %get-tuple-element.104.sent_ref), channel_id=1, source_target_pairs={{0,2},{1,3},{226,224},{227,225},{4,6},{5,7},{230,228},{231,229},{8... | collective-permute-start | bytes 196616 | tf_op jit(solution)/shard_map/ppermute | solution.py:536
  52.1 4.3 %collective-permute-start.17 = (f32[64,256]{1,0:T(8,128)S(1)}, f32[64,256]{1,0:T(8,128)S(1)}, u32[]{:S(2)}, u32[]{:S(2)}) collective-permute-start(f32[64,256]{1,0:T(8,128)S(1)} %shard_map.115), channel_id=1, source_target_pairs={{0,8},{1,9},{226,234},{227,235},{4,12},{5,13},{230,238},{231,239},... | collective-permute-start | bytes 196616 | tf_op jit(solution)/shard_map/ppermute | solution.py:536
  53.9 4.3 %collective-permute-start.18 = (f32[64,256]{1,0:T(8,128)S(1)}, f32[64,256]{1,0:T(8,128)S(1)}, u32[]{:S(2)}, u32[]{:S(2)}) collective-permute-start(f32[64,256]{1,0:T(8,128)S(1)} %get-tuple-element.107), channel_id=1, source_target_pairs={{0,2},{1,3},{226,224},{227,225},{4,6},{5,7},{230,228},{231,229},{8... | collective-permute-start | bytes 196616 | tf_op jit(solution)/shard_map/ppermute | solution.py:536
  59.0 4.7 %collective-permute-start.19 = (f32[1,128]{1,0:T(1,128)S(1)}, f32[1,128]{1,0:T(1,128)S(1)}, u32[]{:S(2)}, u32[]{:S(2)}) collective-permute-start(f32[1,128]{1,0:T(1,128)S(1)} %shard_map.119), channel_id=1, source_target_pairs={{0,1},{1,0},{2,3},{3,2},{4,5},{5,4},{6,7},{7,6},{8,9},{9,8},{10,11... | collective-permute-start | bytes 1544 | tf_op jit(solution)/shard_map/ppermute | solution.py:540
  61.4 20.1 %collective-permute-start.20 = (f32[3,64,128]{2,1,0:T(8,128)S(1)}, f32[3,64,128]{2,1,0:T(8,128)S(1)}, u32[]{:S(2)}, u32[]{:S(2)}) collective-permute-start(f32[3,64,128]{2,1,0:T(8,128)S(1)} %get-tuple-element.108), channel_id=1, source_target_pairs={{0,0},{1,1},{2,2},{3,3},{4,4},{5,5},{6,6},{7,7},{8,8},{9,9},{10,10... | collective-permute-start | bytes 294920 | tf_op jit(solution)/shard_map/ppermute | solution.py:564
  62.1 19.4 %collective-permute-start.21 = (f32[3,64,128]{2,1,0:T(8,128)S(1)}, f32[3,64,128]{2,1,0:T(8,128)S(1)}, u32[]{:S(2)}, u32[]{:S(2)}) collective-permute-start(f32[3,64,128]{2,1,0:T(8,128)S(1)} %get-tuple-element.109), channel_id=1, source_target_pairs={{0,2},{1,3},{2,0},{3,1},{4,6},{5,7},{6,4},{7,5},{8,10},{9,11},{10,... | collective-permute-start | bytes 294920 | tf_op jit(solution)/shard_map/ppermute | solution.py:564
  82.9 2.7 %collective-permute-start.22 = (f32[2,32,64]{2,1,0:T(8,128)S(1)}, f32[2,32,64]{2,1,0:T(8,128)S(1)}, u32[]{:S(2)}, u32[]{:S(2)}) collective-permute-start(f32[2,32,64]{2,1,0:T(8,128)S(1)} %get-tuple-element.111), channel_id=1, source_target_pairs={{0,1},{1,0},{2,3},{3,2},{4,5},{5,4},{6,7},{7,6},{8,9},{9,8},{10,11... | collective-permute-start | bytes 49160 | tf_op jit(solution)/shard_map/ppermute | solution.py:540

commit v12 on v11

--- a/solution.py
+++ b/solution.py
@@ -76,7 +76,7 @@
         fx = fx_ref[blk, side, ms, :]
         acc = None
         for q in range(8):
-            row = rows[8 * q : 8 * q + 8]
+            row = rows[q]
             left = jnp.take_along_axis(row, col, axis=0, mode="promise_in_bounds")
             right = jnp.take_along_axis(row, nxt, axis=0, mode="promise_in_bounds")
             term = wy_ref[blk, side, q, ms, :] * (left + fx * (right - left))
@@ -135,7 +135,7 @@
     if add:
         before_own, before_down, before_stiff = refs[:3]
         refs = refs[3:]
-    wx_ref, wy_ref, fx_ref, col_ref, live_ref, ohf_ref, ohs_ref, own_ref, down_ref, stiff_ref = refs
+    wx_ref, wy_ref, fx_ref, col_ref, live_ref, ohf_ref, ohs_ref, ids_ref, own_ref, down_ref, stiff_ref = refs
     comp = lax.axis_index("tile") & 1
     columns = [[], []]
     for blk, data_ref in enumerate(datas):
@@ -151,6 +151,8 @@
             goal.append(jnp.where(live, data_ref[pl.ds(at, 8), :], 0.0))
         first = data_ref[256, :][None, :].astype(jnp.int32)
         second = data_ref[257, :][None, :].astype(jnp.int32)
+        ids_ref[blk, 0] = jnp.broadcast_to(first, (8, 128))
+        ids_ref[blk, 1] = jnp.broadcast_to(second, (8, 128))
         ids = lax.broadcasted_iota(jnp.int32, (256, 128), 0)
         ohf_ref[:, lanes] = jnp.where(ids == first, 1.0, 0.0).astype(jnp.bfloat16)
         ohs_ref[0:256, lanes] = jnp.where(ids == second, 1.0, 0.0).astype(jnp.bfloat16)
@@ -233,28 +235,39 @@
 AT = (0, 2, 6)
 
 
-def passed(parts, hot_in, hot_out, tables, side_in, side_out, scale):
+def columns_of(fields, ids):
+    place = ids & 127
+    half = ids >> 7
+    rows = []
+    for q in range(8):
+        out = None
+        for k in range(2 * len(fields)):
+            part = fields[k // 2][8 * q : 8 * q + 8, 128 * (k % 2) : 128 * (k % 2) + 128]
+            got = jnp.take_along_axis(part, place, axis=1, mode="promise_in_bounds")
+            out = got if out is None else jnp.where(half == k, got, out)
+        rows.append(out)
+    return rows
+
+
+def passed(fields, hot_out, tables, side_in, side_out, scale):
     terms = []
     for h, blocks in enumerate(BLOCKS):
-        wx_ref, wy_ref, fx_ref, col_ref = tables[h][2:6]
+        wx_ref, wy_ref, fx_ref, col_ref, _, ids_ref = tables[h][2:8]
         columns = []
-        for start in range(0, blocks, 2):
-            stop = min(start + 2, blocks)
-            rows = merge3(jnp.dot(parts, hot_in[h][:, 128 * start : 128 * stop], preferred_element_type=F32))
-            for blk in range(start, stop):
-                at = 128 * (blk - start)
-                got = sample_block(rows[:, at : at + 128], wy_ref, fx_ref, col_ref, blk, side_in)
-                gap = scale(h, blk, got)
-                tops = load_table(wy_ref, blk, side_out)
-                tops = [[tops[q][g] * gap[g] for g in range(4)] for q in range(8)]
-                columns.append(spread_rows(tops, load_table(wx_ref, blk, side_out)))
+        for blk in range(blocks):
+            rows = columns_of(fields, ids_ref[blk, side_in])
+            got = sample_block(rows, wy_ref, fx_ref, col_ref, blk, side_in)
+            gap = scale(h, blk, got)
+            tops = load_table(wy_ref, blk, side_out)
+            tops = [[tops[q][g] * gap[g] for g in range(4)] for q in range(8)]
+            columns.append(spread_rows(tops, load_table(wx_ref, blk, side_out)))
         terms.append(split3(jnp.concatenate(columns, 1)))
     return scatter(terms, hot_out)
 
 
 def up_kernel(v_ref, *refs):
-    tables = [refs[7 * h : 7 * h + 7] for h in range(len(BLOCKS))]
-    own_ref, down_ref, gap_ref = refs[7 * len(BLOCKS) :]
+    tables = [refs[8 * h : 8 * h + 8] for h in range(len(BLOCKS))]
+    own_ref, down_ref, gap_ref = refs[8 * len(BLOCKS) :]
 
     def scale(h, blk, got):
         gap = []
@@ -264,7 +277,7 @@
             gap_ref[blk + AT[h], ms, :] = gap[g]
         return gap
 
-    forces = passed(split3(v_ref[...]), [t[0] for t in tables], [t[1] for t in tables], tables, 0, 1, scale)
+    forces = passed([v_ref[...]], [t[1] for t in tables], tables, 0, 1, scale)
     own_ref[...] = forces[:, :256]
     down_ref[...] = forces[:, 256:]
 
@@ -298,10 +311,10 @@
     if back:
         prev_ref, mine_ref, other_ref = refs[:3]
         refs = refs[3:]
-    tables = [refs[7 * h : 7 * h + 7] for h in range(len(BLOCKS))]
-    (out_ref,) = refs[7 * len(BLOCKS) :]
+    tables = [refs[8 * h : 8 * h + 8] for h in range(len(BLOCKS))]
+    (out_ref,) = refs[8 * len(BLOCKS) :]
     v = v_ref[...]
-    parts = jnp.concatenate([split3(v), split3(raw_ref[...] - sent_ref[...])], 1)
+    below_v = raw_ref[...] - sent_ref[...]
 
     def scale(h, blk, got):
         return [
@@ -309,7 +322,7 @@
             for g in range(4)
         ]
 
-    forces = passed(parts, [t[1] for t in tables], [t[0] for t in tables], tables, 1, 0, scale)
+    forces = passed([v, below_v], [t[0] for t in tables], tables, 1, 0, scale)
     node = lax.broadcasted_iota(jnp.int32, (64, 256), 0)
     right = jnp.where((node & 7) < 7, up(v, 1) - v, 0.0)
     below = jnp.where(node < 56, up(v, 8) - v, 0.0)
@@ -371,7 +384,6 @@
 
 def dots(fields, pairs):
     sub = lax.broadcasted_iota(jnp.int32, (16, 128), 0)
-    lane = lax.broadcasted_iota(jnp.int32, (16, 128), 1)
     high = jnp.zeros((16, 128), F32)
     low = jnp.zeros((16, 128), F32)
     cut = [halves(f) for f in fields]
@@ -388,15 +400,13 @@
         here = sub == PAIRS.index((i, j))
         high = jnp.where(here, wide[0], high)
         low = jnp.where(here, wide[1], low)
-    acc = (high, low)
-    for d in (64, 32, 16, 8, 4, 2, 1):
-        acc = dd_add(acc, (pltpu.roll(acc[0], d, 1), pltpu.roll(acc[1], d, 1)))
-    row = jnp.where(lane == sub, acc[0], 0.0) + jnp.where(lane == sub + 16, acc[1], 0.0)
-    return jnp.sum(row, 0, keepdims=True)
-
-
-def dots_kernel(v0, v1, v2, v3, out_ref):
-    out_ref[...] = dots([r[...] for r in (v0, v1, v2, v3)], [p for p in PAIRS if p[1] < 4])
+    return high, low
+
+
+def dots_kernel(v0, v1, v2, v3, high_ref, low_ref):
+    high, low = dots([r[...] for r in (v0, v1, v2, v3)], [p for p in PAIRS if p[1] < 4])
+    high_ref[...] = high
+    low_ref[...] = low
 
 
 def slice_kernel(v0, v1, v2, v3, v4, even_ref, odd_ref):
@@ -413,8 +423,15 @@
         odd_ref[k] = jnp.where(low, pltpu.roll(left, 64, 1), right)
 
 
-def last_kernel(row_ref, v0, v1, v2, v3, v4, out_ref):
-    out_ref[...] = row_ref[...] + dots([r[...] for r in (v0, v1, v2, v3, v4)], [p for p in PAIRS if p[1] == 4])
+def last_kernel(high_ref, low_ref, v0, v1, v2, v3, v4, out_ref):
+    sub = lax.broadcasted_iota(jnp.int32, (16, 128), 0)
+    lane = lax.broadcasted_iota(jnp.int32, (16, 128), 1)
+    high, low = dots([r[...] for r in (v0, v1, v2, v3, v4)], [p for p in PAIRS if p[1] == 4])
+    acc = (high + high_ref[...], low + low_ref[...])
+    for d in (64, 32, 16, 8, 4, 2, 1):
+        acc = dd_add(acc, (pltpu.roll(acc[0], d, 1), pltpu.roll(acc[1], d, 1)))
+    row = jnp.where(lane == sub, acc[0], 0.0) + jnp.where(lane == sub + 16, acc[1], 0.0)
+    out_ref[...] = jnp.sum(row, 0, keepdims=True)
 
 
 def finish_kernel(gram_ref, even_ref, odd_ref, mine_ref, other_ref):
@@ -619,6 +636,7 @@
                 ((blocks, 32, 128), F32),
                 ((256, 128 * blocks), bf16),
                 ((512, 128 * blocks), bf16),
+                ((blocks, 2, 8, 128), jnp.int32),
                 field,
                 field,
                 ((1, 256), F32),
@@ -626,8 +644,8 @@
             blocks + len(sums),
             us=0.4 * blocks,
         )(*datas, *sums)
-        groups.append(outs[:7])
-        sums = tuple(outs[7:])
+        groups.append(outs[:8])
+        sums = tuple(outs[8:])
     own, down, stiff = sums
     parts = [x for g in groups for x in (g[0], g[1], g[4], g[6])]
     above = shifted(down, -1)
@@ -637,8 +655,8 @@
     got = shifted(send, -1)
     fields = [own - above]
     tables = []
-    for wx, wy, fx, col, live, ohf, ohs in groups:
-        tables += [ohf, ohs, wx, wy, fx, col, live]
+    for wx, wy, fx, col, live, ohf, ohs, ids in groups:
+        tables += [ohf, ohs, wx, wy, fx, col, live, ids]
     for k in range(ITERS):
         v = fields[-1]
         sent = down
@@ -655,11 +673,11 @@
         if k < ITERS - 1:
             raw = shifted(partial, 1)
         fields.append(partial - above)
-    row = call(dots_kernel, [((1, 128), F32)], 4, us=1.0)(*fields[:4])[0]
+    begun = call(dots_kernel, [((16, 128), F32)] * 2, 4, us=1.0)(*fields[:4])
     even, odd = call(slice_kernel, [((3, 64, 128), F32)] * 2, 5, us=0.1)(*fields)
     even = returned(even, 0)
     odd = returned(odd, 1)
-    row = call(last_kernel, [((1, 128), F32)], 6, us=1.0)(row, *fields)[0]
+    row = call(last_kernel, [((1, 128), F32)], 7, us=1.0)(*begun, *fields)[0]
     row = row + jnp.roll(swapped(row), 32, 1)
     gram = lax.all_to_all(jnp.broadcast_to(row, (32, 128)), "sec", 0, 0, tiled=True)
     mine, other = call(finish_kernel, [((2, 32, 64), F32), ((2, 32, 64), F32)], 3)(gram, even, odd)

time: 86.6 us -> 86.1 us (level)
  Pallas kernels: 23.4 us -> 22 us
  transfers between devices with their start and end apart: 23 -> 23, of which waited for: 4 -> 5; matrix products, arithmetic and copies ran while one was open for 0% -> 0% of each run, Pallas kernels for 22% -> 20%
where the time goes in v12:
time: 86.1 us; the launch traced here: 85.7 us
  starting transfers between devices  41 us (48%)
  Pallas kernels  22 us (26%)
  blocking collectives  17.9 us (21%)
  waiting for transfers between devices  2.99 us (3%)
  between operations  0.88 us (1%)
    all_to_all x1, blocking collectives, on_device(): lax.all_to_all(jnp.broadcast_to(row, (32, 128)), 'sec', 0, 0, tiled=True)  17.9 us
    ppermute x7, starting transfers between devices, swapped(): return lax.ppermute(block, 'tile', [(i, i ^ 1) for i in range(8)])  15.6 us
    ppermute x10, starting transfers between devices, shifted(): return lax.ppermute(block, ('sec', 'tile'), route)  11.5 us
    ppermute x4, starting transfers between devices, dealt(): return lax.ppermute(block, ('sec', 'tile'), route)  11.4 us
    pallas_call x4, Pallas kernels, on_device(): call(functools.partial(down_kernel, back=k > 0), [field], 6 + len(more) +...  5.94 us
    pallas_call x4, Pallas kernels, on_device(): call(up_kernel, [field, field, ((8, 32, 128), F32)], 1 + len(tables))  5.94 us
    pallas_call x3, Pallas kernels, on_device(): call(functools.partial(tables_kernel, blocks=blocks, add=len(sums) > 0),...  3.32 us
    ppermute x2, starting transfers between devices, returned(): return lax.ppermute(block, ('sec', 'tile'), route)  2.47 us
  transfers between devices with their start and end apart: 23, of which 5 were waited for; matrix products, arithmetic and copies ran while one was open for 0% of the time, Pallas kernels for 20%

profile of v12, /device:TPU:1, one launch (start us, length us, event | category | flops | bytes accessed | tf_op | source)
XLA Modules:
  0.0 85.7 jit_solution(13267456241376662344)
XLA Ops:
  0.6 1.7 %shard_map.104 = f32[264,128]{1,0:T(8,128)} custom-call(s32[1,128]{1,0:T(1,128)} %bitcast.18, s32[1,128]{1,0:T(1,128)} %bitcast.19, s32[1,128]{1,0:T(1,128)} %bitcast.20, s32[32,128]{1,0:T(8,128)} %cell1_hbm.1, s32[32,128]{1,0:T(8,128)} %cell2_hbm.1, f32[2,32,128]{2,1,0:T(8,128)} %frac1_hbm.1, f32[2,32,128]{2,1,0:T(8,128)} %frac2_hbm.1, ...), custom_call_target="tpu_custom_call" | custom-call | flops 2000000000 | bytes 262144 | tf_op jit(solution)/shard_map/pallas_call | solution.py:591
  2.3 8.9 %collective-permute-start.2 = (f32[264,128]{1,0:T(8,128)}, f32[264,128]{1,0:T(8,128)S(1)}, u32[]{:S(2)}, u32[]{:S(2)}) collective-permute-start(f32[264,128]{1,0:T(8,128)} %shard_map.104), channel_id=1, source_target_pairs={{0,230},{1,231},{2,0},{3,1},{4,226},{5,227},{6,4},{7,5},{8,238},{9... | collective-permute-start | bytes 405512 | tf_op jit(solution)/shard_map/ppermute | solution.py:568
  12.2 1.6 %collective-permute-start.1 = (f32[264,128]{1,0:T(8,128)}, f32[264,128]{1,0:T(8,128)S(1)}, u32[]{:S(2)}, u32[]{:S(2)}) collective-permute-start(f32[264,128]{1,0:T(8,128)} %shard_map.104), channel_id=1, source_target_pairs={{0,0},{1,1},{2,226},{3,227},{4,4},{5,5},{6,230},{7,231},{8,8},{9,9... | collective-permute-start | bytes 405512 | tf_op jit(solution)/shard_map/ppermute | solution.py:568
  13.8 8.3 %collective-permute-start.6 = (f32[264,128]{1,0:T(8,128)S(1)}, f32[264,128]{1,0:T(8,128)S(1)}, u32[]{:S(2)}, u32[]{:S(2)}) collective-permute-start(f32[264,128]{1,0:T(8,128)S(1)} %collective-permute-done.2.refs_0_), channel_id=1, source_target_pairs={{0,1},{1,0},{2,3},{3,2},{4,5},{5,4},{6,7},{7,6},{8,9},{9,8},{10,11... | collective-permute-start | bytes 405512 | tf_op jit(solution)/shard_map/ppermute | solution.py:557
  24.1 1.6 %shard_map.106 = (f32[4,2,8,32,128]{4,3,2,1,0:T(8,128)S(1)}, f32[4,2,8,32,128]{4,3,2,1,0:T(8,128)S(1)}, f32[4,2,32,128]{3,2,1,0:T(8,128)S(1)}, s32[4,2,32,128]{3...) custom-call(f32[264,128]{1,0:T(8,128)S(1)} %collective-permute-done., ...), custom_call_target="tpu_custom_call" | custom-call | flops 1600000000 | bytes 262144 | tf_op jit(solution)/shard_map/pallas_call | solution.py:629
  26.6 3.8 %collective-permute-start.8 = (f32[64,256]{1,0:T(8,128)S(1)}, f32[64,256]{1,0:T(8,128)S(1)}, u32[]{:S(2)}, u32[]{:S(2)}) collective-permute-start(f32[64,256]{1,0:T(8,128)S(1)} %get-tuple-element.74.sent_ref), channel_id=1, source_target_pairs={{0,2},{1,3},{226,224},{227,225},{4,6},{5,7},{230,228},{231,229},{8... | collective-permute-start | bytes 196616 | tf_op jit(solution)/shard_map/ppermute | solution.py:553
  30.4 2.2 %shard_map.108 = (f32[2,64,256]{2,1,0:T(8,128)S(1)}, f32[2,64,256]{2,1,0:T(8,128)S(1)}) custom-call(f32[2,2,8,32,128]{4,3,2,1,0:T(8,128)S(1)} %get-tuple-element.75.refs_0_.refs_2_.refs_5_, f32[2,2,8,32,128]{4,3,2,1,0:T(8,128)S(1)} %get-tuple-element.76.refs_1_.refs_3_.refs_6_, f32[2,32,128]{2,1,0:T(8,128)S(1)} %get-tuple-element.77.refs_2_.refs_6_.refs_9_, ...), custom_call_target="tpu_custom_call" | custom-call | flops 4000000000 | bytes 262144 | tf_op jit(solution)/shard_map/pallas_call | solution.py:653
  32.6 1.7 %collective-permute-start.10 = (f32[2,64,256]{2,1,0:T(8,128)S(1)}, f32[2,64,256]{2,1,0:T(8,128)S(1)}, u32[]{:S(2)}, u32[]{:S(2)}) collective-permute-start(f32[2,64,256]{2,1,0:T(8,128)S(1)} %get-tuple-element.105), channel_id=1, source_target_pairs={{0,2},{1,3},{226,224},{227,225},{4,6},{5,7},{230,228},{231,229},{8... | collective-permute-start | bytes 393224 | tf_op jit(solution)/shard_map/ppermute | solution.py:553
  34.4 1.5 %shard_map.109 = (f32[64,256]{1,0:T(8,128)S(1)}, f32[64,256]{1,0:T(8,128)S(1)}, f32[8,32,128]{2,1,0:T(8,128)S(1)}) custom-call(f32[64,256]{1,0:T(8,128)S(1)} %sub.15.v_ref.refs_0_.v0, bf16[256,256]{1,0:T(8,128)(2,1)S(1)} %get-tuple-element.89.refs_0_.refs_3_, bf16[512,256]{1,0:T(8,128)(2,1)S(1)} %get-tuple-element.78.refs_3_.refs_1_.refs_4_, ...), custom_call_target="tpu_custom_call" | custom-call | flops 2000000000 | bytes 262144 | tf_op jit(solution)/shard_map/pallas_call | solution.py:663
  37.1 1.8 %collective-permute-start.11 = (f32[2,64,256]{2,1,0:T(8,128)S(1)}, f32[2,64,256]{2,1,0:T(8,128)S(1)}, u32[]{:S(2)}, u32[]{:S(2)}) collective-permute-start(f32[2,64,256]{2,1,0:T(8,128)S(1)} %add.13.mine_ref.refs_1_), channel_id=1, source_target_pairs={{0,1},{1,0},{2,3},{3,2},{4,5},{5,4},{6,7},{7,6},{8,9},{9,8},{10,11... | collective-permute-start | bytes 393224 | tf_op jit(solution)/shard_map/ppermute | solution.py:557
  39.0 1.4 %shard_map.110.part_ref = f32[64,256]{1,0:T(8,128)S(1)} custom-call(f32[64,256]{1,0:T(8,128)S(1)} %sub.15.v_ref.refs_0_.v0, f32[64,256]{1,0:T(8,128)S(1)} %collective-permute-done.9.raw_ref, f32[64,256]{1,0:T(8,128)S(1)} %get-tuple-element.74.sent_ref, f32[64,256]{1,0:T(8,128)S(1)} %get-tuple-element.101.part_ref, ...), custom_call_target="tpu_custom_call" | custom-call | flops 2000000000 | bytes 262144 | tf_op jit(solution)/shard_map/pallas_call | solution.py:666
  40.8 1.5 %shard_map.112 = (f32[64,256]{1,0:T(8,128)S(1)}, f32[64,256]{1,0:T(8,128)S(1)}, f32[8,32,128]{2,1,0:T(8,128)S(1)}) custom-call(f32[64,256]{1,0:T(8,128)S(1)} %sub.16.v_ref.refs_0_.v1, bf16[256,256]{1,0:T(8,128)(2,1)S(1)} %get-tuple-element.89.refs_0_.refs_3_, bf16[512,256]{1,0:T(8,128)(2,1)S(1)} %get-tuple-element.78.refs_3_.refs_1_.refs_4_, ...), custom_call_target="tpu_custom_call" | custom-call | flops 2000000000 | bytes 262144 | tf_op jit(solution)/shard_map/pallas_call | solution.py:663
  42.3 2.2 %collective-permute-start.14 = (f32[64,256]{1,0:T(8,128)S(1)}, f32[64,256]{1,0:T(8,128)S(1)}, u32[]{:S(2)}, u32[]{:S(2)}) collective-permute-start(f32[64,256]{1,0:T(8,128)S(1)} %get-tuple-element.109.sent_ref), channel_id=1, source_target_pairs={{0,2},{1,3},{226,224},{227,225},{4,6},{5,7},{230,228},{231,229},{8... | collective-permute-start | bytes 196616 | tf_op jit(solution)/shard_map/ppermute | solution.py:553
  45.2 1.5 %shard_map.113 = f32[64,256]{1,0:T(8,128)S(1)} custom-call(f32[64,256]{1,0:T(8,128)S(1)} %sub.16.v_ref.refs_0_.v1, f32[64,256]{1,0:T(8,128)S(1)} %collective-permute-done.13.raw_ref, f32[64,256]{1,0:T(8,128)S(1)} %get-tuple-element.106.sent_ref, f32[64,256]{1,0:T(8,128)S(1)} %get-tuple-element.107.part_ref, f32[8,32,128]{2,1,0:T(8,128)S(1)} %get-tuple-element.108.gap_ref, ...), custom_call_target="tpu_custom_call" | custom-call | flops 2000000000 | bytes 262144 | tf_op jit(solution)/shard_map/pallas_call | solution.py:666
  46.9 1.5 %shard_map.114 = (f32[64,256]{1,0:T(8,128)S(1)}, f32[64,256]{1,0:T(8,128)S(1)}, f32[8,32,128]{2,1,0:T(8,128)S(1)}) custom-call(f32[64,256]{1,0:T(8,128)S(1)} %sub.17.v_ref.v2.refs_0_, bf16[256,256]{1,0:T(8,128)(2,1)S(1)} %get-tuple-element.89.refs_0_.refs_3_, bf16[512,256]{1,0:T(8,128)(2,1)S(1)} %get-tuple-element.78.refs_3_.refs_1_.refs_4_, ...), custom_call_target="tpu_custom_call" | custom-call | flops 2000000000 | bytes 262144 | tf_op jit(solution)/shard_map/pallas_call | solution.py:663
  48.3 1.7 %collective-permute-start.16 = (f32[64,256]{1,0:T(8,128)S(1)}, f32[64,256]{1,0:T(8,128)S(1)}, u32[]{:S(2)}, u32[]{:S(2)}) collective-permute-start(f32[64,256]{1,0:T(8,128)S(1)} %get-tuple-element.112.sent_ref), channel_id=1, source_target_pairs={{0,2},{1,3},{226,224},{227,225},{4,6},{5,7},{230,228},{231,229},{8... | collective-permute-start | bytes 196616 | tf_op jit(solution)/shard_map/ppermute | solution.py:553
  50.1 1.5 %shard_map.115 = f32[64,256]{1,0:T(8,128)S(1)} custom-call(f32[64,256]{1,0:T(8,128)S(1)} %sub.17.v_ref.v2.refs_0_, f32[64,256]{1,0:T(8,128)S(1)} %collective-permute-done.15.raw_ref, f32[64,256]{1,0:T(8,128)S(1)} %get-tuple-element.109.sent_ref, f32[64,256]{1,0:T(8,128)S(1)} %get-tuple-element.110.part_ref, f32[8,32,128]{2,1,0:T(8,128)S(1)} %get-tuple-element.111.gap_ref, ...), custom_call_target="tpu_custom_call" | custom-call | flops 2000000000 | bytes 262144 | tf_op jit(solution)/shard_map/pallas_call | solution.py:666
  51.8 1.5 %shard_map.117 = (f32[64,256]{1,0:T(8,128)S(1)}, f32[64,256]{1,0:T(8,128)S(1)}, f32[8,32,128]{2,1,0:T(8,128)S(1)}) custom-call(f32[64,256]{1,0:T(8,128)S(1)} %sub.18.v3.v_ref, bf16[256,256]{1,0:T(8,128)(2,1)S(1)} %get-tuple-element.89.refs_0_.refs_3_, bf16[512,256]{1,0:T(8,128)(2,1)S(1)} %get-tuple-element.78.refs_3_.refs_1_.refs_4_, ...), custom_call_target="tpu_custom_call" | custom-call | flops 2000000000 | bytes 262144 | tf_op jit(solution)/shard_map/pallas_call | solution.py:663
  53.3 1.5 %collective-permute-start.18 = (f32[64,256]{1,0:T(8,128)S(1)}, f32[64,256]{1,0:T(8,128)S(1)}, u32[]{:S(2)}, u32[]{:S(2)}) collective-permute-start(f32[64,256]{1,0:T(8,128)S(1)} %get-tuple-element.117), channel_id=1, source_target_pairs={{0,2},{1,3},{226,224},{227,225},{4,6},{5,7},{230,228},{231,229},{8... | collective-permute-start | bytes 196616 | tf_op jit(solution)/shard_map/ppermute | solution.py:553
  55.3 1.5 %shard_map.118 = f32[64,256]{1,0:T(8,128)S(1)} custom-call(f32[64,256]{1,0:T(8,128)S(1)} %sub.18.v3.v_ref, f32[64,256]{1,0:T(8,128)S(1)} %collective-permute-done.17.raw_ref, f32[64,256]{1,0:T(8,128)S(1)} %get-tuple-element.112.sent_ref, f32[64,256]{1,0:T(8,128)S(1)} %get-tuple-element.115.part_ref, f32[8,32,128]{2,1,0:T(8,128)S(1)} %get-tuple-element.116.gap_ref, ...), custom_call_target="tpu_custom_call" | custom-call | flops 2000000000 | bytes 262144 | tf_op jit(solution)/shard_map/pallas_call | solution.py:666
  57.7 2.6 %collective-permute-start.19 = (f32[1,128]{1,0:T(1,128)S(1)}, f32[1,128]{1,0:T(1,128)S(1)}, u32[]{:S(2)}, u32[]{:S(2)}) collective-permute-start(f32[1,128]{1,0:T(1,128)S(1)} %shard_map.119), channel_id=1, source_target_pairs={{0,1},{1,0},{2,3},{3,2},{4,5},{5,4},{6,7},{7,6},{8,9},{9,8},{10,11... | collective-permute-start | bytes 1544 | tf_op jit(solution)/shard_map/ppermute | solution.py:557
  61.1 1.8 %collective-permute-start.21 = (f32[3,64,128]{2,1,0:T(8,128)S(1)}, f32[3,64,128]{2,1,0:T(8,128)S(1)}, u32[]{:S(2)}, u32[]{:S(2)}) collective-permute-start(f32[3,64,128]{2,1,0:T(8,128)S(1)} %get-tuple-element.119), channel_id=1, source_target_pairs={{0,2},{1,3},{2,0},{3,1},{4,6},{5,7},{6,4},{7,5},{8,10},{9,11},{10,... | collective-permute-start | bytes 294920 | tf_op jit(solution)/shard_map/ppermute | solution.py:581
  63.1 17.9 %all_to_all.8 = f32[32,1,128]{2,1,0:T(1,128)S(1)} all-to-all(f32[32,1,128]{2,1,0:T(1,128)S(1)} %broadcast_in_dim.2), channel_id=1, replica_groups=mesh['sec'=32,'tile'=8] {'sec'}, dimensions={0} | all-to-all | bytes 32768 | tf_op jit(solution)/shard_map/all_to_all | solution.py:682
  82.3 1.8 %collective-permute-start.22 = (f32[2,32,64]{2,1,0:T(8,128)S(1)}, f32[2,32,64]{2,1,0:T(8,128)S(1)}, u32[]{:S(2)}, u32[]{:S(2)}) collective-permute-start(f32[2,32,64]{2,1,0:T(8,128)S(1)} %get-tuple-element.121), channel_id=1, source_target_pairs={{0,1},{1,0},{2,3},{3,2},{4,5},{5,4},{6,7},{7,6},{8,9},{9,8},{10,11... | collective-permute-start | bytes 49160 | tf_op jit(solution)/shard_map/ppermute | solution.py:557
  (52 shorter events, 11.8 us)
Async XLA Ops:
  2.3 11.5 %collective-permute-start.2 = (f32[264,128]{1,0:T(8,128)}, f32[264,128]{1,0:T(8,128)S(1)}, u32[]{:S(2)}, u32[]{:S(2)}) collective-permute-start(f32[264,128]{1,0:T(8,128)} %shard_map.104), channel_id=1, source_target_pairs={{0,230},{1,231},{2,0},{3,1},{4,226},{5,227},{6,4},{7,5},{8,238},{9... | collective-permute-start | bytes 405512 | tf_op jit(solution)/shard_map/ppermute | solution.py:568
  11.3 10.9 %collective-permute-start.3 = (f32[264,128]{1,0:T(8,128)}, f32[264,128]{1,0:T(8,128)S(1)}, u32[]{:S(2)}, u32[]{:S(2)}) collective-permute-start(f32[264,128]{1,0:T(8,128)} %shard_map.104), channel_id=1, source_target_pairs={{0,4},{1,5},{2,230},{3,231},{4,0},{5,1},{6,226},{7,227},{8,12},{9,... | collective-permute-start | bytes 405512 | tf_op jit(solution)/shard_map/ppermute | solution.py:568
  11.6 11.4 %collective-permute-start = (f32[264,128]{1,0:T(8,128)}, f32[264,128]{1,0:T(8,128)S(1)}, u32[]{:S(2)}, u32[]{:S(2)}) collective-permute-start(f32[264,128]{1,0:T(8,128)} %shard_map.104), channel_id=1, source_target_pairs={{0,226},{1,227},{2,4},{3,5},{4,230},{5,231},{6,0},{7,1},{8,234},{9... | collective-permute-start | bytes 405512 | tf_op jit(solution)/shard_map/ppermute | solution.py:568
  12.2 10.9 %collective-permute-start.1 = (f32[264,128]{1,0:T(8,128)}, f32[264,128]{1,0:T(8,128)S(1)}, u32[]{:S(2)}, u32[]{:S(2)}) collective-permute-start(f32[264,128]{1,0:T(8,128)} %shard_map.104), channel_id=1, source_target_pairs={{0,0},{1,1},{2,226},{3,227},{4,4},{5,5},{6,230},{7,231},{8,8},{9,9... | collective-permute-start | bytes 405512 | tf_op jit(solution)/shard_map/ppermute | solution.py:568
  13.8 10.2 %collective-permute-start.6 = (f32[264,128]{1,0:T(8,128)S(1)}, f32[264,128]{1,0:T(8,128)S(1)}, u32[]{:S(2)}, u32[]{:S(2)}) collective-permute-start(f32[264,128]{1,0:T(8,128)S(1)} %collective-permute-done.2.refs_0_), channel_id=1, source_target_pairs={{0,1},{1,0},{2,3},{3,2},{4,5},{5,4},{6,7},{7,6},{8,9},{9,8},{10,11... | collective-permute-start | bytes 405512 | tf_op jit(solution)/shard_map/ppermute | solution.py:557
  22.2 1.9 %collective-permute-start.7 = (f32[264,128]{1,0:T(8,128)S(1)}, f32[264,128]{1,0:T(8,128)S(1)}, u32[]{:S(2)}, u32[]{:S(2)}) collective-permute-start(f32[264,128]{1,0:T(8,128)S(1)} %collective-permute-done.3.refs_1_), channel_id=1, source_target_pairs={{0,1},{1,0},{2,3},{3,2},{4,5},{5,4},{6,7},{7,6},{8,9},{9,8},{10,11... | collective-permute-start | bytes 405512 | tf_op jit(solution)/shard_map/ppermute | solution.py:557
  23.1 2.6 %collective-permute-start.4 = (f32[264,128]{1,0:T(8,128)S(1)}, f32[264,128]{1,0:T(8,128)S(1)}, u32[]{:S(2)}, u32[]{:S(2)}) collective-permute-start(f32[264,128]{1,0:T(8,128)S(1)} %collective-permute-done.refs_2_), channel_id=1, source_target_pairs={{0,1},{1,0},{2,3},{3,2},{4,5},{5,4},{6,7},{7,6},{8,9},{9,8},{10,11... | collective-permute-start | bytes 405512 | tf_op jit(solution)/shard_map/ppermute | solution.py:557
  24.1 1.6 %collective-permute-start.5 = (f32[264,128]{1,0:T(8,128)S(1)}, f32[264,128]{1,0:T(8,128)S(1)}, u32[]{:S(2)}, u32[]{:S(2)}) collective-permute-start(f32[264,128]{1,0:T(8,128)S(1)} %collective-permute-done.1.refs_3_), channel_id=1, source_target_pairs={{0,1},{1,0},{2,3},{3,2},{4,5},{5,4},{6,7},{7,6},{8,9},{9,8},{10,11... | collective-permute-start | bytes 405512 | tf_op jit(solution)/shard_map/ppermute | solution.py:557
  26.6 6.0 %collective-permute-start.8 = (f32[64,256]{1,0:T(8,128)S(1)}, f32[64,256]{1,0:T(8,128)S(1)}, u32[]{:S(2)}, u32[]{:S(2)}) collective-permute-start(f32[64,256]{1,0:T(8,128)S(1)} %get-tuple-element.74.sent_ref), channel_id=1, source_target_pairs={{0,2},{1,3},{226,224},{227,225},{4,6},{5,7},{230,228},{231,229},{8... | collective-permute-start | bytes 196616 | tf_op jit(solution)/shard_map/ppermute | solution.py:553
  30.4 8.6 %collective-permute-start.9 = (f32[64,256]{1,0:T(8,128)S(1)}, f32[64,256]{1,0:T(8,128)S(1)}, u32[]{:S(2)}, u32[]{:S(2)}) collective-permute-start(f32[64,256]{1,0:T(8,128)S(1)} %get-tuple-element.73), channel_id=1, source_target_pairs={{0,8},{1,9},{226,234},{227,235},{4,12},{5,13},{230,238},{231,239},... | collective-permute-start | bytes 196616 | tf_op jit(solution)/shard_map/ppermute | solution.py:553
  32.6 4.5 %collective-permute-start.10 = (f32[2,64,256]{2,1,0:T(8,128)S(1)}, f32[2,64,256]{2,1,0:T(8,128)S(1)}, u32[]{:S(2)}, u32[]{:S(2)}) collective-permute-start(f32[2,64,256]{2,1,0:T(8,128)S(1)} %get-tuple-element.105), channel_id=1, source_target_pairs={{0,2},{1,3},{226,224},{227,225},{4,6},{5,7},{230,228},{231,229},{8... | collective-permute-start | bytes 393224 | tf_op jit(solution)/shard_map/ppermute | solution.py:553
  35.8 4.9 %collective-permute-start.12 = (f32[64,256]{1,0:T(8,128)S(1)}, f32[64,256]{1,0:T(8,128)S(1)}, u32[]{:S(2)}, u32[]{:S(2)}) collective-permute-start(f32[64,256]{1,0:T(8,128)S(1)} %get-tuple-element.106.sent_ref), channel_id=1, source_target_pairs={{0,2},{1,3},{226,224},{227,225},{4,6},{5,7},{230,228},{231,229},{8... | collective-permute-start | bytes 196616 | tf_op jit(solution)/shard_map/ppermute | solution.py:553
  37.1 3.3 %collective-permute-start.11 = (f32[2,64,256]{2,1,0:T(8,128)S(1)}, f32[2,64,256]{2,1,0:T(8,128)S(1)}, u32[]{:S(2)}, u32[]{:S(2)}) collective-permute-start(f32[2,64,256]{2,1,0:T(8,128)S(1)} %add.13.mine_ref.refs_1_), channel_id=1, source_target_pairs={{0,1},{1,0},{2,3},{3,2},{4,5},{5,4},{6,7},{7,6},{8,9},{9,8},{10,11... | collective-permute-start | bytes 393224 | tf_op jit(solution)/shard_map/ppermute | solution.py:557
  40.5 4.7 %collective-permute-start.13 = (f32[64,256]{1,0:T(8,128)S(1)}, f32[64,256]{1,0:T(8,128)S(1)}, u32[]{:S(2)}, u32[]{:S(2)}) collective-permute-start(f32[64,256]{1,0:T(8,128)S(1)} %shard_map.111), channel_id=1, source_target_pairs={{0,8},{1,9},{226,234},{227,235},{4,12},{5,13},{230,238},{231,239},... | collective-permute-start | bytes 196616 | tf_op jit(solution)/shard_map/ppermute | solution.py:553
  42.3 4.6 %collective-permute-start.14 = (f32[64,256]{1,0:T(8,128)S(1)}, f32[64,256]{1,0:T(8,128)S(1)}, u32[]{:S(2)}, u32[]{:S(2)}) collective-permute-start(f32[64,256]{1,0:T(8,128)S(1)} %get-tuple-element.109.sent_ref), channel_id=1, source_target_pairs={{0,2},{1,3},{226,224},{227,225},{4,6},{5,7},{230,228},{231,229},{8... | collective-permute-start | bytes 196616 | tf_op jit(solution)/shard_map/ppermute | solution.py:553
  46.7 3.4 %collective-permute-start.15 = (f32[64,256]{1,0:T(8,128)S(1)}, f32[64,256]{1,0:T(8,128)S(1)}, u32[]{:S(2)}, u32[]{:S(2)}) collective-permute-start(f32[64,256]{1,0:T(8,128)S(1)} %shard_map.113), channel_id=1, source_target_pairs={{0,8},{1,9},{226,234},{227,235},{4,12},{5,13},{230,238},{231,239},... | collective-permute-start | bytes 196616 | tf_op jit(solution)/shard_map/ppermute | solution.py:553
  48.3 3.4 %collective-permute-start.16 = (f32[64,256]{1,0:T(8,128)S(1)}, f32[64,256]{1,0:T(8,128)S(1)}, u32[]{:S(2)}, u32[]{:S(2)}) collective-permute-start(f32[64,256]{1,0:T(8,128)S(1)} %get-tuple-element.112.sent_ref), channel_id=1, source_target_pairs={{0,2},{1,3},{226,224},{227,225},{4,6},{5,7},{230,228},{231,229},{8... | collective-permute-start | bytes 196616 | tf_op jit(solution)/shard_map/ppermute | solution.py:553
  51.6 3.8 %collective-permute-start.17 = (f32[64,256]{1,0:T(8,128)S(1)}, f32[64,256]{1,0:T(8,128)S(1)}, u32[]{:S(2)}, u32[]{:S(2)}) collective-permute-start(f32[64,256]{1,0:T(8,128)S(1)} %shard_map.115), channel_id=1, source_target_pairs={{0,8},{1,9},{226,234},{227,235},{4,12},{5,13},{230,238},{231,239},... | collective-permute-start | bytes 196616 | tf_op jit(solution)/shard_map/ppermute | solution.py:553
  53.3 3.6 %collective-permute-start.18 = (f32[64,256]{1,0:T(8,128)S(1)}, f32[64,256]{1,0:T(8,128)S(1)}, u32[]{:S(2)}, u32[]{:S(2)}) collective-permute-start(f32[64,256]{1,0:T(8,128)S(1)} %get-tuple-element.117), channel_id=1, source_target_pairs={{0,2},{1,3},{226,224},{227,225},{4,6},{5,7},{230,228},{231,229},{8... | collective-permute-start | bytes 196616 | tf_op jit(solution)/shard_map/ppermute | solution.py:553
  57.7 5.2 %collective-permute-start.19 = (f32[1,128]{1,0:T(1,128)S(1)}, f32[1,128]{1,0:T(1,128)S(1)}, u32[]{:S(2)}, u32[]{:S(2)}) collective-permute-start(f32[1,128]{1,0:T(1,128)S(1)} %shard_map.119), channel_id=1, source_target_pairs={{0,1},{1,0},{2,3},{3,2},{4,5},{5,4},{6,7},{7,6},{8,9},{9,8},{10,11... | collective-permute-start | bytes 1544 | tf_op jit(solution)/shard_map/ppermute | solution.py:557
  60.4 20.5 %collective-permute-start.20 = (f32[3,64,128]{2,1,0:T(8,128)S(1)}, f32[3,64,128]{2,1,0:T(8,128)S(1)}, u32[]{:S(2)}, u32[]{:S(2)}) collective-permute-start(f32[3,64,128]{2,1,0:T(8,128)S(1)} %get-tuple-element.118), channel_id=1, source_target_pairs={{0,0},{1,1},{2,2},{3,3},{4,4},{5,5},{6,6},{7,7},{8,8},{9,9},{10,10... | collective-permute-start | bytes 294920 | tf_op jit(solution)/shard_map/ppermute | solution.py:581
  61.1 19.9 %collective-permute-start.21 = (f32[3,64,128]{2,1,0:T(8,128)S(1)}, f32[3,64,128]{2,1,0:T(8,128)S(1)}, u32[]{:S(2)}, u32[]{:S(2)}) collective-permute-start(f32[3,64,128]{2,1,0:T(8,128)S(1)} %get-tuple-element.119), channel_id=1, source_target_pairs={{0,2},{1,3},{2,0},{3,1},{4,6},{5,7},{6,4},{7,5},{8,10},{9,11},{10,... | collective-permute-start | bytes 294920 | tf_op jit(solution)/shard_map/ppermute | solution.py:581
  82.3 2.7 %collective-permute-start.22 = (f32[2,32,64]{2,1,0:T(8,128)S(1)}, f32[2,32,64]{2,1,0:T(8,128)S(1)}, u32[]{:S(2)}, u32[]{:S(2)}) collective-permute-start(f32[2,32,64]{2,1,0:T(8,128)S(1)} %get-tuple-element.121), channel_id=1, source_target_pairs={{0,1},{1,0},{2,3},{3,2},{4,5},{5,4},{6,7},{7,6},{8,9},{9,8},{10,11... | collective-permute-start | bytes 49160 | tf_op jit(solution)/shard_map/ppermute | solution.py:557
